TPU v7x, 32 devices: a whole 2x2x4 slice. The times are simulated.
32 devices in a mesh: dp: 8 (over z, core), mp: 4 (over y, x).
Axes of the slice: x: 2, y: 2, z: 4, core: 2. Of those that a mesh axis runs over, the one named last changes fastest.
Arguments:
- frames_in: bfloat16 [16, 1024, 1536], P('dp', 'mp'), may hold values from -6 to 6
- prompt: bfloat16 [16, 128, 768], P('dp'), may hold values from -6 to 6
- lengths: int32 [16], P('dp'), may hold values from 4 to 128, as said below
- tsteps: int32 [16], P('dp'), may hold values from 0 to 999
- table: float32 [1000, 1536], replicated, may hold values from -6 to 6
- gain_one: float32 [1536], replicated, may hold values from 0.25 to 1.75
- shift_one: float32 [1536], replicated, may hold values from -2 to 2
- gain_two: float32 [1536], replicated, may hold values from 0.25 to 1.75
- shift_two: float32 [1536], replicated, may hold values from -2 to 2
- gain_three: float32 [1536], replicated, may hold values from 0.25 to 1.75
- shift_three: float32 [1536], replicated, may hold values from -2 to 2
- w_query: bfloat16 [1536, 1536], P(None, 'mp'), may hold values from -0.15625 to 0.15625
- w_key: bfloat16 [1536, 1536], P(None, 'mp'), may hold values from -0.15625 to 0.15625
- w_value: bfloat16 [1536, 1536], P(None, 'mp'), may hold values from -0.15625 to 0.15625
- w_out: bfloat16 [1536, 1536], P('mp'), may hold values from -2.5 to 2.5
- c_query: bfloat16 [1536, 1536], P(None, 'mp'), may hold values from -0.15625 to 0.15625
- c_key: bfloat16 [768, 1536], P(None, 'mp'), may hold values from -0.21875 to 0.21875
- c_value: bfloat16 [768, 1536], P(None, 'mp'), may hold values from -0.21875 to 0.21875
- c_out: bfloat16 [1536, 1536], P('mp'), may hold values from -0.75 to 0.75
- w_gate: bfloat16 [1536, 6144], P(None, 'mp'), may hold values from -0.15625 to 0.15625
- w_up: bfloat16 [1536, 6144], P(None, 'mp'), may hold values from -0.15625 to 0.15625
- w_down: bfloat16 [6144, 1536], P('mp'), may hold values from -0.078125 to 0.078125
- cotangent: bfloat16 [16, 1024, 1536], P('dp', 'mp'), may hold values from -6 to 6
Outputs:
- output: float32 [16, 1024, 1536], P('dp', 'mp')
- grad_frames: float32 [16, 1024, 1536], P('dp', 'mp')
- grad_table: float32 [1000, 1536], replicated
- grad_gain_one: float32 [1536], replicated
- grad_shift_one: float32 [1536], replicated
- grad_gain_two: float32 [1536], replicated
- grad_shift_two: float32 [1536], replicated
- grad_gain_three: float32 [1536], replicated
- grad_shift_three: float32 [1536], replicated
- grad_w_query: float32 [1536, 1536], P('dp', 'mp')
- grad_w_key: float32 [1536, 1536], P('dp', 'mp')
- grad_w_value: float32 [1536, 1536], P('dp', 'mp')
- grad_w_out: float32 [1536, 1536], P('mp', 'dp')
- grad_c_query: float32 [1536, 1536], P('dp', 'mp')
- grad_c_key: float32 [768, 1536], P('dp', 'mp')
- grad_c_value: float32 [768, 1536], P('dp', 'mp')
- grad_c_out: float32 [1536, 1536], P('mp', 'dp')
- grad_w_gate: float32 [1536, 6144], P('dp', 'mp')
- grad_w_up: float32 [1536, 6144], P('dp', 'mp')
- grad_w_down: float32 [6144, 1536], P('mp', 'dp')
Inputs may be any that keep to these rules, and one draw needn't show every extreme that they name: lengths: some clip has all 128 prompt tokens live and another has 4.
All inputs are finite; a program needn't handle non-finite values.
Results may differ from a plain program's by a relative error of at most 0.025.
Values may be sent and summed in bfloat16 or wider, within the bound.
No kernel may reach another device: no remote copies, remote signals or barrier semaphores. Data moves between devices by JAX's collectives and lax.ppermute only.
A program may use at most 384 MiB of HBM per device.

v0:
```python
import math

import jax
import jax.numpy as jnp
from jax import lax
from jax.sharding import PartitionSpec as P

HEAD_DIM = 64


norm_eps = 1e-05


def product(form, left, right):
    return jnp.einsum(form, left, right, preferred_element_type=jnp.float32)


def norm_forward(values, gain, shift):
    center = values - jnp.mean(values, axis=-1, keepdims=True)
    scale = lax.rsqrt(jnp.mean(center * center, axis=-1, keepdims=True) + norm_eps)
    normal = center * scale
    return (normal * gain + shift, normal, scale)


def norm_backward(grad, normal, scale, gain):
    inner = grad * gain
    return scale * (
        inner
        - jnp.mean(inner, axis=-1, keepdims=True)
        - normal * jnp.mean(inner * normal, axis=-1, keepdims=True)
    )


def turning(count, start):
    half = HEAD_DIM // 2
    places = (jnp.arange(count) + start).astype(jnp.float32)
    rates = jnp.exp(jnp.arange(half).astype(jnp.float32) * (-2.0 * math.log(10000.0) / HEAD_DIM))
    angles = places[:, None] * rates[None, :]
    return (jnp.cos(angles), jnp.sin(angles))


def rotate(values, cosine, sine):
    half = values.shape[-1] // 2
    first_half = values[..., :half]
    second_half = values[..., half:]
    cosine = cosine[:, None, :]
    sine = sine[:, None, :]
    return jnp.concatenate(
        [first_half * cosine - second_half * sine, second_half * cosine + first_half * sine],
        axis=-1,
    )


def split_heads(values):
    return values.reshape(values.shape[:-1] + (values.shape[-1] // HEAD_DIM, HEAD_DIM))


def join_heads(values):
    return values.reshape(values.shape[:-2] + (values.shape[-2] * values.shape[-1],))


def spread_rows(rows):
    return lax.all_gather(rows.astype(jnp.bfloat16), "mp", axis=1, tiled=True)


def spread_grads(grads):
    return lax.all_gather(grads.astype(jnp.bfloat16), "mp", axis=1, tiled=True)


def settle_branch(partial_value):
    return lax.psum_scatter(partial_value, "mp", scatter_dimension=1, tiled=True)


def settle_input(partial_value):
    return lax.psum_scatter(partial_value, "mp", scatter_dimension=1, tiled=True)


def self_scores(queries, keys, prefix_keys, factor):
    scores = product("bqhd,bkhd->bhqk", queries, keys) * factor
    front = product("bqhd,bhd->bhq", queries, prefix_keys) * factor
    return (scores, front)


def cross_scores(cross_query, cross_key, live, factor):
    scores = product("bqhd,bkhd->bhqk", cross_query, cross_key) * factor
    return jnp.where(live, scores, -1e30)


def shards(
    frames_in,
    prompt,
    lengths,
    tsteps,
    table,
    gain_one,
    shift_one,
    gain_two,
    shift_two,
    gain_three,
    shift_three,
    w_query,
    w_key,
    w_value,
    w_out,
    c_query,
    c_key,
    c_value,
    c_out,
    w_gate,
    w_up,
    w_down,
    cotangent,
):
    frames = frames_in.shape[1] * lax.axis_size("mp")
    prompt_len = prompt.shape[1]
    factor = 1.0 / math.sqrt(HEAD_DIM)
    cosine, sine = turning(frames, 1)
    resid_in = frames_in.astype(jnp.float32)
    normed_one, normal_one, scale_one = norm_forward(resid_in, gain_one, shift_one)
    whole_one = spread_rows(normed_one)
    picked = jnp.take(table, tsteps, axis=0)
    prefix_normed, prefix_normal, prefix_scale = norm_forward(picked, gain_one, shift_one)
    prefix_low = prefix_normed.astype(jnp.bfloat16)
    queries = rotate(split_heads(product("bfd,dc->bfc", whole_one, w_query)), cosine, sine).astype(
        jnp.bfloat16
    )
    keys = rotate(split_heads(product("bfd,dc->bfc", whole_one, w_key)), cosine, sine).astype(
        jnp.bfloat16
    )
    values = split_heads(product("bfd,dc->bfc", whole_one, w_value)).astype(jnp.bfloat16)
    prefix_keys = split_heads(product("bd,dc->bc", prefix_low, w_key)).astype(jnp.bfloat16)
    prefix_values = split_heads(product("bd,dc->bc", prefix_low, w_value)).astype(jnp.bfloat16)
    scores, front = self_scores(queries, keys, prefix_keys, factor)
    top = jnp.maximum(jnp.max(scores, axis=-1), front)
    weights = jnp.exp(scores - top[..., None])
    front_weight = jnp.exp(front - top)
    total = jnp.sum(weights, axis=-1) + front_weight
    logsum = top + jnp.log(total)
    mixed = product("bhqk,bkhd->bqhd", (weights / total[..., None]).astype(jnp.bfloat16), values)
    mixed = mixed + product(
        "bhq,bhd->bqhd", (front_weight / total).astype(jnp.bfloat16), prefix_values
    )
    mixed_low = join_heads(mixed).astype(jnp.bfloat16)
    first = resid_in + settle_branch(product("bfc,cd->bfd", mixed_low, w_out))
    normed_two, normal_two, scale_two = norm_forward(first, gain_two, shift_two)
    whole_two = spread_rows(normed_two)
    cross_query = split_heads(product("bfd,dc->bfc", whole_two, c_query)).astype(jnp.bfloat16)
    cross_key = split_heads(product("bpt,tc->bpc", prompt, c_key)).astype(jnp.bfloat16)
    cross_value = split_heads(product("bpt,tc->bpc", prompt, c_value)).astype(jnp.bfloat16)
    live = (jnp.arange(prompt_len)[None, :] < lengths[:, None])[:, None, None, :]
    cross_s = cross_scores(cross_query, cross_key, live, factor)
    cross_top = jnp.max(cross_s, axis=-1, keepdims=True)
    cross_weight = jnp.exp(cross_s - cross_top)
    cross_total = jnp.sum(cross_weight, axis=-1, keepdims=True)
    cross_log = cross_top + jnp.log(cross_total)
    cross_probs = (cross_weight / cross_total).astype(jnp.bfloat16)
    cross_mixed = join_heads(product("bhqk,bkhd->bqhd", cross_probs, cross_value)).astype(
        jnp.bfloat16
    )
    second = first + settle_branch(product("bfc,cd->bfd", cross_mixed, c_out))
    normed_three, normal_three, scale_three = norm_forward(second, gain_three, shift_three)
    whole_three = spread_rows(normed_three)
    gate = product("bfd,dh->bfh", whole_three, w_gate)
    upper = product("bfd,dh->bfh", whole_three, w_up)
    sigma = jax.nn.sigmoid(gate)
    hidden = (gate * sigma * upper).astype(jnp.bfloat16)
    output = second + settle_branch(product("bfh,hd->bfd", hidden, w_down))
    grad_three = cotangent.astype(jnp.float32)
    down_in = spread_grads(grad_three)
    grad_w_down = product("bfh,bfd->hd", hidden, down_in)
    grad_hidden = product("bfd,hd->bfh", down_in, w_down)
    grad_gate = (grad_hidden * upper * sigma * (1.0 + gate * (1.0 - sigma))).astype(jnp.bfloat16)
    grad_upper = (grad_hidden * gate * sigma).astype(jnp.bfloat16)
    grad_w_gate = product("bfd,bfh->dh", whole_three, grad_gate)
    grad_w_up = product("bfd,bfh->dh", whole_three, grad_upper)
    back_three = settle_input(
        product("bfh,dh->bfd", grad_gate, w_gate) + product("bfh,dh->bfd", grad_upper, w_up)
    )
    grad_two = grad_three + norm_backward(back_three, normal_three, scale_three, gain_three)
    gain_three_term = jnp.sum(back_three * normal_three, axis=(0, 1))
    shift_three_term = jnp.sum(back_three, axis=(0, 1))
    cross_in = spread_grads(grad_two)
    grad_c_out = product("bfc,bfd->cd", cross_mixed, cross_in)
    grad_cross_mixed = split_heads(product("bfd,cd->bfc", cross_in, c_out)).astype(jnp.bfloat16)
    cross_p = jnp.exp(cross_scores(cross_query, cross_key, live, factor) - cross_log)
    cross_gp = product("bqhd,bkhd->bhqk", grad_cross_mixed, cross_value)
    cross_ds = (cross_p * (cross_gp - jnp.sum(cross_p * cross_gp, axis=-1, keepdims=True))).astype(
        jnp.bfloat16
    )
    grad_cross_query = (product("bhqk,bkhd->bqhd", cross_ds, cross_key) * factor).astype(
        jnp.bfloat16
    )
    grad_cross_key = (product("bhqk,bqhd->bkhd", cross_ds, cross_query) * factor).astype(
        jnp.bfloat16
    )
    grad_cross_value = product(
        "bhqk,bqhd->bkhd", cross_p.astype(jnp.bfloat16), grad_cross_mixed
    ).astype(jnp.bfloat16)
    grad_c_query = product("bfd,bfc->dc", whole_two, join_heads(grad_cross_query))
    grad_c_key = product("bpt,bpc->tc", prompt, join_heads(grad_cross_key))
    grad_c_value = product("bpt,bpc->tc", prompt, join_heads(grad_cross_value))
    back_two = settle_input(product("bfc,dc->bfd", join_heads(grad_cross_query), c_query))
    grad_one = grad_two + norm_backward(back_two, normal_two, scale_two, gain_two)
    gain_two_term = jnp.sum(back_two * normal_two, axis=(0, 1))
    shift_two_term = jnp.sum(back_two, axis=(0, 1))
    self_in = spread_grads(grad_one)
    grad_w_out = product("bfc,bfd->cd", mixed_low, self_in)
    grad_mixed = split_heads(product("bfd,cd->bfc", self_in, w_out)).astype(jnp.bfloat16)
    scores, front = self_scores(queries, keys, prefix_keys, factor)
    probs = jnp.exp(scores - logsum[..., None])
    front_probs = jnp.exp(front - logsum)
    grad_probs = product("bqhd,bkhd->bhqk", grad_mixed, values)
    grad_front = product("bqhd,bhd->bhq", grad_mixed, prefix_values)
    mixsum = jnp.sum(probs * grad_probs, axis=-1) + front_probs * grad_front
    grad_scores = (probs * (grad_probs - mixsum[..., None])).astype(jnp.bfloat16)
    grad_front_scores = (front_probs * (grad_front - mixsum)).astype(jnp.bfloat16)
    grad_vals = product("bhqk,bqhd->bkhd", probs.astype(jnp.bfloat16), grad_mixed)
    grad_prefix_vals = product("bhq,bqhd->bhd", front_probs.astype(jnp.bfloat16), grad_mixed)
    grad_turned_q = (
        product("bhqk,bkhd->bqhd", grad_scores, keys)
        + product("bhq,bhd->bqhd", grad_front_scores, prefix_keys)
    ) * factor
    grad_turned_k = product("bhqk,bqhd->bkhd", grad_scores, queries) * factor
    grad_prefix_keys = product("bhq,bqhd->bhd", grad_front_scores, queries) * factor
    grad_queries = join_heads(rotate(grad_turned_q, cosine, -sine)).astype(jnp.bfloat16)
    grad_keys = join_heads(rotate(grad_turned_k, cosine, -sine)).astype(jnp.bfloat16)
    grad_values = join_heads(grad_vals).astype(jnp.bfloat16)
    grad_pkeys = join_heads(grad_prefix_keys).astype(jnp.bfloat16)
    grad_pvalues = join_heads(grad_prefix_vals).astype(jnp.bfloat16)
    grad_w_query = product("bfd,bfc->dc", whole_one, grad_queries)
    grad_w_key = product("bfd,bfc->dc", whole_one, grad_keys) + product(
        "bd,bc->dc", prefix_low, grad_pkeys
    )
    grad_w_value = product("bfd,bfc->dc", whole_one, grad_values) + product(
        "bd,bc->dc", prefix_low, grad_pvalues
    )
    results = (
        lax.psum_scatter(
            grad_w_query.astype(jnp.bfloat16), "dp", scatter_dimension=0, tiled=True
        ).astype(jnp.float32),
        lax.psum_scatter(
            grad_w_key.astype(jnp.bfloat16), "dp", scatter_dimension=0, tiled=True
        ).astype(jnp.float32),
        lax.psum_scatter(
            grad_w_value.astype(jnp.bfloat16), "dp", scatter_dimension=0, tiled=True
        ).astype(jnp.float32),
        lax.psum_scatter(
            grad_w_out.astype(jnp.bfloat16), "dp", scatter_dimension=1, tiled=True
        ).astype(jnp.float32),
        lax.psum_scatter(
            grad_c_query.astype(jnp.bfloat16), "dp", scatter_dimension=0, tiled=True
        ).astype(jnp.float32),
        lax.psum_scatter(
            grad_c_key.astype(jnp.bfloat16), "dp", scatter_dimension=0, tiled=True
        ).astype(jnp.float32),
        lax.psum_scatter(
            grad_c_value.astype(jnp.bfloat16), "dp", scatter_dimension=0, tiled=True
        ).astype(jnp.float32),
        lax.psum_scatter(
            grad_c_out.astype(jnp.bfloat16), "dp", scatter_dimension=1, tiled=True
        ).astype(jnp.float32),
        lax.psum_scatter(
            grad_w_gate.astype(jnp.bfloat16), "dp", scatter_dimension=0, tiled=True
        ).astype(jnp.float32),
        lax.psum_scatter(
            grad_w_up.astype(jnp.bfloat16), "dp", scatter_dimension=0, tiled=True
        ).astype(jnp.float32),
        lax.psum_scatter(
            grad_w_down.astype(jnp.bfloat16), "dp", scatter_dimension=1, tiled=True
        ).astype(jnp.float32),
    )
    back_one = settle_input(
        product("bfc,dc->bfd", grad_queries, w_query)
        + product("bfc,dc->bfd", grad_keys, w_key)
        + product("bfc,dc->bfd", grad_values, w_value)
    )
    grad_frames = grad_one + norm_backward(back_one, normal_one, scale_one, gain_one)
    back_prefix = product("bc,dc->bd", grad_pkeys, w_key) + product(
        "bc,dc->bd", grad_pvalues, w_value
    )
    grad_picked = norm_backward(back_prefix, prefix_normal, prefix_scale, gain_one)
    gain_one_term = jnp.sum(back_one * normal_one, axis=(0, 1)) + jnp.sum(
        back_prefix * prefix_normal, axis=0
    )
    shift_one_term = jnp.sum(back_one, axis=(0, 1)) + jnp.sum(back_prefix, axis=0)
    stacked = jnp.stack(
        [
            gain_one_term,
            shift_one_term,
            gain_two_term,
            shift_two_term,
            gain_three_term,
            shift_three_term,
        ]
    )
    matches = tsteps[:, None] == jnp.arange(table.shape[0])[None, :]
    table_term = jnp.sum(jnp.where(matches[:, :, None], grad_picked[:, None, :], 0.0), axis=0)
    summed_small, summed_table = lax.psum((stacked, table_term), ("dp", "mp"))
    return (
        output,
        grad_frames,
        summed_table,
        summed_small[0],
        summed_small[1],
        summed_small[2],
        summed_small[3],
        summed_small[4],
        summed_small[5],
        results[0],
        results[1],
        results[2],
        results[3],
        results[4],
        results[5],
        results[6],
        results[7],
        results[8],
        results[9],
        results[10],
    )


def solution(mesh):
    placed = (
        P("dp", "mp", None),
        P("dp", None, None),
        P("dp"),
        P("dp"),
        P(),
        P(),
        P(),
        P(),
        P(),
        P(),
        P(),
        P(None, "mp"),
        P(None, "mp"),
        P(None, "mp"),
        P("mp", None),
        P(None, "mp"),
        P(None, "mp"),
        P(None, "mp"),
        P("mp", None),
        P(None, "mp"),
        P(None, "mp"),
        P("mp", None),
        P("dp", "mp", None),
    )
    return jax.shard_map(
        shards,
        mesh=mesh,
        in_specs=placed,
        out_specs=(
            P("dp", "mp", None),
            P("dp", "mp", None),
            P(),
            P(),
            P(),
            P(),
            P(),
            P(),
            P(),
            P("dp", "mp"),
            P("dp", "mp"),
            P("dp", "mp"),
            P("mp", "dp"),
            P("dp", "mp"),
            P("dp", "mp"),
            P("dp", "mp"),
            P("mp", "dp"),
            P("dp", "mp"),
            P("dp", "mp"),
            P("mp", "dp"),
        ),
        check_vma=False,
    )
```

profile of v0, /device:TPU:0, one launch (start us, length us, event | category | flops | bytes accessed | tf_op | source)
XLA Modules:
  0.0 1992.2 jit_solution(10489696362126786158)
XLA Ops:
  21.3 64.7 %all-gather.7.cloned.1.call-done = bf16[2,1024,1536]{2,1,0:T(8,128)(2,1)} async-done(((bf16[2,256,1536]{2,1,0:T(8,128)(2,1)}), bf16[2,1024,1536]{2,1,0:T(8,128)(2,1)}) %all-gather.7.cloned.1.call-update) | async-done | bytes 6291472 | tf_op jit(solution)/shard_map/all_gather | solution.py:63
  98.8 21.5 %multiply_reduce_fusion.1 = (f32[2,6,1024]{2,1,0:T(8,128)}, f32[2,6,1024,1024]{2,3,1,0:T(8,128)}) fusion(bf16[2,1024,6,32]{1,3,2,0:T(8,128)(2,1)} %get-tuple-element.151, bf16[2,1024,6,32]{1,3,2,0:T(8,128)(2,1)} %get-tuple-element.152, bf16[2,1024,6,32]{1,3,2,0:T(8,128)(2,1)} %copy-done.16, bf16[2,1024,6,32]{1,3,2,0:T(8,128)(2,1)S(1)} %get-tuple-element.144), kind=kOutput, calls=%fused_computation.7 | convolution fusion | flops 1642057728 | bytes 53526528 | tf_op jit(solution)/shard_map/bqhd,bkhd->bhqk/dot_general | solution.py:15
  121.2 20.0 %fusion = f32[2,6,1024]{2,1,0:T(8,128)S(1)} fusion(f32[2,6,1024,1024]{2,3,1,0:T(8,128)} %get-tuple-element.158, f32[2,6,1024]{2,1,0:T(8,128)S(1)} %fusion.82), kind=kLoop, calls=%fused_computation.6 | loop fusion | flops 37736448 | bytes 50429952 | tf_op jit(solution)/shard_map/reduce_sum | solution.py:137
  147.3 19.6 add_convert_fusion.2
  168.1 6.3 fusion.57
  174.4 120.8 %reduce-scatter.22.cloned.1.call-done = f32[2,256,1536]{2,1,0:T(8,128)} async-done(((f32[2,1024,1536]{2,1,0:T(8,128)}), f32[2,256,1536]{2,1,0:T(8,128)}) %reduce-scatter.22.cloned.1.call-update) | async-done | bytes 3145744 | tf_op jit(solution)/shard_map/reduce_scatter | solution.py:71
  305.1 66.8 %all-gather.9.cloned.1.call-done = bf16[2,1024,1536]{2,1,0:T(8,128)(2,1)} async-done(((bf16[2,256,1536]{2,1,0:T(8,128)(2,1)}), bf16[2,1024,1536]{2,1,0:T(8,128)(2,1)}) %all-gather.9.cloned.1.call-update) | async-done | bytes 6291472 | tf_op jit(solution)/shard_map/all_gather | solution.py:63
  383.8 6.3 fusion.51
  390.2 120.8 %reduce-scatter.24.cloned.1.call-done = f32[2,256,1536]{2,1,0:T(8,128)} async-done(((f32[2,1024,1536]{2,1,0:T(8,128)}), f32[2,256,1536]{2,1,0:T(8,128)}) %reduce-scatter.24.cloned.1.call-update) | async-done | bytes 3145744 | tf_op jit(solution)/shard_map/reduce_scatter | solution.py:71
  518.5 69.5 %all-gather.11.cloned.1.call-done = bf16[2,1024,1536]{2,1,0:T(8,128)(2,1)} async-done(((bf16[2,256,1536]{2,1,0:T(8,128)(2,1)}), bf16[2,1024,1536]{2,1,0:T(8,128)(2,1)}) %all-gather.11.cloned.1.call-update) | async-done | bytes 6291472 | tf_op jit(solution)/shard_map/all_gather | solution.py:63
  588.0 16.1 fusion.12
  604.1 15.2 fusion.16
  619.3 40.6 %all-gather.13.cloned.1.call-done = bf16[2,1024,1536]{2,1,0:T(8,128)(2,1)} async-done(((bf16[2,256,1536]{2,1,0:T(8,128)(2,1)}), bf16[2,1024,1536]{2,1,0:T(8,128)(2,1)}) %all-gather.13.cloned.1.call-update) | async-done | bytes 6291472 | tf_op jit(solution)/shard_map/all_gather | solution.py:67
  659.9 25.4 %multiply_convert_fusion.1 = (bf16[2,1024,1536]{2,1,0:T(8,128)(2,1)}, bf16[2,1024,1536]{2,1,0:T(8,128)(2,1)S(1)}, bf16[2,1024,1536]{2,1,0:T(8,128)(2,1)}) fusion(f32[2,1024,1536]{2,1,0:T(8,128)} %fusion.16, f32[2,1024,1536]{2,1,0:T(8,128)} %fusion.12, bf16[2,1024,1536]{2,1,0:T(8,128)(2,1)} %all-gather.13.cloned.1.call-done, bf16[1536,1536]{1,0:T(8,128)(2,1)} %param.44), kind=kOutput, calls=%fused_computation.12 | convolution fusion | flops 9714008064 | bytes 55050240 | tf_op jit(solution)/shard_map/bfd,hd->bfh/dot_general | solution.py:15
  685.2 16.4 fusion.14
  701.6 17.8 convolution_add_fusion
  719.7 120.7 %reduce-scatter.28.cloned.1.call-done = f32[2,256,1536]{2,1,0:T(8,128)} async-done(((f32[2,1024,1536]{2,1,0:T(8,128)}), f32[2,256,1536]{2,1,0:T(8,128)}) %reduce-scatter.28.cloned.1.call-update) | async-done | bytes 3145744 | tf_op jit(solution)/shard_map/reduce_scatter | solution.py:75
  848.0 70.2 %all-gather.15.cloned.1.call-done = bf16[2,1024,1536]{2,1,0:T(8,128)(2,1)} async-done(((bf16[2,256,1536]{2,1,0:T(8,128)(2,1)}), bf16[2,1024,1536]{2,1,0:T(8,128)(2,1)}) %all-gather.15.cloned.1.call-update) | async-done | bytes 6291472 | tf_op jit(solution)/shard_map/all_gather | solution.py:67
  934.5 6.5 fusion.53
  941.3 16.0 fusion.9
  957.3 104.6 %reduce-scatter.30.cloned.1.call-done = f32[2,256,1536]{2,1,0:T(8,128)} async-done(((f32[2,1024,1536]{2,1,0:T(8,128)}), f32[2,256,1536]{2,1,0:T(8,128)}) %reduce-scatter.30.cloned.1.call-update) | async-done | bytes 3145744 | tf_op jit(solution)/shard_map/reduce_scatter | solution.py:75
  1066.9 118.7 %reduce-scatter.26.cloned.1.call-done = f32[2,256,1536]{2,1,0:T(8,128)} async-done(((f32[2,1024,1536]{2,1,0:T(8,128)}), f32[2,256,1536]{2,1,0:T(8,128)}) %reduce-scatter.26.cloned.1.call-update) | async-done | bytes 3145744 | tf_op jit(solution)/shard_map/reduce_scatter | solution.py:71
  1185.6 8.8 fusion.101
  1194.5 15.4 bitcast_convert_fusion
  1210.3 15.5 bitcast_convert_fusion.1
  1225.9 16.3 bitcast_convert_fusion.2
  1255.6 7.9 fusion.39
  1263.8 7.3 fusion.38
  1278.5 7.9 fusion.37
  1286.4 19.8 fusion.42
  1314.0 32.9 %multiply_reduce_fusion = (f32[2,6,1024]{2,1,0:T(8,128)S(1)}, f32[2,6,1024,1024]{2,3,1,0:T(8,128)}) fusion(f32[2,6,1024,1024]{2,3,1,0:T(8,128)} %get-tuple-element.158, f32[2,6,1024]{2,1,0:T(8,128)S(1)} %copy-done.13, bf16[2,1024,6,64]{1,3,2,0:T(8,128)(2,1)S(1)} %bitcast.260, bf16[2,1024,6,64]{1,3,2,0:T(8,128)(2,1)} %bitcast.282), kind=kOutput, calls=%fused_computation.2 | convolution fusion | flops 1660932096 | bytes 103907328 | tf_op jit(solution)/shard_map/bqhd,bkhd->bhqk/dot_general | solution.py:15
  1348.1 41.8 %multiply_convert_fusion = bf16[2,6,1024,1024]{2,3,1,0:T(8,128)(2,1)} fusion(f32[2,6,1024,1024]{2,3,1,0:T(8,128)} %get-tuple-element.164, f32[2,6,1024,1024]{2,3,1,0:T(8,128)} %get-tuple-element.158, f32[2,6,1024]{2,1,0:T(8,128)S(1)} %get-tuple-element.153, f32[2,6,1024]{2,1,0:T(8,128)S(1)} %copy-done.13), kind=kLoop, calls=%fused_computation.1 | loop fusion | flops 62914560 | bytes 125927424 | tf_op jit(solution)/shard_map/convert_element_type | solution.py:215
  1389.9 15.2 multiply_bitcast_fusion.1
  1405.1 14.3 multiply_bitcast_fusion
  1433.4 6.2 convolution_bitcast_fusion.4
  1441.3 8.2 fusion.59
  1449.4 6.4 fusion.63
  1455.9 14.6 add_add_fusion
  1484.4 11.7 reduce-scatter.52.cloned.1.call-done
  1497.9 31.5 %reduce-scatter.44.cloned.1.call-done = bf16[384,192]{0,1:T(8,128)(2,1)} async-done(((bf16[384,1536]{0,1:T(8,128)(2,1)}), bf16[384,192]{0,1:T(8,128)(2,1)}) %reduce-scatter.44.cloned.1.call-update) | async-done | bytes 147472 | tf_op jit(solution)/shard_map/reduce_scatter | solution.py:259
  1531.0 31.5 %reduce-scatter.42.cloned.1.call-done = bf16[192,384]{1,0:T(8,128)(2,1)} async-done(((bf16[1536,384]{1,0:T(8,128)(2,1)}), bf16[192,384]{1,0:T(8,128)(2,1)}) %reduce-scatter.42.cloned.1.call-update) | async-done | bytes 147472 | tf_op jit(solution)/shard_map/reduce_scatter | solution.py:250
  1564.1 31.6 %reduce-scatter.40.cloned.1.call-done = bf16[384,192]{0,1:T(8,128)(2,1)} async-done(((bf16[384,1536]{0,1:T(8,128)(2,1)}), bf16[384,192]{0,1:T(8,128)(2,1)}) %reduce-scatter.40.cloned.1.call-update) | async-done | bytes 147472 | tf_op jit(solution)/shard_map/reduce_scatter | solution.py:247
  1597.4 31.5 %reduce-scatter.38.cloned.1.call-done = bf16[192,384]{1,0:T(8,128)(2,1)} async-done(((bf16[1536,384]{1,0:T(8,128)(2,1)}), bf16[192,384]{1,0:T(8,128)(2,1)}) %reduce-scatter.38.cloned.1.call-update) | async-done | bytes 147472 | tf_op jit(solution)/shard_map/reduce_scatter | solution.py:244
  1630.5 31.6 %reduce-scatter.34.cloned.1.call-done = bf16[192,384]{1,0:T(8,128)(2,1)} async-done(((bf16[1536,384]{1,0:T(8,128)(2,1)}), bf16[192,384]{1,0:T(8,128)(2,1)}) %reduce-scatter.34.cloned.1.call-update) | async-done | bytes 147472 | tf_op jit(solution)/shard_map/reduce_scatter | solution.py:238
  1663.8 31.7 %reduce-scatter.36.cloned.1.call-done = bf16[192,384]{1,0:T(8,128)(2,1)} async-done(((bf16[1536,384]{1,0:T(8,128)(2,1)}), bf16[192,384]{1,0:T(8,128)(2,1)}) %reduce-scatter.36.cloned.1.call-update) | async-done | bytes 147472 | tf_op jit(solution)/shard_map/reduce_scatter | solution.py:241
  1697.1 120.4 %reduce-scatter.32.cloned.1.call-done = f32[2,256,1536]{2,1,0:T(8,128)} async-done(((f32[2,1024,1536]{2,1,0:T(8,128)}), f32[2,256,1536]{2,1,0:T(8,128)}) %reduce-scatter.32.cloned.1.call-update) | async-done | bytes 3145744 | tf_op jit(solution)/shard_map/reduce_scatter | solution.py:75
  1821.0 41.3 %psum.15 = f32[6,1536]{1,0:T(8,128)S(1)} all-reduce(f32[6,1536]{1,0:T(8,128)S(1)} %stack.21), channel_id=1, replica_groups=mesh['dp'=8,'mp'=4] {'dp','mp'}, use_global_device_ids=true, to_apply=%region_38.39 | all-reduce | flops 9216 | bytes 73728 | tf_op jit(solution)/shard_map/psum | solution.py:298
  1868.6 110.8 %all-reduce.2.cloned.1.call-done = f32[1000,1536]{1,0:T(8,128)} async-done(((f32[1000,1536]{1,0:T(8,128)}), f32[1000,1536]{1,0:T(8,128)}) %all-reduce.2.cloned.1.call-update) | async-done | bytes 6144016 | tf_op jit(solution)/shard_map/psum | solution.py:298
  (343 shorter events, 180.3 us)
Async XLA Ops:
  7.2 78.8 %all-gather.7.cloned.1.call-start = ((), (), s32[]{:S(2)}) async-start(), calls=%async_computation.17 | async-start | bytes 7864320 | tf_op jit(solution)/shard_map/all_gather | solution.py:63
  13.0 282.3 %reduce-scatter.22.cloned.1.call-start = ((), (), s32[]{:S(2)}) async-start(), calls=%async_computation.18 | async-start | bytes 15728640 | tf_op jit(solution)/shard_map/reduce_scatter | solution.py:71
  16.8 75.1 %copy-start.72 = (f32[2]{0:T(128)}, f32[2]{0:T(128)S(1)}, u32[]{:S(2)}) copy-start(f32[2]{0:T(128)S(1)} %add_rsqrt_fusion.3) | copy-start | bytes 28
  17.5 74.4 %copy-start.46 = (bf16[2,1536]{1,0:T(2,128)(2,1)}, bf16[2,1536]{1,0:T(2,128)(2,1)S(1)}, u32[]{:S(2)}) copy-start(bf16[2,1536]{1,0:T(2,128)(2,1)S(1)} %get-tuple-element.133) | copy-start | bytes 18436
  17.8 74.1 %copy-start.66 = (bf16[2,384]{1,0:T(2,128)(2,1)}, bf16[2,384]{1,0:T(2,128)(2,1)S(1)}, u32[]{:S(2)}) copy-start(bf16[2,384]{1,0:T(2,128)(2,1)S(1)} %convolution_convert_fusion.6) | copy-start | bytes 4612
  97.0 23.3 %copy-start.14 = (bf16[2,1024,6,32]{1,3,2,0:T(8,128)(2,1)}, bf16[2,1024,6,32]{1,3,2,0:T(8,128)(2,1)S(1)}, u32[]{:S(2)}) copy-start(bf16[2,1024,6,32]{1,3,2,0:T(8,128)(2,1)S(1)} %get-tuple-element.144) | copy-start | bytes 2359300
  121.2 20.0 %copy-start.41 = (f32[2,6,1,1024]{3,2,1,0:T(1,128)S(1)}, f32[2,6,1,1024]{3,2,1,0:T(1,128)}, u32[]{:S(2)}) copy-start(f32[2,6,1,1024]{3,2,1,0:T(1,128)} %fusion.97) | copy-start | bytes 147460
  147.3 19.6 copy-start.33
  147.3 20.8 %copy-start.38 = (bf16[384,1536]{1,0:T(8,128)(2,1)S(1)}, bf16[384,1536]{1,0:T(8,128)(2,1)}, u32[]{:S(2)}) copy-start(bf16[384,1536]{1,0:T(8,128)(2,1)} %param.37) | copy-start | bytes 3538948
  174.4 197.5 %all-gather.9.cloned.1.call-start = ((), (), s32[]{:S(2)}) async-start(), calls=%async_computation.19 | async-start | bytes 7864320 | tf_op jit(solution)/shard_map/all_gather | solution.py:63
  301.5 70.3 %copy-start.36 = (bf16[1536,384]{1,0:T(8,128)(2,1)S(1)}, bf16[1536,384]{1,0:T(8,128)(2,1)}, u32[]{:S(2)}) copy-start(bf16[1536,384]{1,0:T(8,128)(2,1)} %param.38) | copy-start | bytes 3538948
  301.6 209.5 %reduce-scatter.24.cloned.1.call-start = ((), (), s32[]{:S(2)}) async-start(), calls=%async_computation.20 | async-start | bytes 15728640 | tf_op jit(solution)/shard_map/reduce_scatter | solution.py:71
  303.3 74.0 %copy-start.29 = (bf16[2,128,384]{1,2,0:T(8,128)(2,1)}, bf16[2,128,384]{1,2,0:T(8,128)(2,1)S(1)}, u32[]{:S(2)}) copy-start(bf16[2,128,384]{1,2,0:T(8,128)(2,1)S(1)} %copy.163) | copy-start | bytes 589828
  390.1 197.9 %all-gather.11.cloned.1.call-start = ((), (), s32[]{:S(2)}) async-start(), calls=%async_computation.21 | async-start | bytes 7864320 | tf_op jit(solution)/shard_map/all_gather | solution.py:63
  517.7 142.2 %all-gather.13.cloned.1.call-start = ((), (), s32[]{:S(2)}) async-start(), calls=%async_computation.23 | async-start | bytes 7864320 | tf_op jit(solution)/shard_map/all_gather | solution.py:67
  518.3 322.1 %reduce-scatter.28.cloned.1.call-start = ((), (), s32[]{:S(2)}) async-start(), calls=%async_computation.24 | async-start | bytes 15728640 | tf_op jit(solution)/shard_map/reduce_scatter | solution.py:75
  588.0 16.1 copy-start.77
  685.2 16.4 copy-start.79
  719.5 126.0 %copy-start.9 = (bf16[2,256,1536]{2,1,0:T(8,128)(2,1)S(1)}, bf16[2,256,1536]{2,1,0:T(8,128)(2,1)}, u32[]{:S(2)}) copy-start(bf16[2,256,1536]{2,1,0:T(8,128)(2,1)} %param.45) | copy-start | bytes 4718596
  719.5 198.7 %all-gather.15.cloned.1.call-start = ((), (), s32[]{:S(2)}) async-start(), calls=%async_computation.25 | async-start | bytes 7864320 | tf_op jit(solution)/shard_map/all_gather | solution.py:67
  847.9 214.0 %reduce-scatter.30.cloned.1.call-start = ((), (), s32[]{:S(2)}) async-start(), calls=%async_computation.26 | async-start | bytes 15728640 | tf_op jit(solution)/shard_map/reduce_scatter | solution.py:75
  941.0 244.6 %reduce-scatter.26.cloned.1.call-start = ((), (), s32[]{:S(2)}) async-start(), calls=%async_computation.22 | async-start | bytes 15728640 | tf_op jit(solution)/shard_map/reduce_scatter | solution.py:71
  957.3 104.7 %copy-start.51 = (f32[1536]{0:T(1024)S(1)}, f32[1536]{0:T(1024)}, u32[]{:S(2)}) copy-start(f32[1536]{0:T(1024)} %param.30) | copy-start | bytes 18436
  957.3 104.7 %copy-start.53 = (f32[2,256]{1,0:T(2,128)S(1)}, f32[2,256]{1,0:T(2,128)}, u32[]{:S(2)}) copy-start(f32[2,256]{1,0:T(2,128)} %copy-done.52) | copy-start | bytes 6148
  957.3 104.7 %copy-start.57 = (f32[2,256]{1,0:T(2,128)S(1)}, f32[2,256]{1,0:T(2,128)}, u32[]{:S(2)}) copy-start(f32[2,256]{1,0:T(2,128)} %copy-done.56) | copy-start | bytes 6148
  957.3 228.3 %copy-start.10 = (bf16[2,256,1536]{2,1,0:T(8,128)(2,1)S(1)}, bf16[2,256,1536]{2,1,0:T(8,128)(2,1)}, u32[]{:S(2)}) copy-start(bf16[2,256,1536]{2,1,0:T(8,128)(2,1)} %param.45) | copy-start | bytes 4718596
  957.3 314.1 %all-gather.17.cloned.1.call-start = ((), (), s32[]{:S(2)}) async-start(), calls=%async_computation.27 | async-start | bytes 7864320 | tf_op jit(solution)/shard_map/all_gather | solution.py:67
  1194.4 281.4 %reduce-scatter.50.cloned.1.call-start = ((), (), s32[]{:S(2)}) async-start(), calls=%async_computation.38 | async-start | bytes 5308416 | tf_op jit(solution)/shard_map/reduce_scatter | solution.py:268
  1209.9 268.2 %reduce-scatter.48.cloned.1.call-start = ((), (), s32[]{:S(2)}) async-start(), calls=%async_computation.37 | async-start | bytes 5308416 | tf_op jit(solution)/shard_map/reduce_scatter | solution.py:265
  1225.8 254.6 %reduce-scatter.46.cloned.1.call-start = ((), (), s32[]{:S(2)}) async-start(), calls=%async_computation.36 | async-start | bytes 5308416 | tf_op jit(solution)/shard_map/reduce_scatter | solution.py:262
  1242.2 240.5 %reduce-scatter.54.cloned.1.call-start = ((), (), s32[]{:S(2)}) async-start(), calls=%async_computation.40 | async-start | bytes 663552
  1250.8 245.3 %reduce-scatter.52.cloned.1.call-start = ((), (), s32[]{:S(2)}) async-start(), calls=%async_computation.39 | async-start | bytes 663552
  1255.6 273.7 %reduce-scatter.44.cloned.1.call-start = ((), (), s32[]{:S(2)}) async-start(), calls=%async_computation.35 | async-start | bytes 1327104 | tf_op jit(solution)/shard_map/reduce_scatter | solution.py:259
  1263.5 298.9 %reduce-scatter.42.cloned.1.call-start = ((), (), s32[]{:S(2)}) async-start(), calls=%async_computation.34 | async-start | bytes 1327104 | tf_op jit(solution)/shard_map/reduce_scatter | solution.py:250
  1271.1 324.6 %reduce-scatter.40.cloned.1.call-start = ((), (), s32[]{:S(2)}) async-start(), calls=%async_computation.33 | async-start | bytes 1327104 | tf_op jit(solution)/shard_map/reduce_scatter | solution.py:247
  1306.2 322.7 %reduce-scatter.38.cloned.1.call-start = ((), (), s32[]{:S(2)}) async-start(), calls=%async_computation.32 | async-start | bytes 1327104 | tf_op jit(solution)/shard_map/reduce_scatter | solution.py:244
  1314.0 33.4 %copy-start.42 = (f32[2,6,1,1024]{3,2,1,0:T(1,128)S(1)}, f32[2,6,1,1024]{3,2,1,0:T(1,128)}, u32[]{:S(2)}) copy-start(f32[2,6,1,1024]{3,2,1,0:T(1,128)} %fusion.97) | copy-start | bytes 147460
  1346.9 315.2 %reduce-scatter.34.cloned.1.call-start = ((), (), s32[]{:S(2)}) async-start(), calls=%async_computation.30 | async-start | bytes 1327104 | tf_op jit(solution)/shard_map/reduce_scatter | solution.py:238
  1389.9 15.2 copy-start.15
  1389.9 15.2 copy-start.17
  1430.5 265.0 %reduce-scatter.36.cloned.1.call-start = ((), (), s32[]{:S(2)}) async-start(), calls=%async_computation.31 | async-start | bytes 1327104 | tf_op jit(solution)/shard_map/reduce_scatter | solution.py:241
  1441.2 376.3 %reduce-scatter.32.cloned.1.call-start = ((), (), s32[]{:S(2)}) async-start(), calls=%async_computation.28 | async-start | bytes 15728640 | tf_op jit(solution)/shard_map/reduce_scatter | solution.py:75
  1470.5 508.9 %all-reduce.2.cloned.1.call-start = ((), (), s32[]{:S(2)}) async-start(), calls=%async_computation.29 | async-start | bytes 12288000 | tf_op jit(solution)/shard_map/psum | solution.py:298
  1475.7 88.3 %copy-start.61 = (f32[1536]{0:T(1024)S(1)}, f32[1536]{0:T(1024)}, u32[]{:S(2)}) copy-start(f32[1536]{0:T(1024)} %get-tuple-element.102) | copy-start | bytes 18436
  1475.8 88.3 %copy-start.60 = (f32[1536]{0:T(1024)S(1)}, f32[1536]{0:T(1024)}, u32[]{:S(2)}) copy-start(f32[1536]{0:T(1024)} %get-tuple-element.110) | copy-start | bytes 18436
  1478.0 339.5 %copy-start.6 = (bf16[2,256,1536]{2,1,0:T(8,128)(2,1)S(1)}, bf16[2,256,1536]{2,1,0:T(8,128)(2,1)}, u32[]{:S(2)}) copy-start(bf16[2,256,1536]{2,1,0:T(8,128)(2,1)} %param.23) | copy-start | bytes 4718596
  1478.0 339.5 %copy-start.55 = (f32[2,256]{1,0:T(2,128)S(1)}, f32[2,256]{1,0:T(2,128)}, u32[]{:S(2)}) copy-start(f32[2,256]{1,0:T(2,128)} %copy-done.54) | copy-start | bytes 6148
  1478.0 339.5 %copy-start.65 = (f32[2,256]{1,0:T(2,128)S(1)}, f32[2,256]{1,0:T(2,128)}, u32[]{:S(2)}) copy-start(f32[2,256]{1,0:T(2,128)} %copy-done.64) | copy-start | bytes 6148
  (60 other events, 228.0 us)
Sparse Core Ops, SparseCore 0:
  13.1 72.8 all-gather.6
  174.5 120.7 reduce-scatter.21
  301.7 70.1 all-gather.8
  390.2 120.7 reduce-scatter.23
  517.8 70.1 all-gather.10
  589.7 70.1 all-gather.12
  719.6 120.7 reduce-scatter.27
  848.0 70.1 all-gather.14
  941.1 120.7 reduce-scatter.29
  1064.9 120.7 reduce-scatter.25
  1194.5 70.1 all-gather.16
  1266.9 54.9 reduce-scatter.49
  1324.2 53.2 reduce-scatter.47
  1379.7 53.3 reduce-scatter.45
  1435.1 29.5 reduce-scatter.53
  1466.8 29.2 reduce-scatter.51
  1498.2 31.0 reduce-scatter.43
  1531.5 30.9 reduce-scatter.41
  1564.7 30.9 reduce-scatter.39
  1597.9 30.9 reduce-scatter.37
  1631.2 30.9 reduce-scatter.33
  1664.4 30.9 reduce-scatter.35
  1698.6 118.8 reduce-scatter.31
  1823.7 155.6 all-reduce.1
where the time goes:
time: 2000 us; the launch traced here: 1990 us
  waiting for transfers between devices  1330 us (66%)
  matrix products  426 us (21%)
  other arithmetic  144 us (7%)
  blocking collectives  41.3 us (2%)
  local copies, waits for them, and re-layouts  31.8 us (2%)
    dot_general x53, matrix products, product(): return jnp.einsum(form, left, right, preferred_element_type=jnp.float32)  426 us
    reduce_scatter x3, waiting for transfers between devices, settle_branch(): lax.psum_scatter(partial_value, 'mp', scatter_dimension=1, tiled=True)  360 us
    reduce_scatter x3, waiting for transfers between devices, settle_input(): lax.psum_scatter(partial_value, 'mp', scatter_dimension=1, tiled=True)  346 us
    all_gather x3, waiting for transfers between devices, spread_rows(): return lax.all_gather(rows.astype(jnp.bfloat16), 'mp', axis=1, tiled=True)  201 us
    all_gather x3, waiting for transfers between devices, spread_grads(): return lax.all_gather(grads.astype(jnp.bfloat16), 'mp', axis=1, tiled=True)  111 us
    psum x1, waiting for transfers between devices, shards(): summed_small, summed_table = lax.psum((stacked, table_term), ('dp', 'mp'))  111 us
    convert_element_type x1, other arithmetic, shards(): (probs * (grad_probs - mixsum[..., None])).astype(jnp.bfloat16)  41.8 us
    psum x1, blocking collectives, shards(): summed_small, summed_table = lax.psum((stacked, table_term), ('dp', 'mp'))  41.3 us
  transfers between devices with their start and end apart: 24, of which 19 were waited for; matrix products, arithmetic and copies ran while one was open for 19% of the time, Pallas kernels for 0%

commit v1 on v0

v1 whole, which is shorter than its diff:
```python
import functools
import math

import jax
import jax.numpy as jnp
from jax import lax
from jax.experimental import pallas as pl
from jax.experimental.pallas import tpu as pltpu
from jax.sharding import PartitionSpec as P

HEAD_DIM = 64
HALF = HEAD_DIM // 2
FACTOR = 1.0 / math.sqrt(HEAD_DIM)

norm_eps = 1e-05

f32 = jnp.float32
bf16 = jnp.bfloat16


def dot(left, right, left_axis, right_axis):
    return lax.dot_general(
        left, right, (((left_axis,), (right_axis,)), ((), ())), preferred_element_type=f32
    )


def norm_forward(values, gain, shift):
    center = values - jnp.mean(values, axis=-1, keepdims=True)
    scale = lax.rsqrt(jnp.mean(center * center, axis=-1, keepdims=True) + norm_eps)
    normal = center * scale
    return (normal * gain + shift, normal, scale)


def norm_backward(grad, normal, scale, gain):
    inner = grad * gain
    return scale * (
        inner
        - jnp.mean(inner, axis=-1, keepdims=True)
        - normal * jnp.mean(inner * normal, axis=-1, keepdims=True)
    )


def bits_of(size):
    return [1 << place for place in range(size.bit_length() - 1)]


def swap(values, axis, k):
    return lax.ppermute(values, axis, [(i, i ^ k) for i in range(lax.axis_size(axis))])


def spread(values):
    size = lax.axis_size("mp")
    half = values.shape[0] // 2
    orders = (bits_of(size), bits_of(size)[::-1])
    parts = []
    for piece, order in zip((values[:half], values[half:]), orders):
        have = {0: piece}
        for bit in order:
            for k in list(have):
                have[k ^ bit] = swap(have[k], "mp", bit)
        parts.append(have)
    return [parts[p][k] for k in range(size) for p in (0, 1)]


def trade(blocks):
    return [blocks[0]] + [swap(blocks[k], "mp", k) for k in range(1, len(blocks))]


def settle(blocks):
    got = trade(blocks)
    total = got[0].astype(f32)
    for block in got[1:]:
        total = total + block.astype(f32)
    return total


def all_sum(values):
    for axis in ("mp", "dp"):
        for bit in bits_of(lax.axis_size(axis)):
            values = values + swap(values, axis, bit)
    return values


def whole_rows(shard):
    size = lax.axis_size("mp")
    rows, width = shard.shape
    core = lax.axis_index("dp") & 1
    mine = lax.dynamic_slice_in_dim(shard, core * (rows // 2), rows // 2, 0)
    got = jnp.concatenate(spread(mine)[2:], axis=0).reshape(size - 1, rows // 2, width)
    other = swap(got, "dp", 1)
    low = jnp.where(core == 0, got, other)
    high = jnp.where(core == 0, other, got)
    rest = jnp.concatenate([low, high], axis=1).reshape((size - 1) * rows, width)
    return jnp.concatenate([shard, rest], axis=0)


def whole_columns(shard):
    size = lax.axis_size("mp")
    depth = shard.shape[0] // lax.axis_size("dp")
    mine = lax.dynamic_slice_in_dim(shard, lax.axis_index("dp") * depth, depth, 0)
    wide = jnp.concatenate([mine] + [swap(mine, "mp", k) for k in range(1, size)], axis=1)
    return lax.all_gather(wide, "dp", axis=0, tiled=True)


def self_forward_kernel(block, q_ref, k_ref, v_ref, pk_ref, pv_ref, o_ref, l_ref):
    keys = k_ref[...]
    values = v_ref[...]
    front_key = pk_ref[...].astype(f32)
    front_value = pv_ref[...].astype(f32)
    for start in range(0, q_ref.shape[1], block):
        part = slice(start, start + block)
        queries = q_ref[:, part]
        scores = dot(keys, queries, 0, 0)
        front = jnp.sum(queries.astype(f32) * front_key, axis=0, keepdims=True)
        top = jnp.maximum(jnp.max(scores, axis=0, keepdims=True), front)
        weights = jnp.exp(scores - top)
        front_weight = jnp.exp(front - top)
        total = jnp.sum(weights, axis=0, keepdims=True) + front_weight
        mixed = dot(values, weights.astype(bf16), 1, 0)
        mixed = mixed + front_value * front_weight.astype(bf16).astype(f32)
        o_ref[:, part] = (mixed * (1.0 / total)).astype(bf16)
        l_ref[0, :, part] = top + jnp.log(total)


def self_backward_kernel(
    block,
    q_ref,
    k_ref,
    v_ref,
    g_ref,
    o_ref,
    l_ref,
    pk_ref,
    pv_ref,
    cos_ref,
    sin_ref,
    d_ref,
    dpk_ref,
    dpv_ref,
):
    frames = q_ref.shape[1]
    keys = k_ref[...]
    values = v_ref[...]
    front_key = pk_ref[...].astype(f32)
    front_value = pv_ref[...].astype(f32)
    grad_keys = jnp.zeros((HEAD_DIM, frames), f32)
    grad_values = jnp.zeros((HEAD_DIM, frames), f32)
    grad_front_key = jnp.zeros((HEAD_DIM, 1), f32)
    grad_front_value = jnp.zeros((HEAD_DIM, 1), f32)
    for start in range(0, frames, block):
        part = slice(start, start + block)
        queries = q_ref[:, part]
        grads = g_ref[:, part]
        wide_queries = queries.astype(f32)
        wide_grads = grads.astype(f32)
        logsum = l_ref[0, :, part]
        mixsum = jnp.sum(o_ref[:, part].astype(f32) * wide_grads, axis=0, keepdims=True)
        probs = jnp.exp(dot(keys, queries, 0, 0) - logsum)
        grad_probs = dot(values, grads, 0, 0)
        grad_scores = (probs * (grad_probs - mixsum)).astype(bf16)
        grad_values = grad_values + dot(grads, probs.astype(bf16), 1, 1)
        grad_keys = grad_keys + dot(queries, grad_scores, 1, 1)
        grad_queries = dot(keys, grad_scores, 1, 0)
        front = jnp.exp(jnp.sum(wide_queries * front_key, axis=0, keepdims=True) - logsum)
        grad_front = jnp.sum(wide_grads * front_value, axis=0, keepdims=True)
        grad_front = (front * (grad_front - mixsum)).astype(bf16).astype(f32)
        front = front.astype(bf16).astype(f32)
        grad_front_key += jnp.sum(wide_queries * grad_front, axis=1, keepdims=True)
        grad_front_value += jnp.sum(wide_grads * front, axis=1, keepdims=True)
        grad_queries = (grad_queries + front_key * grad_front) * FACTOR
        cosine = cos_ref[:, part]
        sine = sin_ref[:, part]
        upper, lower = grad_queries[:HALF], grad_queries[HALF:]
        d_ref[0, :HALF, part] = (upper * cosine + lower * sine).astype(bf16)
        d_ref[0, HALF:, part] = (lower * cosine - upper * sine).astype(bf16)
    cosine = cos_ref[...]
    sine = sin_ref[...]
    upper, lower = grad_keys[:HALF], grad_keys[HALF:]
    d_ref[1, :HALF, :] = (upper * cosine + lower * sine).astype(bf16)
    d_ref[1, HALF:, :] = (lower * cosine - upper * sine).astype(bf16)
    d_ref[2] = grad_values.astype(bf16)
    dpk_ref[...] = grad_front_key.astype(bf16)
    dpv_ref[...] = grad_front_value.astype(bf16)


def cross_forward_kernel(clip, heads, n_ref, q_ref, k_ref, v_ref, o_ref, l_ref):
    live = lax.broadcasted_iota(jnp.int32, (k_ref.shape[1], 1), 0) < n_ref[clip]
    for head in range(heads):
        part = slice(head * HEAD_DIM, (head + 1) * HEAD_DIM)
        scores = jnp.where(live, dot(k_ref[part], q_ref[part], 0, 0), -1e30)
        top = jnp.max(scores, axis=0, keepdims=True)
        weights = jnp.exp(scores - top)
        total = jnp.sum(weights, axis=0, keepdims=True)
        mixed = dot(v_ref[part], weights.astype(bf16), 1, 0)
        o_ref[part] = (mixed * (1.0 / total)).astype(bf16)
        l_ref[head] = top + jnp.log(total)


def cross_backward_kernel(
    clip, heads, n_ref, q_ref, k_ref, v_ref, g_ref, o_ref, l_ref, dq_ref, dk_ref, dv_ref
):
    live = lax.broadcasted_iota(jnp.int32, (k_ref.shape[1], 1), 0) < n_ref[clip]
    for head in range(heads):
        part = slice(head * HEAD_DIM, (head + 1) * HEAD_DIM)
        queries = q_ref[part]
        keys = k_ref[part]
        grads = g_ref[part]
        mixsum = jnp.sum(o_ref[part].astype(f32) * grads.astype(f32), axis=0, keepdims=True)
        scores = jnp.where(live, dot(keys, queries, 0, 0), -1e30)
        probs = jnp.exp(scores - l_ref[head])
        grad_scores = (probs * (dot(v_ref[part], grads, 0, 0) - mixsum)).astype(bf16)
        dq_ref[part] = (dot(keys, grad_scores, 1, 0) * FACTOR).astype(bf16)
        dk_ref[part] = dot(queries, grad_scores, 1, 1).astype(bf16)
        dv_ref[part] = dot(grads, probs.astype(bf16), 1, 1).astype(bf16)


def shape_of(shape, kind):
    return jax.ShapeDtypeStruct(shape, kind)


def params():
    return pltpu.CompilerParams(vmem_limit_bytes=40 * 2**20)


def self_cost(heads, frames, products):
    return pl.CostEstimate(
        flops=products * 2 * heads * frames * frames * HEAD_DIM * 4,
        bytes_accessed=products * 2 * heads * frames * HEAD_DIM * 2,
        transcendentals=heads * frames * frames,
    )


def self_forward(turned, front_keys, front_values):
    heads = front_keys.shape[0] // HEAD_DIM
    frames = turned.shape[1]

    def at(third):
        return pl.BlockSpec((HEAD_DIM, frames), lambda h: (third * heads + h, 0))

    column = pl.BlockSpec((HEAD_DIM, 1), lambda h: (h, 0))
    return pl.pallas_call(
        functools.partial(self_forward_kernel, frames),
        grid=(heads,),
        in_specs=[at(0), at(1), at(2), column, column],
        out_specs=[at(0), pl.BlockSpec((1, 1, frames), lambda h: (h, 0, 0))],
        out_shape=[
            shape_of((heads * HEAD_DIM, frames), bf16),
            shape_of((heads, 1, frames), f32),
        ],
        compiler_params=params(),
        cost_estimate=self_cost(heads, frames, 2),
        name="self_forward",
    )(turned, turned, turned, front_keys, front_values)


def self_backward(turned, grads, mixed, logsum, front_keys, front_values, cosine, sine):
    heads = front_keys.shape[0] // HEAD_DIM
    frames = turned.shape[1]

    def at(third):
        return pl.BlockSpec((HEAD_DIM, frames), lambda h: (third * heads + h, 0))

    column = pl.BlockSpec((HEAD_DIM, 1), lambda h: (h, 0))
    angles = pl.BlockSpec((HALF, frames), lambda h: (0, 0))
    return pl.pallas_call(
        functools.partial(self_backward_kernel, min(256, frames)),
        grid=(heads,),
        in_specs=[
            at(0),
            at(1),
            at(2),
            at(0),
            at(0),
            pl.BlockSpec((1, 1, frames), lambda h: (h, 0, 0)),
            column,
            column,
            angles,
            angles,
        ],
        out_specs=[
            pl.BlockSpec((3, HEAD_DIM, frames), lambda h: (0, h, 0)),
            column,
            column,
        ],
        out_shape=[
            shape_of((3, heads * HEAD_DIM, frames), bf16),
            shape_of((heads * HEAD_DIM, 1), bf16),
            shape_of((heads * HEAD_DIM, 1), bf16),
        ],
        compiler_params=params(),
        cost_estimate=self_cost(heads, frames, 5),
        name="self_backward",
    )(turned, turned, turned, grads, mixed, logsum, front_keys, front_values, cosine, sine)


def cross_specs(groups, heads, frames, slots):
    at_frames = pl.BlockSpec((heads * HEAD_DIM, frames), lambda h: (h, 0))
    at_slots = pl.BlockSpec((heads * HEAD_DIM, slots), lambda h: (h, 0))
    at_sums = pl.BlockSpec((heads, 1, frames), lambda h: (h, 0, 0))
    return (at_frames, at_slots, at_sums)


def cross_cost(rows, frames, slots, products):
    return pl.CostEstimate(
        flops=products * 2 * rows * frames * slots * 4,
        bytes_accessed=products * 2 * rows * frames,
        transcendentals=rows // HEAD_DIM * frames * slots,
    )


def cross_forward(clip, groups, lengths, queries, keys, values):
    rows, frames = queries.shape
    heads = rows // HEAD_DIM // groups
    slots = keys.shape[1]
    at_frames, at_slots, at_sums = cross_specs(groups, heads, frames, slots)
    return pl.pallas_call(
        functools.partial(cross_forward_kernel, clip, heads),
        grid=(groups,),
        in_specs=[pl.BlockSpec(memory_space=pltpu.SMEM), at_frames, at_slots, at_slots],
        out_specs=[at_frames, at_sums],
        out_shape=[
            shape_of((rows, frames), bf16),
            shape_of((rows // HEAD_DIM, 1, frames), f32),
        ],
        compiler_params=params(),
        cost_estimate=cross_cost(rows, frames, slots, 2),
        name="cross_forward",
    )(lengths, queries, keys, values)


def cross_backward(clip, groups, lengths, queries, keys, values, grads, mixed, logsum):
    rows, frames = queries.shape
    heads = rows // HEAD_DIM // groups
    slots = keys.shape[1]
    at_frames, at_slots, at_sums = cross_specs(groups, heads, frames, slots)
    return pl.pallas_call(
        functools.partial(cross_backward_kernel, clip, heads),
        grid=(groups,),
        in_specs=[
            pl.BlockSpec(memory_space=pltpu.SMEM),
            at_frames,
            at_slots,
            at_slots,
            at_frames,
            at_frames,
            at_sums,
        ],
        out_specs=[at_frames, at_slots, at_slots],
        out_shape=[
            shape_of((rows, frames), bf16),
            shape_of((rows, slots), bf16),
            shape_of((rows, slots), bf16),
        ],
        compiler_params=params(),
        cost_estimate=cross_cost(rows, frames, slots, 5),
        name="cross_backward",
    )(lengths, queries, keys, values, grads, mixed, logsum)


def turning(rows):
    size = lax.axis_size("mp")
    me = lax.axis_index("mp")
    starts = jnp.stack([(me ^ k) * rows for k in range(size)])
    places = (starts[:, None] + jnp.arange(rows)[None, :] + 1).reshape(-1).astype(f32)
    rates = jnp.exp(jnp.arange(HALF).astype(f32) * (-2.0 * math.log(10000.0) / HEAD_DIM))
    angles = rates[:, None] * places[None, :]
    return (jnp.cos(angles), jnp.sin(angles))


def turn(values, cosine, sine):
    pairs = values.reshape(-1, 2, HALF, values.shape[-1])
    upper, lower = pairs[:, 0], pairs[:, 1]
    return jnp.stack([upper * cosine - lower * sine, lower * cosine + upper * sine], axis=1).reshape(
        values.shape
    )


def row_blocks(values, count):
    return jnp.split(values, count, axis=0)


def sum_over_clips(values, axis):
    return lax.psum_scatter(values.astype(bf16), "dp", scatter_dimension=axis, tiled=True)


def shards(
    frames_in,
    prompt,
    lengths,
    tsteps,
    table,
    gain_one,
    shift_one,
    gain_two,
    shift_two,
    gain_three,
    shift_three,
    w_query,
    w_key,
    w_value,
    w_out,
    c_query,
    c_key,
    c_value,
    c_out,
    w_gate,
    w_up,
    w_down,
    cotangent,
):
    size = lax.axis_size("mp")
    count, rows, width = frames_in.shape
    clips = range(count)
    local = w_query.shape[1]

    resid = [frames_in[b].astype(f32) for b in clips]
    ones = [norm_forward(resid[b], gain_one, shift_one) for b in clips]
    whole_one = [jnp.concatenate(spread(ones[b][0].astype(bf16)), axis=0) for b in clips]

    picked = jnp.take(table, tsteps, axis=0)
    prefix_normed, prefix_normal, prefix_scale = norm_forward(picked, gain_one, shift_one)
    prefix_low = prefix_normed.astype(bf16)
    cosine, sine = turning(rows)

    w_self = jnp.concatenate([w_query, w_key, w_value], axis=1)
    front = dot(w_self[:, local:], prefix_low, 0, 1).astype(bf16)
    front_keys = [front[:local, b : b + 1] for b in clips]
    front_values = [front[local:, b : b + 1] for b in clips]

    out_all = whole_rows(w_out)
    c_out_all = whole_rows(c_out)
    c_query_all = whole_columns(c_query)

    memory = jnp.concatenate([c_key, c_value], axis=1)
    memory = jnp.stack([dot(memory, prompt[b], 0, 1).astype(bf16) for b in clips])
    memory = jnp.stack([memory] + [swap(memory, "mp", k) for k in range(1, size)], axis=1)
    cross_keys = [memory[b, :, :local].reshape(size * local, -1) for b in clips]
    cross_values = [memory[b, :, local:].reshape(size * local, -1) for b in clips]

    turned, mixed_part, logsum, mixed = [], [], [], []
    for b in clips:
        raw = dot(w_self, whole_one[b], 0, 1)
        queries = (turn(raw[:local], cosine, sine) * FACTOR).astype(bf16)
        keys = turn(raw[local : 2 * local], cosine, sine).astype(bf16)
        turned.append(jnp.concatenate([queries, keys, raw[2 * local :].astype(bf16)], axis=0))
        out, sums = self_forward(turned[b], front_keys[b], front_values[b])
        mixed_part.append(out)
        logsum.append(sums)
        mixed.append(jnp.concatenate(trade(jnp.split(out, size, axis=1)), axis=0))

    first, twos, normed_two, cross_query, cross_sums, cross_mixed = [], [], [], [], [], []
    second, threes, whole_three = [], [], []
    for b in clips:
        first.append(resid[b] + dot(mixed[b], out_all, 0, 0))
        twos.append(norm_forward(first[b], gain_two, shift_two))
        normed_two.append(twos[b][0].astype(bf16))
        cross_query.append((dot(c_query_all, normed_two[b], 0, 1) * FACTOR).astype(bf16))
        out, sums = cross_forward(
            b, size, lengths, cross_query[b], cross_keys[b], cross_values[b]
        )
        cross_mixed.append(out)
        cross_sums.append(sums)
        second.append(first[b] + dot(out, c_out_all, 0, 0))
        threes.append(norm_forward(second[b], gain_three, shift_three))
        whole_three.append(jnp.concatenate(spread(threes[b][0].astype(bf16)), axis=0))

    down_in = [jnp.concatenate(spread(cotangent[b]), axis=0) for b in clips]
    hidden, grad_gate, grad_upper, back_three, output = [], [], [], [], []
    for b in clips:
        grad_hidden = dot(down_in[b], w_down, 1, 1)
        gate = dot(whole_three[b], w_gate, 1, 0)
        upper = dot(whole_three[b], w_up, 1, 0)
        sigma = jax.nn.sigmoid(gate)
        hidden.append((gate * sigma * upper).astype(bf16))
        grad_gate.append(
            (grad_hidden * upper * sigma * (1.0 + gate * (1.0 - sigma))).astype(bf16)
        )
        grad_upper.append((grad_hidden * gate * sigma).astype(bf16))
        back = dot(grad_gate[b], w_gate, 1, 1) + dot(grad_upper[b], w_up, 1, 1)
        back_three.append(settle(row_blocks(back.astype(bf16), size)))
        branch = dot(hidden[b], w_down, 1, 0)
        output.append(second[b] + settle(row_blocks(branch.astype(bf16), size)))

    grad_two, grad_one, cross_in, self_in = [], [], [], []
    grad_cross_query, grad_memory, grad_mixed, back_two = [], [], [], []
    for b in clips:
        cot = cotangent[b].astype(f32)
        grad_two.append(cot + norm_backward(back_three[b], threes[b][1], threes[b][2], gain_three))
        cross_in.append(grad_two[b].astype(bf16))
        grads = dot(c_out_all, cross_in[b], 1, 1).astype(bf16)
        grad_queries, grad_keys, grad_values = cross_backward(
            b,
            size,
            lengths,
            cross_query[b],
            cross_keys[b],
            cross_values[b],
            grads,
            cross_mixed[b],
            cross_sums[b],
        )
        grad_cross_query.append(grad_queries)
        grad_memory.append(
            jnp.concatenate(
                [grad_keys.reshape(size, local, -1), grad_values.reshape(size, local, -1)], axis=1
            )
        )
        back_two.append(dot(grad_queries, c_query_all, 0, 1))
        grad_one.append(
            grad_two[b] + norm_backward(back_two[b], twos[b][1], twos[b][2], gain_two)
        )
        self_in.append(grad_one[b].astype(bf16))
        grads = dot(out_all, self_in[b], 1, 1).astype(bf16)
        grad_mixed.append(jnp.concatenate(trade(row_blocks(grads, size)), axis=1))

    grad_self, grad_front, back_one = [], [], []
    for b in clips:
        grads, grad_front_key, grad_front_value = self_backward(
            turned[b],
            grad_mixed[b],
            mixed_part[b],
            logsum[b],
            front_keys[b],
            front_values[b],
            cosine,
            sine,
        )
        grad_self.append(grads.reshape(3 * local, -1))
        grad_front.append(jnp.concatenate([grad_front_key, grad_front_value], axis=0))
        back = dot(grad_self[b], w_self, 0, 1).astype(bf16)
        back_one.append(settle(row_blocks(back, size)))
    grad_frames = [
        grad_one[b] + norm_backward(back_one[b], ones[b][1], ones[b][2], gain_one) for b in clips
    ]

    def joined(parts, axis):
        return jnp.concatenate(parts, axis=axis)

    hidden_all = joined(hidden, 0)
    three_all = joined(whole_three, 0)
    grad_w_down = sum_over_clips(dot(hidden_all, joined(down_in, 0), 0, 0), 1)
    grad_w_gate = sum_over_clips(dot(three_all, joined(grad_gate, 0), 0, 0), 0)
    grad_w_up = sum_over_clips(dot(three_all, joined(grad_upper, 0), 0, 0), 0)

    def from_rows(grad):
        return settle(row_blocks(sum_over_clips(grad, 1), size))

    grad_c_out = from_rows(dot(joined(cross_mixed, 1), joined(cross_in, 0), 1, 0))
    grad_w_out = from_rows(dot(joined(mixed, 1), joined(self_in, 0), 1, 0))
    grad_c_query = dot(joined(normed_two, 0), joined(grad_cross_query, 1), 0, 1)
    grad_c_query = settle(jnp.split(sum_over_clips(grad_c_query, 0), size, axis=1))

    grad_memory = jnp.stack(grad_memory)
    grad_memory = settle([grad_memory[:, k] for k in range(size)]).astype(bf16)
    grad_memory = joined([grad_memory[b] for b in clips], 1)
    grad_c_memory = dot(prompt.reshape(-1, prompt.shape[-1]), grad_memory, 0, 1)
    grad_c_memory = sum_over_clips(grad_c_memory, 0)

    grad_front = joined(grad_front, 1)
    grad_w_self = dot(joined(whole_one, 0), joined(grad_self, 1), 0, 1)
    grad_w_front = dot(prefix_low, grad_front, 0, 1)
    grad_w_self = joined(
        [grad_w_self[:, :local], grad_w_self[:, local:] + grad_w_front], 1
    )
    grad_w_self = sum_over_clips(grad_w_self, 0)

    early = []
    for back, kept in ((back_two, twos), (back_three, threes)):
        early.append(sum(jnp.sum(back[b] * kept[b][1], axis=0) for b in clips))
        early.append(sum(jnp.sum(back[b], axis=0) for b in clips))
    early = all_sum(jnp.stack(early))

    back_prefix = dot(grad_front, w_self[:, local:], 0, 1)
    grad_picked = norm_backward(back_prefix, prefix_normal, prefix_scale, gain_one)
    groups = lax.axis_size("dp")
    spots = jnp.arange(groups)[:, None, None] == lax.axis_index("dp")
    spots = jnp.where(spots, grad_picked[None], 0.0).reshape(groups * count, width)
    gain_term = jnp.sum(back_prefix * prefix_normal, axis=0)
    shift_term = jnp.sum(back_prefix, axis=0)
    for b in clips:
        gain_term = gain_term + jnp.sum(back_one[b] * ones[b][1], axis=0)
        shift_term = shift_term + jnp.sum(back_one[b], axis=0)
    late = all_sum(jnp.concatenate([gain_term[None], shift_term[None], spots], axis=0))
    all_steps = lax.all_gather(tsteps, "dp", axis=0, tiled=True)
    matches = (jnp.arange(table.shape[0])[:, None] == all_steps[None, :]).astype(f32)
    grad_table = jnp.dot(matches, late[2:], precision=lax.Precision.HIGHEST)

    wide = lambda value: value.astype(f32)
    return (
        jnp.stack(output),
        jnp.stack(grad_frames),
        grad_table,
        late[0],
        late[1],
        early[0],
        early[1],
        early[2],
        early[3],
        wide(grad_w_self[:, :local]),
        wide(grad_w_self[:, local : 2 * local]),
        wide(grad_w_self[:, 2 * local :]),
        grad_w_out,
        grad_c_query,
        wide(grad_c_memory[:, :local]),
        wide(grad_c_memory[:, local:]),
        grad_c_out,
        wide(grad_w_gate),
        wide(grad_w_up),
        wide(grad_w_down),
    )


def solution(mesh):
    placed = (
        P("dp", "mp", None),
        P("dp", None, None),
        P("dp"),
        P("dp"),
        P(),
        P(),
        P(),
        P(),
        P(),
        P(),
        P(),
        P(None, "mp"),
        P(None, "mp"),
        P(None, "mp"),
        P("mp", None),
        P(None, "mp"),
        P(None, "mp"),
        P(None, "mp"),
        P("mp", None),
        P(None, "mp"),
        P(None, "mp"),
        P("mp", None),
        P("dp", "mp", None),
    )
    return jax.shard_map(
        shards,
        mesh=mesh,
        in_specs=placed,
        out_specs=(
            P("dp", "mp", None),
            P("dp", "mp", None),
            P(),
            P(),
            P(),
            P(),
            P(),
            P(),
            P(),
            P("dp", "mp"),
            P("dp", "mp"),
            P("dp", "mp"),
            P("mp", "dp"),
            P("dp", "mp"),
            P("dp", "mp"),
            P("dp", "mp"),
            P("mp", "dp"),
            P("dp", "mp"),
            P("dp", "mp"),
            P("mp", "dp"),
        ),
        check_vma=False,
    )
```

time: 2000 us -> 1080 us (0.54)
  waiting for transfers between devices: 1330 us -> 467 us
  matrix products: 426 us -> 231 us
  starting transfers between devices: 3.17 us -> 109 us
  Pallas kernels: 0 us -> 81.2 us
  other arithmetic: 144 us -> 65.2 us
  local copies, waits for them, and re-layouts: 31.8 us -> 92.8 us
  blocking collectives: 41.3 us -> 9.79 us
    reduce_scatter x15 -> x6, waiting for transfers between devices: 895 us -> 153 us  [sum_over_clips(): lax.psum_scatter(values.astype(bf16), 'dp', scatter_dimension=axis, tiled...]
    ppermute x0 -> x108, waiting for transfers between devices: none -> 315 us  [swap(): lax.ppermute(values, axis, [(i, i ^ k) for i in range(lax.axis_size(axis))])]
    all_gather x6 -> x1, waiting for transfers between devices: 312 us -> 0.01 us  [whole_columns(): return lax.all_gather(wide, 'dp', axis=0, tiled=True)]
    dot_general x53 -> x42, matrix products: 426 us -> 231 us  [the longest x41 226 us: dot(): lax.dot_general(left, right, (((left_axis,), (right_axis,)), ((), ())), p...]
    psum x1 -> x0, waiting for transfers between devices: 111 us -> none  [shards(): summed_small, summed_table = lax.psum((stacked, table_term), ('dp', 'mp'))]
    ppermute x0 -> x108, starting transfers between devices: none -> 108 us  [swap(): lax.ppermute(values, axis, [(i, i ^ k) for i in range(lax.axis_size(axis))])]
    pallas_call x0 -> x8, Pallas kernels: none -> 81.2 us  [the longest x2 34 us: self_backward(): pl.pallas_call(functools.partial(self_backward_kernel, min(256, frames)),...]
    convert_element_type x20 -> x11, other arithmetic: 78.1 us -> 17.9 us  [the longest x3 6.72 us: shards(): wide = lambda value: value.astype(f32)]
  transfers between devices with their start and end apart: 24 -> 117, of which waited for: 19 -> 49; matrix products, arithmetic and copies ran while one was open for 19% -> 33% of each run, Pallas kernels for 0% -> 6%
where the time goes in v1:
time: 1080 us; the launch traced here: 1070 us
  waiting for transfers between devices  467 us (43%)
  matrix products  231 us (21%)
  starting transfers between devices  109 us (10%)
  local copies, waits for them, and re-layouts  92.8 us (9%)
  Pallas kernels  81.2 us (8%)
  other arithmetic  65.2 us (6%)
  between operations  17.5 us (2%)
    ppermute x108, waiting for transfers between devices, swap(): lax.ppermute(values, axis, [(i, i ^ k) for i in range(lax.axis_size(axis))])  315 us
    dot_general x41, matrix products, dot(): lax.dot_general(left, right, (((left_axis,), (right_axis,)), ((), ())), p...  226 us
    reduce_scatter x6, waiting for transfers between devices, sum_over_clips(): lax.psum_scatter(values.astype(bf16), 'dp', scatter_dimension=axis, tiled...  153 us
    ppermute x108, starting transfers between devices, swap(): lax.ppermute(values, axis, [(i, i ^ k) for i in range(lax.axis_size(axis))])  108 us
    unnamed x391, local copies, waits for them, and re-layouts  63.4 us
    pallas_call x2, Pallas kernels, self_backward(): pl.pallas_call(functools.partial(self_backward_kernel, min(256, frames)),...  34 us
  transfers between devices with their start and end apart: 117, of which 49 were waited for; matrix products, arithmetic and copies ran while one was open for 33% of the time, Pallas kernels for 6%

profile of v1, /device:TPU:0, one launch (start us, length us, event | category | flops | bytes accessed | tf_op | source)
XLA Modules:
  0.0 1073.7 jit_solution(10306249931063289029)
XLA Ops:
  71.3 8.5 collective-permute-done.20
  82.2 13.9 %collective-permute-done = bf16[128,1536]{1,0:T(8,128)(2,1)S(1)} collective-permute-done((bf16[128,1536]{1,0:T(8,128)(2,1)}, bf16[128,1536]{1,0:T(8,128)(2,1)S(1)}, u32[]{:S(2)}, u32[]{:S(2)}) %collective-permute-start) | collective-permute-done | bytes 393248 | tf_op jit(solution)/shard_map/ppermute | solution.py:48
  118.8 8.5 collective-permute-done.13
  135.2 8.6 collective-permute-done.27
  145.2 9.3 collective-permute-done.61
  185.8 9.1 collective-permute-done.38
  198.8 8.1 collective-permute-done.40
  221.0 10.6 self_forward.3
  235.7 10.6 self_forward.2
  265.4 6.7 cross_forward.2
  290.1 7.2 collective-permute-done.32
  313.7 7.0 fusion.167
  320.7 6.9 fusion.168
  327.7 14.1 %multiply_convert_fusion.2 = (bf16[1024,1536]{1,0:T(8,128)(2,1)}, bf16[1024,1536]{1,0:T(8,128)(2,1)}, bf16[1024,1536]{1,0:T(8,128)(2,1)}) fusion(f32[1024,1536]{1,0:T(8,128)} %fusion.167, f32[1024,1536]{1,0:T(8,128)} %fusion.168, bf16[1024,1536]{1,0:T(8,128)(2,1)S(1)} %copy-done.94, bf16[1536,1536]{1,0:T(8,128)(2,1)} %param.44), kind=kOutput, calls=%fused_computation.20 | convolution fusion | flops 4857004032 | bytes 29884416 | tf_op jit(solution)/shard_map/dot_general | solution.py:22
  341.9 9.1 fusion.172
  351.0 8.6 add_convert_fusion.1
  376.6 29.0 %collective-permute-done.51 = bf16[128,1536]{1,0:T(8,128)(2,1)S(1)} collective-permute-done((bf16[128,1536]{1,0:T(8,128)(2,1)S(1)}, bf16[128,1536]{1,0:T(8,128)(2,1)S(1)}, u32[]{:S(2)}, u32[]{:S(2)}) %collective-permute-start.51) | collective-permute-done | bytes 393248 | tf_op jit(solution)/shard_map/ppermute | solution.py:48
  408.3 7.0 fusion.170
  415.3 7.0 fusion.171
  422.3 14.3 %multiply_convert_fusion = (bf16[1024,1536]{1,0:T(8,128)(2,1)}, bf16[1024,1536]{1,0:T(8,128)(2,1)}, bf16[1024,1536]{1,0:T(8,128)(2,1)}) fusion(f32[1024,1536]{1,0:T(8,128)} %fusion.170, f32[1024,1536]{1,0:T(8,128)} %fusion.171, bf16[1024,1536]{1,0:T(8,128)(2,1)S(1)} %copy-done.93, bf16[1536,1536]{1,0:T(8,128)(2,1)} %param.44), kind=kOutput, calls=%fused_computation.17 | convolution fusion | flops 4857004032 | bytes 29884416 | tf_op jit(solution)/shard_map/dot_general | solution.py:22
  436.6 9.9 fusion.173
  446.4 8.7 add_convert_fusion
  455.2 7.1 convolution_convert_fusion.6
  468.9 15.0 %collective-permute-done.37 = bf16[256,1536]{1,0:T(8,128)(2,1)S(1)} collective-permute-done((bf16[256,1536]{1,0:T(8,128)(2,1)S(1)}, bf16[256,1536]{1,0:T(8,128)(2,1)S(1)}, u32[]{:S(2)}, u32[]{:S(2)}) %collective-permute-start.37) | collective-permute-done | bytes 786464 | tf_op jit(solution)/shard_map/ppermute | solution.py:48
  489.9 10.3 collective-permute-done.77
  502.7 14.9 %collective-permute-done.79 = bf16[256,1536]{1,0:T(8,128)(2,1)S(1)} collective-permute-done((bf16[256,1536]{1,0:T(8,128)(2,1)S(1)}, bf16[256,1536]{1,0:T(8,128)(2,1)S(1)}, u32[]{:S(2)}, u32[]{:S(2)}) %collective-permute-start.79) | collective-permute-done | bytes 786464 | tf_op jit(solution)/shard_map/ppermute | solution.py:48
  519.3 13.4 %collective-permute-done.53 = bf16[256,1536]{1,0:T(8,128)(2,1)S(1)} collective-permute-done((bf16[256,1536]{1,0:T(8,128)(2,1)S(1)}, bf16[256,1536]{1,0:T(8,128)(2,1)S(1)}, u32[]{:S(2)}, u32[]{:S(2)}) %collective-permute-start.53) | collective-permute-done | bytes 786464 | tf_op jit(solution)/shard_map/ppermute | solution.py:48
  533.4 8.6 collective-permute-done.55
  547.9 6.5 cross_backward.3
  554.5 6.5 cross_backward.2
  589.2 16.9 %self_backward.3 = (bf16[3,384,1024]{2,1,0:T(8,128)(2,1)S(1)}, bf16[384,1]{1,0:T(8,128)(2,1)S(1)}, bf16[384,1]{1,0:T(8,128)(2,1)S(1)}) custom-call(bf16[1152,1024]{1,0:T(8,128)(2,1)S(1)} %copy-done.5, bf16[1152,1024]{1,0:T(8,128)(2,1)S(1)} %copy-done.5, bf16[1152,1024]{1,0:T(8,128)(2,1)S(1)} %copy-done.5, bf16[384,1024]{1,0:T(8,128)(2,1)S(1)} %pad_maximum_fusion.13.g_ref, ...), custom_call_target="tpu_custom_call" | custom-call | flops 16106127360 | bytes 7864320 | tf_op jit(solution)/shard_map/self_backward/pallas_call | solution.py:265
  609.3 17.1 %self_backward.2 = (bf16[3,384,1024]{2,1,0:T(8,128)(2,1)S(1)}, bf16[384,1]{1,0:T(8,128)(2,1)S(1)}, bf16[384,1]{1,0:T(8,128)(2,1)S(1)}) custom-call(bf16[1152,1024]{1,0:T(8,128)(2,1)S(1)} %copy-done.3, bf16[1152,1024]{1,0:T(8,128)(2,1)S(1)} %copy-done.3, bf16[1152,1024]{1,0:T(8,128)(2,1)S(1)} %copy-done.3, bf16[384,1024]{1,0:T(8,128)(2,1)S(1)} %pad_maximum_fusion.12.g_ref, ...), custom_call_target="tpu_custom_call" | custom-call | flops 16106127360 | bytes 7864320 | tf_op jit(solution)/shard_map/self_backward/pallas_call | solution.py:265
  632.8 10.4 fusion.10
  652.1 15.9 %convolution_convert_fusion.3 = bf16[1536,1536]{0,1:T(8,128)(2,1)} fusion(bf16[2048,1536]{1,0:T(8,128)(2,1)} %get-tuple-element.291, bf16[1024,1536]{1,0:T(8,128)(2,1)} %get-tuple-element.189, bf16[1024,1536]{1,0:T(8,128)(2,1)} %get-tuple-element.186), kind=kOutput, calls=%fused_computation.4 | convolution fusion | flops 9678618624 | bytes 17301504 | tf_op jit(solution)/shard_map/dot_general | solution.py:22
  668.1 15.6 %convolution_convert_fusion.4 = bf16[1536,1536]{1,0:T(8,128)(2,1)} fusion(bf16[2048,1536]{1,0:T(8,128)(2,1)} %get-tuple-element.303, bf16[1024,1536]{1,0:T(8,128)(2,1)} %get-tuple-element.187, bf16[1024,1536]{1,0:T(8,128)(2,1)} %get-tuple-element.184), kind=kOutput, calls=%fused_computation.5 | convolution fusion | flops 9678618624 | bytes 17301504 | tf_op jit(solution)/shard_map/dot_general | solution.py:22
  683.7 15.8 %convolution_convert_fusion.5 = bf16[1536,1536]{1,0:T(8,128)(2,1)} fusion(bf16[2048,1536]{1,0:T(8,128)(2,1)} %get-tuple-element.303, bf16[1024,1536]{1,0:T(8,128)(2,1)} %get-tuple-element.188, bf16[1024,1536]{1,0:T(8,128)(2,1)} %get-tuple-element.185), kind=kOutput, calls=%fused_computation.6 | convolution fusion | flops 9678618624 | bytes 17301504 | tf_op jit(solution)/shard_map/dot_general | solution.py:22
  708.2 6.5 convolution_convert_fusion.1
  729.2 9.8 all-reduce
  741.4 6.5 convolution_convert_fusion.2
  772.6 8.1 collective-permute-done.83
  783.1 15.6 %collective-permute-done.84 = bf16[256,1536]{1,0:T(8,128)(2,1)} collective-permute-done((bf16[256,1536]{1,0:T(8,128)(2,1)S(1)}, bf16[256,1536]{1,0:T(8,128)(2,1)}, u32[]{:S(2)}, u32[]{:S(2)}) %collective-permute-start.84) | collective-permute-done | bytes 786464 | tf_op jit(solution)/shard_map/ppermute | solution.py:48
  798.7 15.8 %collective-permute-done.68 = bf16[256,1536]{1,0:T(8,128)(2,1)} collective-permute-done((bf16[256,1536]{1,0:T(8,128)(2,1)}, bf16[256,1536]{1,0:T(8,128)(2,1)}, u32[]{:S(2)}, u32[]{:S(2)}) %collective-permute-start.68) | collective-permute-done | bytes 786464 | tf_op jit(solution)/shard_map/ppermute | solution.py:48
  814.6 14.4 %collective-permute-done.69 = bf16[256,1536]{1,0:T(8,128)(2,1)} collective-permute-done((bf16[256,1536]{1,0:T(8,128)(2,1)}, bf16[256,1536]{1,0:T(8,128)(2,1)}, u32[]{:S(2)}, u32[]{:S(2)}) %collective-permute-start.69) | collective-permute-done | bytes 786464 | tf_op jit(solution)/shard_map/ppermute | solution.py:48
  848.3 7.1 collective-permute-done.89
  859.0 13.0 %collective-permute-done.90 = f32[18,1536]{1,0:T(8,128)S(1)} collective-permute-done((f32[18,1536]{1,0:T(8,128)S(1)}, f32[18,1536]{1,0:T(8,128)S(1)}, u32[]{:S(2)}, u32[]{:S(2)}) %collective-permute-start.90) | collective-permute-done | bytes 110624 | tf_op jit(solution)/shard_map/ppermute | solution.py:48
  891.3 49.9 %reduce-scatter.17.cloned.1.call-done = bf16[1536,192]{0,1:T(8,128)(2,1)} async-done(((bf16[1536,1536]{0,1:T(8,128)(2,1)}), bf16[1536,192]{0,1:T(8,128)(2,1)}) %reduce-scatter.17.cloned.1.call-update) | async-done | bytes 589840 | tf_op jit(solution)/shard_map/reduce_scatter | solution.py:383
  945.9 51.1 %reduce-scatter.15.cloned.1.call-done = bf16[192,1536]{1,0:T(8,128)(2,1)} async-done(((bf16[1536,1536]{1,0:T(8,128)(2,1)}), bf16[192,1536]{1,0:T(8,128)(2,1)}) %reduce-scatter.15.cloned.1.call-update) | async-done | bytes 589840 | tf_op jit(solution)/shard_map/reduce_scatter | solution.py:383
  1001.1 51.7 %reduce-scatter.13.cloned.1.call-done = bf16[1536,192]{0,1:T(8,128)(2,1)} async-done(((bf16[1536,1536]{0,1:T(8,128)(2,1)}), bf16[1536,192]{0,1:T(8,128)(2,1)}) %reduce-scatter.13.cloned.1.call-update) | async-done | bytes 589840 | tf_op jit(solution)/shard_map/reduce_scatter | solution.py:383
  (808 shorter events, 409.9 us)
Async XLA Ops:
  7.2 254.0 %all-gather.2.cloned.1.call-start = ((), (), s32[]{:S(2)}) async-start(), calls=%async_computation.8 | async-start | bytes 5308416 | tf_op jit(solution)/shard_map/all_gather | solution.py:102
  9.3 33.9 %collective-permute-start.9 = (bf16[96,1536]{1,0:T(8,128)(2,1)}, bf16[96,1536]{1,0:T(8,128)(2,1)}, u32[]{:S(2)}, u32[]{:S(2)}) collective-permute-start(bf16[96,1536]{1,0:T(8,128)(2,1)} %get-tuple-element.250), channel_id=1, source_target_pairs={{0,1},{1,0},{2,3},{3,2},{4,5},{5,4},{6,7},{7,6},{8,9},{9,8},{10,11... | collective-permute-start | bytes 884744 | tf_op jit(solution)/shard_map/ppermute | solution.py:48
  12.3 40.9 %collective-permute-start.11 = (bf16[96,1536]{1,0:T(8,128)(2,1)}, bf16[96,1536]{1,0:T(8,128)(2,1)}, u32[]{:S(2)}, u32[]{:S(2)}) collective-permute-start(bf16[96,1536]{1,0:T(8,128)(2,1)} %get-tuple-element.250), channel_id=1, source_target_pairs={{0,2},{1,3},{2,0},{3,1},{4,6},{5,7},{6,4},{7,5},{8,10},{9,11},{10,... | collective-permute-start | bytes 884744 | tf_op jit(solution)/shard_map/ppermute | solution.py:48
  43.0 834.9 %reduce-scatter.27.cloned.1.call-start = ((), (), s32[]{:S(2)}) async-start(), calls=%async_computation.16 | async-start | bytes 1327104
  62.7 45.0 %collective-permute-start.56 = (bf16[128,1536]{1,0:T(8,128)(2,1)}, bf16[128,1536]{1,0:T(8,128)(2,1)S(1)}, u32[]{:S(2)}, u32[]{:S(2)}) collective-permute-start(bf16[128,1536]{1,0:T(8,128)(2,1)} %get-tuple-element.240), channel_id=1, source_target_pairs={{0,1},{1,0},{2,3},{3,2},{4,5},{5,4},{6,7},{7,6},{8,9},{9,8},{10,11... | collective-permute-start | bytes 1179656 | tf_op jit(solution)/shard_map/ppermute | solution.py:48
  64.5 50.7 %collective-permute-start.58 = (bf16[128,1536]{1,0:T(8,128)(2,1)}, bf16[128,1536]{1,0:T(8,128)(2,1)S(1)}, u32[]{:S(2)}, u32[]{:S(2)}) collective-permute-start(bf16[128,1536]{1,0:T(8,128)(2,1)} %get-tuple-element.240), channel_id=1, source_target_pairs={{0,2},{1,3},{2,0},{3,1},{4,6},{5,7},{6,4},{7,5},{8,10},{9,11},{10,... | collective-permute-start | bytes 1179656 | tf_op jit(solution)/shard_map/ppermute | solution.py:48
  70.8 25.3 %collective-permute-start = (bf16[128,1536]{1,0:T(8,128)(2,1)}, bf16[128,1536]{1,0:T(8,128)(2,1)S(1)}, u32[]{:S(2)}, u32[]{:S(2)}) collective-permute-start(bf16[128,1536]{1,0:T(8,128)(2,1)} %get-tuple-element.278), channel_id=1, source_target_pairs={{0,1},{1,0},{2,3},{3,2},{4,5},{5,4},{6,7},{7,6},{8,9},{9,8},{10,11... | collective-permute-start | bytes 1179656 | tf_op jit(solution)/shard_map/ppermute | solution.py:48
  106.9 67.0 %collective-permute-start.72 = (bf16[128,1536]{1,0:T(8,128)(2,1)S(1)}, bf16[128,1536]{1,0:T(8,128)(2,1)S(1)}, u32[]{:S(2)}, u32[]{:S(2)}) collective-permute-start(bf16[128,1536]{1,0:T(8,128)(2,1)S(1)} %copy-done.69), channel_id=1, source_target_pairs={{0,1},{1,0},{2,3},{3,2},{4,5},{5,4},{6,7},{7,6},{8,9},{9,8},{10,11... | collective-permute-start | bytes 1179656 | tf_op jit(solution)/shard_map/ppermute | solution.py:48
  107.7 47.6 %collective-permute-start.74 = (bf16[128,1536]{1,0:T(8,128)(2,1)S(1)}, bf16[128,1536]{1,0:T(8,128)(2,1)S(1)}, u32[]{:S(2)}, u32[]{:S(2)}) collective-permute-start(bf16[128,1536]{1,0:T(8,128)(2,1)S(1)} %copy-done.69), channel_id=1, source_target_pairs={{0,2},{1,3},{2,0},{3,1},{4,6},{5,7},{6,4},{7,5},{8,10},{9,11},{10,... | collective-permute-start | bytes 1179656 | tf_op jit(solution)/shard_map/ppermute | solution.py:48
  113.8 41.5 %collective-permute-start.71 = (bf16[128,1536]{1,0:T(8,128)(2,1)S(1)}, bf16[128,1536]{1,0:T(8,128)(2,1)S(1)}, u32[]{:S(2)}, u32[]{:S(2)}) collective-permute-start(bf16[128,1536]{1,0:T(8,128)(2,1)S(1)} %get-tuple-element.242), channel_id=1, source_target_pairs={{0,1},{1,0},{2,3},{3,2},{4,5},{5,4},{6,7},{7,6},{8,9},{9,8},{10,11... | collective-permute-start | bytes 1179656 | tf_op jit(solution)/shard_map/ppermute | solution.py:48
  164.2 82.1 %collective-permute-start.15 = (bf16[3,192,1536]{2,1,0:T(8,128)(2,1)S(1)}, bf16[3,192,1536]{2,1,0:T(8,128)(2,1)S(1)}, u32[]{:S(2)}, u32[]{:S(2)}) collective-permute-start(bf16[3,192,1536]{2,1,0:T(8,128)(2,1)S(1)} %bitcast.280), channel_id=1, source_target_pairs={{0,4},{4,0},{8,12},{12,8},{16,20},{20,16},{24,28},{28,24},{1,5},{5... | collective-permute-start | bytes 5308424 | tf_op jit(solution)/shard_map/ppermute | solution.py:48
  173.9 73.0 %collective-permute-start.28 = (bf16[3,192,1536]{2,1,0:T(8,128)(2,1)S(1)}, bf16[3,192,1536]{2,1,0:T(8,128)(2,1)S(1)}, u32[]{:S(2)}, u32[]{:S(2)}) collective-permute-start(bf16[3,192,1536]{2,1,0:T(8,128)(2,1)S(1)} %bitcast.278), channel_id=1, source_target_pairs={{0,4},{4,0},{8,12},{12,8},{16,20},{20,16},{24,28},{28,24},{1,5},{5... | collective-permute-start | bytes 5308424 | tf_op jit(solution)/shard_map/ppermute | solution.py:48
  309.6 59.2 %collective-permute-start.47 = (bf16[128,1536]{1,0:T(8,128)(2,1)S(1)}, bf16[128,1536]{1,0:T(8,128)(2,1)S(1)}, u32[]{:S(2)}, u32[]{:S(2)}) collective-permute-start(bf16[128,1536]{1,0:T(8,128)(2,1)S(1)} %get-tuple-element.264), channel_id=1, source_target_pairs={{0,1},{1,0},{2,3},{3,2},{4,5},{5,4},{6,7},{7,6},{8,9},{9,8},{10,11... | collective-permute-start | bytes 1179656 | tf_op jit(solution)/shard_map/ppermute | solution.py:48
  309.6 63.2 %collective-permute-start.49 = (bf16[128,1536]{1,0:T(8,128)(2,1)S(1)}, bf16[128,1536]{1,0:T(8,128)(2,1)S(1)}, u32[]{:S(2)}, u32[]{:S(2)}) collective-permute-start(bf16[128,1536]{1,0:T(8,128)(2,1)S(1)} %get-tuple-element.264), channel_id=1, source_target_pairs={{0,2},{1,3},{2,0},{3,1},{4,6},{5,7},{6,4},{7,5},{8,10},{9,11},{10,... | collective-permute-start | bytes 1179656 | tf_op jit(solution)/shard_map/ppermute | solution.py:48
  310.8 59.9 %collective-permute-start.48 = (bf16[128,1536]{1,0:T(8,128)(2,1)S(1)}, bf16[128,1536]{1,0:T(8,128)(2,1)S(1)}, u32[]{:S(2)}, u32[]{:S(2)}) collective-permute-start(bf16[128,1536]{1,0:T(8,128)(2,1)S(1)} %get-tuple-element.263), channel_id=1, source_target_pairs={{0,1},{1,0},{2,3},{3,2},{4,5},{5,4},{6,7},{7,6},{8,9},{9,8},{10,11... | collective-permute-start | bytes 1179656 | tf_op jit(solution)/shard_map/ppermute | solution.py:48
  312.7 61.2 %collective-permute-start.50 = (bf16[128,1536]{1,0:T(8,128)(2,1)S(1)}, bf16[128,1536]{1,0:T(8,128)(2,1)S(1)}, u32[]{:S(2)}, u32[]{:S(2)}) collective-permute-start(bf16[128,1536]{1,0:T(8,128)(2,1)S(1)} %get-tuple-element.263), channel_id=1, source_target_pairs={{0,2},{1,3},{2,0},{3,1},{4,6},{5,7},{6,4},{7,5},{8,10},{9,11},{10,... | collective-permute-start | bytes 1179656 | tf_op jit(solution)/shard_map/ppermute | solution.py:48
  360.9 101.4 %collective-permute-start.62 = (bf16[256,1536]{1,0:T(8,128)(2,1)S(1)}, bf16[256,1536]{1,0:T(8,128)(2,1)S(1)}, u32[]{:S(2)}, u32[]{:S(2)}) collective-permute-start(bf16[256,1536]{1,0:T(8,128)(2,1)S(1)} %get-tuple-element.204), channel_id=1, source_target_pairs={{0,1},{1,0},{2,3},{3,2},{4,5},{5,4},{6,7},{7,6},{8,9},{9,8},{10,11... | collective-permute-start | bytes 2359304 | tf_op jit(solution)/shard_map/ppermute | solution.py:48
  368.8 96.4 %collective-permute-start.63 = (bf16[256,1536]{1,0:T(8,128)(2,1)}, bf16[256,1536]{1,0:T(8,128)(2,1)S(1)}, u32[]{:S(2)}, u32[]{:S(2)}) collective-permute-start(bf16[256,1536]{1,0:T(8,128)(2,1)} %get-tuple-element.206), channel_id=1, source_target_pairs={{0,2},{1,3},{2,0},{3,1},{4,6},{5,7},{6,4},{7,5},{8,10},{9,11},{10,... | collective-permute-start | bytes 2359304 | tf_op jit(solution)/shard_map/ppermute | solution.py:48
  370.7 94.6 %collective-permute-start.64 = (bf16[256,1536]{1,0:T(8,128)(2,1)}, bf16[256,1536]{1,0:T(8,128)(2,1)}, u32[]{:S(2)}, u32[]{:S(2)}) collective-permute-start(bf16[256,1536]{1,0:T(8,128)(2,1)} %get-tuple-element.205), channel_id=1, source_target_pairs={{0,3},{1,2},{2,1},{3,0},{4,7},{5,6},{6,5},{7,4},{8,11},{9,10},{10,... | collective-permute-start | bytes 2359304 | tf_op jit(solution)/shard_map/ppermute | solution.py:48
  372.8 32.8 %collective-permute-start.51 = (bf16[128,1536]{1,0:T(8,128)(2,1)S(1)}, bf16[128,1536]{1,0:T(8,128)(2,1)S(1)}, u32[]{:S(2)}, u32[]{:S(2)}) collective-permute-start(bf16[128,1536]{1,0:T(8,128)(2,1)S(1)} %collective-permute-done.47), channel_id=1, source_target_pairs={{0,2},{1,3},{2,0},{3,1},{4,6},{5,7},{6,4},{7,5},{8,10},{9,11},{10,... | collective-permute-start | bytes 1179656 | tf_op jit(solution)/shard_map/ppermute | solution.py:48
  373.9 32.5 %collective-permute-start.52 = (bf16[128,1536]{1,0:T(8,128)(2,1)S(1)}, bf16[128,1536]{1,0:T(8,128)(2,1)S(1)}, u32[]{:S(2)}, u32[]{:S(2)}) collective-permute-start(bf16[128,1536]{1,0:T(8,128)(2,1)S(1)} %collective-permute-done.50), channel_id=1, source_target_pairs={{0,1},{1,0},{2,3},{3,2},{4,5},{5,4},{6,7},{7,6},{8,9},{9,8},{10,11... | collective-permute-start | bytes 1179656 | tf_op jit(solution)/shard_map/ppermute | solution.py:48
  405.6 60.8 %collective-permute-start.35 = (bf16[256,1536]{1,0:T(8,128)(2,1)}, bf16[256,1536]{1,0:T(8,128)(2,1)}, u32[]{:S(2)}, u32[]{:S(2)}) collective-permute-start(bf16[256,1536]{1,0:T(8,128)(2,1)} %get-tuple-element.210), channel_id=1, source_target_pairs={{0,1},{1,0},{2,3},{3,2},{4,5},{5,4},{6,7},{7,6},{8,9},{9,8},{10,11... | collective-permute-start | bytes 2359304 | tf_op jit(solution)/shard_map/ppermute | solution.py:48
  406.4 62.3 %collective-permute-start.36 = (bf16[256,1536]{1,0:T(8,128)(2,1)}, bf16[256,1536]{1,0:T(8,128)(2,1)}, u32[]{:S(2)}, u32[]{:S(2)}) collective-permute-start(bf16[256,1536]{1,0:T(8,128)(2,1)} %get-tuple-element.212), channel_id=1, source_target_pairs={{0,2},{1,3},{2,0},{3,1},{4,6},{5,7},{6,4},{7,5},{8,10},{9,11},{10,... | collective-permute-start | bytes 2359304 | tf_op jit(solution)/shard_map/ppermute | solution.py:48
  465.2 35.0 %collective-permute-start.77 = (bf16[256,1536]{1,0:T(8,128)(2,1)S(1)}, bf16[256,1536]{1,0:T(8,128)(2,1)S(1)}, u32[]{:S(2)}, u32[]{:S(2)}) collective-permute-start(bf16[256,1536]{1,0:T(8,128)(2,1)S(1)} %get-tuple-element.207), channel_id=1, source_target_pairs={{0,1},{1,0},{2,3},{3,2},{4,5},{5,4},{6,7},{7,6},{8,9},{9,8},{10,11... | collective-permute-start | bytes 2359304 | tf_op jit(solution)/shard_map/ppermute | solution.py:48
  465.3 37.4 %collective-permute-start.78 = (bf16[256,1536]{1,0:T(8,128)(2,1)S(1)}, bf16[256,1536]{1,0:T(8,128)(2,1)S(1)}, u32[]{:S(2)}, u32[]{:S(2)}) collective-permute-start(bf16[256,1536]{1,0:T(8,128)(2,1)S(1)} %get-tuple-element.209), channel_id=1, source_target_pairs={{0,2},{1,3},{2,0},{3,1},{4,6},{5,7},{6,4},{7,5},{8,10},{9,11},{10,... | collective-permute-start | bytes 2359304 | tf_op jit(solution)/shard_map/ppermute | solution.py:48
  466.4 51.2 %collective-permute-start.79 = (bf16[256,1536]{1,0:T(8,128)(2,1)S(1)}, bf16[256,1536]{1,0:T(8,128)(2,1)S(1)}, u32[]{:S(2)}, u32[]{:S(2)}) collective-permute-start(bf16[256,1536]{1,0:T(8,128)(2,1)S(1)} %get-tuple-element.208), channel_id=1, source_target_pairs={{0,3},{1,2},{2,1},{3,0},{4,7},{5,6},{6,5},{7,4},{8,11},{9,10},{10,... | collective-permute-start | bytes 2359304 | tf_op jit(solution)/shard_map/ppermute | solution.py:48
  468.8 63.9 %collective-permute-start.53 = (bf16[256,1536]{1,0:T(8,128)(2,1)S(1)}, bf16[256,1536]{1,0:T(8,128)(2,1)S(1)}, u32[]{:S(2)}, u32[]{:S(2)}) collective-permute-start(bf16[256,1536]{1,0:T(8,128)(2,1)S(1)} %get-tuple-element.213), channel_id=1, source_target_pairs={{0,1},{1,0},{2,3},{3,2},{4,5},{5,4},{6,7},{7,6},{8,9},{9,8},{10,11... | collective-permute-start | bytes 2359304 | tf_op jit(solution)/shard_map/ppermute | solution.py:48
  483.9 49.5 %collective-permute-start.54 = (bf16[256,1536]{1,0:T(8,128)(2,1)S(1)}, bf16[256,1536]{1,0:T(8,128)(2,1)S(1)}, u32[]{:S(2)}, u32[]{:S(2)}) collective-permute-start(bf16[256,1536]{1,0:T(8,128)(2,1)S(1)} %get-tuple-element.215), channel_id=1, source_target_pairs={{0,2},{1,3},{2,0},{3,1},{4,6},{5,7},{6,4},{7,5},{8,10},{9,11},{10,... | collective-permute-start | bytes 2359304 | tf_op jit(solution)/shard_map/ppermute | solution.py:48
  500.2 41.8 %collective-permute-start.55 = (bf16[256,1536]{1,0:T(8,128)(2,1)S(1)}, bf16[256,1536]{1,0:T(8,128)(2,1)S(1)}, u32[]{:S(2)}, u32[]{:S(2)}) collective-permute-start(bf16[256,1536]{1,0:T(8,128)(2,1)S(1)} %get-tuple-element.214), channel_id=1, source_target_pairs={{0,3},{1,2},{2,1},{3,0},{4,7},{5,6},{6,5},{7,4},{8,11},{9,10},{10,... | collective-permute-start | bytes 2359304 | tf_op jit(solution)/shard_map/ppermute | solution.py:48
  562.2 66.1 %collective-permute-start.102 = (bf16[2,768,128]{2,1,0:T(8,128)(2,1)}, bf16[2,768,128]{2,1,0:T(8,128)(2,1)S(1)}, u32[]{:S(2)}, u32[]{:S(2)}) collective-permute-start(bf16[2,768,128]{2,1,0:T(8,128)(2,1)} %get-tuple-element.235), channel_id=1, source_target_pairs={{0,1},{1,0},{2,3},{3,2},{4,5},{5,4},{6,7},{7,6},{8,9},{9,8},{10,11... | collective-permute-start | bytes 1179656 | tf_op jit(solution)/shard_map/ppermute | solution.py:48
  564.0 64.4 %collective-permute-start.103 = (bf16[2,768,128]{2,1,0:T(8,128)(2,1)}, bf16[2,768,128]{2,1,0:T(8,128)(2,1)}, u32[]{:S(2)}, u32[]{:S(2)}) collective-permute-start(bf16[2,768,128]{2,1,0:T(8,128)(2,1)} %get-tuple-element.237), channel_id=1, source_target_pairs={{0,2},{1,3},{2,0},{3,1},{4,6},{5,7},{6,4},{7,5},{8,10},{9,11},{10,... | collective-permute-start | bytes 1179656 | tf_op jit(solution)/shard_map/ppermute | solution.py:48
  632.7 247.8 %reduce-scatter.25.cloned.1.call-start = ((), (), s32[]{:S(2)}) async-start(), calls=%async_computation.15 | async-start | bytes 3981312
  652.0 232.6 %reduce-scatter.23.cloned.1.call-start = ((), (), s32[]{:S(2)}) async-start(), calls=%async_computation.14 | async-start | bytes 5308416 | tf_op jit(solution)/shard_map/reduce_scatter | solution.py:383
  668.0 218.8 %reduce-scatter.21.cloned.1.call-start = ((), (), s32[]{:S(2)}) async-start(), calls=%async_computation.13 | async-start | bytes 5308416 | tf_op jit(solution)/shard_map/reduce_scatter | solution.py:383
  683.7 205.5 %reduce-scatter.19.cloned.1.call-start = ((), (), s32[]{:S(2)}) async-start(), calls=%async_computation.12 | async-start | bytes 5308416 | tf_op jit(solution)/shard_map/reduce_scatter | solution.py:383
  699.6 241.7 %reduce-scatter.17.cloned.1.call-start = ((), (), s32[]{:S(2)}) async-start(), calls=%async_computation.11 | async-start | bytes 5308416 | tf_op jit(solution)/shard_map/reduce_scatter | solution.py:383
  707.1 289.9 %reduce-scatter.15.cloned.1.call-start = ((), (), s32[]{:S(2)}) async-start(), calls=%async_computation.10 | async-start | bytes 5308416 | tf_op jit(solution)/shard_map/reduce_scatter | solution.py:383
  714.8 338.0 %reduce-scatter.13.cloned.1.call-start = ((), (), s32[]{:S(2)}) async-start(), calls=%async_computation.9 | async-start | bytes 5308416 | tf_op jit(solution)/shard_map/reduce_scatter | solution.py:383
  761.3 37.4 %collective-permute-start.84 = (bf16[256,1536]{1,0:T(8,128)(2,1)S(1)}, bf16[256,1536]{1,0:T(8,128)(2,1)}, u32[]{:S(2)}, u32[]{:S(2)}) collective-permute-start(bf16[256,1536]{1,0:T(8,128)(2,1)S(1)} %get-tuple-element.200), channel_id=1, source_target_pairs={{0,2},{1,3},{2,0},{3,1},{4,6},{5,7},{6,4},{7,5},{8,10},{9,11},{10,... | collective-permute-start | bytes 2359304 | tf_op jit(solution)/shard_map/ppermute | solution.py:48
  762.0 36.7 %collective-permute-start.85 = (bf16[256,1536]{1,0:T(8,128)(2,1)S(1)}, bf16[256,1536]{1,0:T(8,128)(2,1)}, u32[]{:S(2)}, u32[]{:S(2)}) collective-permute-start(bf16[256,1536]{1,0:T(8,128)(2,1)S(1)} %get-tuple-element.199), channel_id=1, source_target_pairs={{0,3},{1,2},{2,1},{3,0},{4,7},{5,6},{6,5},{7,4},{8,11},{9,10},{10,... | collective-permute-start | bytes 2359304 | tf_op jit(solution)/shard_map/ppermute | solution.py:48
  769.9 44.7 %collective-permute-start.68 = (bf16[256,1536]{1,0:T(8,128)(2,1)}, bf16[256,1536]{1,0:T(8,128)(2,1)}, u32[]{:S(2)}, u32[]{:S(2)}) collective-permute-start(bf16[256,1536]{1,0:T(8,128)(2,1)} %get-tuple-element.201), channel_id=1, source_target_pairs={{0,1},{1,0},{2,3},{3,2},{4,5},{5,4},{6,7},{7,6},{8,9},{9,8},{10,11... | collective-permute-start | bytes 2359304 | tf_op jit(solution)/shard_map/ppermute | solution.py:48
  771.0 58.0 %collective-permute-start.69 = (bf16[256,1536]{1,0:T(8,128)(2,1)}, bf16[256,1536]{1,0:T(8,128)(2,1)}, u32[]{:S(2)}, u32[]{:S(2)}) collective-permute-start(bf16[256,1536]{1,0:T(8,128)(2,1)} %get-tuple-element.203), channel_id=1, source_target_pairs={{0,2},{1,3},{2,0},{3,1},{4,6},{5,7},{6,4},{7,5},{8,10},{9,11},{10,... | collective-permute-start | bytes 2359304 | tf_op jit(solution)/shard_map/ppermute | solution.py:48
  781.6 47.4 %collective-permute-start.70 = (bf16[256,1536]{1,0:T(8,128)(2,1)}, bf16[256,1536]{1,0:T(8,128)(2,1)}, u32[]{:S(2)}, u32[]{:S(2)}) collective-permute-start(bf16[256,1536]{1,0:T(8,128)(2,1)} %get-tuple-element.202), channel_id=1, source_target_pairs={{0,3},{1,2},{2,1},{3,0},{4,7},{5,6},{6,5},{7,4},{8,11},{9,10},{10,... | collective-permute-start | bytes 2359304 | tf_op jit(solution)/shard_map/ppermute | solution.py:48
  942.3 111.5 %collective-permute-start.105 = (bf16[384,192]{0,1:T(8,128)(2,1)S(1)}, bf16[384,192]{0,1:T(8,128)(2,1)S(1)}, u32[]{:S(2)}, u32[]{:S(2)}) collective-permute-start(bf16[384,192]{0,1:T(8,128)(2,1)S(1)} %get-tuple-element.279), channel_id=1, source_target_pairs={{0,1},{1,0},{2,3},{3,2},{4,5},{5,4},{6,7},{7,6},{8,9},{9,8},{10,11... | collective-permute-start | bytes 442376 | tf_op jit(solution)/shard_map/ppermute | solution.py:48
  943.9 111.5 %collective-permute-start.106 = (bf16[384,192]{0,1:T(8,128)(2,1)S(1)}, bf16[384,192]{0,1:T(8,128)(2,1)S(1)}, u32[]{:S(2)}, u32[]{:S(2)}) collective-permute-start(bf16[384,192]{0,1:T(8,128)(2,1)S(1)} %get-tuple-element.281), channel_id=1, source_target_pairs={{0,2},{1,3},{2,0},{3,1},{4,6},{5,7},{6,4},{7,5},{8,10},{9,11},{10,... | collective-permute-start | bytes 442376 | tf_op jit(solution)/shard_map/ppermute | solution.py:48
  945.4 110.6 %collective-permute-start.107 = (bf16[384,192]{0,1:T(8,128)(2,1)S(1)}, bf16[384,192]{0,1:T(8,128)(2,1)S(1)}, u32[]{:S(2)}, u32[]{:S(2)}) collective-permute-start(bf16[384,192]{0,1:T(8,128)(2,1)S(1)} %get-tuple-element.280), channel_id=1, source_target_pairs={{0,3},{1,2},{2,1},{3,0},{4,7},{5,6},{6,5},{7,4},{8,11},{9,10},{10,... | collective-permute-start | bytes 442376 | tf_op jit(solution)/shard_map/ppermute | solution.py:48
  998.1 61.0 %collective-permute-start.100 = (bf16[192,384]{1,0:T(8,128)(2,1)S(1)}, bf16[192,384]{1,0:T(8,128)(2,1)S(1)}, u32[]{:S(2)}, u32[]{:S(2)}) collective-permute-start(bf16[192,384]{1,0:T(8,128)(2,1)S(1)} %get-tuple-element.284), channel_id=1, source_target_pairs={{0,2},{1,3},{2,0},{3,1},{4,6},{5,7},{6,4},{7,5},{8,10},{9,11},{10,... | collective-permute-start | bytes 442376 | tf_op jit(solution)/shard_map/ppermute | solution.py:48
  999.6 61.0 %collective-permute-start.101 = (bf16[192,384]{1,0:T(8,128)(2,1)S(1)}, bf16[192,384]{1,0:T(8,128)(2,1)S(1)}, u32[]{:S(2)}, u32[]{:S(2)}) collective-permute-start(bf16[192,384]{1,0:T(8,128)(2,1)S(1)} %get-tuple-element.283), channel_id=1, source_target_pairs={{0,3},{1,2},{2,1},{3,0},{4,7},{5,6},{6,5},{7,4},{8,11},{9,10},{10,... | collective-permute-start | bytes 442376 | tf_op jit(solution)/shard_map/ppermute | solution.py:48
  (228 other events, 3265.6 us)
Sparse Core Ops, SparseCore 0:
  43.1 52.0 all-gather.1
  632.8 32.6 reduce-scatter.26
  667.9 42.1 reduce-scatter.24
  712.4 54.6 reduce-scatter.22
  769.3 53.3 reduce-scatter.20
  825.0 59.6 reduce-scatter.18
  887.0 54.1 reduce-scatter.16
  943.6 53.3 reduce-scatter.14
  999.4 53.3 reduce-scatter.12

commit v2 on v1

--- a/solution.py
+++ b/solution.py
@@ -48,18 +48,20 @@
     return lax.ppermute(values, axis, [(i, i ^ k) for i in range(lax.axis_size(axis))])
 
 
+def after(values, *others):
+    return lax.optimization_barrier((values,) + others)[0]
+
+
 def spread(values):
     size = lax.axis_size("mp")
+    if size != 4:
+        pieces = [values] + [swap(values, "mp", k) for k in range(1, size)]
+        return (pieces, tuple(pieces[1:2]))
     half = values.shape[0] // 2
-    orders = (bits_of(size), bits_of(size)[::-1])
-    parts = []
-    for piece, order in zip((values[:half], values[half:]), orders):
-        have = {0: piece}
-        for bit in order:
-            for k in list(have):
-                have[k ^ bit] = swap(have[k], "mp", bit)
-        parts.append(have)
-    return [parts[p][k] for k in range(size) for p in (0, 1)]
+    one = swap(values, "mp", 1)
+    two = swap(values, "mp", 2)
+    pieces = [values, one, two, swap(one[:half], "mp", 2), swap(two[half:], "mp", 1)]
+    return (pieces, (one, two))
 
 
 def trade(blocks):
@@ -67,11 +69,25 @@
 
 
 def settle(blocks):
-    got = trade(blocks)
-    total = got[0].astype(f32)
-    for block in got[1:]:
-        total = total + block.astype(f32)
-    return total
+    if len(blocks) != 4:
+        return trade(blocks)
+    half = blocks[0].shape[0] // 2
+    high = swap(blocks[3][:half], "mp", 2)
+    low = swap(blocks[3][half:], "mp", 1)
+    one = jnp.concatenate([plus(blocks[1][:half], high), blocks[1][half:]], axis=0)
+    two = jnp.concatenate([blocks[2][:half], plus(blocks[2][half:], low)], axis=0)
+    return [blocks[0], swap(one, "mp", 1), swap(two, "mp", 2)]
+
+
+def plus(left, right):
+    return (left.astype(f32) + right.astype(f32)).astype(bf16)
+
+
+def total(terms):
+    result = terms[0].astype(f32)
+    for term in terms[1:]:
+        result = result + term.astype(f32)
+    return result
 
 
 def all_sum(values):
@@ -81,12 +97,28 @@
     return values
 
 
+def core_half(blocks):
+    core = lax.axis_index("dp") & 1
+    pairs = blocks.reshape((blocks.shape[0] // 2, 2) + blocks.shape[1:])
+    mine = lax.dynamic_index_in_dim(pairs, core, 1, False)
+    other = lax.dynamic_index_in_dim(pairs, 1 - core, 1, False)
+    return (mine, swap(other, "dp", 1))
+
+
+def chips_sum(blocks):
+    here = lax.axis_index("dp") >> 1
+    mine = [
+        lax.dynamic_index_in_dim(blocks, here ^ k, 0, False) for k in range(blocks.shape[0])
+    ]
+    return total([mine[0]] + [swap(mine[k], "dp", 2 * k) for k in range(1, len(mine))])
+
+
 def whole_rows(shard):
     size = lax.axis_size("mp")
     rows, width = shard.shape
     core = lax.axis_index("dp") & 1
     mine = lax.dynamic_slice_in_dim(shard, core * (rows // 2), rows // 2, 0)
-    got = jnp.concatenate(spread(mine)[2:], axis=0).reshape(size - 1, rows // 2, width)
+    got = jnp.concatenate(spread(mine)[0][1:], axis=0).reshape(size - 1, rows // 2, width)
     other = swap(got, "dp", 1)
     low = jnp.where(core == 0, got, other)
     high = jnp.where(core == 0, other, got)
@@ -99,7 +131,7 @@
     depth = shard.shape[0] // lax.axis_size("dp")
     mine = lax.dynamic_slice_in_dim(shard, lax.axis_index("dp") * depth, depth, 0)
     wide = jnp.concatenate([mine] + [swap(mine, "mp", k) for k in range(1, size)], axis=1)
-    return lax.all_gather(wide, "dp", axis=0, tiled=True)
+    return (wide, lax.all_gather(wide, "dp", axis=0, tiled=True))
 
 
 def self_forward_kernel(block, q_ref, k_ref, v_ref, pk_ref, pv_ref, o_ref, l_ref):
@@ -357,6 +389,71 @@
     )(lengths, queries, keys, values, grads, mixed, logsum)
 
 
+def glu_kernel(block, x_ref, c_ref, gate_ref, up_ref, down_ref, h_ref, dg_ref, du_ref):
+    for start in range(0, x_ref.shape[0], block):
+        part = slice(start, start + block)
+        gate = dot(x_ref[part], gate_ref[...], 1, 0)
+        upper = dot(x_ref[part], up_ref[...], 1, 0)
+        grad_hidden = dot(c_ref[part], down_ref[...], 1, 1)
+        sigma = 1.0 / (1.0 + jnp.exp(-gate))
+        silu = gate * sigma
+        h_ref[part] = (silu * upper).astype(bf16)
+        dg_ref[part] = (grad_hidden * upper * (sigma + silu * (1.0 - sigma))).astype(bf16)
+        du_ref[part] = (grad_hidden * silu).astype(bf16)
+
+
+def glu(frames, grads, w_gate, w_up, w_down):
+    rows, width = frames.shape
+    hidden = w_gate.shape[1]
+    block = 256
+    whole = pl.BlockSpec((rows, width), lambda j: (0, 0))
+    columns = pl.BlockSpec((width, block), lambda j: (0, j))
+    out = pl.BlockSpec((rows, block), lambda j: (0, j))
+    return pl.pallas_call(
+        functools.partial(glu_kernel, 256),
+        grid=(hidden // block,),
+        in_specs=[whole, whole, columns, columns, pl.BlockSpec((block, width), lambda j: (j, 0))],
+        out_specs=[out, out, out],
+        out_shape=[shape_of((rows, hidden), bf16)] * 3,
+        compiler_params=params(),
+        cost_estimate=pl.CostEstimate(
+            flops=6 * rows * width * hidden,
+            bytes_accessed=4 * rows * width + 6 * width * hidden + 6 * rows * hidden,
+            transcendentals=rows * hidden,
+        ),
+        name="glu",
+    )(frames, grads, w_gate, w_up, w_down)
+
+
+def glu_back_kernel(block, dg_ref, du_ref, gate_ref, up_ref, o_ref):
+    for start in range(0, dg_ref.shape[0], block):
+        part = slice(start, start + block)
+        back = dot(dg_ref[part], gate_ref[...], 1, 1) + dot(du_ref[part], up_ref[...], 1, 1)
+        o_ref[part] = back.astype(bf16)
+
+
+def glu_back(grad_gate, grad_upper, w_gate, w_up):
+    rows, hidden = grad_gate.shape
+    width = w_gate.shape[0]
+    block = 256
+    whole = pl.BlockSpec((rows, hidden), lambda j: (0, 0))
+    part = pl.BlockSpec((block, hidden), lambda j: (j, 0))
+    return pl.pallas_call(
+        functools.partial(glu_back_kernel, 256),
+        grid=(width // block,),
+        in_specs=[whole, whole, part, part],
+        out_specs=pl.BlockSpec((rows, block), lambda j: (0, j)),
+        out_shape=shape_of((rows, width), bf16),
+        compiler_params=params(),
+        cost_estimate=pl.CostEstimate(
+            flops=4 * rows * width * hidden,
+            bytes_accessed=4 * rows * hidden + 4 * width * hidden + 2 * rows * width,
+            transcendentals=0,
+        ),
+        name="glu_back",
+    )(grad_gate, grad_upper, w_gate, w_up)
+
+
 def turning(rows):
     size = lax.axis_size("mp")
     me = lax.axis_index("mp")
@@ -409,48 +506,62 @@
     cotangent,
 ):
     size = lax.axis_size("mp")
+    groups = lax.axis_size("dp")
     count, rows, width = frames_in.shape
     clips = range(count)
+    last = count - 1
     local = w_query.shape[1]
+
+    def joined(parts, axis):
+        return jnp.concatenate(parts, axis=axis)
 
     resid = [frames_in[b].astype(f32) for b in clips]
     ones = [norm_forward(resid[b], gain_one, shift_one) for b in clips]
-    whole_one = [jnp.concatenate(spread(ones[b][0].astype(bf16)), axis=0) for b in clips]
+    whole_one = []
+    held = ()
+    for b in clips:
+        pieces, held = spread(after(ones[b][0].astype(bf16), *held))
+        whole_one.append(joined(pieces, 0))
+        if b == 0:
+            seen = held
+    c_query_wide, c_query_all = whole_columns(c_query)
+    c_out_side, c_query_side = after((c_out.T, c_query_all), *seen)
+    c_out_wide, c_out_all = whole_columns(c_out_side)
+    out_all = whole_rows(after(w_out, whole_one[0]))
+
+    memory = joined([c_key, c_value], 1)
+    memory = jnp.stack([dot(memory, prompt[b], 0, 1).astype(bf16) for b in clips])
+    memory = after(memory, *held)
+    memory = jnp.stack([memory] + [swap(memory, "mp", k) for k in range(1, size)], axis=1)
+    cross_keys = [memory[b, :, :local].reshape(size * local, -1) for b in clips]
+    cross_values = [memory[b, :, local:].reshape(size * local, -1) for b in clips]
 
     picked = jnp.take(table, tsteps, axis=0)
     prefix_normed, prefix_normal, prefix_scale = norm_forward(picked, gain_one, shift_one)
     prefix_low = prefix_normed.astype(bf16)
     cosine, sine = turning(rows)
-
-    w_self = jnp.concatenate([w_query, w_key, w_value], axis=1)
+    w_self = joined([w_query, w_key, w_value], 1)
     front = dot(w_self[:, local:], prefix_low, 0, 1).astype(bf16)
     front_keys = [front[:local, b : b + 1] for b in clips]
     front_values = [front[local:, b : b + 1] for b in clips]
-
-    out_all = whole_rows(w_out)
-    c_out_all = whole_rows(c_out)
-    c_query_all = whole_columns(c_query)
-
-    memory = jnp.concatenate([c_key, c_value], axis=1)
-    memory = jnp.stack([dot(memory, prompt[b], 0, 1).astype(bf16) for b in clips])
-    memory = jnp.stack([memory] + [swap(memory, "mp", k) for k in range(1, size)], axis=1)
-    cross_keys = [memory[b, :, :local].reshape(size * local, -1) for b in clips]
-    cross_values = [memory[b, :, local:].reshape(size * local, -1) for b in clips]
 
     turned, mixed_part, logsum, mixed = [], [], [], []
     for b in clips:
         raw = dot(w_self, whole_one[b], 0, 1)
         queries = (turn(raw[:local], cosine, sine) * FACTOR).astype(bf16)
         keys = turn(raw[local : 2 * local], cosine, sine).astype(bf16)
-        turned.append(jnp.concatenate([queries, keys, raw[2 * local :].astype(bf16)], axis=0))
+        turned.append(joined([queries, keys, raw[2 * local :].astype(bf16)], 0))
         out, sums = self_forward(turned[b], front_keys[b], front_values[b])
         mixed_part.append(out)
         logsum.append(sums)
-        mixed.append(jnp.concatenate(trade(jnp.split(out, size, axis=1)), axis=0))
+        mixed.append(joined(trade(jnp.split(out, size, axis=1)), 0))
 
     first, twos, normed_two, cross_query, cross_sums, cross_mixed = [], [], [], [], [], []
-    second, threes, whole_three = [], [], []
+    second, threes, whole_three, down_in = [], [], [], []
+    held = (whole_one[last],)
     for b in clips:
+        pieces, held = spread(after(cotangent[b], *held))
+        down_in.append(joined(pieces, 0))
         first.append(resid[b] + dot(mixed[b], out_all, 0, 0))
         twos.append(norm_forward(first[b], gain_two, shift_two))
         normed_two.append(twos[b][0].astype(bf16))
@@ -460,34 +571,40 @@
         )
         cross_mixed.append(out)
         cross_sums.append(sums)
-        second.append(first[b] + dot(out, c_out_all, 0, 0))
+        second.append(first[b] + dot(out, c_out_all, 0, 1))
         threes.append(norm_forward(second[b], gain_three, shift_three))
-        whole_three.append(jnp.concatenate(spread(threes[b][0].astype(bf16)), axis=0))
-
-    down_in = [jnp.concatenate(spread(cotangent[b]), axis=0) for b in clips]
-    hidden, grad_gate, grad_upper, back_three, output = [], [], [], [], []
+        pieces, held = spread(threes[b][0].astype(bf16))
+        whole_three.append(joined(pieces, 0))
+
+    hidden, grad_gate, grad_upper, back_three, branch = [], [], [], [], []
+    done = ()
     for b in clips:
-        grad_hidden = dot(down_in[b], w_down, 1, 1)
-        gate = dot(whole_three[b], w_gate, 1, 0)
-        upper = dot(whole_three[b], w_up, 1, 0)
-        sigma = jax.nn.sigmoid(gate)
-        hidden.append((gate * sigma * upper).astype(bf16))
-        grad_gate.append(
-            (grad_hidden * upper * sigma * (1.0 + gate * (1.0 - sigma))).astype(bf16)
-        )
-        grad_upper.append((grad_hidden * gate * sigma).astype(bf16))
-        back = dot(grad_gate[b], w_gate, 1, 1) + dot(grad_upper[b], w_up, 1, 1)
-        back_three.append(settle(row_blocks(back.astype(bf16), size)))
-        branch = dot(hidden[b], w_down, 1, 0)
-        output.append(second[b] + settle(row_blocks(branch.astype(bf16), size)))
+        parts = glu(after(whole_three[b], *done), down_in[b], w_gate, w_up, w_down)
+        hidden.append(parts[0])
+        grad_gate.append(parts[1])
+        grad_upper.append(parts[2])
+        back = glu_back(grad_gate[b], grad_upper[b], w_gate, w_up)
+        back_three.append(settle(row_blocks(back, size)))
+        if b < last:
+            branch.append(dot(after(hidden[b], back), w_down, 1, 0).astype(bf16))
+            done = (branch[b],)
+        else:
+            done = (back,)
+
+    hidden_all = joined(hidden, 0)
+    three_all = joined(whole_three, 0)
+    raw_w_down = dot(after(hidden_all, *done), joined(down_in, 0), 0, 0).astype(bf16)
+    grad_w_down = sum_over_clips(raw_w_down, 1)
+    done = (raw_w_down,)
 
     grad_two, grad_one, cross_in, self_in = [], [], [], []
     grad_cross_query, grad_memory, grad_mixed, back_two = [], [], [], []
     for b in clips:
+        back_three[b] = total(after(back_three[b], *done))
         cot = cotangent[b].astype(f32)
         grad_two.append(cot + norm_backward(back_three[b], threes[b][1], threes[b][2], gain_three))
         cross_in.append(grad_two[b].astype(bf16))
-        grads = dot(c_out_all, cross_in[b], 1, 1).astype(bf16)
+        grads = dot(c_out_all, cross_in[b], 0, 1).astype(bf16)
         grad_queries, grad_keys, grad_values = cross_backward(
             b,
             size,
@@ -501,9 +618,7 @@
         )
         grad_cross_query.append(grad_queries)
         grad_memory.append(
-            jnp.concatenate(
-                [grad_keys.reshape(size, local, -1), grad_values.reshape(size, local, -1)], axis=1
-            )
+            joined([grad_keys.reshape(size, local, -1), grad_values.reshape(size, local, -1)], 1)
         )
         back_two.append(dot(grad_queries, c_query_all, 0, 1))
         grad_one.append(
@@ -511,13 +626,22 @@
         )
         self_in.append(grad_one[b].astype(bf16))
         grads = dot(out_all, self_in[b], 1, 1).astype(bf16)
-        grad_mixed.append(jnp.concatenate(trade(row_blocks(grads, size)), axis=1))
+        grad_mixed.append(joined(trade(row_blocks(grads, size)), 1))
+        done = (grads,)
+
+    branch.append(dot(after(hidden[last], *done), w_down, 1, 0).astype(bf16))
+    raw_w_gate = dot(after(three_all, branch[last]), joined(grad_gate, 0), 0, 0).astype(bf16)
+    grad_w_gate = sum_over_clips(raw_w_gate, 0)
+    done = (raw_w_gate,)
+    output = [
+        second[b] + total(settle(row_blocks(branch[b], size))) for b in clips
+    ]
 
     grad_self, grad_front, back_one = [], [], []
     for b in clips:
         grads, grad_front_key, grad_front_value = self_backward(
             turned[b],
-            grad_mixed[b],
+            after(grad_mixed[b], *done),
             mixed_part[b],
             logsum[b],
             front_keys[b],
@@ -526,84 +650,91 @@
             sine,
         )
         grad_self.append(grads.reshape(3 * local, -1))
-        grad_front.append(jnp.concatenate([grad_front_key, grad_front_value], axis=0))
+        grad_front.append(joined([grad_front_key, grad_front_value], 0))
         back = dot(grad_self[b], w_self, 0, 1).astype(bf16)
-        back_one.append(settle(row_blocks(back, size)))
+        done = (back,)
+        back_one.append(total(settle(row_blocks(back, size))))
     grad_frames = [
         grad_one[b] + norm_backward(back_one[b], ones[b][1], ones[b][2], gain_one) for b in clips
     ]
 
-    def joined(parts, axis):
-        return jnp.concatenate(parts, axis=axis)
-
-    hidden_all = joined(hidden, 0)
-    three_all = joined(whole_three, 0)
-    grad_w_down = sum_over_clips(dot(hidden_all, joined(down_in, 0), 0, 0), 1)
-    grad_w_gate = sum_over_clips(dot(three_all, joined(grad_gate, 0), 0, 0), 0)
-    grad_w_up = sum_over_clips(dot(three_all, joined(grad_upper, 0), 0, 0), 0)
-
-    def from_rows(grad):
-        return settle(row_blocks(sum_over_clips(grad, 1), size))
-
-    grad_c_out = from_rows(dot(joined(cross_mixed, 1), joined(cross_in, 0), 1, 0))
-    grad_w_out = from_rows(dot(joined(mixed, 1), joined(self_in, 0), 1, 0))
-    grad_c_query = dot(joined(normed_two, 0), joined(grad_cross_query, 1), 0, 1)
-    grad_c_query = settle(jnp.split(sum_over_clips(grad_c_query, 0), size, axis=1))
+    grad_front = joined(grad_front, 1)
+    turned_grads = after(joined(grad_self, 1), *done)
+    raw_w_self = dot(joined(whole_one, 0), turned_grads, 0, 1)
+    raw_w_front = dot(prefix_low, grad_front, 0, 1)
+    raw_w_self = joined([raw_w_self[:, :local], raw_w_self[:, local:] + raw_w_front], 1)
+    low_w_self = raw_w_self.astype(bf16).reshape(groups, -1, 3 * local)
+    grad_w_self = chips_sum(plus(*core_half(low_w_self)))
+
+    raw_w_up = dot(after(three_all, raw_w_self), joined(grad_upper, 0), 0, 0).astype(bf16)
+    grad_w_up = sum_over_clips(raw_w_up, 0)
+
+    cross_all = after(joined(cross_in, 0), raw_w_up)
+    raws = [
+        dot(joined(normed_two, 0), joined(grad_cross_query, 1), 0, 1),
+        dot(cross_all, joined(cross_mixed, 1), 0, 1),
+        dot(joined(self_in, 0), joined(mixed, 1), 0, 1),
+    ]
+    raws = joined([raw.astype(bf16).reshape(groups, -1, size, local) for raw in raws], 3)
+    mine, other = core_half(raws)
+    raws = [plus(mine[:, :, k], other[:, :, k]).reshape(-1, 3 * local) for k in range(size)]
+    raws = total(settle(raws)).astype(bf16).reshape(groups // 2, -1, 3 * local)
+    raws = chips_sum(raws)
 
     grad_memory = jnp.stack(grad_memory)
-    grad_memory = settle([grad_memory[:, k] for k in range(size)]).astype(bf16)
+    grad_memory = total(trade([grad_memory[:, k] for k in range(size)])).astype(bf16)
     grad_memory = joined([grad_memory[b] for b in clips], 1)
     grad_c_memory = dot(prompt.reshape(-1, prompt.shape[-1]), grad_memory, 0, 1)
     grad_c_memory = sum_over_clips(grad_c_memory, 0)
 
-    grad_front = joined(grad_front, 1)
-    grad_w_self = dot(joined(whole_one, 0), joined(grad_self, 1), 0, 1)
-    grad_w_front = dot(prefix_low, grad_front, 0, 1)
-    grad_w_self = joined(
-        [grad_w_self[:, :local], grad_w_self[:, local:] + grad_w_front], 1
-    )
-    grad_w_self = sum_over_clips(grad_w_self, 0)
-
-    early = []
+    small = []
+    wide_w_self = w_self.astype(f32)
+    sums = jnp.sum(turned_grads.astype(f32), axis=1)
+    front_sums = jnp.sum(grad_front.astype(f32), axis=1)
+    sums = joined([sums[:local], sums[local:] + front_sums], 0)
+    shift_term = jnp.sum(wide_w_self * sums[None, :], axis=1)
+    gain_term = jnp.sum(wide_w_self * raw_w_self, axis=1)
+    small.append((gain_term - shift_one * shift_term) / gain_one)
+    small.append(shift_term)
     for back, kept in ((back_two, twos), (back_three, threes)):
-        early.append(sum(jnp.sum(back[b] * kept[b][1], axis=0) for b in clips))
-        early.append(sum(jnp.sum(back[b], axis=0) for b in clips))
-    early = all_sum(jnp.stack(early))
+        small.append(sum(jnp.sum(back[b] * kept[b][1], axis=0) for b in clips))
+        small.append(sum(jnp.sum(back[b], axis=0) for b in clips))
+
+    me = lax.axis_index("dp")
+    steps = jnp.where(lax.axis_index("mp") == 0, tsteps, 0).astype(f32)
+    steps = lax.dynamic_update_slice(jnp.zeros((width,), f32), steps, (me * count,))
+    small.append(steps)
 
     back_prefix = dot(grad_front, w_self[:, local:], 0, 1)
     grad_picked = norm_backward(back_prefix, prefix_normal, prefix_scale, gain_one)
-    groups = lax.axis_size("dp")
-    spots = jnp.arange(groups)[:, None, None] == lax.axis_index("dp")
+    spots = jnp.arange(groups)[:, None, None] == me
     spots = jnp.where(spots, grad_picked[None], 0.0).reshape(groups * count, width)
-    gain_term = jnp.sum(back_prefix * prefix_normal, axis=0)
-    shift_term = jnp.sum(back_prefix, axis=0)
-    for b in clips:
-        gain_term = gain_term + jnp.sum(back_one[b] * ones[b][1], axis=0)
-        shift_term = shift_term + jnp.sum(back_one[b], axis=0)
-    late = all_sum(jnp.concatenate([gain_term[None], shift_term[None], spots], axis=0))
-    all_steps = lax.all_gather(tsteps, "dp", axis=0, tiled=True)
-    matches = (jnp.arange(table.shape[0])[:, None] == all_steps[None, :]).astype(f32)
-    grad_table = jnp.dot(matches, late[2:], precision=lax.Precision.HIGHEST)
-
-    wide = lambda value: value.astype(f32)
+    small = all_sum(joined([jnp.stack(small), spots], 0))
+    all_steps = small[6, : groups * count]
+    matches = jnp.arange(table.shape[0])[:, None].astype(f32) == all_steps[None, :]
+    grad_table = jnp.dot(matches.astype(f32), small[7:], precision=lax.Precision.HIGHEST)
+
+    def wide(value):
+        return value.astype(f32)
+
     return (
         jnp.stack(output),
         jnp.stack(grad_frames),
         grad_table,
-        late[0],
-        late[1],
-        early[0],
-        early[1],
-        early[2],
-        early[3],
-        wide(grad_w_self[:, :local]),
-        wide(grad_w_self[:, local : 2 * local]),
-        wide(grad_w_self[:, 2 * local :]),
-        grad_w_out,
-        grad_c_query,
+        small[0],
+        small[1],
+        small[2],
+        small[3],
+        small[4],
+        small[5],
+        grad_w_self[:, :local],
+        grad_w_self[:, local : 2 * local],
+        grad_w_self[:, 2 * local :],
+        raws[:, 2 * local :].T,
+        raws[:, :local],
         wide(grad_c_memory[:, :local]),
         wide(grad_c_memory[:, local:]),
-        grad_c_out,
+        raws[:, local : 2 * local].T,
         wide(grad_w_gate),
         wide(grad_w_up),
         wide(grad_w_down),

time: 1080 us -> 989 us (0.916)
  waiting for transfers between devices: 467 us -> 293 us
  matrix products: 231 us -> 151 us
  local copies, waits for them, and re-layouts: 92.8 us -> 165 us
  Pallas kernels: 81.2 us -> 145 us
  other arithmetic: 65.2 us -> 92 us
    reduce_scatter x6 -> x2, waiting for transfers between devices: 153 us -> 0.01 us  [sum_over_clips(): lax.psum_scatter(values.astype(bf16), 'dp', scatter_dimension=axis, tiled...]
    dot_general x41 -> x31, matrix products: 226 us -> 146 us  [dot(): lax.dot_general(left, right, (((left_axis,), (right_axis,)), ((), ())), p...]
    pallas_call x0 -> x4, Pallas kernels: none -> 64.1 us  [the longest x2 39 us: glu(): pl.pallas_call(functools.partial(glu_kernel, 256), grid=(hidden // block,...]
    concatenate x3 -> x11, local copies, waits for them, and re-layouts: 2.55 us -> 39.5 us  [joined(): return jnp.concatenate(parts, axis=axis)]
    ppermute x108 -> x94, waiting for transfers between devices: 315 us -> 293 us  [swap(): lax.ppermute(values, axis, [(i, i ^ k) for i in range(lax.axis_size(axis))])]
    unnamed x391 -> x485, local copies, waits for them, and re-layouts: 63.4 us -> 77.2 us
    squeeze x0 -> x4, local copies, waits for them, and re-layouts: none -> 13.6 us  [the longest x1 11.2 us: core_half(): mine = lax.dynamic_index_in_dim(pairs, core, 1, False)]
    ppermute x108 -> x94, starting transfers between devices: 108 us -> 118 us  [swap(): lax.ppermute(values, axis, [(i, i ^ k) for i in range(lax.axis_size(axis))])]
  transfers between devices with their start and end apart: 117 -> 100, of which waited for: 49 -> 40; matrix products, arithmetic and copies ran while one was open for 33% -> 36% of each run, Pallas kernels for 6% -> 14%
where the time goes in v2:
time: 989 us; the launch traced here: 982 us
  waiting for transfers between devices  293 us (30%)
  local copies, waits for them, and re-layouts  165 us (17%)
  matrix products  151 us (15%)
  Pallas kernels  145 us (15%)
  starting transfers between devices  118 us (12%)
  other arithmetic  92 us (9%)
  between operations  17.9 us (2%)
    ppermute x94, waiting for transfers between devices, swap(): lax.ppermute(values, axis, [(i, i ^ k) for i in range(lax.axis_size(axis))])  293 us
    dot_general x31, matrix products, dot(): lax.dot_general(left, right, (((left_axis,), (right_axis,)), ((), ())), p...  146 us
    ppermute x94, starting transfers between devices, swap(): lax.ppermute(values, axis, [(i, i ^ k) for i in range(lax.axis_size(axis))])  118 us
    unnamed x485, local copies, waits for them, and re-layouts  77.2 us
    concatenate x11, local copies, waits for them, and re-layouts, joined(): return jnp.concatenate(parts, axis=axis)  39.5 us
    pallas_call x2, Pallas kernels, glu(): pl.pallas_call(functools.partial(glu_kernel, 256), grid=(hidden // block,...  39 us
    pallas_call x2, Pallas kernels, self_backward(): pl.pallas_call(functools.partial(self_backward_kernel, min(256, frames)),...  33.8 us
    pallas_call x2, Pallas kernels, glu_back(): pl.pallas_call(functools.partial(glu_back_kernel, 256), grid=(width // bl...  25.1 us
  transfers between devices with their start and end apart: 100, of which 40 were waited for; matrix products, arithmetic and copies ran while one was open for 36% of the time, Pallas kernels for 14%

profile of v2, /device:TPU:0, one launch (start us, length us, event | category | flops | bytes accessed | tf_op | source)
XLA Modules:
  0.0 982.3 jit_solution(257887788069697756)
XLA Ops:
  61.2 18.2 %collective-permute-done.2 = bf16[128,1536]{1,0:T(8,128)(2,1)S(1)} collective-permute-done((bf16[128,1536]{1,0:T(8,128)(2,1)S(1)}, bf16[128,1536]{1,0:T(8,128)(2,1)S(1)}, u32[]{:S(2)}, u32[]{:S(2)}) %collective-permute-start.2) | collective-permute-done | bytes 393248 | tf_op jit(solution)/shard_map/ppermute | solution.py:48
  98.8 13.9 %collective-permute-done.27 = bf16[128,1536]{1,0:T(8,128)(2,1)S(1)} collective-permute-done((bf16[128,1536]{1,0:T(8,128)(2,1)S(1)}, bf16[128,1536]{1,0:T(8,128)(2,1)S(1)}, u32[]{:S(2)}, u32[]{:S(2)}) %collective-permute-start.27) | collective-permute-done | bytes 393248 | tf_op jit(solution)/shard_map/ppermute | solution.py:48
  120.3 10.5 %self_forward.3 = (bf16[384,1024]{1,0:T(8,128)(2,1)S(1)}, f32[6,1,1024]{2,1,0:T(1,128)S(1)}) custom-call(bf16[1152,1024]{1,0:T(8,128)(2,1)S(1)} %pad_maximum_fusion.8.q_ref.k_ref.v_ref, bf16[1152,1024]{1,0:T(8,128)(2,1)S(1)} %pad_maximum_fusion.8.q_ref.k_ref.v_ref, bf16[1152,1024]{1,0:T(8,128)(2,1)S(1)} %pad_maximum_fusion.8.q_ref.k_ref.v_ref, ...), custom_call_target="tpu_custom_call" | custom-call | flops 6442450944 | bytes 3145728 | tf_op jit(solution)/shard_map/self_forward/pallas_call | solution.py:273
  147.0 10.5 %self_forward.2 = (bf16[384,1024]{1,0:T(8,128)(2,1)S(1)}, f32[6,1,1024]{2,1,0:T(1,128)S(1)}) custom-call(bf16[1152,1024]{1,0:T(8,128)(2,1)S(1)} %pad_maximum_fusion.7.q_ref.k_ref.v_ref, bf16[1152,1024]{1,0:T(8,128)(2,1)S(1)} %pad_maximum_fusion.7.q_ref.k_ref.v_ref, bf16[1152,1024]{1,0:T(8,128)(2,1)S(1)} %pad_maximum_fusion.7.q_ref.k_ref.v_ref, ...), custom_call_target="tpu_custom_call" | custom-call | flops 6442450944 | bytes 3145728 | tf_op jit(solution)/shard_map/self_forward/pallas_call | solution.py:273
  167.6 8.5 collective-permute-done.29
  183.0 10.0 %collective-permute-done.31 = bf16[128,1536]{1,0:T(8,128)(2,1)S(1)} collective-permute-done((bf16[128,1536]{1,0:T(8,128)(2,1)S(1)}, bf16[128,1536]{1,0:T(8,128)(2,1)S(1)}, u32[]{:S(2)}, u32[]{:S(2)}) %collective-permute-start.31) | collective-permute-done | bytes 393248 | tf_op jit(solution)/shard_map/ppermute | solution.py:48
  210.0 6.3 cross_forward.3
  217.8 6.5 cross_forward.2
  236.7 13.1 %collective-permute-done.23 = bf16[256,1536]{1,0:T(8,128)(2,1)S(1)} collective-permute-done((bf16[256,1536]{1,0:T(8,128)(2,1)S(1)}, bf16[256,1536]{1,0:T(8,128)(2,1)S(1)}, u32[]{:S(2)}, u32[]{:S(2)}) %collective-permute-start.23) | collective-permute-done | bytes 786464 | tf_op jit(solution)/shard_map/ppermute | solution.py:48
  258.3 12.1 %collective-permute-done.25 = bf16[128,1536]{1,0:T(8,128)(2,1)S(1)} collective-permute-done((bf16[128,1536]{1,0:T(8,128)(2,1)S(1)}, bf16[128,1536]{1,0:T(8,128)(2,1)S(1)}, u32[]{:S(2)}, u32[]{:S(2)}) %collective-permute-start.25) | collective-permute-done | bytes 393248 | tf_op jit(solution)/shard_map/ppermute | solution.py:48
  278.7 19.5 %glu.2 = (bf16[1024,1536]{1,0:T(8,128)(2,1)S(1)}, bf16[1024,1536]{1,0:T(8,128)(2,1)S(1)}, bf16[1024,1536]{1,0:T(8,128)(2,1)S(1)}) custom-call(bf16[1024,1536]{1,0:T(8,128)(2,1)S(1)} %get-tuple-element.394.x_ref, bf16[1024,1536]{1,0:T(8,128)(2,1)} %copy-done.146, bf16[1536,1536]{1,0:T(8,128)(2,1)} %gate_ref.7, bf16[1536,1536]{1,0:T(8,128)(2,1)} %up_ref.7, ...), custom_call_target="tpu_custom_call" | custom-call | flops 14495514624 | bytes 29884416 | tf_op jit(solution)/shard_map/glu/pallas_call | solution.py:412
  298.3 12.8 %glu_back.2 = bf16[1024,1536]{1,0:T(8,128)(2,1)S(1)} custom-call(bf16[1024,1536]{1,0:T(8,128)(2,1)S(1)} %get-tuple-element.76.dg_ref, bf16[1024,1536]{1,0:T(8,128)(2,1)S(1)} %get-tuple-element.77.du_ref, bf16[1536,1536]{1,0:T(8,128)(2,1)S(1)} %bitcast.275, bf16[1536,1536]{1,0:T(8,128)(2,1)} %up_ref.7), custom_call_target="tpu_custom_call" | custom-call | flops 9663676416 | bytes 18874368 | tf_op jit(solution)/shard_map/glu_back/pallas_call | solution.py:441
  311.3 7.8 convolution_convert_fusion.7
  324.7 7.0 collective-permute-done.54
  353.1 7.5 collective-permute-done.41
  374.9 18.0 %collective-permute-done.42 = bf16[128,1536]{1,0:T(8,128)(2,1)S(1)} collective-permute-done((bf16[128,1536]{1,0:T(8,128)(2,1)S(1)}, bf16[128,1536]{1,0:T(8,128)(2,1)S(1)}, u32[]{:S(2)}, u32[]{:S(2)}) %collective-permute-start.42) | collective-permute-done | bytes 393248 | tf_op jit(solution)/shard_map/ppermute | solution.py:48
  394.8 19.5 %glu.3 = (bf16[1024,1536]{1,0:T(8,128)(2,1)S(1)}, bf16[1024,1536]{1,0:T(8,128)(2,1)S(1)}, bf16[1024,1536]{1,0:T(8,128)(2,1)S(1)}) custom-call(bf16[1024,1536]{1,0:T(8,128)(2,1)S(1)} %get-tuple-element.81.x_ref, bf16[1024,1536]{1,0:T(8,128)(2,1)} %get-tuple-element.387.c_ref, bf16[1536,1536]{1,0:T(8,128)(2,1)} %gate_ref.7, bf16[1536,1536]{1,0:T(8,128)(2,1)} %up_ref.7, ...), custom_call_target="tpu_custom_call" | custom-call | flops 14495514624 | bytes 29884416 | tf_op jit(solution)/shard_map/glu/pallas_call | solution.py:412
  418.9 12.3 %glu_back.3 = bf16[1024,1536]{1,0:T(8,128)(2,1)S(1)} custom-call(bf16[1024,1536]{1,0:T(8,128)(2,1)S(1)} %get-tuple-element.84.dg_ref, bf16[1024,1536]{1,0:T(8,128)(2,1)S(1)} %get-tuple-element.85.du_ref, bf16[1536,1536]{1,0:T(8,128)(2,1)S(1)} %copy-done.33, bf16[1536,1536]{1,0:T(8,128)(2,1)} %up_ref.7), custom_call_target="tpu_custom_call" | custom-call | flops 9663676416 | bytes 18874368 | tf_op jit(solution)/shard_map/glu_back/pallas_call | solution.py:441
  437.2 16.0 %convolution_convert_fusion.5 = bf16[1536,1536]{1,0:T(8,128)(2,1)} fusion(bf16[2048,1536]{1,0:T(8,128)(2,1)} %pad_maximum_fusion.1, bf16[2048,1536]{1,0:T(8,128)(2,1)} %get-tuple-element.386), kind=kOutput, calls=%fused_computation.9 | convolution fusion | flops 9666035712 | bytes 17301504 | tf_op jit(solution)/shard_map/dot_general | solution.py:22
  464.0 6.5 cross_backward.2
  484.3 8.3 collective-permute-done.49
  502.3 6.7 cross_backward.3
  514.0 6.8 collective-permute-done.93
  520.8 6.3 collective-permute-done.92
  531.3 6.7 copy.97
  545.6 15.6 %convolution_convert_fusion.3 = bf16[1536,1536]{1,0:T(8,128)(2,1)} fusion(bf16[2048,1536]{1,0:T(8,128)(2,1)} %get-tuple-element.110, bf16[1024,1536]{1,0:T(8,128)(2,1)} %copy-done.56, bf16[1024,1536]{1,0:T(8,128)(2,1)} %copy-done.53), kind=kOutput, calls=%fused_computation.7 | convolution fusion | flops 9678618624 | bytes 17301504 | tf_op jit(solution)/shard_map/dot_general | solution.py:22
  563.4 5.7 multiply_reduce_fusion.2
  588.9 11.6 %convolution_convert_fusion.4 = bf16[1536,1536]{1,0:T(8,128)(2,1)} fusion(bf16[2048,1536]{1,0:T(8,128)(2,1)S(1)} %bitcast.307, bf16[1024,1536]{1,0:T(8,128)(2,1)S(1)} %copy-done.55, bf16[1024,1536]{1,0:T(8,128)(2,1)S(1)} %copy-done.52), kind=kOutput, calls=%fused_computation.8 | convolution fusion | flops 9678618624 | bytes 17301504 | tf_op jit(solution)/shard_map/dot_general | solution.py:22
  602.6 16.9 %self_backward.2 = (bf16[3,384,1024]{2,1,0:T(8,128)(2,1)S(1)}, bf16[384,1]{1,0:T(8,128)(2,1)S(1)}, bf16[384,1]{1,0:T(8,128)(2,1)S(1)}) custom-call(bf16[1152,1024]{1,0:T(8,128)(2,1)S(1)} %copy-done.5, bf16[1152,1024]{1,0:T(8,128)(2,1)S(1)} %copy-done.5, bf16[1152,1024]{1,0:T(8,128)(2,1)S(1)} %copy-done.5, bf16[384,1024]{1,0:T(8,128)(2,1)S(1)} %copy-done.12, ...), custom_call_target="tpu_custom_call" | custom-call | flops 16106127360 | bytes 7864320 | tf_op jit(solution)/shard_map/self_backward/pallas_call | solution.py:297
  628.8 6.7 convolution_convert_fusion.2
  635.5 9.2 concatenate.238
  650.8 9.2 concatenate.242
  660.2 10.6 %convolution_convert_fusion = bf16[1536,1536]{1,0:T(8,128)(2,1)} fusion(bf16[256,1536]{1,0:T(8,128)(2,1)S(1)} %copy-done.128, bf16[256,1536]{1,0:T(8,128)(2,1)S(1)} %copy-done.126, bf16[384,256]{1,0:T(8,128)(2,1)S(1)} %copy-done.197, bf16[384,256]{1,0:T(8,128)(2,1)S(1)} %copy-done.199, bf16[384,256]{1,0:T(8,128)(2,1)S(1)} %copy-done.207, ...), kind=kOutput, calls=%fused_computation.4 | convolution fusion | flops 2434007040 | bytes 7864320 | tf_op jit(solution)/shard_map/dot_general | solution.py:22
  670.8 9.1 concatenate.245
  679.8 5.6 copy_dynamic-update-slice_fusion.2
  698.6 5.8 copy_dynamic-update-slice_fusion
  704.5 11.2 %dynamic-slice_bitcast_fusion.1 = (bf16[4,192,4,1152]{3,1,2,0:T(8,128)(2,1)}, bf16[4,192,4,1152]{3,1,2,0:T(8,128)(2,1)}) fusion(bf16[4,2,192,4,1152]{4,2,3,1,0:T(8,128)(2,1)} %copy_dynamic-update-slice_fusion, s32[]{:T(128)S(6)} %select_n.82, s32[]{:T(128)S(6)} %select_n.83), kind=kLoop, calls=%fused_computation.14 | loop fusion | bytes 28311560 | tf_op jit(solution)/shard_map/jit(dynamic_index_in_dim)/squeeze | solution.py:103
  717.8 16.9 %self_backward.3 = (bf16[3,384,1024]{2,1,0:T(8,128)(2,1)S(1)}, bf16[384,1]{1,0:T(8,128)(2,1)S(1)}, bf16[384,1]{1,0:T(8,128)(2,1)S(1)}) custom-call(bf16[1152,1024]{1,0:T(8,128)(2,1)S(1)} %copy-done.3, bf16[1152,1024]{1,0:T(8,128)(2,1)S(1)} %copy-done.3, bf16[1152,1024]{1,0:T(8,128)(2,1)S(1)} %copy-done.3, bf16[384,1024]{1,0:T(8,128)(2,1)S(1)} %pad_maximum_fusion.27.g_ref, ...), custom_call_target="tpu_custom_call" | custom-call | flops 16106127360 | bytes 7864320 | tf_op jit(solution)/shard_map/self_backward/pallas_call | solution.py:297
  747.7 10.8 %fusion.165 = f32[1536,1152]{1,0:T(8,128)S(1)} fusion(bf16[2048,1536]{1,0:T(8,128)(2,1)} %copy-done.150, bf16[1152,2048]{1,0:T(8,128)(2,1)S(1)} %copy-done.68), kind=kOutput, calls=%fused_computation.462 | convolution fusion | flops 7247757312 | bytes 18087936 | tf_op jit(solution)/shard_map/dot_general | solution.py:22
  777.1 6.1 collective-permute-done.74
  789.0 6.2 collective-permute-done.65
  813.8 6.4 collective-permute-done.78
  836.3 10.3 %collective-permute-done.64 = bf16[256,1536]{1,0:T(8,128)(2,1)S(1)} collective-permute-done((bf16[256,1536]{1,0:T(8,128)(2,1)S(1)}, bf16[256,1536]{1,0:T(8,128)(2,1)S(1)}, u32[]{:S(2)}, u32[]{:S(2)}) %collective-permute-start.64) | collective-permute-done | bytes 786464 | tf_op jit(solution)/shard_map/ppermute | solution.py:48
  847.9 15.2 %collective-permute-done.71 = bf16[256,1536]{1,0:T(8,128)(2,1)S(1)} collective-permute-done((bf16[256,1536]{1,0:T(8,128)(2,1)S(1)}, bf16[256,1536]{1,0:T(8,128)(2,1)S(1)}, u32[]{:S(2)}, u32[]{:S(2)}) %collective-permute-start.71) | collective-permute-done | bytes 786464 | tf_op jit(solution)/shard_map/ppermute | solution.py:48
  871.5 19.4 %collective-permute-done.86 = bf16[384,1152]{1,0:T(8,128)(2,1)S(1)} collective-permute-done((bf16[384,1152]{1,0:T(8,128)(2,1)S(1)}, bf16[384,1152]{1,0:T(8,128)(2,1)S(1)}, u32[]{:S(2)}, u32[]{:S(2)}) %collective-permute-start.86) | collective-permute-done | bytes 884768 | tf_op jit(solution)/shard_map/ppermute | solution.py:48
  901.7 7.0 collective-permute-done.82
  908.7 23.9 %collective-permute-done.81 = bf16[192,1152]{1,0:T(8,128)(2,1)S(1)} collective-permute-done((bf16[192,1152]{1,0:T(8,128)(2,1)S(1)}, bf16[192,1152]{1,0:T(8,128)(2,1)S(1)}, u32[]{:S(2)}, u32[]{:S(2)}) %collective-permute-start.81) | collective-permute-done | bytes 442400 | tf_op jit(solution)/shard_map/ppermute | solution.py:48
  950.1 22.7 %collective-permute-done.89 = bf16[192,1152]{1,0:T(8,128)(2,1)} collective-permute-done((bf16[192,1152]{1,0:T(8,128)(2,1)}, bf16[192,1152]{1,0:T(8,128)(2,1)}, u32[]{:S(2)}, u32[]{:S(2)}) %collective-permute-start.89) | collective-permute-done | bytes 442400 | tf_op jit(solution)/shard_map/ppermute | solution.py:48
  (904 shorter events, 431.2 us)
Async XLA Ops:
  7.2 125.7 %all-gather.3.cloned.1.call-start = ((), (), s32[]{:S(2)}) async-start(), calls=%async_computation.4 | async-start | bytes 5308416 | tf_op jit(solution)/shard_map/all_gather | solution.py:134
  11.3 41.0 %collective-permute-start = (bf16[256,1536]{1,0:T(8,128)(2,1)S(1)}, bf16[256,1536]{1,0:T(8,128)(2,1)}, u32[]{:S(2)}, u32[]{:S(2)}) collective-permute-start(bf16[256,1536]{1,0:T(8,128)(2,1)S(1)} %get-tuple-element.300), channel_id=1, source_target_pairs={{0,1},{1,0},{2,3},{3,2},{4,5},{5,4},{6,7},{7,6},{8,9},{9,8},{10,11... | collective-permute-start | bytes 2359304 | tf_op jit(solution)/shard_map/ppermute | solution.py:48
  14.3 38.0 %collective-permute-start.1 = (bf16[256,1536]{1,0:T(8,128)(2,1)S(1)}, bf16[256,1536]{1,0:T(8,128)(2,1)}, u32[]{:S(2)}, u32[]{:S(2)}) collective-permute-start(bf16[256,1536]{1,0:T(8,128)(2,1)S(1)} %get-tuple-element.300), channel_id=1, source_target_pairs={{0,2},{1,3},{2,0},{3,1},{4,6},{5,7},{6,4},{7,5},{8,10},{9,11},{10,... | collective-permute-start | bytes 2359304 | tf_op jit(solution)/shard_map/ppermute | solution.py:48
  41.7 184.0 %all-gather.5.cloned.1.call-start = ((), (), s32[]{:S(2)}) async-start(), calls=%async_computation.5 | async-start | bytes 5308416 | tf_op jit(solution)/shard_map/all_gather | solution.py:134
  52.3 36.0 %collective-permute-start.15 = (bf16[256,1536]{1,0:T(8,128)(2,1)}, bf16[256,1536]{1,0:T(8,128)(2,1)S(1)}, u32[]{:S(2)}, u32[]{:S(2)}) collective-permute-start(bf16[256,1536]{1,0:T(8,128)(2,1)} %get-tuple-element.70), channel_id=1, source_target_pairs={{0,1},{1,0},{2,3},{3,2},{4,5},{5,4},{6,7},{7,6},{8,9},{9,8},{10,11... | collective-permute-start | bytes 2359304 | tf_op jit(solution)/shard_map/ppermute | solution.py:48
  52.7 36.2 %collective-permute-start.16 = (bf16[256,1536]{1,0:T(8,128)(2,1)}, bf16[256,1536]{1,0:T(8,128)(2,1)S(1)}, u32[]{:S(2)}, u32[]{:S(2)}) collective-permute-start(bf16[256,1536]{1,0:T(8,128)(2,1)} %get-tuple-element.70), channel_id=1, source_target_pairs={{0,2},{1,3},{2,0},{3,1},{4,6},{5,7},{6,4},{7,5},{8,10},{9,11},{10,... | collective-permute-start | bytes 2359304 | tf_op jit(solution)/shard_map/ppermute | solution.py:48
  55.4 23.9 %collective-permute-start.2 = (bf16[128,1536]{1,0:T(8,128)(2,1)S(1)}, bf16[128,1536]{1,0:T(8,128)(2,1)S(1)}, u32[]{:S(2)}, u32[]{:S(2)}) collective-permute-start(bf16[128,1536]{1,0:T(8,128)(2,1)S(1)} %slice.541), channel_id=1, source_target_pairs={{0,2},{1,3},{2,0},{3,1},{4,6},{5,7},{6,4},{7,5},{8,10},{9,11},{10,... | collective-permute-start | bytes 1179656 | tf_op jit(solution)/shard_map/ppermute | solution.py:48
  88.4 24.4 %collective-permute-start.27 = (bf16[128,1536]{1,0:T(8,128)(2,1)S(1)}, bf16[128,1536]{1,0:T(8,128)(2,1)S(1)}, u32[]{:S(2)}, u32[]{:S(2)}) collective-permute-start(bf16[128,1536]{1,0:T(8,128)(2,1)S(1)} %slice.558), channel_id=1, source_target_pairs={{0,2},{1,3},{2,0},{3,1},{4,6},{5,7},{6,4},{7,5},{8,10},{9,11},{10,... | collective-permute-start | bytes 1179656 | tf_op jit(solution)/shard_map/ppermute | solution.py:48
  88.9 23.8 %collective-permute-start.28 = (bf16[128,1536]{1,0:T(8,128)(2,1)S(1)}, bf16[128,1536]{1,0:T(8,128)(2,1)S(1)}, u32[]{:S(2)}, u32[]{:S(2)}) collective-permute-start(bf16[128,1536]{1,0:T(8,128)(2,1)S(1)} %slice.559), channel_id=1, source_target_pairs={{0,1},{1,0},{2,3},{3,2},{4,5},{5,4},{6,7},{7,6},{8,9},{9,8},{10,11... | collective-permute-start | bytes 1179656 | tf_op jit(solution)/shard_map/ppermute | solution.py:48
  90.3 73.0 %collective-permute-start.19 = (bf16[2,768,128]{2,1,0:T(8,128)(2,1)}, bf16[2,768,128]{2,1,0:T(8,128)(2,1)}, u32[]{:S(2)}, u32[]{:S(2)}) collective-permute-start(bf16[2,768,128]{2,1,0:T(8,128)(2,1)} %pad_maximum_fusion.33), channel_id=1, source_target_pairs={{0,3},{1,2},{2,1},{3,0},{4,7},{5,6},{6,5},{7,4},{8,11},{9,10},{10,... | collective-permute-start | bytes 1179656 | tf_op jit(solution)/shard_map/ppermute | solution.py:48
  95.9 67.6 %collective-permute-start.18 = (bf16[2,768,128]{2,1,0:T(8,128)(2,1)}, bf16[2,768,128]{2,1,0:T(8,128)(2,1)}, u32[]{:S(2)}, u32[]{:S(2)}) collective-permute-start(bf16[2,768,128]{2,1,0:T(8,128)(2,1)} %pad_maximum_fusion.33), channel_id=1, source_target_pairs={{0,2},{1,3},{2,0},{3,1},{4,6},{5,7},{6,4},{7,5},{8,10},{9,11},{10,... | collective-permute-start | bytes 1179656 | tf_op jit(solution)/shard_map/ppermute | solution.py:48
  145.3 794.8 %reduce-scatter.13.cloned.1.call-start = ((), (), s32[]{:S(2)}) async-start(), calls=%async_computation.8 | async-start | bytes 1327104
  163.3 31.8 %collective-permute-start.11 = (bf16[3,192,1536]{2,1,0:T(8,128)(2,1)S(1)}, bf16[3,192,1536]{2,1,0:T(8,128)(2,1)S(1)}, u32[]{:S(2)}, u32[]{:S(2)}) collective-permute-start(bf16[3,192,1536]{2,1,0:T(8,128)(2,1)S(1)} %bitcast.283), channel_id=1, source_target_pairs={{0,4},{4,0},{8,12},{12,8},{16,20},{20,16},{24,28},{28,24},{1,5},{5... | collective-permute-start | bytes 5308424 | tf_op jit(solution)/shard_map/ppermute | solution.py:48
  163.4 41.8 %collective-permute-start.39 = (bf16[384,256]{1,0:T(8,128)(2,1)S(1)}, bf16[384,256]{1,0:T(8,128)(2,1)S(1)}, u32[]{:S(2)}, u32[]{:S(2)}) collective-permute-start(bf16[384,256]{1,0:T(8,128)(2,1)S(1)} %get-tuple-element.369), channel_id=1, source_target_pairs={{0,3},{1,2},{2,1},{3,0},{4,7},{5,6},{6,5},{7,4},{8,11},{9,10},{10,... | collective-permute-start | bytes 589832 | tf_op jit(solution)/shard_map/ppermute | solution.py:48
  164.4 40.9 %collective-permute-start.38 = (bf16[384,256]{1,0:T(8,128)(2,1)S(1)}, bf16[384,256]{1,0:T(8,128)(2,1)S(1)}, u32[]{:S(2)}, u32[]{:S(2)}) collective-permute-start(bf16[384,256]{1,0:T(8,128)(2,1)S(1)} %get-tuple-element.370), channel_id=1, source_target_pairs={{0,2},{1,3},{2,0},{3,1},{4,6},{5,7},{6,4},{7,5},{8,10},{9,11},{10,... | collective-permute-start | bytes 589832 | tf_op jit(solution)/shard_map/ppermute | solution.py:48
  252.6 84.2 %collective-permute-start.44 = (bf16[256,1536]{1,0:T(8,128)(2,1)S(1)}, bf16[256,1536]{1,0:T(8,128)(2,1)}, u32[]{:S(2)}, u32[]{:S(2)}) collective-permute-start(bf16[256,1536]{1,0:T(8,128)(2,1)S(1)} %copy-done.100), channel_id=1, source_target_pairs={{0,1},{1,0},{2,3},{3,2},{4,5},{5,4},{6,7},{7,6},{8,9},{9,8},{10,11... | collective-permute-start | bytes 2359304 | tf_op jit(solution)/shard_map/ppermute | solution.py:48
  252.6 85.3 %collective-permute-start.45 = (bf16[256,1536]{1,0:T(8,128)(2,1)S(1)}, bf16[256,1536]{1,0:T(8,128)(2,1)S(1)}, u32[]{:S(2)}, u32[]{:S(2)}) collective-permute-start(bf16[256,1536]{1,0:T(8,128)(2,1)S(1)} %copy-done.100), channel_id=1, source_target_pairs={{0,2},{1,3},{2,0},{3,1},{4,6},{5,7},{6,4},{7,5},{8,10},{9,11},{10,... | collective-permute-start | bytes 2359304 | tf_op jit(solution)/shard_map/ppermute | solution.py:48
  275.7 75.5 %collective-permute-start.40 = (bf16[256,1536]{1,0:T(8,128)(2,1)S(1)}, bf16[256,1536]{1,0:T(8,128)(2,1)S(1)}, u32[]{:S(2)}, u32[]{:S(2)}) collective-permute-start(bf16[256,1536]{1,0:T(8,128)(2,1)S(1)} %get-tuple-element.217), channel_id=1, source_target_pairs={{0,1},{1,0},{2,3},{3,2},{4,5},{5,4},{6,7},{7,6},{8,9},{9,8},{10,11... | collective-permute-start | bytes 2359304 | tf_op jit(solution)/shard_map/ppermute | solution.py:48
  336.8 23.8 %collective-permute-start.41 = (bf16[256,1536]{1,0:T(8,128)(2,1)S(1)}, bf16[256,1536]{1,0:T(8,128)(2,1)S(1)}, u32[]{:S(2)}, u32[]{:S(2)}) collective-permute-start(bf16[256,1536]{1,0:T(8,128)(2,1)S(1)} %get-tuple-element.217), channel_id=1, source_target_pairs={{0,2},{1,3},{2,0},{3,1},{4,6},{5,7},{6,4},{7,5},{8,10},{9,11},{10,... | collective-permute-start | bytes 2359304 | tf_op jit(solution)/shard_map/ppermute | solution.py:48
  337.9 31.1 %collective-permute-start.46 = (bf16[128,1536]{1,0:T(8,128)(2,1)S(1)}, bf16[128,1536]{1,0:T(8,128)(2,1)S(1)}, u32[]{:S(2)}, u32[]{:S(2)}) collective-permute-start(bf16[128,1536]{1,0:T(8,128)(2,1)S(1)} %slice.581), channel_id=1, source_target_pairs={{0,2},{1,3},{2,0},{3,1},{4,6},{5,7},{6,4},{7,5},{8,10},{9,11},{10,... | collective-permute-start | bytes 1179656 | tf_op jit(solution)/shard_map/ppermute | solution.py:48
  343.7 28.2 %collective-permute-start.47 = (bf16[128,1536]{1,0:T(8,128)(2,1)S(1)}, bf16[128,1536]{1,0:T(8,128)(2,1)S(1)}, u32[]{:S(2)}, u32[]{:S(2)}) collective-permute-start(bf16[128,1536]{1,0:T(8,128)(2,1)S(1)} %slice.582), channel_id=1, source_target_pairs={{0,1},{1,0},{2,3},{3,2},{4,5},{5,4},{6,7},{7,6},{8,9},{9,8},{10,11... | collective-permute-start | bytes 1179656 | tf_op jit(solution)/shard_map/ppermute | solution.py:48
  345.8 107.5 %collective-permute-start.53 = (bf16[256,1536]{1,0:T(8,128)(2,1)}, bf16[256,1536]{1,0:T(8,128)(2,1)}, u32[]{:S(2)}, u32[]{:S(2)}) collective-permute-start(bf16[256,1536]{1,0:T(8,128)(2,1)} %pad_maximum_fusion.20), channel_id=1, source_target_pairs={{0,1},{1,0},{2,3},{3,2},{4,5},{5,4},{6,7},{7,6},{8,9},{9,8},{10,11... | collective-permute-start | bytes 2359304 | tf_op jit(solution)/shard_map/ppermute | solution.py:48
  351.2 103.4 %collective-permute-start.55 = (bf16[256,1536]{1,0:T(8,128)(2,1)}, bf16[256,1536]{1,0:T(8,128)(2,1)}, u32[]{:S(2)}, u32[]{:S(2)}) collective-permute-start(bf16[256,1536]{1,0:T(8,128)(2,1)} %pad_maximum_fusion.21), channel_id=1, source_target_pairs={{0,2},{1,3},{2,0},{3,1},{4,6},{5,7},{6,4},{7,5},{8,10},{9,11},{10,... | collective-permute-start | bytes 2359304 | tf_op jit(solution)/shard_map/ppermute | solution.py:48
  360.6 96.8 %collective-permute-start.36 = (bf16[256,1536]{1,0:T(8,128)(2,1)}, bf16[256,1536]{1,0:T(8,128)(2,1)}, u32[]{:S(2)}, u32[]{:S(2)}) collective-permute-start(bf16[256,1536]{1,0:T(8,128)(2,1)} %pad_maximum_fusion.16), channel_id=1, source_target_pairs={{0,2},{1,3},{2,0},{3,1},{4,6},{5,7},{6,4},{7,5},{8,10},{9,11},{10,... | collective-permute-start | bytes 2359304 | tf_op jit(solution)/shard_map/ppermute | solution.py:48
  369.0 23.9 %collective-permute-start.42 = (bf16[128,1536]{1,0:T(8,128)(2,1)S(1)}, bf16[128,1536]{1,0:T(8,128)(2,1)S(1)}, u32[]{:S(2)}, u32[]{:S(2)}) collective-permute-start(bf16[128,1536]{1,0:T(8,128)(2,1)S(1)} %slice.579), channel_id=1, source_target_pairs={{0,2},{1,3},{2,0},{3,1},{4,6},{5,7},{6,4},{7,5},{8,10},{9,11},{10,... | collective-permute-start | bytes 1179656 | tf_op jit(solution)/shard_map/ppermute | solution.py:48
  392.9 64.5 %collective-permute-start.34 = (bf16[256,1536]{1,0:T(8,128)(2,1)}, bf16[256,1536]{1,0:T(8,128)(2,1)}, u32[]{:S(2)}, u32[]{:S(2)}) collective-permute-start(bf16[256,1536]{1,0:T(8,128)(2,1)} %pad_maximum_fusion.15), channel_id=1, source_target_pairs={{0,1},{1,0},{2,3},{3,2},{4,5},{5,4},{6,7},{7,6},{8,9},{9,8},{10,11... | collective-permute-start | bytes 2359304 | tf_op jit(solution)/shard_map/ppermute | solution.py:48
  432.4 43.2 %collective-permute-start.50 = (bf16[128,1536]{1,0:T(8,128)(2,1)}, bf16[128,1536]{1,0:T(8,128)(2,1)}, u32[]{:S(2)}, u32[]{:S(2)}) collective-permute-start(bf16[128,1536]{1,0:T(8,128)(2,1)} %get-tuple-element.275), channel_id=1, source_target_pairs={{0,1},{1,0},{2,3},{3,2},{4,5},{5,4},{6,7},{7,6},{8,9},{9,8},{10,11... | collective-permute-start | bytes 1179656 | tf_op jit(solution)/shard_map/ppermute | solution.py:48
  531.3 411.6 %reduce-scatter.15.cloned.1.call-start = ((), (), s32[]{:S(2)}) async-start(), calls=%async_computation.9 | async-start | bytes 5308416
  538.0 407.5 %reduce-scatter.11.cloned.1.call-start = ((), (), s32[]{:S(2)}) async-start(), calls=%async_computation.7 | async-start | bytes 5308416 | tf_op jit(solution)/shard_map/reduce_scatter | solution.py:480
  561.2 386.4 %reduce-scatter.9.cloned.1.call-start = ((), (), s32[]{:S(2)}) async-start(), calls=%async_computation.6 | async-start | bytes 5308416 | tf_op jit(solution)/shard_map/reduce_scatter | solution.py:480
  581.2 202.2 %collective-permute-start.56 = (bf16[128,1536]{1,0:T(8,128)(2,1)}, bf16[128,1536]{1,0:T(8,128)(2,1)}, u32[]{:S(2)}, u32[]{:S(2)}) collective-permute-start(bf16[128,1536]{1,0:T(8,128)(2,1)} %get-tuple-element.264), channel_id=1, source_target_pairs={{0,2},{1,3},{2,0},{3,1},{4,6},{5,7},{6,4},{7,5},{8,10},{9,11},{10,... | collective-permute-start | bytes 1179656 | tf_op jit(solution)/shard_map/ppermute | solution.py:48
  582.6 202.3 %collective-permute-start.58 = (bf16[128,1536]{1,0:T(8,128)(2,1)}, bf16[128,1536]{1,0:T(8,128)(2,1)}, u32[]{:S(2)}, u32[]{:S(2)}) collective-permute-start(bf16[128,1536]{1,0:T(8,128)(2,1)} %get-tuple-element.265), channel_id=1, source_target_pairs={{0,1},{1,0},{2,3},{3,2},{4,5},{5,4},{6,7},{7,6},{8,9},{9,8},{10,11... | collective-permute-start | bytes 1179656 | tf_op jit(solution)/shard_map/ppermute | solution.py:48
  585.3 130.3 %collective-permute-start.69 = (bf16[384,256]{1,0:T(8,128)(2,1)}, bf16[384,256]{1,0:T(8,128)(2,1)}, u32[]{:S(2)}, u32[]{:S(2)}) collective-permute-start(bf16[384,256]{1,0:T(8,128)(2,1)} %get-tuple-element.345), channel_id=1, source_target_pairs={{0,3},{1,2},{2,1},{3,0},{4,7},{5,6},{6,5},{7,4},{8,11},{9,10},{10,... | collective-permute-start | bytes 589832 | tf_op jit(solution)/shard_map/ppermute | solution.py:48
  585.6 130.8 %collective-permute-start.68 = (bf16[384,256]{1,0:T(8,128)(2,1)}, bf16[384,256]{1,0:T(8,128)(2,1)}, u32[]{:S(2)}, u32[]{:S(2)}) collective-permute-start(bf16[384,256]{1,0:T(8,128)(2,1)} %get-tuple-element.346), channel_id=1, source_target_pairs={{0,2},{1,3},{2,0},{3,1},{4,6},{5,7},{6,4},{7,5},{8,10},{9,11},{10,... | collective-permute-start | bytes 589832 | tf_op jit(solution)/shard_map/ppermute | solution.py:48
  587.0 129.5 %collective-permute-start.67 = (bf16[384,256]{1,0:T(8,128)(2,1)}, bf16[384,256]{1,0:T(8,128)(2,1)}, u32[]{:S(2)}, u32[]{:S(2)}) collective-permute-start(bf16[384,256]{1,0:T(8,128)(2,1)} %get-tuple-element.347), channel_id=1, source_target_pairs={{0,1},{1,0},{2,3},{3,2},{4,5},{5,4},{6,7},{7,6},{8,9},{9,8},{10,11... | collective-permute-start | bytes 589832 | tf_op jit(solution)/shard_map/ppermute | solution.py:48
  715.6 72.5 %collective-permute-start.63 = (bf16[128,1536]{1,0:T(8,128)(2,1)}, bf16[128,1536]{1,0:T(8,128)(2,1)}, u32[]{:S(2)}, u32[]{:S(2)}) collective-permute-start(bf16[128,1536]{1,0:T(8,128)(2,1)} %get-tuple-element.246), channel_id=1, source_target_pairs={{0,2},{1,3},{2,0},{3,1},{4,6},{5,7},{6,4},{7,5},{8,10},{9,11},{10,... | collective-permute-start | bytes 1179656 | tf_op jit(solution)/shard_map/ppermute | solution.py:48
  716.4 148.6 %collective-permute-start.83 = (bf16[4,192,4,1152]{3,1,2,0:T(8,128)(2,1)}, bf16[4,192,4,1152]{3,1,2,0:T(8,128)(2,1)}, u32[]{:S(2)}, u32[]{:S(2)}) collective-permute-start(bf16[4,192,4,1152]{3,1,2,0:T(8,128)(2,1)} %get-tuple-element.237), channel_id=1, source_target_pairs={{0,4},{4,0},{8,12},{12,8},{16,20},{20,16},{24,28},{28,24},{1,5},{5... | collective-permute-start | bytes 21233672 | tf_op jit(solution)/shard_map/ppermute | solution.py:48
  795.2 31.1 %collective-permute-start.59 = (bf16[256,1536]{1,0:T(8,128)(2,1)S(1)}, bf16[256,1536]{1,0:T(8,128)(2,1)S(1)}, u32[]{:S(2)}, u32[]{:S(2)}) collective-permute-start(bf16[256,1536]{1,0:T(8,128)(2,1)S(1)} %pad_maximum_fusion.23), channel_id=1, source_target_pairs={{0,2},{1,3},{2,0},{3,1},{4,6},{5,7},{6,4},{7,5},{8,10},{9,11},{10,... | collective-permute-start | bytes 2359304 | tf_op jit(solution)/shard_map/ppermute | solution.py:48
  798.8 28.6 %collective-permute-start.57 = (bf16[256,1536]{1,0:T(8,128)(2,1)S(1)}, bf16[256,1536]{1,0:T(8,128)(2,1)S(1)}, u32[]{:S(2)}, u32[]{:S(2)}) collective-permute-start(bf16[256,1536]{1,0:T(8,128)(2,1)S(1)} %pad_maximum_fusion.22), channel_id=1, source_target_pairs={{0,1},{1,0},{2,3},{3,2},{4,5},{5,4},{6,7},{7,6},{8,9},{9,8},{10,11... | collective-permute-start | bytes 2359304 | tf_op jit(solution)/shard_map/ppermute | solution.py:48
  800.6 31.2 %collective-permute-start.66 = (bf16[256,1536]{1,0:T(8,128)(2,1)S(1)}, bf16[256,1536]{1,0:T(8,128)(2,1)S(1)}, u32[]{:S(2)}, u32[]{:S(2)}) collective-permute-start(bf16[256,1536]{1,0:T(8,128)(2,1)S(1)} %pad_maximum_fusion.26), channel_id=1, source_target_pairs={{0,2},{1,3},{2,0},{3,1},{4,6},{5,7},{6,4},{7,5},{8,10},{9,11},{10,... | collective-permute-start | bytes 2359304 | tf_op jit(solution)/shard_map/ppermute | solution.py:48
  820.3 44.3 %collective-permute-start.79 = (bf16[4,192,1152]{2,1,0:T(8,128)(2,1)S(1)}, bf16[4,192,1152]{2,1,0:T(8,128)(2,1)S(1)}, u32[]{:S(2)}, u32[]{:S(2)}) collective-permute-start(bf16[4,192,1152]{2,1,0:T(8,128)(2,1)S(1)} %fusion.26), channel_id=1, source_target_pairs={{0,4},{4,0},{8,12},{12,8},{16,20},{20,16},{24,28},{28,24},{1,5},{5... | collective-permute-start | bytes 5308424 | tf_op jit(solution)/shard_map/ppermute | solution.py:48
  831.8 31.3 %collective-permute-start.71 = (bf16[256,1536]{1,0:T(8,128)(2,1)S(1)}, bf16[256,1536]{1,0:T(8,128)(2,1)S(1)}, u32[]{:S(2)}, u32[]{:S(2)}) collective-permute-start(bf16[256,1536]{1,0:T(8,128)(2,1)S(1)} %pad_maximum_fusion.28), channel_id=1, source_target_pairs={{0,1},{1,0},{2,3},{3,2},{4,5},{5,4},{6,7},{7,6},{8,9},{9,8},{10,11... | collective-permute-start | bytes 2359304 | tf_op jit(solution)/shard_map/ppermute | solution.py:48
  891.3 41.5 %collective-permute-start.87 = (bf16[768,1152]{1,0:T(8,128)(2,1)S(1)}, bf16[768,1152]{1,0:T(8,128)(2,1)S(1)}, u32[]{:S(2)}, u32[]{:S(2)}) collective-permute-start(bf16[768,1152]{1,0:T(8,128)(2,1)S(1)} %pad_maximum_fusion.11), channel_id=1, source_target_pairs={{0,2},{1,3},{2,0},{3,1},{4,6},{5,7},{6,4},{7,5},{8,10},{9,11},{10,... | collective-permute-start | bytes 5308424 | tf_op jit(solution)/shard_map/ppermute | solution.py:48
  893.1 39.8 %collective-permute-start.85 = (bf16[768,1152]{1,0:T(8,128)(2,1)S(1)}, bf16[768,1152]{1,0:T(8,128)(2,1)S(1)}, u32[]{:S(2)}, u32[]{:S(2)}) collective-permute-start(bf16[768,1152]{1,0:T(8,128)(2,1)S(1)} %pad_maximum_fusion.10), channel_id=1, source_target_pairs={{0,1},{1,0},{2,3},{3,2},{4,5},{5,4},{6,7},{7,6},{8,9},{9,8},{10,11... | collective-permute-start | bytes 5308424 | tf_op jit(solution)/shard_map/ppermute | solution.py:48
  897.3 35.4 %collective-permute-start.81 = (bf16[192,1152]{1,0:T(8,128)(2,1)S(1)}, bf16[192,1152]{1,0:T(8,128)(2,1)S(1)}, u32[]{:S(2)}, u32[]{:S(2)}) collective-permute-start(bf16[192,1152]{1,0:T(8,128)(2,1)S(1)} %get-tuple-element.299), channel_id=1, source_target_pairs={{0,16},{4,20},{8,24},{12,28},{16,0},{20,4},{24,8},{28,12},{1,17},{... | collective-permute-start | bytes 1327112 | tf_op jit(solution)/shard_map/ppermute | solution.py:48
  897.3 35.4 %collective-permute-start.80 = (bf16[192,1152]{1,0:T(8,128)(2,1)S(1)}, bf16[192,1152]{1,0:T(8,128)(2,1)S(1)}, u32[]{:S(2)}, u32[]{:S(2)}) collective-permute-start(bf16[192,1152]{1,0:T(8,128)(2,1)S(1)} %get-tuple-element.297), channel_id=1, source_target_pairs={{0,8},{4,12},{8,0},{12,4},{16,24},{20,28},{24,16},{28,20},{1,9},{5... | collective-permute-start | bytes 1327112 | tf_op jit(solution)/shard_map/ppermute | solution.py:48
  937.7 35.1 %collective-permute-start.89 = (bf16[192,1152]{1,0:T(8,128)(2,1)}, bf16[192,1152]{1,0:T(8,128)(2,1)}, u32[]{:S(2)}, u32[]{:S(2)}) collective-permute-start(bf16[192,1152]{1,0:T(8,128)(2,1)} %get-tuple-element.290), channel_id=1, source_target_pairs={{0,16},{4,20},{8,24},{12,28},{16,0},{20,4},{24,8},{28,12},{1,17},{... | collective-permute-start | bytes 1327112 | tf_op jit(solution)/shard_map/ppermute | solution.py:48
  937.7 35.1 %collective-permute-start.88 = (bf16[192,1152]{1,0:T(8,128)(2,1)S(1)}, bf16[192,1152]{1,0:T(8,128)(2,1)}, u32[]{:S(2)}, u32[]{:S(2)}) collective-permute-start(bf16[192,1152]{1,0:T(8,128)(2,1)S(1)} %get-tuple-element.288), channel_id=1, source_target_pairs={{0,8},{4,12},{8,0},{12,4},{16,24},{20,28},{24,16},{28,20},{1,9},{5... | collective-permute-start | bytes 1327112 | tf_op jit(solution)/shard_map/ppermute | solution.py:48
  (275 other events, 3259.9 us)
Sparse Core Ops, SparseCore 0:
  41.9 52.0 all-gather.2
  145.5 51.8 all-gather.4
  531.4 34.1 reduce-scatter.12
  567.8 53.3 reduce-scatter.14
  623.4 53.2 reduce-scatter.10
  693.2 55.2 reduce-scatter.8

commit v3 on v2

--- a/solution.py
+++ b/solution.py
@@ -52,31 +52,65 @@
     return lax.optimization_barrier((values,) + others)[0]
 
 
-def spread(values):
-    size = lax.axis_size("mp")
-    if size != 4:
-        pieces = [values] + [swap(values, "mp", k) for k in range(1, size)]
-        return (pieces, tuple(pieces[1:2]))
-    half = values.shape[0] // 2
-    one = swap(values, "mp", 1)
-    two = swap(values, "mp", 2)
-    pieces = [values, one, two, swap(one[:half], "mp", 2), swap(two[half:], "mp", 1)]
-    return (pieces, (one, two))
+class Spread:
+    def __init__(self, values):
+        self.values = values
+        if lax.axis_size("mp") == 4:
+            self.first = (swap(values, "mp", 1), swap(values, "mp", 2))
+        else:
+            self.first = tuple(swap(values, "mp", k) for k in range(1, lax.axis_size("mp")))
+        self.last = ()
+
+    def second_step(self):
+        if lax.axis_size("mp") == 4:
+            half = self.values.shape[0] // 2
+            one, two = self.first
+            self.last = (swap(one[:half], "mp", 2), swap(two[half:], "mp", 1))
+
+    def pieces(self):
+        return [self.values, *self.first, *self.last]
 
 
 def trade(blocks):
     return [blocks[0]] + [swap(blocks[k], "mp", k) for k in range(1, len(blocks))]
 
 
-def settle(blocks):
-    if len(blocks) != 4:
-        return trade(blocks)
-    half = blocks[0].shape[0] // 2
-    high = swap(blocks[3][:half], "mp", 2)
-    low = swap(blocks[3][half:], "mp", 1)
-    one = jnp.concatenate([plus(blocks[1][:half], high), blocks[1][half:]], axis=0)
-    two = jnp.concatenate([blocks[2][:half], plus(blocks[2][half:], low)], axis=0)
-    return [blocks[0], swap(one, "mp", 1), swap(two, "mp", 2)]
+def cut(values):
+    size = lax.axis_size("mp")
+    blocks = jnp.split(values, size, axis=0)
+    return blocks[:3] + jnp.split(blocks[3], 2, axis=0) if size == 4 else blocks
+
+
+def settle_first(pieces):
+    if lax.axis_size("mp") != 4:
+        return ()
+    return (swap(pieces[3], "mp", 2), swap(pieces[4], "mp", 1))
+
+
+def settle_last(pieces, came):
+    if lax.axis_size("mp") != 4:
+        return trade(pieces)
+    high, low = came
+    half = high.shape[0]
+    one = jnp.concatenate([plus(pieces[1][:half], high), pieces[1][half:]], axis=0)
+    two = jnp.concatenate([pieces[2][:half], plus(pieces[2][half:], low)], axis=0)
+    return [pieces[0], swap(one, "mp", 1), swap(two, "mp", 2)]
+
+
+class Chain:
+    def __init__(self):
+        self.last = ()
+
+    def hold(self, values):
+        return after(values, *self.last) if self.last else values
+
+    def mark(self, *values):
+        self.last = values
+
+    def arrive(self, values):
+        values = self.hold(values)
+        self.mark(values)
+        return values
 
 
 def plus(left, right):
@@ -111,27 +145,6 @@
         lax.dynamic_index_in_dim(blocks, here ^ k, 0, False) for k in range(blocks.shape[0])
     ]
     return total([mine[0]] + [swap(mine[k], "dp", 2 * k) for k in range(1, len(mine))])
-
-
-def whole_rows(shard):
-    size = lax.axis_size("mp")
-    rows, width = shard.shape
-    core = lax.axis_index("dp") & 1
-    mine = lax.dynamic_slice_in_dim(shard, core * (rows // 2), rows // 2, 0)
-    got = jnp.concatenate(spread(mine)[0][1:], axis=0).reshape(size - 1, rows // 2, width)
-    other = swap(got, "dp", 1)
-    low = jnp.where(core == 0, got, other)
-    high = jnp.where(core == 0, other, got)
-    rest = jnp.concatenate([low, high], axis=1).reshape((size - 1) * rows, width)
-    return jnp.concatenate([shard, rest], axis=0)
-
-
-def whole_columns(shard):
-    size = lax.axis_size("mp")
-    depth = shard.shape[0] // lax.axis_size("dp")
-    mine = lax.dynamic_slice_in_dim(shard, lax.axis_index("dp") * depth, depth, 0)
-    wide = jnp.concatenate([mine] + [swap(mine, "mp", k) for k in range(1, size)], axis=1)
-    return (wide, lax.all_gather(wide, "dp", axis=0, tiled=True))
 
 
 def self_forward_kernel(block, q_ref, k_ref, v_ref, pk_ref, pv_ref, o_ref, l_ref):
@@ -389,69 +402,213 @@
     )(lengths, queries, keys, values, grads, mixed, logsum)
 
 
-def glu_kernel(block, x_ref, c_ref, gate_ref, up_ref, down_ref, h_ref, dg_ref, du_ref):
-    for start in range(0, x_ref.shape[0], block):
-        part = slice(start, start + block)
-        gate = dot(x_ref[part], gate_ref[...], 1, 0)
-        upper = dot(x_ref[part], up_ref[...], 1, 0)
-        grad_hidden = dot(c_ref[part], down_ref[...], 1, 1)
+def block_refs(refs, size):
+    return [refs[0:1], refs[1:2], refs[2:3], refs[3:5]] if size == 4 else [[r] for r in refs]
+
+
+def block_value(refs):
+    parts = [ref[...] for ref in refs]
+    return parts[0] if len(parts) == 1 else jnp.concatenate(parts, axis=0)
+
+
+def whole_specs(pieces):
+    return [pl.BlockSpec(piece.shape, lambda j: (0, 0)) for piece in pieces]
+
+
+def project_kernel(size, heads, w_ref, cos_ref, sin_ref, *refs):
+    d_ref, x_ref = refs[-2:]
+    blocks = block_refs(refs[: 5 if size == 4 else size], size)
+    for k in range(size):
+
+        @pl.when(pl.program_id(0) == k)
+        def _(k=k):
+            frames = block_value(blocks[k])
+            x_ref[0] = frames
+            raw = dot(w_ref[...], frames, 1, 1)
+            cosine = cos_ref[...]
+            sine = sin_ref[...]
+            for head in range(2 * heads):
+                at = head * HEAD_DIM
+                upper = raw[at : at + HALF]
+                lower = raw[at + HALF : at + HEAD_DIM]
+                first = upper * cosine - lower * sine
+                second = lower * cosine + upper * sine
+                if head < heads:
+                    first, second = first * FACTOR, second * FACTOR
+                d_ref[at : at + HALF] = first.astype(bf16)
+                d_ref[at + HALF : at + HEAD_DIM] = second.astype(bf16)
+            at = 2 * heads * HEAD_DIM
+            d_ref[at:] = raw[at:].astype(bf16)
+
+
+def project(clip, count, pieces, w_turned, cosine, sine, earlier):
+    size = lax.axis_size("mp")
+    depth, width = w_turned.shape
+    rows = pieces[0].shape[0]
+    angles = pl.BlockSpec((HALF, rows), lambda k: (0, k))
+    return pl.pallas_call(
+        functools.partial(project_kernel, size, depth // 3 // HEAD_DIM),
+        grid=(size,),
+        in_specs=[pl.BlockSpec((depth, width), lambda k: (0, 0)), angles, angles]
+        + whole_specs(pieces)
+        + [pl.BlockSpec(memory_space=pl.ANY)] * len(earlier),
+        out_specs=[
+            pl.BlockSpec((depth, rows), lambda k: (0, k)),
+            pl.BlockSpec((1, rows, width), lambda k: (clip, k, 0)),
+        ],
+        out_shape=[
+            shape_of((depth, size * rows), bf16),
+            shape_of((count, size * rows, width), bf16),
+        ],
+        input_output_aliases={3 + len(pieces): 1} if earlier else {},
+        compiler_params=params(),
+        cost_estimate=pl.CostEstimate(
+            flops=2 * depth * width * size * rows,
+            bytes_accessed=4 * size * rows * width + 2 * depth * (width + size * rows),
+            transcendentals=0,
+        ),
+        name="project",
+    )(w_turned, cosine, sine, *pieces, *earlier)
+
+
+def glu_kernel(size, given, n_ref, gate_ref, up_ref, down_ref, c_ref, *refs):
+    h_ref, dg_ref, du_ref, x_ref = refs[-4:]
+    blocks = block_refs(refs[:given], size)
+    rows = h_ref.shape[1] // size
+
+    @pl.when(pl.program_id(0) == 0)
+    def _():
+        for k in range(size):
+            x_ref[0, k * rows : (k + 1) * rows] = block_value(blocks[k])
+
+    for k in range(size):
+        frames = block_value(blocks[k])
+        part = slice(k * rows, (k + 1) * rows)
+        there = pl.ds(pl.multiple_of(n_ref[k] * rows, rows), rows)
+        gate = dot(frames, gate_ref[...], 1, 0)
+        upper = dot(frames, up_ref[...], 1, 0)
+        grad_hidden = dot(c_ref[0, there], down_ref[...], 1, 1)
         sigma = 1.0 / (1.0 + jnp.exp(-gate))
         silu = gate * sigma
-        h_ref[part] = (silu * upper).astype(bf16)
-        dg_ref[part] = (grad_hidden * upper * (sigma + silu * (1.0 - sigma))).astype(bf16)
-        du_ref[part] = (grad_hidden * silu).astype(bf16)
-
-
-def glu(frames, grads, w_gate, w_up, w_down):
-    rows, width = frames.shape
+        h_ref[0, there] = (silu * upper).astype(bf16)
+        dg_ref[0, part] = (grad_hidden * upper * (sigma + silu * (1.0 - sigma))).astype(bf16)
+        du_ref[0, part] = (grad_hidden * silu).astype(bf16)
+
+
+def glu(clip, order, pieces, grads, w_gate, w_up, w_down, earlier):
+    size = lax.axis_size("mp")
+    count, rows, width = grads.shape
     hidden = w_gate.shape[1]
     block = 256
-    whole = pl.BlockSpec((rows, width), lambda j: (0, 0))
     columns = pl.BlockSpec((width, block), lambda j: (0, j))
-    out = pl.BlockSpec((rows, block), lambda j: (0, j))
+    out = pl.BlockSpec((1, rows, block), lambda j: (clip, 0, j))
+    whole = pl.BlockSpec((1, rows, width), lambda j: (clip, 0, 0))
     return pl.pallas_call(
-        functools.partial(glu_kernel, 256),
+        functools.partial(glu_kernel, size, len(pieces)),
         grid=(hidden // block,),
-        in_specs=[whole, whole, columns, columns, pl.BlockSpec((block, width), lambda j: (j, 0))],
-        out_specs=[out, out, out],
-        out_shape=[shape_of((rows, hidden), bf16)] * 3,
+        in_specs=[
+            pl.BlockSpec(memory_space=pltpu.SMEM),
+            columns,
+            columns,
+            pl.BlockSpec((block, width), lambda j: (j, 0)),
+            whole,
+        ]
+        + whole_specs(pieces)
+        + [pl.BlockSpec(memory_space=pl.ANY)] * len(earlier),
+        out_specs=[out, out, out, whole],
+        out_shape=[shape_of((count, rows, hidden), bf16)] * 3
+        + [shape_of((count, rows, width), bf16)],
+        input_output_aliases={5 + len(pieces) + i: i for i in range(len(earlier))},
         compiler_params=params(),
         cost_estimate=pl.CostEstimate(
             flops=6 * rows * width * hidden,
-            bytes_accessed=4 * rows * width + 6 * width * hidden + 6 * rows * hidden,
+            bytes_accessed=6 * rows * width + 6 * width * hidden + 6 * rows * hidden,
             transcendentals=rows * hidden,
         ),
         name="glu",
-    )(frames, grads, w_gate, w_up, w_down)
-
-
-def glu_back_kernel(block, dg_ref, du_ref, gate_ref, up_ref, o_ref):
-    for start in range(0, dg_ref.shape[0], block):
-        part = slice(start, start + block)
-        back = dot(dg_ref[part], gate_ref[...], 1, 1) + dot(du_ref[part], up_ref[...], 1, 1)
-        o_ref[part] = back.astype(bf16)
-
-
-def glu_back(grad_gate, grad_upper, w_gate, w_up):
-    rows, hidden = grad_gate.shape
+    )(order, w_gate, w_up, w_down, grads, *pieces, *earlier)
+
+
+def glu_back_kernel(size, dg_ref, du_ref, gate_ref, up_ref, *refs):
+    blocks = block_refs(refs, size)
+    rows = dg_ref.shape[1] // size
+    for k in range(size):
+        part = slice(k * rows, (k + 1) * rows)
+        back = dot(dg_ref[0, part], gate_ref[...], 1, 1) + dot(du_ref[0, part], up_ref[...], 1, 1)
+        at = 0
+        for ref in blocks[k]:
+            ref[...] = back[at : at + ref.shape[0]].astype(bf16)
+            at += ref.shape[0]
+
+
+def glu_back(clip, grad_gate, grad_upper, w_gate, w_up):
+    size = lax.axis_size("mp")
+    _, frames, hidden = grad_gate.shape
+    rows = frames // size
     width = w_gate.shape[0]
     block = 256
-    whole = pl.BlockSpec((rows, hidden), lambda j: (0, 0))
+    sizes = [rows] * 3 + [rows // 2] * 2 if size == 4 else [rows] * size
+    whole = pl.BlockSpec((1, frames, hidden), lambda j: (clip, 0, 0))
     part = pl.BlockSpec((block, hidden), lambda j: (j, 0))
     return pl.pallas_call(
-        functools.partial(glu_back_kernel, 256),
+        functools.partial(glu_back_kernel, size),
         grid=(width // block,),
         in_specs=[whole, whole, part, part],
-        out_specs=pl.BlockSpec((rows, block), lambda j: (0, j)),
-        out_shape=shape_of((rows, width), bf16),
+        out_specs=[pl.BlockSpec((n, block), lambda j: (0, j)) for n in sizes],
+        out_shape=[shape_of((n, width), bf16) for n in sizes],
         compiler_params=params(),
         cost_estimate=pl.CostEstimate(
-            flops=4 * rows * width * hidden,
-            bytes_accessed=4 * rows * hidden + 4 * width * hidden + 2 * rows * width,
+            flops=4 * frames * width * hidden,
+            bytes_accessed=4 * frames * hidden + 4 * width * hidden + 2 * frames * width,
             transcendentals=0,
         ),
         name="glu_back",
     )(grad_gate, grad_upper, w_gate, w_up)
+
+
+def whole_grad_kernel(chips, given, core_ref, x_ref, y_ref, *refs):
+    o_ref, turned_ref = refs[-2:]
+    depth = o_ref.shape[3]
+
+    @pl.when(pl.program_id(1) == 0)
+    def _():
+        turned_ref[...] = x_ref[0].T
+
+    for z in range(chips):
+        at = pl.multiple_of((2 * z + core_ref[0]) * depth, depth)
+        result = dot(turned_ref[pl.ds(at, depth)], y_ref[0], 1, 1)
+        if given:
+            result = result + refs[0][0, z, 0].astype(f32)
+        o_ref[0, z, 0] = result.astype(bf16)
+
+
+def whole_grad(core, groups, lefts, rights, earlier):
+    size = lax.axis_size("mp")
+    n, frames, width = lefts.shape
+    local = rights.shape[1] // size
+    chips = groups // 2
+    depth = width // groups
+    out = pl.BlockSpec((1, chips, 1, depth, local), lambda w, m: (m, 0, w, 0, 0))
+    return pl.pallas_call(
+        functools.partial(whole_grad_kernel, chips, len(earlier)),
+        grid=(n, size),
+        in_specs=[
+            pl.BlockSpec(memory_space=pltpu.SMEM),
+            pl.BlockSpec((1, frames, width), lambda w, m: (w, 0, 0)),
+            pl.BlockSpec((1, local, frames), lambda w, m: (w, m, 0)),
+        ]
+        + [out] * len(earlier),
+        out_specs=out,
+        out_shape=shape_of((size, chips, n, depth, local), bf16),
+        scratch_shapes=[pltpu.VMEM((width, frames), bf16)],
+        compiler_params=params(),
+        cost_estimate=pl.CostEstimate(
+            flops=n * frames * width * local * size,
+            bytes_accessed=2 * n * (frames * width + 2 * width * local * size),
+            transcendentals=0,
+        ),
+        name="whole_grad",
+    )(core, lefts, rights, *earlier)
 
 
 def turning(rows):
@@ -462,14 +619,6 @@
     rates = jnp.exp(jnp.arange(HALF).astype(f32) * (-2.0 * math.log(10000.0) / HEAD_DIM))
     angles = rates[:, None] * places[None, :]
     return (jnp.cos(angles), jnp.sin(angles))
-
-
-def turn(values, cosine, sine):
-    pairs = values.reshape(-1, 2, HALF, values.shape[-1])
-    upper, lower = pairs[:, 0], pairs[:, 1]
-    return jnp.stack([upper * cosine - lower * sine, lower * cosine + upper * sine], axis=1).reshape(
-        values.shape
-    )
 
 
 def row_blocks(values, count):
@@ -509,59 +658,99 @@
     groups = lax.axis_size("dp")
     count, rows, width = frames_in.shape
     clips = range(count)
-    last = count - 1
     local = w_query.shape[1]
+    here = lax.axis_index("mp")
+    there = lax.axis_index("dp")
+    core = there & 1
+    chain = Chain()
+    hold, mark, arrive = chain.hold, chain.mark, chain.arrive
 
     def joined(parts, axis):
         return jnp.concatenate(parts, axis=axis)
 
-    resid = [frames_in[b].astype(f32) for b in clips]
-    ones = [norm_forward(resid[b], gain_one, shift_one) for b in clips]
-    whole_one = []
-    held = ()
+    resid, ones, low = [], [], []
     for b in clips:
-        pieces, held = spread(after(ones[b][0].astype(bf16), *held))
-        whole_one.append(joined(pieces, 0))
+        resid.append(hold(frames_in[b]).astype(f32))
+        ones.append(norm_forward(resid[b], gain_one, shift_one))
+        low.append(ones[b][0].astype(bf16))
+        mark(low[b])
         if b == 0:
-            seen = held
-    c_query_wide, c_query_all = whole_columns(c_query)
-    c_out_side, c_query_side = after((c_out.T, c_query_all), *seen)
-    c_out_wide, c_out_all = whole_columns(c_out_side)
-    out_all = whole_rows(after(w_out, whole_one[0]))
-
-    memory = joined([c_key, c_value], 1)
+            spread_one = [Spread(low[0])]
+
+    depth = width // groups
+    query_part = lax.dynamic_slice_in_dim(hold(c_query), there * depth, depth, 0)
+    out_part = lax.dynamic_slice_in_dim(hold(c_out), there * depth, depth, 1).T
+    side = jnp.stack([query_part, out_part])
+    side = [side] + [swap(side, "mp", k) for k in range(1, size)]
+    w_turned = joined([hold(w_query).T, w_key.T, w_value.T], 0)
+    cosine, sine = turning(rows)
+    mark(w_turned)
+    memory = joined([hold(c_key), c_value], 1)
     memory = jnp.stack([dot(memory, prompt[b], 0, 1).astype(bf16) for b in clips])
-    memory = after(memory, *held)
-    memory = jnp.stack([memory] + [swap(memory, "mp", k) for k in range(1, size)], axis=1)
+    mark(memory)
+    for b in clips:
+        spread_one[b].first = arrive(spread_one[b].first)
+        spread_one[b].second_step()
+        if b + 1 < count:
+            spread_one.append(Spread(hold(low[b + 1])))
+        if b == 0:
+            side = arrive(side)
+            query_wide = joined([part[0] for part in side], 1)
+            out_wide = joined([part[1] for part in side], 1)
+            mark(query_wide, out_wide)
+            c_query_all = lax.all_gather(query_wide, "dp", axis=0, tiled=True)
+            out_wide = after(out_wide, c_query_all)
+            c_out_all = lax.all_gather(out_wide, "dp", axis=0, tiled=True)
+            picked = jnp.take(hold(table), tsteps, axis=0)
+            prefix_normed, prefix_normal, prefix_scale = norm_forward(picked, gain_one, shift_one)
+            prefix_low = prefix_normed.astype(bf16)
+            front = dot(w_turned[local:], prefix_low, 1, 1).astype(bf16)
+            mark(front)
+            spread_one[0].last = arrive(spread_one[0].last)
+            half = lax.dynamic_slice_in_dim(hold(w_out), core * (local // 2), local // 2, 0)
+            spread_out = Spread(half)
+    front_keys = [front[:local, b : b + 1] for b in clips]
+    front_values = [front[local:, b : b + 1] for b in clips]
+
+    turned, mixed_part, logsum, mixed = [], [], [], []
+    frames_one = ()
+    for b in clips:
+        if b:
+            spread_one[b].last = arrive(spread_one[b].last)
+        pieces = hold(spread_one[b].pieces())
+        out, frames_one = project(b, count, pieces, w_turned, cosine, sine, list(frames_one))
+        frames_one = (frames_one,)
+        turned.append(out)
+        mark(out)
+        if b == 0:
+            spread_out.first = arrive(spread_out.first)
+            spread_out.second_step()
+        out, sums = self_forward(hold(turned[b]), front_keys[b], front_values[b])
+        mixed_part.append(out)
+        logsum.append(sums)
+        mark(out)
+        mixed.append(trade(jnp.split(out, size, axis=1)))
+        if b == 0:
+            memory = hold(memory)
+            memory = [memory] + [swap(memory, "mp", k) for k in range(1, size)]
+            spread_out.last = arrive(spread_out.last)
+            got = spread_out.pieces()[1:]
+            got = joined(got, 0).reshape(size - 1, local // 2, width)
+            other = swap(got, "dp", 1)
+    frames_one = frames_one[0]
+    down_in = lax.all_gather(hold(cotangent), "mp", axis=1, tiled=True)
+    other = arrive(other)
+    rest = joined([jnp.where(core == 0, got, other), jnp.where(core == 0, other, got)], 1)
+    out_all = joined([w_out, rest.reshape(-1, width)], 0)
+    memory = jnp.stack(memory, axis=1)
     cross_keys = [memory[b, :, :local].reshape(size * local, -1) for b in clips]
     cross_values = [memory[b, :, local:].reshape(size * local, -1) for b in clips]
-
-    picked = jnp.take(table, tsteps, axis=0)
-    prefix_normed, prefix_normal, prefix_scale = norm_forward(picked, gain_one, shift_one)
-    prefix_low = prefix_normed.astype(bf16)
-    cosine, sine = turning(rows)
-    w_self = joined([w_query, w_key, w_value], 1)
-    front = dot(w_self[:, local:], prefix_low, 0, 1).astype(bf16)
-    front_keys = [front[:local, b : b + 1] for b in clips]
-    front_values = [front[local:, b : b + 1] for b in clips]
-
-    turned, mixed_part, logsum, mixed = [], [], [], []
+    mark(out_all)
+
+    first, twos, normed_two, cross_query, cross_sums, cross_mixed = [], [], [], [], [], []
+    second, threes, low = [], [], []
     for b in clips:
-        raw = dot(w_self, whole_one[b], 0, 1)
-        queries = (turn(raw[:local], cosine, sine) * FACTOR).astype(bf16)
-        keys = turn(raw[local : 2 * local], cosine, sine).astype(bf16)
-        turned.append(joined([queries, keys, raw[2 * local :].astype(bf16)], 0))
-        out, sums = self_forward(turned[b], front_keys[b], front_values[b])
-        mixed_part.append(out)
-        logsum.append(sums)
-        mixed.append(joined(trade(jnp.split(out, size, axis=1)), 0))
-
-    first, twos, normed_two, cross_query, cross_sums, cross_mixed = [], [], [], [], [], []
-    second, threes, whole_three, down_in = [], [], [], []
-    held = (whole_one[last],)
-    for b in clips:
-        pieces, held = spread(after(cotangent[b], *held))
-        down_in.append(joined(pieces, 0))
+        mixed[b] = joined(hold(mixed[b]), 0)
         first.append(resid[b] + dot(mixed[b], out_all, 0, 0))
         twos.append(norm_forward(first[b], gain_two, shift_two))
         normed_two.append(twos[b][0].astype(bf16))
@@ -571,36 +760,53 @@
         )
         cross_mixed.append(out)
         cross_sums.append(sums)
-        second.append(first[b] + dot(out, c_out_all, 0, 1))
+        mark(out)
+    spread_three = []
+    for b in clips:
+        second.append(first[b] + dot(hold(cross_mixed[b]), c_out_all, 0, 1))
         threes.append(norm_forward(second[b], gain_three, shift_three))
-        pieces, held = spread(threes[b][0].astype(bf16))
-        whole_three.append(joined(pieces, 0))
-
-    hidden, grad_gate, grad_upper, back_three, branch = [], [], [], [], []
-    done = ()
+        low.append(threes[b][0].astype(bf16))
+        mark(low[b])
+        if b == 0:
+            spread_three.append(Spread(low[b]))
+
+    order = jnp.stack([here ^ k for k in range(size)]).astype(jnp.int32)
+    back_pieces, back_three = [], []
+    parts = ()
     for b in clips:
-        parts = glu(after(whole_three[b], *done), down_in[b], w_gate, w_up, w_down)
-        hidden.append(parts[0])
-        grad_gate.append(parts[1])
-        grad_upper.append(parts[2])
-        back = glu_back(grad_gate[b], grad_upper[b], w_gate, w_up)
-        back_three.append(settle(row_blocks(back, size)))
-        if b < last:
-            branch.append(dot(after(hidden[b], back), w_down, 1, 0).astype(bf16))
-            done = (branch[b],)
-        else:
-            done = (back,)
-
-    hidden_all = joined(hidden, 0)
-    three_all = joined(whole_three, 0)
-    raw_w_down = dot(after(hidden_all, *done), joined(down_in, 0), 0, 0).astype(bf16)
-    grad_w_down = sum_over_clips(raw_w_down, 1)
-    done = (raw_w_down,)
+        if b + 1 < count:
+            spread_three[b].first = arrive(spread_three[b].first)
+            spread_three[b].second_step()
+            spread_three.append(Spread(hold(low[b + 1])))
+            spread_three[b].last = arrive(spread_three[b].last)
+            spread_three[b + 1].first = arrive(spread_three[b + 1].first)
+            spread_three[b + 1].second_step()
+        pieces = hold(spread_three[b].pieces())
+        parts = glu(b, order, pieces, down_in, w_gate, w_up, w_down, list(parts))
+        mark(parts[1])
+        if b:
+            came = arrive(came)
+            back_three.append(settle_last(back_pieces[b - 1], came))
+        grad_gate, grad_upper = hold((parts[1], parts[2]))
+        back_pieces.append(glu_back(b, grad_gate, grad_upper, w_gate, w_up))
+        mark(back_pieces[b][0])
+        came = settle_first(back_pieces[b])
+        if b + 1 < count:
+            spread_three[b + 1].last = arrive(spread_three[b + 1].last)
+
+    def flat(values):
+        return values.reshape(-1, values.shape[-1])
+
+    hidden, grad_gate, grad_upper, frames_three = parts
+    raw_w_down = dot(flat(hold(down_in)), flat(hidden), 0, 0).astype(bf16)
+    grad_w_down = sum_over_clips(raw_w_down, 0)
+    mark(raw_w_down)
+    back_three.append(settle_last(back_pieces[-1], arrive(came)))
 
     grad_two, grad_one, cross_in, self_in = [], [], [], []
     grad_cross_query, grad_memory, grad_mixed, back_two = [], [], [], []
     for b in clips:
-        back_three[b] = total(after(back_three[b], *done))
+        back_three[b] = total(hold(back_three[b]))
         cot = cotangent[b].astype(f32)
         grad_two.append(cot + norm_backward(back_three[b], threes[b][1], threes[b][2], gain_three))
         cross_in.append(grad_two[b].astype(bf16))
@@ -626,22 +832,27 @@
         )
         self_in.append(grad_one[b].astype(bf16))
         grads = dot(out_all, self_in[b], 1, 1).astype(bf16)
-        grad_mixed.append(joined(trade(row_blocks(grads, size)), 1))
-        done = (grads,)
-
-    branch.append(dot(after(hidden[last], *done), w_down, 1, 0).astype(bf16))
-    raw_w_gate = dot(after(three_all, branch[last]), joined(grad_gate, 0), 0, 0).astype(bf16)
-    grad_w_gate = sum_over_clips(raw_w_gate, 0)
-    done = (raw_w_gate,)
-    output = [
-        second[b] + total(settle(row_blocks(branch[b], size))) for b in clips
-    ]
-
+        mark(grads)
+        grad_mixed.append(trade(row_blocks(grads, size)))
+        if b == 0:
+            raw_w_gate = dot(flat(hold(frames_three)), flat(grad_gate), 0, 0).astype(bf16)
+            grad_w_gate = sum_over_clips(raw_w_gate, 0)
+            mark(raw_w_gate)
+
+    branch = dot(flat(hold(hidden)), w_down, 1, 0).astype(bf16)
+    mark(branch)
+    branch = lax.psum_scatter(
+        branch.reshape(count, size * rows, width), "mp", scatter_dimension=1, tiled=True
+    )
+    grad_memory = jnp.stack(grad_memory)
+    grad_memory = trade([grad_memory[:, k] for k in range(size)])
+
+    w_self = w_turned.T
     grad_self, grad_front, back_one = [], [], []
     for b in clips:
         grads, grad_front_key, grad_front_value = self_backward(
             turned[b],
-            after(grad_mixed[b], *done),
+            joined(hold(grad_mixed[b]), 1),
             mixed_part[b],
             logsum[b],
             front_keys[b],
@@ -651,41 +862,48 @@
         )
         grad_self.append(grads.reshape(3 * local, -1))
         grad_front.append(joined([grad_front_key, grad_front_value], 0))
-        back = dot(grad_self[b], w_self, 0, 1).astype(bf16)
-        done = (back,)
-        back_one.append(total(settle(row_blocks(back, size))))
-    grad_frames = [
-        grad_one[b] + norm_backward(back_one[b], ones[b][1], ones[b][2], gain_one) for b in clips
-    ]
+        mark(grads)
+        if b:
+            came = arrive(came)
+            back_one.append(settle_last(pieces, came))
+        pieces = cut(dot(hold(grad_self[b]), w_turned, 0, 0).astype(bf16))
+        mark(*pieces)
+        came = settle_first(pieces)
+        if b == 0:
+            raw_w_up = dot(flat(hold(frames_three)), flat(grad_upper), 0, 0).astype(bf16)
+            grad_w_up = sum_over_clips(raw_w_up, 0)
+            mark(raw_w_up)
 
     grad_front = joined(grad_front, 1)
-    turned_grads = after(joined(grad_self, 1), *done)
-    raw_w_self = dot(joined(whole_one, 0), turned_grads, 0, 1)
-    raw_w_front = dot(prefix_low, grad_front, 0, 1)
-    raw_w_self = joined([raw_w_self[:, :local], raw_w_self[:, local:] + raw_w_front], 1)
+    turned_grads = joined(hold(grad_self), 1)
+    raw_w_self = dot(flat(frames_one), turned_grads, 0, 1)
+    filled = joined([jnp.zeros((local, count), bf16), grad_front], 0)
+    raw_w_self = raw_w_self + dot(prefix_low, filled, 0, 1)
     low_w_self = raw_w_self.astype(bf16).reshape(groups, -1, 3 * local)
-    grad_w_self = chips_sum(plus(*core_half(low_w_self)))
-
-    raw_w_up = dot(after(three_all, raw_w_self), joined(grad_upper, 0), 0, 0).astype(bf16)
-    grad_w_up = sum_over_clips(raw_w_up, 0)
-
-    cross_all = after(joined(cross_in, 0), raw_w_up)
-    raws = [
-        dot(joined(normed_two, 0), joined(grad_cross_query, 1), 0, 1),
-        dot(cross_all, joined(cross_mixed, 1), 0, 1),
-        dot(joined(self_in, 0), joined(mixed, 1), 0, 1),
-    ]
-    raws = joined([raw.astype(bf16).reshape(groups, -1, size, local) for raw in raws], 3)
-    mine, other = core_half(raws)
-    raws = [plus(mine[:, :, k], other[:, :, k]).reshape(-1, 3 * local) for k in range(size)]
-    raws = total(settle(raws)).astype(bf16).reshape(groups // 2, -1, 3 * local)
-    raws = chips_sum(raws)
-
-    grad_memory = jnp.stack(grad_memory)
-    grad_memory = total(trade([grad_memory[:, k] for k in range(size)])).astype(bf16)
+    mark(low_w_self)
+    mine, other = core_half(low_w_self)
+    back_one.append(settle_last(pieces, arrive(came)))
+
+    lefts = jnp.stack([joined(hold(part), 0) for part in (normed_two, cross_in, self_in)])
+    rights = jnp.stack([joined(part, 1) for part in (grad_cross_query, cross_mixed, mixed)])
+    other_raws = whole_grad(jnp.stack([1 - core]), groups, lefts, rights, [])
+    mark(other_raws)
+    other_raws = swap(other_raws, "dp", 1)
+    low_w_self = plus(mine, arrive(other))
+    mark(low_w_self)
+    grad_w_self = chips_sum(low_w_self)
+
+    grad_memory = total(arrive(grad_memory)).astype(bf16)
     grad_memory = joined([grad_memory[b] for b in clips], 1)
-    grad_c_memory = dot(prompt.reshape(-1, prompt.shape[-1]), grad_memory, 0, 1)
+    grad_c_memory = dot(prompt.reshape(-1, prompt.shape[-1]), grad_memory, 0, 1).astype(bf16)
+    mark(grad_c_memory)
     grad_c_memory = sum_over_clips(grad_c_memory, 0)
+
+    raws = whole_grad(jnp.stack([core]), groups, lefts, rights, [arrive(other_raws)])
+    mark(raws)
+    pieces = [raws[k].reshape(-1, local) for k in range(size)]
+    pieces = cut(joined(pieces, 0))
+    came = settle_first(pieces)
 
     small = []
     wide_w_self = w_self.astype(f32)
@@ -700,19 +918,30 @@
         small.append(sum(jnp.sum(back[b] * kept[b][1], axis=0) for b in clips))
         small.append(sum(jnp.sum(back[b], axis=0) for b in clips))
 
-    me = lax.axis_index("dp")
-    steps = jnp.where(lax.axis_index("mp") == 0, tsteps, 0).astype(f32)
-    steps = lax.dynamic_update_slice(jnp.zeros((width,), f32), steps, (me * count,))
+    steps = jnp.where(here == 0, tsteps, 0).astype(f32)
+    steps = lax.dynamic_update_slice(jnp.zeros((width,), f32), steps, (there * count,))
     small.append(steps)
 
-    back_prefix = dot(grad_front, w_self[:, local:], 0, 1)
+    back_prefix = dot(grad_front, w_turned[local:], 0, 0)
     grad_picked = norm_backward(back_prefix, prefix_normal, prefix_scale, gain_one)
-    spots = jnp.arange(groups)[:, None, None] == me
+    spots = jnp.arange(groups)[:, None, None] == there
     spots = jnp.where(spots, grad_picked[None], 0.0).reshape(groups * count, width)
-    small = all_sum(joined([jnp.stack(small), spots], 0))
+    small = joined([jnp.stack(small), spots], 0)
+    mark(small)
+    raws = total(settle_last(pieces, arrive(came)))
+    raws = raws.astype(bf16).reshape(groups // 2, -1, local)
+    mark(raws)
+    raws = chips_sum(raws).reshape(3, -1, local)
+    small = all_sum(small)
     all_steps = small[6, : groups * count]
     matches = jnp.arange(table.shape[0])[:, None].astype(f32) == all_steps[None, :]
     grad_table = jnp.dot(matches.astype(f32), small[7:], precision=lax.Precision.HIGHEST)
+
+    back_one = [total(terms) for terms in back_one]
+    grad_frames = [
+        grad_one[b] + norm_backward(back_one[b], ones[b][1], ones[b][2], gain_one) for b in clips
+    ]
+    output = [second[b] + branch[b].astype(f32) for b in clips]
 
     def wide(value):
         return value.astype(f32)
@@ -730,14 +959,14 @@
         grad_w_self[:, :local],
         grad_w_self[:, local : 2 * local],
         grad_w_self[:, 2 * local :],
-        raws[:, 2 * local :].T,
-        raws[:, :local],
+        raws[2].T,
+        raws[0],
         wide(grad_c_memory[:, :local]),
         wide(grad_c_memory[:, local:]),
-        raws[:, local : 2 * local].T,
+        raws[1].T,
         wide(grad_w_gate),
         wide(grad_w_up),
-        wide(grad_w_down),
+        wide(grad_w_down.T),
     )
 
 

time: 989 us -> 1040 us (1.052)
  waiting for transfers between devices: 293 us -> 395 us
  Pallas kernels: 145 us -> 194 us
  local copies, waits for them, and re-layouts: 165 us -> 118 us
  matrix products: 151 us -> 115 us
  starting transfers between devices: 118 us -> 92.8 us
    ppermute x94 -> x75, waiting for transfers between devices: 293 us -> 173 us  [swap(): lax.ppermute(values, axis, [(i, i ^ k) for i in range(lax.axis_size(axis))])]
    reduce_scatter x2 -> x3, waiting for transfers between devices: 0.01 us -> 103 us  [sum_over_clips(): lax.psum_scatter(values.astype(bf16), 'dp', scatter_dimension=axis, tiled...]
    reduce_scatter x0 -> x1, waiting for transfers between devices: none -> 66.6 us  [shards(): lax.psum_scatter(branch.reshape(count, size * rows, width), 'mp', scatter...]
    all_gather x2 -> x3, waiting for transfers between devices: 0.01 us -> 50.2 us  [the longest x1 50.1 us: shards(): c_query_all = lax.all_gather(query_wide, 'dp', axis=0, tiled=True)]
    pallas_call x4 -> x8, Pallas kernels: 64.1 us -> 113 us  [the longest x2 42.5 us: glu(): pl.pallas_call(functools.partial(glu_kernel, size, len(pieces)), grid=(hi...]
    concatenate x11 -> x5, local copies, waits for them, and re-layouts: 39.5 us -> 1.5 us  [joined(): return jnp.concatenate(parts, axis=axis)]
    dot_general x31 -> x25, matrix products: 146 us -> 109 us  [dot(): lax.dot_general(left, right, (((left_axis,), (right_axis,)), ((), ())), p...]
    ppermute x94 -> x75, starting transfers between devices: 118 us -> 92.5 us  [swap(): lax.ppermute(values, axis, [(i, i ^ k) for i in range(lax.axis_size(axis))])]
  transfers between devices with their start and end apart: 100 -> 83, of which waited for: 40 -> 25; matrix products, arithmetic and copies ran while one was open for 36% -> 24% of each run, Pallas kernels for 14% -> 15%
where the time goes in v3:
time: 1040 us; the launch traced here: 1030 us
  waiting for transfers between devices  395 us (38%)
  Pallas kernels  194 us (19%)
  local copies, waits for them, and re-layouts  118 us (11%)
  matrix products  115 us (11%)
  other arithmetic  95 us (9%)
  starting transfers between devices  92.8 us (9%)
  between operations  17.9 us (2%)
    ppermute x75, waiting for transfers between devices, swap(): lax.ppermute(values, axis, [(i, i ^ k) for i in range(lax.axis_size(axis))])  173 us
    dot_general x25, matrix products, dot(): lax.dot_general(left, right, (((left_axis,), (right_axis,)), ((), ())), p...  109 us
    reduce_scatter x3, waiting for transfers between devices, sum_over_clips(): lax.psum_scatter(values.astype(bf16), 'dp', scatter_dimension=axis, tiled...  103 us
    ppermute x75, starting transfers between devices, swap(): lax.ppermute(values, axis, [(i, i ^ k) for i in range(lax.axis_size(axis))])  92.5 us
    reduce_scatter x1, waiting for transfers between devices, shards(): lax.psum_scatter(branch.reshape(count, size * rows, width), 'mp', scatter...  66.6 us
    unnamed x516, local copies, waits for them, and re-layouts  64.9 us
    all_gather x1, waiting for transfers between devices, shards(): c_query_all = lax.all_gather(query_wide, 'dp', axis=0, tiled=True)  50.1 us
    pallas_call x2, Pallas kernels, glu(): pl.pallas_call(functools.partial(glu_kernel, size, len(pieces)), grid=(hi...  42.5 us
  transfers between devices with their start and end apart: 83, of which 25 were waited for; matrix products, arithmetic and copies ran while one was open for 24% of the time, Pallas kernels for 15%

profile of v3, /device:TPU:0, one launch (start us, length us, event | category | flops | bytes accessed | tf_op | source)
XLA Modules:
  0.0 1028.0 jit_solution(12121409630046288453)
XLA Ops:
  36.0 4.2 collective-permute-done.4
  40.2 7.0 collective-permute-done.5
  53.8 50.1 %all-gather.4.cloned.1.call-done = bf16[1536,1536]{1,0:T(8,128)(2,1)} async-done(((bf16[192,1536]{1,0:T(8,128)(2,1)}), bf16[1536,1536]{1,0:T(8,128)(2,1)}) %all-gather.4.cloned.1.call-update) | async-done | bytes 4718608 | tf_op jit(solution)/shard_map/all_gather | solution.py:701
  116.0 4.0 gather_fusion
  124.3 17.2 %collective-permute-done.2.refs_3_ = bf16[128,1536]{1,0:T(8,128)(2,1)} collective-permute-done((bf16[128,1536]{1,0:T(8,128)(2,1)}, bf16[128,1536]{1,0:T(8,128)(2,1)}, u32[]{:S(2)}, u32[]{:S(2)}) %collective-permute-start.2) | collective-permute-done | bytes 393248 | tf_op jit(solution)/shard_map/ppermute | solution.py:48
  145.0 8.0 project.2
  157.2 10.5 %self_forward.2 = (bf16[384,1024]{1,0:T(8,128)(2,1)S(1)}, f32[6,1,1024]{2,1,0:T(1,128)S(1)}) custom-call(bf16[1152,1024]{1,0:T(8,128)(2,1)S(1)} %get-tuple-element.205.q_ref.k_ref.v_ref, bf16[1152,1024]{1,0:T(8,128)(2,1)S(1)} %get-tuple-element.205.q_ref.k_ref.v_ref, bf16[1152,1024]{1,0:T(8,128)(2,1)S(1)} %get-tuple-element.205.q_ref.k_ref.v_ref, ...), custom_call_target="tpu_custom_call" | custom-call | flops 6442450944 | bytes 3145728 | tf_op jit(solution)/shard_map/self_forward/pallas_call | solution.py:286
  183.8 3.9 collective-permute-done.14
  197.6 7.5 project.3
  205.1 10.5 %self_forward.3 = (bf16[384,1024]{1,0:T(8,128)(2,1)S(1)}, f32[6,1,1024]{2,1,0:T(1,128)S(1)}) custom-call(bf16[1152,1024]{1,0:T(8,128)(2,1)S(1)} %get-tuple-element.218.q_ref.k_ref.v_ref, bf16[1152,1024]{1,0:T(8,128)(2,1)S(1)} %get-tuple-element.218.q_ref.k_ref.v_ref, bf16[1152,1024]{1,0:T(8,128)(2,1)S(1)} %get-tuple-element.218.q_ref.k_ref.v_ref, ...), custom_call_target="tpu_custom_call" | custom-call | flops 6442450944 | bytes 3145728 | tf_op jit(solution)/shard_map/self_forward/pallas_call | solution.py:286
  234.4 6.3 cross_forward.2
  246.2 6.7 cross_forward.3
  254.4 4.7 fusion.96
  265.8 30.9 %collective-permute-done.25.refs_1_ = bf16[256,1536]{1,0:T(8,128)(2,1)S(1)} collective-permute-done((bf16[256,1536]{1,0:T(8,128)(2,1)S(1)}, bf16[256,1536]{1,0:T(8,128)(2,1)S(1)}, u32[]{:S(2)}, u32[]{:S(2)}) %collective-permute-start.25) | collective-permute-done | bytes 786464 | tf_op jit(solution)/shard_map/ppermute | solution.py:48
  306.6 22.1 %collective-permute-done.29.refs_3_ = bf16[128,1536]{1,0:T(8,128)(2,1)S(1)} collective-permute-done((bf16[128,1536]{1,0:T(8,128)(2,1)S(1)}, bf16[128,1536]{1,0:T(8,128)(2,1)S(1)}, u32[]{:S(2)}, u32[]{:S(2)}) %collective-permute-start.29) | collective-permute-done | bytes 393248 | tf_op jit(solution)/shard_map/ppermute | solution.py:48
  343.9 21.0 %glu.2 = (bf16[2,1024,1536]{2,1,0:T(8,128)(2,1)}, bf16[2,1024,1536]{2,1,0:T(8,128)(2,1)}, bf16[2,1024,1536]{2,1,0:T(8,128)(2,1)}, bf16[2,1024,1536]{2,1,0:T(8,128)(2,1)}) custom-call(s32[4]{0:T(128)S(1)} %pad_add_fusion.1.n_ref, bf16[1536,1536]{1,0:T(8,128)(2,1)S(1)} %copy-done.69, bf16[1536,1536]{1,0:T(8,128)(2,1)S(1)} %copy-done.71, ...), custom_call_target="tpu_custom_call" | custom-call | flops 14495514624 | bytes 33030144 | tf_op jit(solution)/shard_map/glu/pallas_call | solution.py:506
  371.6 14.2 %glu_back.2 = (bf16[256,1536]{1,0:T(8,128)(2,1)S(1)}, bf16[256,1536]{1,0:T(8,128)(2,1)S(1)}, bf16[256,1536]{1,0:T(8,128)(2,1)S(1)}, bf16[128,1536]{1,0:T(8,128)(2,1)S(1)}, bf16[128,1536]{1,0:T(8,128)(2,1)S(1)}) custom-call(bf16[2,1024,1536]{2,1,0:T(8,128)(2,1)} %get-tuple-element.250.dg_ref.refs_6_, ...), custom_call_target="tpu_custom_call" | custom-call | flops 9663676416 | bytes 18874368 | tf_op jit(solution)/shard_map/glu_back/pallas_call | solution.py:553
  388.7 21.6 %glu.3 = (bf16[2,1024,1536]{2,1,0:T(8,128)(2,1)}, bf16[2,1024,1536]{2,1,0:T(8,128)(2,1)}, bf16[2,1024,1536]{2,1,0:T(8,128)(2,1)}, bf16[2,1024,1536]{2,1,0:T(8,128)(2,1)}) custom-call(s32[4]{0:T(128)S(1)} %pad_add_fusion.1.n_ref, bf16[1536,1536]{1,0:T(8,128)(2,1)S(1)} %copy-done.70, ...), custom_call_target="tpu_custom_call", output_to_operand_aliasing={{0}: (10, {}), {1}: (11, {}), {2}: (12, {}), {3}: (13, {})} | custom-call | flops 14495514624 | bytes 33030144 | tf_op jit(solution)/shard_map/glu/pallas_call | solution.py:506
  416.8 14.9 %glu_back.3 = (bf16[256,1536]{1,0:T(8,128)(2,1)S(1)}, bf16[256,1536]{1,0:T(8,128)(2,1)S(1)}, bf16[256,1536]{1,0:T(8,128)(2,1)S(1)}, bf16[128,1536]{1,0:T(8,128)(2,1)}, bf16[128,1536]{1,0:T(8,128)(2,1)}) custom-call(bf16[2,1024,1536]{2,1,0:T(8,128)(2,1)} %get-tuple-element.269.dg_ref, bf16[2,1024,1536]{2,1,0:T(8,128)(2,1)} %get-tuple-element.270.du_ref, ...), custom_call_target="tpu_custom_call" | custom-call | flops 9663676416 | bytes 18874368 | tf_op jit(solution)/shard_map/glu_back/pallas_call | solution.py:553
  436.4 15.5 %bitcast_convert_fusion.2 = bf16[1536,1536]{1,0:T(8,128)(2,1)} fusion(bf16[2,1024,1536]{2,1,0:T(8,128)(2,1)} %all-gather.8.cloned.1.call-done.c_ref, bf16[2,1024,1536]{2,1,0:T(8,128)(2,1)} %get-tuple-element.293), kind=kOutput, calls=%fused_computation.4 | convolution fusion | flops 9666035712 | bytes 17301504 | tf_op jit(solution)/shard_map/dot_general | solution.py:22
  465.8 4.1 convolution_convert_fusion.6.g_ref
  470.0 6.7 cross_backward.2
  486.6 11.6 %bitcast_convert_fusion.1 = bf16[1536,1536]{1,0:T(8,128)(2,1)} fusion(bf16[2,1024,1536]{2,1,0:T(8,128)(2,1)S(1)} %bitcast.329, bf16[2,1024,1536]{2,1,0:T(8,128)(2,1)S(1)} %bitcast.325), kind=kOutput, calls=%fused_computation.3 | convolution fusion | flops 9666035712 | bytes 17301504 | tf_op jit(solution)/shard_map/dot_general | solution.py:22
  509.5 4.1 convolution_convert_fusion.4.g_ref
  513.7 6.9 cross_backward.3
  531.9 12.2 %convolution_convert_fusion = bf16[2048,1536]{1,0:T(8,128)(2,1)} fusion(bf16[2048,1536]{1,0:T(8,128)(2,1)S(1)} %bitcast.323, bf16[1536,1536]{1,0:T(8,128)(2,1)S(1)} %bitcast.311), kind=kOutput, calls=%fused_computation.6 | convolution fusion | flops 9666822144 | bytes 17301504 | tf_op jit(solution)/shard_map/dot_general | solution.py:22
  545.6 16.9 %self_backward.2 = (bf16[3,384,1024]{2,1,0:T(8,128)(2,1)S(1)}, bf16[384,1]{1,0:T(8,128)(2,1)S(1)}, bf16[384,1]{1,0:T(8,128)(2,1)S(1)}) custom-call(bf16[1152,1024]{1,0:T(8,128)(2,1)S(1)} %copy-done.86, bf16[1152,1024]{1,0:T(8,128)(2,1)S(1)} %copy-done.86, bf16[1152,1024]{1,0:T(8,128)(2,1)S(1)} %copy-done.86, bf16[384,1024]{1,0:T(8,128)(2,1)S(1)} %pad_maximum_fusion.20.g_ref, ...), custom_call_target="tpu_custom_call" | custom-call | flops 16106127360 | bytes 7864320 | tf_op jit(solution)/shard_map/self_backward/pallas_call | solution.py:310
  562.6 4.7 convolution_convert_fusion.2
  571.4 14.0 %bitcast_convert_fusion = bf16[1536,1536]{1,0:T(8,128)(2,1)} fusion(bf16[2,1024,1536]{2,1,0:T(8,128)(2,1)} %get-tuple-element.301, bf16[2,1024,1536]{2,1,0:T(8,128)(2,1)S(1)} %bitcast.327), kind=kOutput, calls=%fused_computation.2 | convolution fusion | flops 9666035712 | bytes 17301504 | tf_op jit(solution)/shard_map/dot_general | solution.py:22
  599.2 16.9 %self_backward.3 = (bf16[3,384,1024]{2,1,0:T(8,128)(2,1)S(1)}, bf16[384,1]{1,0:T(8,128)(2,1)S(1)}, bf16[384,1]{1,0:T(8,128)(2,1)S(1)}) custom-call(bf16[1152,1024]{1,0:T(8,128)(2,1)S(1)} %copy-done.80, bf16[1152,1024]{1,0:T(8,128)(2,1)S(1)} %copy-done.80, bf16[1152,1024]{1,0:T(8,128)(2,1)S(1)} %copy-done.80, bf16[384,1024]{1,0:T(8,128)(2,1)S(1)} %pad_maximum_fusion.21.g_ref, ...), custom_call_target="tpu_custom_call" | custom-call | flops 16106127360 | bytes 7864320 | tf_op jit(solution)/shard_map/self_backward/pallas_call | solution.py:310
  620.9 6.5 convolution_convert_fusion.1
  634.9 7.5 fusion.98
  642.5 3.6 fusion.1
  646.1 4.4 copy.95
  660.0 11.1 %whole_grad.2 = bf16[4,4,3,192,384]{4,3,2,1,0:T(8,128)(2,1)} custom-call(s32[1]{0:T(128)} %bitcast.60.core_ref, bf16[3,512,1536]{2,1,0:T(8,128)(2,1)S(1)} %pad_maximum_fusion.1.x_ref, bf16[3,1536,512]{2,1,0:T(8,128)(2,1)S(1)} %pad_maximum_fusion.2.y_ref), custom_call_target="tpu_custom_call" | custom-call | flops 3623878656 | bytes 33030144 | tf_op jit(solution)/shard_map/whole_grad/pallas_call | solution.py:592
  690.9 4.6 collective-permute-done.56
  699.9 6.5 collective-permute-done.58
  708.3 8.3 collective-permute-done.59
  718.1 5.3 fusion.47
  723.3 12.5 %collective-permute-done.54 = bf16[256,1536]{1,0:T(8,128)(2,1)S(1)} collective-permute-done((bf16[256,1536]{1,0:T(8,128)(2,1)S(1)}, bf16[256,1536]{1,0:T(8,128)(2,1)S(1)}, u32[]{:S(2)}, u32[]{:S(2)}) %collective-permute-start.54) | collective-permute-done | bytes 786464 | tf_op jit(solution)/shard_map/ppermute | solution.py:48
  737.4 14.6 %whole_grad.3 = bf16[4,4,3,192,384]{4,3,2,1,0:T(8,128)(2,1)} custom-call(s32[1]{0:T(128)} %bitcast.71.core_ref, bf16[3,512,1536]{2,1,0:T(8,128)(2,1)S(1)} %bitcast.269, bf16[3,1536,512]{2,1,0:T(8,128)(2,1)S(1)} %bitcast.267, bf16[4,4,3,192,384]{4,3,2,1,0:T(8,128)(2,1)} %collective-permute-done.64.refs_0_), custom_call_target="tpu_custom_call" | custom-call | flops 3623878656 | bytes 33030144 | tf_op jit(solution)/shard_map/whole_grad/pallas_call | solution.py:592
  761.7 14.2 %collective-permute-done.68 = bf16[1152,384]{1,0:T(8,128)(2,1)S(1)} collective-permute-done((bf16[1152,384]{1,0:T(8,128)(2,1)S(1)}, bf16[1152,384]{1,0:T(8,128)(2,1)S(1)}, u32[]{:S(2)}, u32[]{:S(2)}) %collective-permute-start.68) | collective-permute-done | bytes 884768 | tf_op jit(solution)/shard_map/ppermute | solution.py:48
  786.4 11.4 %collective-permute-done.62 = bf16[192,1152]{1,0:T(8,128)(2,1)S(1)} collective-permute-done((bf16[192,1152]{1,0:T(8,128)(2,1)S(1)}, bf16[192,1152]{1,0:T(8,128)(2,1)S(1)}, u32[]{:S(2)}, u32[]{:S(2)}) %collective-permute-start.62) | collective-permute-done | bytes 442400 | tf_op jit(solution)/shard_map/ppermute | solution.py:48
  801.7 15.1 %collective-permute-done.70 = bf16[2304,384]{1,0:T(8,128)(2,1)} collective-permute-done((bf16[2304,384]{1,0:T(8,128)(2,1)}, bf16[2304,384]{1,0:T(8,128)(2,1)}, u32[]{:S(2)}, u32[]{:S(2)}) %collective-permute-start.70) | collective-permute-done | bytes 1769504 | tf_op jit(solution)/shard_map/ppermute | solution.py:48
  823.5 12.1 %collective-permute-start.72 = (bf16[576,384]{1,0:T(8,128)(2,1)}, bf16[576,384]{1,0:T(8,128)(2,1)}, u32[]{:S(2)}, u32[]{:S(2)}) collective-permute-start(bf16[576,384]{1,0:T(8,128)(2,1)} %get-tuple-element.465), channel_id=1, source_target_pairs={{0,8},{4,12},{8,0},{12,4},{16,24},{20,28},{24,16},{28,20},{1,9},{5... | collective-permute-start | bytes 1327112 | tf_op jit(solution)/shard_map/ppermute | solution.py:48
  840.1 24.7 %reduce-scatter.10.cloned.1.call-done = bf16[192,1536]{1,0:T(8,128)(2,1)} async-done(((bf16[1536,1536]{1,0:T(8,128)(2,1)}), bf16[192,1536]{1,0:T(8,128)(2,1)}) %reduce-scatter.10.cloned.1.call-update) | async-done | bytes 589840 | tf_op jit(solution)/shard_map/reduce_scatter | solution.py:629
  867.0 78.3 %reduce-scatter.12.cloned.1.call-done = bf16[192,1536]{1,0:T(8,128)(2,1)} async-done(((bf16[1536,1536]{1,0:T(8,128)(2,1)}), bf16[192,1536]{1,0:T(8,128)(2,1)}) %reduce-scatter.12.cloned.1.call-update) | async-done | bytes 589840 | tf_op jit(solution)/shard_map/reduce_scatter | solution.py:629
  950.2 66.6 %reduce-scatter.8.cloned.1.call-done = bf16[2,256,1536]{2,1,0:T(8,128)(2,1)} async-done(((bf16[2,1024,1536]{2,1,0:T(8,128)(2,1)}), bf16[2,256,1536]{2,1,0:T(8,128)(2,1)}) %reduce-scatter.8.cloned.1.call-update) | async-done | bytes 1572880 | tf_op jit(solution)/shard_map/reduce_scatter | solution.py:844
  (892 shorter events, 323.9 us)
Async XLA Ops:
  7.2 96.8 %all-gather.4.cloned.1.call-start = ((), (), s32[]{:S(2)}) async-start(), calls=%async_computation.5 | async-start | bytes 5308416 | tf_op jit(solution)/shard_map/all_gather | solution.py:701
  22.5 24.6 %collective-permute-start.5 = (bf16[2,192,384]{2,1,0:T(8,128)(2,1)}, bf16[2,192,384]{2,1,0:T(8,128)(2,1)}, u32[]{:S(2)}, u32[]{:S(2)}) collective-permute-start(bf16[2,192,384]{2,1,0:T(8,128)(2,1)} %pad_maximum_fusion.30), channel_id=1, source_target_pairs={{0,2},{1,3},{2,0},{3,1},{4,6},{5,7},{6,4},{7,5},{8,10},{9,11},{10,... | collective-permute-start | bytes 884744 | tf_op jit(solution)/shard_map/ppermute | solution.py:48
  51.8 202.6 %all-gather.6.cloned.1.call-start = ((), (), s32[]{:S(2)}) async-start(), calls=%async_computation.6 | async-start | bytes 5308416 | tf_op jit(solution)/shard_map/all_gather | solution.py:703
  104.0 229.8 %all-gather.8.cloned.1.call-start = ((), (), s32[]{:S(2)}) async-start(), calls=%async_computation.7 | async-start | bytes 7864320 | tf_op jit(solution)/shard_map/all_gather | solution.py:741
  111.9 33.1 %collective-permute-start.7 = (bf16[256,1536]{1,0:T(8,128)(2,1)}, bf16[256,1536]{1,0:T(8,128)(2,1)}, u32[]{:S(2)}, u32[]{:S(2)}) collective-permute-start(bf16[256,1536]{1,0:T(8,128)(2,1)} %fusion.21.refs_0_), channel_id=1, source_target_pairs={{0,1},{1,0},{2,3},{3,2},{4,5},{5,4},{6,7},{7,6},{8,9},{9,8},{10,11... | collective-permute-start | bytes 2359304 | tf_op jit(solution)/shard_map/ppermute | solution.py:48
  113.3 31.7 %collective-permute-start.8 = (bf16[256,1536]{1,0:T(8,128)(2,1)}, bf16[256,1536]{1,0:T(8,128)(2,1)}, u32[]{:S(2)}, u32[]{:S(2)}) collective-permute-start(bf16[256,1536]{1,0:T(8,128)(2,1)} %fusion.21.refs_0_), channel_id=1, source_target_pairs={{0,2},{1,3},{2,0},{3,1},{4,6},{5,7},{6,4},{7,5},{8,10},{9,11},{10,... | collective-permute-start | bytes 2359304 | tf_op jit(solution)/shard_map/ppermute | solution.py:48
  114.8 26.7 %collective-permute-start.2 = (bf16[128,1536]{1,0:T(8,128)(2,1)}, bf16[128,1536]{1,0:T(8,128)(2,1)}, u32[]{:S(2)}, u32[]{:S(2)}) collective-permute-start(bf16[128,1536]{1,0:T(8,128)(2,1)} %slice.278), channel_id=1, source_target_pairs={{0,2},{1,3},{2,0},{3,1},{4,6},{5,7},{6,4},{7,5},{8,10},{9,11},{10,... | collective-permute-start | bytes 1179656 | tf_op jit(solution)/shard_map/ppermute | solution.py:48
  115.4 26.1 %collective-permute-start.3 = (bf16[128,1536]{1,0:T(8,128)(2,1)}, bf16[128,1536]{1,0:T(8,128)(2,1)}, u32[]{:S(2)}, u32[]{:S(2)}) collective-permute-start(bf16[128,1536]{1,0:T(8,128)(2,1)} %slice.279), channel_id=1, source_target_pairs={{0,1},{1,0},{2,3},{3,2},{4,5},{5,4},{6,7},{7,6},{8,9},{9,8},{10,11... | collective-permute-start | bytes 1179656 | tf_op jit(solution)/shard_map/ppermute | solution.py:48
  182.7 35.8 %collective-permute-start.19 = (bf16[2,768,128]{2,1,0:T(8,128)(2,1)}, bf16[2,768,128]{2,1,0:T(8,128)(2,1)}, u32[]{:S(2)}, u32[]{:S(2)}) collective-permute-start(bf16[2,768,128]{2,1,0:T(8,128)(2,1)} %pad_maximum_fusion.29), channel_id=1, source_target_pairs={{0,1},{1,0},{2,3},{3,2},{4,5},{5,4},{6,7},{7,6},{8,9},{9,8},{10,11... | collective-permute-start | bytes 1179656 | tf_op jit(solution)/shard_map/ppermute | solution.py:48
  187.7 31.9 %collective-permute-start.20 = (bf16[2,768,128]{2,1,0:T(8,128)(2,1)}, bf16[2,768,128]{2,1,0:T(8,128)(2,1)}, u32[]{:S(2)}, u32[]{:S(2)}) collective-permute-start(bf16[2,768,128]{2,1,0:T(8,128)(2,1)} %pad_maximum_fusion.29), channel_id=1, source_target_pairs={{0,2},{1,3},{2,0},{3,1},{4,6},{5,7},{6,4},{7,5},{8,10},{9,11},{10,... | collective-permute-start | bytes 1179656 | tf_op jit(solution)/shard_map/ppermute | solution.py:48
  191.1 31.8 %collective-permute-start.16 = (bf16[3,192,1536]{2,1,0:T(8,128)(2,1)}, bf16[3,192,1536]{2,1,0:T(8,128)(2,1)}, u32[]{:S(2)}, u32[]{:S(2)}) collective-permute-start(bf16[3,192,1536]{2,1,0:T(8,128)(2,1)} %bitcast.24), channel_id=1, source_target_pairs={{0,4},{4,0},{8,12},{12,8},{16,20},{20,16},{24,28},{28,24},{1,5},{5... | collective-permute-start | bytes 5308424 | tf_op jit(solution)/shard_map/ppermute | solution.py:48
  196.0 25.2 %collective-permute-start.21 = (bf16[2,768,128]{2,1,0:T(8,128)(2,1)}, bf16[2,768,128]{2,1,0:T(8,128)(2,1)}, u32[]{:S(2)}, u32[]{:S(2)}) collective-permute-start(bf16[2,768,128]{2,1,0:T(8,128)(2,1)} %pad_maximum_fusion.29), channel_id=1, source_target_pairs={{0,3},{1,2},{2,1},{3,0},{4,7},{5,6},{6,5},{7,4},{8,11},{9,10},{10,... | collective-permute-start | bytes 1179656 | tf_op jit(solution)/shard_map/ppermute | solution.py:48
  218.4 580.5 %reduce-scatter.16.cloned.1.call-start = ((), (), s32[]{:S(2)}) async-start(), calls=%async_computation.12 | async-start | bytes 1327104
  260.7 36.0 %collective-permute-start.25 = (bf16[256,1536]{1,0:T(8,128)(2,1)S(1)}, bf16[256,1536]{1,0:T(8,128)(2,1)S(1)}, u32[]{:S(2)}, u32[]{:S(2)}) collective-permute-start(bf16[256,1536]{1,0:T(8,128)(2,1)S(1)} %add_convert_fusion.1.refs_0_), channel_id=1, source_target_pairs={{0,1},{1,0},{2,3},{3,2},{4,5},{5,4},{6,7},{7,6},{8,9},{9,8},{10,11... | collective-permute-start | bytes 2359304 | tf_op jit(solution)/shard_map/ppermute | solution.py:48
  261.5 35.8 %collective-permute-start.26 = (bf16[256,1536]{1,0:T(8,128)(2,1)S(1)}, bf16[256,1536]{1,0:T(8,128)(2,1)S(1)}, u32[]{:S(2)}, u32[]{:S(2)}) collective-permute-start(bf16[256,1536]{1,0:T(8,128)(2,1)S(1)} %add_convert_fusion.1.refs_0_), channel_id=1, source_target_pairs={{0,2},{1,3},{2,0},{3,1},{4,6},{5,7},{6,4},{7,5},{8,10},{9,11},{10,... | collective-permute-start | bytes 2359304 | tf_op jit(solution)/shard_map/ppermute | solution.py:48
  297.6 32.7 %collective-permute-start.27 = (bf16[256,1536]{1,0:T(8,128)(2,1)}, bf16[256,1536]{1,0:T(8,128)(2,1)}, u32[]{:S(2)}, u32[]{:S(2)}) collective-permute-start(bf16[256,1536]{1,0:T(8,128)(2,1)} %add_convert_fusion.refs_0_), channel_id=1, source_target_pairs={{0,1},{1,0},{2,3},{3,2},{4,5},{5,4},{6,7},{7,6},{8,9},{9,8},{10,11... | collective-permute-start | bytes 2359304 | tf_op jit(solution)/shard_map/ppermute | solution.py:48
  298.7 31.6 %collective-permute-start.28 = (bf16[256,1536]{1,0:T(8,128)(2,1)}, bf16[256,1536]{1,0:T(8,128)(2,1)}, u32[]{:S(2)}, u32[]{:S(2)}) collective-permute-start(bf16[256,1536]{1,0:T(8,128)(2,1)} %add_convert_fusion.refs_0_), channel_id=1, source_target_pairs={{0,2},{1,3},{2,0},{3,1},{4,6},{5,7},{6,4},{7,5},{8,10},{9,11},{10,... | collective-permute-start | bytes 2359304 | tf_op jit(solution)/shard_map/ppermute | solution.py:48
  302.0 26.7 %collective-permute-start.29 = (bf16[128,1536]{1,0:T(8,128)(2,1)S(1)}, bf16[128,1536]{1,0:T(8,128)(2,1)S(1)}, u32[]{:S(2)}, u32[]{:S(2)}) collective-permute-start(bf16[128,1536]{1,0:T(8,128)(2,1)S(1)} %slice.300), channel_id=1, source_target_pairs={{0,2},{1,3},{2,0},{3,1},{4,6},{5,7},{6,4},{7,5},{8,10},{9,11},{10,... | collective-permute-start | bytes 1179656 | tf_op jit(solution)/shard_map/ppermute | solution.py:48
  303.1 26.5 %collective-permute-start.30 = (bf16[128,1536]{1,0:T(8,128)(2,1)S(1)}, bf16[128,1536]{1,0:T(8,128)(2,1)S(1)}, u32[]{:S(2)}, u32[]{:S(2)}) collective-permute-start(bf16[128,1536]{1,0:T(8,128)(2,1)S(1)} %slice.301), channel_id=1, source_target_pairs={{0,1},{1,0},{2,3},{3,2},{4,5},{5,4},{6,7},{7,6},{8,9},{9,8},{10,11... | collective-permute-start | bytes 1179656 | tf_op jit(solution)/shard_map/ppermute | solution.py:48
  411.4 49.0 %collective-permute-start.40 = (bf16[256,1536]{1,0:T(8,128)(2,1)}, bf16[256,1536]{1,0:T(8,128)(2,1)}, u32[]{:S(2)}, u32[]{:S(2)}) collective-permute-start(bf16[256,1536]{1,0:T(8,128)(2,1)} %pad_maximum_fusion.19), channel_id=1, source_target_pairs={{0,2},{1,3},{2,0},{3,1},{4,6},{5,7},{6,4},{7,5},{8,10},{9,11},{10,... | collective-permute-start | bytes 2359304 | tf_op jit(solution)/shard_map/ppermute | solution.py:48
  413.2 47.2 %collective-permute-start.39 = (bf16[256,1536]{1,0:T(8,128)(2,1)}, bf16[256,1536]{1,0:T(8,128)(2,1)}, u32[]{:S(2)}, u32[]{:S(2)}) collective-permute-start(bf16[256,1536]{1,0:T(8,128)(2,1)} %pad_maximum_fusion.18), channel_id=1, source_target_pairs={{0,1},{1,0},{2,3},{3,2},{4,5},{5,4},{6,7},{7,6},{8,9},{9,8},{10,11... | collective-permute-start | bytes 2359304 | tf_op jit(solution)/shard_map/ppermute | solution.py:48
  456.2 48.0 %collective-permute-start.38 = (bf16[256,1536]{1,0:T(8,128)(2,1)}, bf16[256,1536]{1,0:T(8,128)(2,1)}, u32[]{:S(2)}, u32[]{:S(2)}) collective-permute-start(bf16[256,1536]{1,0:T(8,128)(2,1)} %pad_maximum_fusion.17), channel_id=1, source_target_pairs={{0,2},{1,3},{2,0},{3,1},{4,6},{5,7},{6,4},{7,5},{8,10},{9,11},{10,... | collective-permute-start | bytes 2359304 | tf_op jit(solution)/shard_map/ppermute | solution.py:48
  459.0 45.1 %collective-permute-start.37 = (bf16[256,1536]{1,0:T(8,128)(2,1)}, bf16[256,1536]{1,0:T(8,128)(2,1)}, u32[]{:S(2)}, u32[]{:S(2)}) collective-permute-start(bf16[256,1536]{1,0:T(8,128)(2,1)} %pad_maximum_fusion.16), channel_id=1, source_target_pairs={{0,1},{1,0},{2,3},{3,2},{4,5},{5,4},{6,7},{7,6},{8,9},{9,8},{10,11... | collective-permute-start | bytes 2359304 | tf_op jit(solution)/shard_map/ppermute | solution.py:48
  499.6 45.4 %collective-permute-start.41 = (bf16[384,256]{1,0:T(8,128)(2,1)S(1)}, bf16[384,256]{1,0:T(8,128)(2,1)S(1)}, u32[]{:S(2)}, u32[]{:S(2)}) collective-permute-start(bf16[384,256]{1,0:T(8,128)(2,1)S(1)} %get-tuple-element.493), channel_id=1, source_target_pairs={{0,1},{1,0},{2,3},{3,2},{4,5},{5,4},{6,7},{7,6},{8,9},{9,8},{10,11... | collective-permute-start | bytes 589832 | tf_op jit(solution)/shard_map/ppermute | solution.py:48
  500.3 44.7 %collective-permute-start.42 = (bf16[384,256]{1,0:T(8,128)(2,1)S(1)}, bf16[384,256]{1,0:T(8,128)(2,1)S(1)}, u32[]{:S(2)}, u32[]{:S(2)}) collective-permute-start(bf16[384,256]{1,0:T(8,128)(2,1)S(1)} %get-tuple-element.492), channel_id=1, source_target_pairs={{0,2},{1,3},{2,0},{3,1},{4,6},{5,7},{6,4},{7,5},{8,10},{9,11},{10,... | collective-permute-start | bytes 589832 | tf_op jit(solution)/shard_map/ppermute | solution.py:48
  501.6 43.4 %collective-permute-start.43 = (bf16[384,256]{1,0:T(8,128)(2,1)S(1)}, bf16[384,256]{1,0:T(8,128)(2,1)S(1)}, u32[]{:S(2)}, u32[]{:S(2)}) collective-permute-start(bf16[384,256]{1,0:T(8,128)(2,1)S(1)} %get-tuple-element.491), channel_id=1, source_target_pairs={{0,3},{1,2},{2,1},{3,0},{4,7},{5,6},{6,5},{7,4},{8,11},{9,10},{10,... | collective-permute-start | bytes 589832 | tf_op jit(solution)/shard_map/ppermute | solution.py:48
  569.4 51.4 %collective-permute-start.44 = (bf16[128,1536]{1,0:T(8,128)(2,1)}, bf16[128,1536]{1,0:T(8,128)(2,1)}, u32[]{:S(2)}, u32[]{:S(2)}) collective-permute-start(bf16[128,1536]{1,0:T(8,128)(2,1)} %get-tuple-element.464), channel_id=1, source_target_pairs={{0,2},{1,3},{2,0},{3,1},{4,6},{5,7},{6,4},{7,5},{8,10},{9,11},{10,... | collective-permute-start | bytes 1179656 | tf_op jit(solution)/shard_map/ppermute | solution.py:48
  570.8 50.1 %collective-permute-start.45 = (bf16[128,1536]{1,0:T(8,128)(2,1)}, bf16[128,1536]{1,0:T(8,128)(2,1)}, u32[]{:S(2)}, u32[]{:S(2)}) collective-permute-start(bf16[128,1536]{1,0:T(8,128)(2,1)} %get-tuple-element.463), channel_id=1, source_target_pairs={{0,1},{1,0},{2,3},{3,2},{4,5},{5,4},{6,7},{7,6},{8,9},{9,8},{10,11... | collective-permute-start | bytes 1179656 | tf_op jit(solution)/shard_map/ppermute | solution.py:48
  595.8 76.9 %collective-permute-start.65 = (bf16[2,768,128]{2,1,0:T(8,128)(2,1)}, bf16[2,768,128]{2,1,0:T(8,128)(2,1)}, u32[]{:S(2)}, u32[]{:S(2)}) collective-permute-start(bf16[2,768,128]{2,1,0:T(8,128)(2,1)} %get-tuple-element.473), channel_id=1, source_target_pairs={{0,1},{1,0},{2,3},{3,2},{4,5},{5,4},{6,7},{7,6},{8,9},{9,8},{10,11... | collective-permute-start | bytes 1179656 | tf_op jit(solution)/shard_map/ppermute | solution.py:48
  597.3 75.4 %collective-permute-start.66 = (bf16[2,768,128]{2,1,0:T(8,128)(2,1)}, bf16[2,768,128]{2,1,0:T(8,128)(2,1)}, u32[]{:S(2)}, u32[]{:S(2)}) collective-permute-start(bf16[2,768,128]{2,1,0:T(8,128)(2,1)} %get-tuple-element.474), channel_id=1, source_target_pairs={{0,2},{1,3},{2,0},{3,1},{4,6},{5,7},{6,4},{7,5},{8,10},{9,11},{10,... | collective-permute-start | bytes 1179656 | tf_op jit(solution)/shard_map/ppermute | solution.py:48
  629.8 25.5 %collective-permute-start.51 = (bf16[128,1536]{1,0:T(8,128)(2,1)}, bf16[128,1536]{1,0:T(8,128)(2,1)}, u32[]{:S(2)}, u32[]{:S(2)}) collective-permute-start(bf16[128,1536]{1,0:T(8,128)(2,1)} %get-tuple-element.458), channel_id=1, source_target_pairs={{0,2},{1,3},{2,0},{3,1},{4,6},{5,7},{6,4},{7,5},{8,10},{9,11},{10,... | collective-permute-start | bytes 1179656 | tf_op jit(solution)/shard_map/ppermute | solution.py:48
  631.2 25.5 %collective-permute-start.52 = (bf16[128,1536]{1,0:T(8,128)(2,1)}, bf16[128,1536]{1,0:T(8,128)(2,1)}, u32[]{:S(2)}, u32[]{:S(2)}) collective-permute-start(bf16[128,1536]{1,0:T(8,128)(2,1)} %get-tuple-element.457), channel_id=1, source_target_pairs={{0,1},{1,0},{2,3},{3,2},{4,5},{5,4},{6,7},{7,6},{8,9},{9,8},{10,11... | collective-permute-start | bytes 1179656 | tf_op jit(solution)/shard_map/ppermute | solution.py:48
  676.1 161.8 %reduce-scatter.14.cloned.1.call-start = ((), (), s32[]{:S(2)}) async-start(), calls=%async_computation.11 | async-start | bytes 5308416 | tf_op jit(solution)/shard_map/reduce_scatter | solution.py:629
  676.7 188.2 %reduce-scatter.10.cloned.1.call-start = ((), (), s32[]{:S(2)}) async-start(), calls=%async_computation.9 | async-start | bytes 5308416 | tf_op jit(solution)/shard_map/reduce_scatter | solution.py:629
  677.3 268.0 %reduce-scatter.12.cloned.1.call-start = ((), (), s32[]{:S(2)}) async-start(), calls=%async_computation.10 | async-start | bytes 5308416 | tf_op jit(solution)/shard_map/reduce_scatter | solution.py:629
  678.1 338.8 %reduce-scatter.8.cloned.1.call-start = ((), (), s32[]{:S(2)}) async-start(), calls=%async_computation.8 | async-start | bytes 7864320 | tf_op jit(solution)/shard_map/reduce_scatter | solution.py:844
  678.1 59.2 %collective-permute-start.64 = (bf16[4,4,3,192,384]{4,3,2,1,0:T(8,128)(2,1)}, bf16[4,4,3,192,384]{4,3,2,1,0:T(8,128)(2,1)}, u32[]{:S(2)}, u32[]{:S(2)}) collective-permute-start(bf16[4,4,3,192,384]{4,3,2,1,0:T(8,128)(2,1)} %whole_grad.2), channel_id=1, source_target_pairs={{0,4},{4,0},{8,12},{12,8},{16,20},{20,16},{24,28},{28,24},{1,5},{5... | collective-permute-start | bytes 21233672 | tf_op jit(solution)/shard_map/ppermute | solution.py:48
  684.8 38.5 %collective-permute-start.49 = (bf16[256,1536]{1,0:T(8,128)(2,1)S(1)}, bf16[256,1536]{1,0:T(8,128)(2,1)S(1)}, u32[]{:S(2)}, u32[]{:S(2)}) collective-permute-start(bf16[256,1536]{1,0:T(8,128)(2,1)S(1)} %pad_maximum_fusion.22), channel_id=1, source_target_pairs={{0,1},{1,0},{2,3},{3,2},{4,5},{5,4},{6,7},{7,6},{8,9},{9,8},{10,11... | collective-permute-start | bytes 2359304 | tf_op jit(solution)/shard_map/ppermute | solution.py:48
  689.4 33.9 %collective-permute-start.50 = (bf16[256,1536]{1,0:T(8,128)(2,1)S(1)}, bf16[256,1536]{1,0:T(8,128)(2,1)S(1)}, u32[]{:S(2)}, u32[]{:S(2)}) collective-permute-start(bf16[256,1536]{1,0:T(8,128)(2,1)S(1)} %pad_maximum_fusion.23), channel_id=1, source_target_pairs={{0,2},{1,3},{2,0},{3,1},{4,6},{5,7},{6,4},{7,5},{8,10},{9,11},{10,... | collective-permute-start | bytes 2359304 | tf_op jit(solution)/shard_map/ppermute | solution.py:48
  698.7 24.7 %collective-permute-start.53 = (bf16[256,1536]{1,0:T(8,128)(2,1)S(1)}, bf16[256,1536]{1,0:T(8,128)(2,1)S(1)}, u32[]{:S(2)}, u32[]{:S(2)}) collective-permute-start(bf16[256,1536]{1,0:T(8,128)(2,1)S(1)} %pad_maximum_fusion.24), channel_id=1, source_target_pairs={{0,1},{1,0},{2,3},{3,2},{4,5},{5,4},{6,7},{7,6},{8,9},{9,8},{10,11... | collective-permute-start | bytes 2359304 | tf_op jit(solution)/shard_map/ppermute | solution.py:48
  757.3 29.1 %collective-permute-start.61 = (bf16[192,1152]{1,0:T(8,128)(2,1)S(1)}, bf16[192,1152]{1,0:T(8,128)(2,1)S(1)}, u32[]{:S(2)}, u32[]{:S(2)}) collective-permute-start(bf16[192,1152]{1,0:T(8,128)(2,1)S(1)} %get-tuple-element.468), channel_id=1, source_target_pairs={{0,8},{4,12},{8,0},{12,4},{16,24},{20,28},{24,16},{28,20},{1,9},{5... | collective-permute-start | bytes 1327112 | tf_op jit(solution)/shard_map/ppermute | solution.py:48
  757.4 40.4 %collective-permute-start.62 = (bf16[192,1152]{1,0:T(8,128)(2,1)S(1)}, bf16[192,1152]{1,0:T(8,128)(2,1)S(1)}, u32[]{:S(2)}, u32[]{:S(2)}) collective-permute-start(bf16[192,1152]{1,0:T(8,128)(2,1)S(1)} %get-tuple-element.470), channel_id=1, source_target_pairs={{0,16},{4,20},{8,24},{12,28},{16,0},{20,4},{24,8},{28,12},{1,17},{... | collective-permute-start | bytes 1327112 | tf_op jit(solution)/shard_map/ppermute | solution.py:48
  759.4 38.4 %collective-permute-start.63 = (bf16[192,1152]{1,0:T(8,128)(2,1)S(1)}, bf16[192,1152]{1,0:T(8,128)(2,1)S(1)}, u32[]{:S(2)}, u32[]{:S(2)}) collective-permute-start(bf16[192,1152]{1,0:T(8,128)(2,1)S(1)} %get-tuple-element.469), channel_id=1, source_target_pairs={{0,24},{4,28},{8,16},{12,20},{16,8},{20,12},{24,0},{28,4},{1,25},{... | collective-permute-start | bytes 1327112 | tf_op jit(solution)/shard_map/ppermute | solution.py:48
  778.1 38.8 %collective-permute-start.70 = (bf16[2304,384]{1,0:T(8,128)(2,1)}, bf16[2304,384]{1,0:T(8,128)(2,1)}, u32[]{:S(2)}, u32[]{:S(2)}) collective-permute-start(bf16[2304,384]{1,0:T(8,128)(2,1)} %pad_maximum_fusion.9), channel_id=1, source_target_pairs={{0,1},{1,0},{2,3},{3,2},{4,5},{5,4},{6,7},{7,6},{8,9},{9,8},{10,11... | collective-permute-start | bytes 5308424 | tf_op jit(solution)/shard_map/ppermute | solution.py:48
  780.9 38.6 %collective-permute-start.71 = (bf16[2304,384]{1,0:T(8,128)(2,1)}, bf16[2304,384]{1,0:T(8,128)(2,1)}, u32[]{:S(2)}, u32[]{:S(2)}) collective-permute-start(bf16[2304,384]{1,0:T(8,128)(2,1)} %pad_maximum_fusion.10), channel_id=1, source_target_pairs={{0,2},{1,3},{2,0},{3,1},{4,6},{5,7},{6,4},{7,5},{8,10},{9,11},{10,... | collective-permute-start | bytes 5308424 | tf_op jit(solution)/shard_map/ppermute | solution.py:48
  823.5 124.1 %collective-permute-start.72 = (bf16[576,384]{1,0:T(8,128)(2,1)}, bf16[576,384]{1,0:T(8,128)(2,1)}, u32[]{:S(2)}, u32[]{:S(2)}) collective-permute-start(bf16[576,384]{1,0:T(8,128)(2,1)} %get-tuple-element.465), channel_id=1, source_target_pairs={{0,8},{4,12},{8,0},{12,4},{16,24},{20,28},{24,16},{28,20},{1,9},{5... | collective-permute-start | bytes 1327112 | tf_op jit(solution)/shard_map/ppermute | solution.py:48
  835.5 112.0 %collective-permute-start.73 = (bf16[576,384]{1,0:T(8,128)(2,1)}, bf16[576,384]{1,0:T(8,128)(2,1)}, u32[]{:S(2)}, u32[]{:S(2)}) collective-permute-start(bf16[576,384]{1,0:T(8,128)(2,1)} %get-tuple-element.467), channel_id=1, source_target_pairs={{0,16},{4,20},{8,24},{12,28},{16,0},{20,4},{24,8},{28,12},{1,17},{... | collective-permute-start | bytes 1327112 | tf_op jit(solution)/shard_map/ppermute | solution.py:48
  835.5 112.0 %collective-permute-start.74 = (bf16[576,384]{1,0:T(8,128)(2,1)}, bf16[576,384]{1,0:T(8,128)(2,1)}, u32[]{:S(2)}, u32[]{:S(2)}) collective-permute-start(bf16[576,384]{1,0:T(8,128)(2,1)} %get-tuple-element.466), channel_id=1, source_target_pairs={{0,24},{4,28},{8,16},{12,20},{16,8},{20,12},{24,0},{28,4},{1,25},{... | collective-permute-start | bytes 1327112 | tf_op jit(solution)/shard_map/ppermute | solution.py:48
  (286 other events, 2237.1 us)
Sparse Core Ops, SparseCore 0:
  51.9 52.0 all-gather.3
  105.6 50.5 all-gather.5
  218.5 90.6 all-gather.7
  676.2 37.8 reduce-scatter.15
  716.2 63.5 reduce-scatter.13
  781.9 82.8 reduce-scatter.9
  867.1 78.1 reduce-scatter.11
  948.3 68.5 reduce-scatter.7

commit v4 on v3

--- a/solution.py
+++ b/solution.py
@@ -264,7 +264,7 @@
 
 
 def params():
-    return pltpu.CompilerParams(vmem_limit_bytes=40 * 2**20)
+    return pltpu.CompilerParams(vmem_limit_bytes=48 * 2**20)
 
 
 def self_cost(heads, frames, products):
@@ -471,15 +471,18 @@
     )(w_turned, cosine, sine, *pieces, *earlier)
 
 
-def glu_kernel(size, given, n_ref, gate_ref, up_ref, down_ref, c_ref, *refs):
-    h_ref, dg_ref, du_ref, x_ref = refs[-4:]
+def glu_kernel(size, given, n_ref, gate_ref, up_ref, down_ref, *refs):
+    h_ref, dg_ref, du_ref, x_ref, c_ref = refs[-5:]
     blocks = block_refs(refs[:given], size)
+    grads = block_refs(refs[given : 2 * given], size)
     rows = h_ref.shape[1] // size
 
     @pl.when(pl.program_id(0) == 0)
     def _():
         for k in range(size):
+            there = pl.ds(pl.multiple_of(n_ref[k] * rows, rows), rows)
             x_ref[0, k * rows : (k + 1) * rows] = block_value(blocks[k])
+            c_ref[0, there] = block_value(grads[k])
 
     for k in range(size):
         frames = block_value(blocks[k])
@@ -487,7 +490,7 @@
         there = pl.ds(pl.multiple_of(n_ref[k] * rows, rows), rows)
         gate = dot(frames, gate_ref[...], 1, 0)
         upper = dot(frames, up_ref[...], 1, 0)
-        grad_hidden = dot(c_ref[0, there], down_ref[...], 1, 1)
+        grad_hidden = dot(block_value(grads[k]), down_ref[...], 1, 1)
         sigma = 1.0 / (1.0 + jnp.exp(-gate))
         silu = gate * sigma
         h_ref[0, there] = (silu * upper).astype(bf16)
@@ -495,10 +498,10 @@
         du_ref[0, part] = (grad_hidden * silu).astype(bf16)
 
 
-def glu(clip, order, pieces, grads, w_gate, w_up, w_down, earlier):
+def glu(clip, count, order, pieces, grads, w_gate, w_up, w_down, earlier):
     size = lax.axis_size("mp")
-    count, rows, width = grads.shape
-    hidden = w_gate.shape[1]
+    width, hidden = w_gate.shape
+    rows = size * pieces[0].shape[0]
     block = 256
     columns = pl.BlockSpec((width, block), lambda j: (0, j))
     out = pl.BlockSpec((1, rows, block), lambda j: (clip, 0, j))
@@ -511,22 +514,22 @@
             columns,
             columns,
             pl.BlockSpec((block, width), lambda j: (j, 0)),
-            whole,
         ]
         + whole_specs(pieces)
+        + whole_specs(grads)
         + [pl.BlockSpec(memory_space=pl.ANY)] * len(earlier),
-        out_specs=[out, out, out, whole],
+        out_specs=[out, out, out, whole, whole],
         out_shape=[shape_of((count, rows, hidden), bf16)] * 3
-        + [shape_of((count, rows, width), bf16)],
-        input_output_aliases={5 + len(pieces) + i: i for i in range(len(earlier))},
+        + [shape_of((count, rows, width), bf16)] * 2,
+        input_output_aliases={4 + 2 * len(pieces) + i: i for i in range(len(earlier))},
         compiler_params=params(),
         cost_estimate=pl.CostEstimate(
             flops=6 * rows * width * hidden,
-            bytes_accessed=6 * rows * width + 6 * width * hidden + 6 * rows * hidden,
+            bytes_accessed=8 * rows * width + 6 * width * hidden + 6 * rows * hidden,
             transcendentals=rows * hidden,
         ),
         name="glu",
-    )(order, w_gate, w_up, w_down, grads, *pieces, *earlier)
+    )(order, w_gate, w_up, w_down, *pieces, *grads, *earlier)
 
 
 def glu_back_kernel(size, dg_ref, du_ref, gate_ref, up_ref, *refs):
@@ -678,9 +681,7 @@
             spread_one = [Spread(low[0])]
 
     depth = width // groups
-    query_part = lax.dynamic_slice_in_dim(hold(c_query), there * depth, depth, 0)
-    out_part = lax.dynamic_slice_in_dim(hold(c_out), there * depth, depth, 1).T
-    side = jnp.stack([query_part, out_part])
+    side = lax.dynamic_slice_in_dim(hold(c_query), there * depth, depth, 0)
     side = [side] + [swap(side, "mp", k) for k in range(1, size)]
     w_turned = joined([hold(w_query).T, w_key.T, w_value.T], 0)
     cosine, sine = turning(rows)
@@ -688,29 +689,25 @@
     memory = joined([hold(c_key), c_value], 1)
     memory = jnp.stack([dot(memory, prompt[b], 0, 1).astype(bf16) for b in clips])
     mark(memory)
-    for b in clips:
-        spread_one[b].first = arrive(spread_one[b].first)
-        spread_one[b].second_step()
-        if b + 1 < count:
-            spread_one.append(Spread(hold(low[b + 1])))
-        if b == 0:
-            side = arrive(side)
-            query_wide = joined([part[0] for part in side], 1)
-            out_wide = joined([part[1] for part in side], 1)
-            mark(query_wide, out_wide)
-            c_query_all = lax.all_gather(query_wide, "dp", axis=0, tiled=True)
-            out_wide = after(out_wide, c_query_all)
-            c_out_all = lax.all_gather(out_wide, "dp", axis=0, tiled=True)
-            picked = jnp.take(hold(table), tsteps, axis=0)
-            prefix_normed, prefix_normal, prefix_scale = norm_forward(picked, gain_one, shift_one)
-            prefix_low = prefix_normed.astype(bf16)
-            front = dot(w_turned[local:], prefix_low, 1, 1).astype(bf16)
-            mark(front)
-            spread_one[0].last = arrive(spread_one[0].last)
-            half = lax.dynamic_slice_in_dim(hold(w_out), core * (local // 2), local // 2, 0)
-            spread_out = Spread(half)
+    spread_one[0].first = arrive(spread_one[0].first)
+    spread_one[0].second_step()
+    for b in clips[1:]:
+        spread_one.append(Spread(hold(low[b])))
+    side = joined(arrive(side), 1)
+    mark(side)
+    c_query_all = lax.all_gather(side, "dp", axis=0, tiled=True)
+    side = lax.dynamic_slice_in_dim(hold(c_out), there * depth, depth, 1).T
+    side = [side] + [swap(side, "mp", k) for k in range(1, size)]
+    picked = jnp.take(hold(table), tsteps, axis=0)
+    prefix_normed, prefix_normal, prefix_scale = norm_forward(picked, gain_one, shift_one)
+    prefix_low = prefix_normed.astype(bf16)
+    front = dot(w_turned[local:], prefix_low, 1, 1).astype(bf16)
+    mark(front)
     front_keys = [front[:local, b : b + 1] for b in clips]
     front_values = [front[local:, b : b + 1] for b in clips]
+    spread_one[0].last = arrive(spread_one[0].last)
+    half = lax.dynamic_slice_in_dim(hold(w_out), core * (local // 2), local // 2, 0)
+    spread_out = Spread(half)
 
     turned, mixed_part, logsum, mixed = [], [], [], []
     frames_one = ()
@@ -723,8 +720,19 @@
         turned.append(out)
         mark(out)
         if b == 0:
-            spread_out.first = arrive(spread_out.first)
-            spread_out.second_step()
+            for later in spread_one[1:]:
+                later.first = arrive(later.first)
+                later.second_step()
+            side = joined(arrive(side), 1)
+            mark(side)
+            c_out_all = lax.all_gather(side, "dp", axis=0, tiled=True)
+        else:
+            spread_out.last = arrive(spread_out.last)
+            got = spread_out.pieces()[1:]
+            got = joined(got, 0).reshape(size - 1, local // 2, width)
+            mark(got)
+            other = swap(got, "dp", 1)
+            spread_down = [Spread(hold(cotangent[0]))]
         out, sums = self_forward(hold(turned[b]), front_keys[b], front_values[b])
         mixed_part.append(out)
         logsum.append(sums)
@@ -733,19 +741,17 @@
         if b == 0:
             memory = hold(memory)
             memory = [memory] + [swap(memory, "mp", k) for k in range(1, size)]
-            spread_out.last = arrive(spread_out.last)
-            got = spread_out.pieces()[1:]
-            got = joined(got, 0).reshape(size - 1, local // 2, width)
-            other = swap(got, "dp", 1)
+            spread_out.first = arrive(spread_out.first)
+            spread_out.second_step()
     frames_one = frames_one[0]
-    down_in = lax.all_gather(hold(cotangent), "mp", axis=1, tiled=True)
     other = arrive(other)
     rest = joined([jnp.where(core == 0, got, other), jnp.where(core == 0, other, got)], 1)
     out_all = joined([w_out, rest.reshape(-1, width)], 0)
-    memory = jnp.stack(memory, axis=1)
+    mark(out_all)
+    memory = jnp.stack(arrive(memory), axis=1)
     cross_keys = [memory[b, :, :local].reshape(size * local, -1) for b in clips]
     cross_values = [memory[b, :, local:].reshape(size * local, -1) for b in clips]
-    mark(out_all)
+    mark(memory)
 
     first, twos, normed_two, cross_query, cross_sums, cross_mixed = [], [], [], [], [], []
     second, threes, low = [], [], []
@@ -754,13 +760,18 @@
         first.append(resid[b] + dot(mixed[b], out_all, 0, 0))
         twos.append(norm_forward(first[b], gain_two, shift_two))
         normed_two.append(twos[b][0].astype(bf16))
-        cross_query.append((dot(c_query_all, normed_two[b], 0, 1) * FACTOR).astype(bf16))
+        mark(normed_two[b])
+    for b in clips:
+        cross_query.append((dot(c_query_all, hold(normed_two[b]), 0, 1) * FACTOR).astype(bf16))
         out, sums = cross_forward(
             b, size, lengths, cross_query[b], cross_keys[b], cross_values[b]
         )
         cross_mixed.append(out)
         cross_sums.append(sums)
         mark(out)
+        if b == 0:
+            spread_down[0].first = arrive(spread_down[0].first)
+            spread_down[0].second_step()
     spread_three = []
     for b in clips:
         second.append(first[b] + dot(hold(cross_mixed[b]), c_out_all, 0, 1))
@@ -774,30 +785,36 @@
     back_pieces, back_three = [], []
     parts = ()
     for b in clips:
-        if b + 1 < count:
-            spread_three[b].first = arrive(spread_three[b].first)
-            spread_three[b].second_step()
-            spread_three.append(Spread(hold(low[b + 1])))
-            spread_three[b].last = arrive(spread_three[b].last)
-            spread_three[b + 1].first = arrive(spread_three[b + 1].first)
-            spread_three[b + 1].second_step()
+        if b == 0:
+            spread_down[0].last = arrive(spread_down[0].last)
+            spread_three[0].first = arrive(spread_three[0].first)
+            spread_three[0].second_step()
+            spread_three.extend(Spread(hold(later)) for later in low[1:])
+            spread_down.extend(Spread(hold(later)) for later in cotangent[1:])
+        spread_three[b].last = arrive(spread_three[b].last)
         pieces = hold(spread_three[b].pieces())
-        parts = glu(b, order, pieces, down_in, w_gate, w_up, w_down, list(parts))
+        parts = glu(
+            b, count, order, pieces, spread_down[b].pieces(), w_gate, w_up, w_down, list(parts)
+        )
         mark(parts[1])
-        if b:
-            came = arrive(came)
-            back_three.append(settle_last(back_pieces[b - 1], came))
+        if b == 0:
+            for later in spread_three[1:] + spread_down[1:]:
+                later.first = arrive(later.first)
+                later.second_step()
+        else:
+            back_three.append(settle_last(back_pieces[b - 1], arrive(came)))
         grad_gate, grad_upper = hold((parts[1], parts[2]))
         back_pieces.append(glu_back(b, grad_gate, grad_upper, w_gate, w_up))
         mark(back_pieces[b][0])
         came = settle_first(back_pieces[b])
-        if b + 1 < count:
-            spread_three[b + 1].last = arrive(spread_three[b + 1].last)
+        if b == 0:
+            for later in spread_three[1:] + spread_down[1:]:
+                later.last = arrive(later.last)
 
     def flat(values):
         return values.reshape(-1, values.shape[-1])
 
-    hidden, grad_gate, grad_upper, frames_three = parts
+    hidden, grad_gate, grad_upper, frames_three, down_in = parts
     raw_w_down = dot(flat(hold(down_in)), flat(hidden), 0, 0).astype(bf16)
     grad_w_down = sum_over_clips(raw_w_down, 0)
     mark(raw_w_down)
@@ -839,13 +856,14 @@
             grad_w_gate = sum_over_clips(raw_w_gate, 0)
             mark(raw_w_gate)
 
-    branch = dot(flat(hold(hidden)), w_down, 1, 0).astype(bf16)
-    mark(branch)
-    branch = lax.psum_scatter(
-        branch.reshape(count, size * rows, width), "mp", scatter_dimension=1, tiled=True
-    )
-    grad_memory = jnp.stack(grad_memory)
+    grad_memory = jnp.stack(hold(grad_memory))
+    mark(grad_memory)
     grad_memory = trade([grad_memory[:, k] for k in range(size)])
+    lefts = jnp.stack([joined(hold(part), 0) for part in (normed_two, cross_in, self_in)])
+    rights = jnp.stack([joined(part, 1) for part in (grad_cross_query, cross_mixed, mixed)])
+    other_raws = whole_grad(jnp.stack([1 - core]), groups, lefts, rights, [])
+    mark(other_raws)
+    other_raws = swap(other_raws, "dp", 1)
 
     w_self = w_turned.T
     grad_self, grad_front, back_one = [], [], []
@@ -864,46 +882,57 @@
         grad_front.append(joined([grad_front_key, grad_front_value], 0))
         mark(grads)
         if b:
-            came = arrive(came)
-            back_one.append(settle_last(pieces, came))
+            raws_terms = settle_last(raws_pieces, arrive(raws_came))
         pieces = cut(dot(hold(grad_self[b]), w_turned, 0, 0).astype(bf16))
         mark(*pieces)
         came = settle_first(pieces)
         if b == 0:
+            grad_w_down = arrive(grad_w_down)
             raw_w_up = dot(flat(hold(frames_three)), flat(grad_upper), 0, 0).astype(bf16)
             grad_w_up = sum_over_clips(raw_w_up, 0)
             mark(raw_w_up)
+            back_one.append(settle_last(pieces, arrive(came)))
+            raws = whole_grad(jnp.stack([core]), groups, lefts, rights, [arrive(other_raws)])
+            mark(raws)
+            raws_pieces = cut(raws.reshape(-1, local))
+            raws_came = settle_first(raws_pieces)
+            branch = dot(flat(hold(hidden)), w_down, 1, 0).astype(bf16)
+            mark(branch)
+            branch = branch.reshape(count, size * rows, width)
+            branch = lax.psum_scatter(branch, "mp", scatter_dimension=1, tiled=True)
 
     grad_front = joined(grad_front, 1)
     turned_grads = joined(hold(grad_self), 1)
     raw_w_self = dot(flat(frames_one), turned_grads, 0, 1)
     filled = joined([jnp.zeros((local, count), bf16), grad_front], 0)
     raw_w_self = raw_w_self + dot(prefix_low, filled, 0, 1)
-    low_w_self = raw_w_self.astype(bf16).reshape(groups, -1, 3 * local)
+    mark(raw_w_self)
+    grad_memory = total(hold(grad_memory)).astype(bf16)
+    grad_memory = joined([grad_memory[b] for b in clips], 1)
+    tokens = prompt.reshape(-1, prompt.shape[-1])
+    low_w_self = joined(
+        [
+            raw_w_self.astype(bf16).reshape(groups, -1, 3 * local),
+            joined(
+                [
+                    dot(tokens, part, 0, 1).astype(bf16).reshape(groups, -1, local)
+                    for part in jnp.split(grad_memory, 2, axis=0)
+                ],
+                1,
+            ),
+        ],
+        2,
+    )
     mark(low_w_self)
     mine, other = core_half(low_w_self)
     back_one.append(settle_last(pieces, arrive(came)))
-
-    lefts = jnp.stack([joined(hold(part), 0) for part in (normed_two, cross_in, self_in)])
-    rights = jnp.stack([joined(part, 1) for part in (grad_cross_query, cross_mixed, mixed)])
-    other_raws = whole_grad(jnp.stack([1 - core]), groups, lefts, rights, [])
-    mark(other_raws)
-    other_raws = swap(other_raws, "dp", 1)
+    grad_w_gate = arrive(grad_w_gate)
+    raws = total(hold(raws_terms)).astype(bf16).reshape(groups // 2, -1, local)
+    mark(raws)
+    raws = chips_sum(raws).reshape(3, -1, local)
     low_w_self = plus(mine, arrive(other))
     mark(low_w_self)
     grad_w_self = chips_sum(low_w_self)
-
-    grad_memory = total(arrive(grad_memory)).astype(bf16)
-    grad_memory = joined([grad_memory[b] for b in clips], 1)
-    grad_c_memory = dot(prompt.reshape(-1, prompt.shape[-1]), grad_memory, 0, 1).astype(bf16)
-    mark(grad_c_memory)
-    grad_c_memory = sum_over_clips(grad_c_memory, 0)
-
-    raws = whole_grad(jnp.stack([core]), groups, lefts, rights, [arrive(other_raws)])
-    mark(raws)
-    pieces = [raws[k].reshape(-1, local) for k in range(size)]
-    pieces = cut(joined(pieces, 0))
-    came = settle_first(pieces)
 
     small = []
     wide_w_self = w_self.astype(f32)
@@ -926,13 +955,7 @@
     grad_picked = norm_backward(back_prefix, prefix_normal, prefix_scale, gain_one)
     spots = jnp.arange(groups)[:, None, None] == there
     spots = jnp.where(spots, grad_picked[None], 0.0).reshape(groups * count, width)
-    small = joined([jnp.stack(small), spots], 0)
-    mark(small)
-    raws = total(settle_last(pieces, arrive(came)))
-    raws = raws.astype(bf16).reshape(groups // 2, -1, local)
-    mark(raws)
-    raws = chips_sum(raws).reshape(3, -1, local)
-    small = all_sum(small)
+    small = all_sum(joined([jnp.stack(small), spots], 0))
     all_steps = small[6, : groups * count]
     matches = jnp.arange(table.shape[0])[:, None].astype(f32) == all_steps[None, :]
     grad_table = jnp.dot(matches.astype(f32), small[7:], precision=lax.Precision.HIGHEST)
@@ -941,7 +964,12 @@
     grad_frames = [
         grad_one[b] + norm_backward(back_one[b], ones[b][1], ones[b][2], gain_one) for b in clips
     ]
+    mark(grad_table, *grad_frames)
+    grad_w_up = arrive(grad_w_up)
+    branch = arrive(branch)
     output = [second[b] + branch[b].astype(f32) for b in clips]
+
+    depth_c = prompt.shape[-1] // groups
 
     def wide(value):
         return value.astype(f32)
@@ -958,11 +986,11 @@
         small[5],
         grad_w_self[:, :local],
         grad_w_self[:, local : 2 * local],
-        grad_w_self[:, 2 * local :],
+        grad_w_self[:, 2 * local : 3 * local],
         raws[2].T,
         raws[0],
-        wide(grad_c_memory[:, :local]),
-        wide(grad_c_memory[:, local:]),
+        grad_w_self[: depth_c, 3 * local :],
+        grad_w_self[depth_c:, 3 * local :],
         raws[1].T,
         wide(grad_w_gate),
         wide(grad_w_up),

time: 1040 us -> 857 us (0.82)
  waiting for transfers between devices: 395 us -> 198 us
  matrix products: 115 us -> 131 us
  local copies, waits for them, and re-layouts: 118 us -> 102 us
  Pallas kernels: 194 us -> 205 us
    reduce_scatter x3, waiting for transfers between devices: 103 us -> 0.01 us  [sum_over_clips(): lax.psum_scatter(values.astype(bf16), 'dp', scatter_dimension=axis, tiled...]
    reduce_scatter x1, waiting for transfers between devices: 66.6 us -> 0.01 us  [shards(): branch = lax.psum_scatter(branch, 'mp', scatter_dimension=1, tiled=True)]
    all_gather x3 -> x2, waiting for transfers between devices: 50.2 us -> 0.01 us  [the longest x1 0.01 us: shards(): c_query_all = lax.all_gather(side, 'dp', axis=0, tiled=True)]
    ppermute x75 -> x86, waiting for transfers between devices: 173 us -> 198 us  [swap(): lax.ppermute(values, axis, [(i, i ^ k) for i in range(lax.axis_size(axis))])]
    unnamed x516 -> x419, local copies, waits for them, and re-layouts: 64.9 us -> 47 us
    dot_general x25 -> x26, matrix products: 109 us -> 126 us  [dot(): lax.dot_general(left, right, (((left_axis,), (right_axis,)), ((), ())), p...]
    ppermute x75 -> x86, starting transfers between devices: 92.5 us -> 92.8 us  [swap(): lax.ppermute(values, axis, [(i, i ^ k) for i in range(lax.axis_size(axis))])]
  transfers between devices with their start and end apart: 83 -> 92, of which waited for: 25 -> 26; matrix products, arithmetic and copies ran while one was open for 24% -> 33% of each run, Pallas kernels for 15% -> 23%
where the time goes in v4:
time: 857 us; the launch traced here: 840 us
  Pallas kernels  205 us (24%)
  waiting for transfers between devices  198 us (23%)
  matrix products  131 us (15%)
  local copies, waits for them, and re-layouts  102 us (12%)
  starting transfers between devices  93.9 us (11%)
  other arithmetic  93.3 us (11%)
  between operations  17.2 us (2%)
    ppermute x86, waiting for transfers between devices, swap(): lax.ppermute(values, axis, [(i, i ^ k) for i in range(lax.axis_size(axis))])  198 us
    dot_general x26, matrix products, dot(): lax.dot_general(left, right, (((left_axis,), (right_axis,)), ((), ())), p...  126 us
    ppermute x86, starting transfers between devices, swap(): lax.ppermute(values, axis, [(i, i ^ k) for i in range(lax.axis_size(axis))])  92.8 us
    unnamed x419, local copies, waits for them, and re-layouts  47 us
    pallas_call x2, Pallas kernels, glu(): pl.pallas_call(functools.partial(glu_kernel, size, len(pieces)), grid=(hi...  43.9 us
    pallas_call x2, Pallas kernels, self_backward(): pl.pallas_call(functools.partial(self_backward_kernel, min(256, frames)),...  36.6 us
    pallas_call x2, Pallas kernels, glu_back(): pl.pallas_call(functools.partial(glu_back_kernel, size), grid=(width // b...  30.1 us
    pallas_call x2, Pallas kernels, whole_grad(): pl.pallas_call(functools.partial(whole_grad_kernel, chips, len(earlier)),...  29.9 us
  transfers between devices with their start and end apart: 92, of which 26 were waited for; matrix products, arithmetic and copies ran while one was open for 33% of the time, Pallas kernels for 23%

profile of v4, /device:TPU:0, one launch (start us, length us, event | category | flops | bytes accessed | tf_op | source)
XLA Modules:
  0.0 840.3 jit_solution(6254763012398290988)
XLA Ops:
  36.0 3.8 collective-permute-done.5
  66.1 10.4 %collective-permute-done.2.refs_3_ = bf16[128,1536]{1,0:T(8,128)(2,1)} collective-permute-done((bf16[128,1536]{1,0:T(8,128)(2,1)}, bf16[128,1536]{1,0:T(8,128)(2,1)}, u32[]{:S(2)}, u32[]{:S(2)}) %collective-permute-start.2) | collective-permute-done | bytes 393248 | tf_op jit(solution)/shard_map/ppermute | solution.py:48
  78.6 8.4 %project.2 = (bf16[1152,1024]{1,0:T(8,128)(2,1)S(1)}, bf16[2,1024,1536]{2,1,0:T(8,128)(2,1)}) custom-call(bf16[1152,1536]{1,0:T(8,128)(2,1)} %pad_maximum_fusion.3.w_ref, f32[32,1024]{1,0:T(8,128)S(1)} %get-tuple-element.518.cos_ref, f32[32,1024]{1,0:T(8,128)S(1)} %get-tuple-element.517.sin_ref, bf16[256,1536]{1,0:T(8,128)(2,1)S(1)} %fusion.26.refs_0_, ...), custom_call_target="tpu_custom_call" | custom-call | flops 3623878656 | bytes 12189696 | tf_op jit(solution)/shard_map/project/pallas_call | solution.py:449
  98.3 10.5 %self_forward.2 = (bf16[384,1024]{1,0:T(8,128)(2,1)S(1)}, f32[6,1,1024]{2,1,0:T(1,128)S(1)}) custom-call(bf16[1152,1024]{1,0:T(8,128)(2,1)S(1)} %copy-done.48, bf16[1152,1024]{1,0:T(8,128)(2,1)S(1)} %copy-done.48, bf16[1152,1024]{1,0:T(8,128)(2,1)S(1)} %copy-done.48, bf16[384,1]{1,0:T(8,128)(2,1)S(1)} %copy-done.38, bf16[384,1]{1,0:T(8,128)(2,1)S(1)} %copy-done.36), custom_call_target="tpu_custom_call" | custom-call | flops 6442450944 | bytes 3145728 | tf_op jit(solution)/shard_map/self_forward/pallas_call | solution.py:286
  117.5 9.0 %project.3 = (bf16[1152,1024]{1,0:T(8,128)(2,1)S(1)}, bf16[2,1024,1536]{2,1,0:T(8,128)(2,1)}) custom-call(bf16[1152,1536]{1,0:T(8,128)(2,1)} %pad_maximum_fusion.3.w_ref, f32[32,1024]{1,0:T(8,128)S(1)} %get-tuple-element.518.cos_ref, f32[32,1024]{1,0:T(8,128)S(1)} %get-tuple-element.517.sin_ref, ...), custom_call_target="tpu_custom_call", output_to_operand_aliasing={{1}: (8, {})} | custom-call | flops 3623878656 | bytes 12189696 | tf_op jit(solution)/shard_map/project/pallas_call | solution.py:449
  126.5 7.5 collective-permute-done.20
  148.6 10.5 %self_forward.3 = (bf16[384,1024]{1,0:T(8,128)(2,1)S(1)}, f32[6,1,1024]{2,1,0:T(1,128)S(1)}) custom-call(bf16[1152,1024]{1,0:T(8,128)(2,1)S(1)} %copy-done.42, bf16[1152,1024]{1,0:T(8,128)(2,1)S(1)} %copy-done.42, bf16[1152,1024]{1,0:T(8,128)(2,1)S(1)} %copy-done.42, bf16[384,1]{1,0:T(8,128)(2,1)S(1)} %copy-done.34, bf16[384,1]{1,0:T(8,128)(2,1)S(1)} %get-tuple-element.511.pv_ref), custom_call_target="tpu_custom_call" | custom-call | flops 6442450944 | bytes 3145728 | tf_op jit(solution)/shard_map/self_forward/pallas_call | solution.py:286
  177.5 3.9 fusion.3.q_ref
  181.5 6.5 cross_forward.2
  193.9 6.3 cross_forward.3
  202.9 4.5 fusion.95
  214.7 14.5 %collective-permute-done.30.refs_1_ = bf16[256,1536]{1,0:T(8,128)(2,1)S(1)} collective-permute-done((bf16[256,1536]{1,0:T(8,128)(2,1)S(1)}, bf16[256,1536]{1,0:T(8,128)(2,1)S(1)}, u32[]{:S(2)}, u32[]{:S(2)}) %collective-permute-start.30) | collective-permute-done | bytes 786464 | tf_op jit(solution)/shard_map/ppermute | solution.py:48
  236.3 5.0 collective-permute-done.36.refs_3_
  241.7 21.6 %glu.2 = (bf16[2,1024,1536]{2,1,0:T(8,128)(2,1)}, bf16[2,1024,1536]{2,1,0:T(8,128)(2,1)}, bf16[2,1024,1536]{2,1,0:T(8,128)(2,1)}, bf16[2,1024,1536]{2,1,0:T(8,128)(2,1)}, bf16[2,1024,1536]{2,1,0:T(8,128)(2,1)}) custom-call(s32[4]{0:T(128)S(1)} %get-tuple-element.534.n_ref, bf16[1536,1536]{1,0:T(8,128)(2,1)} %gate_ref.7, bf16[1536,1536]{1,0:T(8,128)(2,1)} %up_ref.7, ...), custom_call_target="tpu_custom_call" | custom-call | flops 14495514624 | bytes 36175872 | tf_op jit(solution)/shard_map/glu/pallas_call | solution.py:509
  263.3 9.5 %collective-permute-done.34.refs_1_ = bf16[256,1536]{1,0:T(8,128)(2,1)S(1)} collective-permute-done((bf16[256,1536]{1,0:T(8,128)(2,1)S(1)}, bf16[256,1536]{1,0:T(8,128)(2,1)S(1)}, u32[]{:S(2)}, u32[]{:S(2)}) %collective-permute-start.34) | collective-permute-done | bytes 786464 | tf_op jit(solution)/shard_map/ppermute | solution.py:48
  277.1 14.6 %glu_back.2 = (bf16[256,1536]{1,0:T(8,128)(2,1)S(1)}, bf16[256,1536]{1,0:T(8,128)(2,1)S(1)}, bf16[256,1536]{1,0:T(8,128)(2,1)S(1)}, bf16[128,1536]{1,0:T(8,128)(2,1)S(1)}, bf16[128,1536]{1,0:T(8,128)(2,1)S(1)}) custom-call(bf16[2,1024,1536]{2,1,0:T(8,128)(2,1)} %get-tuple-element.297.dg_ref.refs_11_, ...), custom_call_target="tpu_custom_call" | custom-call | flops 9663676416 | bytes 18874368 | tf_op jit(solution)/shard_map/glu_back/pallas_call | solution.py:556
  295.5 22.3 %glu.3 = (bf16[2,1024,1536]{2,1,0:T(8,128)(2,1)}, bf16[2,1024,1536]{2,1,0:T(8,128)(2,1)}, bf16[2,1024,1536]{2,1,0:T(8,128)(2,1)}, bf16[2,1024,1536]{2,1,0:T(8,128)(2,1)}, bf16[2,1024,1536]{2,1,0:T(8,128)(2,1)}) custom-call(s32[4]{0:T(128)S(1)} %get-tuple-element.534.n_ref, ...), custom_call_target="tpu_custom_call", output_to_operand_aliasing={{0}: (14, {}), {1}: (15, {}), {2}: (16, {}), {3}: (17, {}),... | custom-call | flops 14495514624 | bytes 36175872 | tf_op jit(solution)/shard_map/glu/pallas_call | solution.py:509
  317.8 15.4 %glu_back.3 = (bf16[256,1536]{1,0:T(8,128)(2,1)S(1)}, bf16[256,1536]{1,0:T(8,128)(2,1)S(1)}, bf16[256,1536]{1,0:T(8,128)(2,1)S(1)}, bf16[128,1536]{1,0:T(8,128)(2,1)}, bf16[128,1536]{1,0:T(8,128)(2,1)}) custom-call(bf16[2,1024,1536]{2,1,0:T(8,128)(2,1)} %get-tuple-element.323.dg_ref, bf16[2,1024,1536]{2,1,0:T(8,128)(2,1)} %get-tuple-element.324.du_ref, ...), custom_call_target="tpu_custom_call" | custom-call | flops 9663676416 | bytes 18874368 | tf_op jit(solution)/shard_map/glu_back/pallas_call | solution.py:556
  337.0 15.5 %bitcast_convert_fusion.2 = bf16[1536,1536]{1,0:T(8,128)(2,1)} fusion(bf16[2,1024,1536]{2,1,0:T(8,128)(2,1)} %get-tuple-element.329, bf16[2,1024,1536]{2,1,0:T(8,128)(2,1)} %get-tuple-element.370), kind=kOutput, calls=%fused_computation.4 | convolution fusion | flops 9666035712 | bytes 17301504 | tf_op jit(solution)/shard_map/dot_general | solution.py:22
  363.9 12.1 %collective-permute-done.47 = bf16[256,1536]{1,0:T(8,128)(2,1)S(1)} collective-permute-done((bf16[256,1536]{1,0:T(8,128)(2,1)S(1)}, bf16[256,1536]{1,0:T(8,128)(2,1)S(1)}, u32[]{:S(2)}, u32[]{:S(2)}) %collective-permute-start.47) | collective-permute-done | bytes 786464 | tf_op jit(solution)/shard_map/ppermute | solution.py:48
  379.4 4.1 convolution_convert_fusion.6.g_ref
  383.7 6.5 cross_backward.2
  390.3 4.8 multiply_reduce_fusion.3
  402.6 11.6 %bitcast_convert_fusion.1 = bf16[1536,1536]{1,0:T(8,128)(2,1)} fusion(bf16[2,1024,1536]{2,1,0:T(8,128)(2,1)S(1)} %bitcast.295, bf16[2,1024,1536]{2,1,0:T(8,128)(2,1)S(1)} %bitcast.293), kind=kOutput, calls=%fused_computation.3 | convolution fusion | flops 9666035712 | bytes 17301504 | tf_op jit(solution)/shard_map/dot_general | solution.py:22
  425.9 3.9 convolution_convert_fusion.4.g_ref
  429.8 6.5 cross_backward.3
  438.1 4.3 multiply_reduce_fusion.2
  456.2 14.6 %whole_grad.2 = bf16[4,4,3,192,384]{4,3,2,1,0:T(8,128)(2,1)} custom-call(s32[1]{0:T(128)} %bitcast.45.core_ref, bf16[3,512,1536]{2,1,0:T(8,128)(2,1)S(1)} %pad_maximum_fusion.1.x_ref, bf16[3,1536,512]{2,1,0:T(8,128)(2,1)} %pad_maximum_fusion.2.y_ref), custom_call_target="tpu_custom_call" | custom-call | flops 3623878656 | bytes 33030144 | tf_op jit(solution)/shard_map/whole_grad/pallas_call | solution.py:595
  472.4 18.3 %self_backward.2 = (bf16[3,384,1024]{2,1,0:T(8,128)(2,1)S(1)}, bf16[384,1]{1,0:T(8,128)(2,1)S(1)}, bf16[384,1]{1,0:T(8,128)(2,1)S(1)}) custom-call(bf16[1152,1024]{1,0:T(8,128)(2,1)} %copy-done.47, bf16[1152,1024]{1,0:T(8,128)(2,1)} %copy-done.47, bf16[1152,1024]{1,0:T(8,128)(2,1)} %copy-done.47, bf16[384,1024]{1,0:T(8,128)(2,1)S(1)} %pad_maximum_fusion.23.g_ref, ...), custom_call_target="tpu_custom_call" | custom-call | flops 16106127360 | bytes 7864320 | tf_op jit(solution)/shard_map/self_backward/pallas_call | solution.py:310
  490.7 4.6 convolution_convert_fusion.2
  498.1 15.9 %bitcast_convert_fusion = bf16[1536,1536]{1,0:T(8,128)(2,1)} fusion(bf16[2,1024,1536]{2,1,0:T(8,128)(2,1)} %get-tuple-element.366, bf16[2,1024,1536]{2,1,0:T(8,128)(2,1)} %get-tuple-element.324.du_ref), kind=kOutput, calls=%fused_computation.2 | convolution fusion | flops 9666035712 | bytes 17301504 | tf_op jit(solution)/shard_map/dot_general | solution.py:22
  533.5 15.3 %whole_grad.3 = bf16[4,4,3,192,384]{4,3,2,1,0:T(8,128)(2,1)} custom-call(s32[1]{0:T(128)} %bitcast.30.core_ref, bf16[3,512,1536]{2,1,0:T(8,128)(2,1)S(1)} %copy-done.3, bf16[3,1536,512]{2,1,0:T(8,128)(2,1)} %pad_maximum_fusion.2.y_ref, bf16[4,4,3,192,384]{4,3,2,1,0:T(8,128)(2,1)} %collective-permute-done.52.refs_0_), custom_call_target="tpu_custom_call" | custom-call | flops 3623878656 | bytes 33030144 | tf_op jit(solution)/shard_map/whole_grad/pallas_call | solution.py:595
  548.8 15.2 %convolution_convert_fusion = bf16[2048,1536]{1,0:T(8,128)(2,1)} fusion(bf16[2048,1536]{1,0:T(8,128)(2,1)} %bitcast.291, bf16[1536,1536]{1,0:T(8,128)(2,1)} %down_ref.3), kind=kOutput, calls=%fused_computation.6 | convolution fusion | flops 9666822144 | bytes 17301504 | tf_op jit(solution)/shard_map/dot_general | solution.py:22
  571.2 18.3 %self_backward.3 = (bf16[3,384,1024]{2,1,0:T(8,128)(2,1)S(1)}, bf16[384,1]{1,0:T(8,128)(2,1)S(1)}, bf16[384,1]{1,0:T(8,128)(2,1)S(1)}) custom-call(bf16[1152,1024]{1,0:T(8,128)(2,1)} %copy-done.41, bf16[1152,1024]{1,0:T(8,128)(2,1)} %copy-done.41, bf16[1152,1024]{1,0:T(8,128)(2,1)} %copy-done.41, bf16[384,1024]{1,0:T(8,128)(2,1)S(1)} %pad_maximum_fusion.24.g_ref, ...), custom_call_target="tpu_custom_call" | custom-call | flops 16106127360 | bytes 7864320 | tf_op jit(solution)/shard_map/self_backward/pallas_call | solution.py:310
  601.4 7.1 convolution_convert_fusion.1
  614.4 7.6 fusion.97
  636.9 3.6 copy.93
  656.1 6.1 collective-permute-done.64
  668.9 3.4 collective-permute-done.66
  682.8 5.2 fusion.44
  689.1 9.6 %collective-permute-done.72 = bf16[256,1536]{1,0:T(8,128)(2,1)} collective-permute-done((bf16[256,1536]{1,0:T(8,128)(2,1)}, bf16[256,1536]{1,0:T(8,128)(2,1)}, u32[]{:S(2)}, u32[]{:S(2)}) %collective-permute-start.72) | collective-permute-done | bytes 786464 | tf_op jit(solution)/shard_map/ppermute | solution.py:48
  698.7 7.0 collective-permute-done.73
  709.1 3.5 fusion.23
  712.6 30.2 %collective-permute-done.79 = bf16[2304,384]{1,0:T(8,128)(2,1)S(1)} collective-permute-done((bf16[2304,384]{1,0:T(8,128)(2,1)S(1)}, bf16[2304,384]{1,0:T(8,128)(2,1)S(1)}, u32[]{:S(2)}, u32[]{:S(2)}) %collective-permute-start.79) | collective-permute-done | bytes 1769504 | tf_op jit(solution)/shard_map/ppermute | solution.py:48
  752.2 13.9 %collective-permute-done.83 = bf16[576,384]{1,0:T(8,128)(2,1)S(1)} collective-permute-done((bf16[576,384]{1,0:T(8,128)(2,1)S(1)}, bf16[576,384]{1,0:T(8,128)(2,1)S(1)}, u32[]{:S(2)}, u32[]{:S(2)}) %collective-permute-start.83) | collective-permute-done | bytes 442400 | tf_op jit(solution)/shard_map/ppermute | solution.py:48
  768.5 8.3 collective-permute-done.84
  779.3 11.9 %collective-permute-done.80 = bf16[192,1536]{1,0:T(8,128)(2,1)S(1)} collective-permute-done((bf16[192,1536]{1,0:T(8,128)(2,1)S(1)}, bf16[192,1536]{1,0:T(8,128)(2,1)S(1)}, u32[]{:S(2)}, u32[]{:S(2)}) %collective-permute-start.80) | collective-permute-done | bytes 589856 | tf_op jit(solution)/shard_map/ppermute | solution.py:48
  791.2 33.8 %collective-permute-done.81 = bf16[192,1536]{1,0:T(8,128)(2,1)S(1)} collective-permute-done((bf16[192,1536]{1,0:T(8,128)(2,1)S(1)}, bf16[192,1536]{1,0:T(8,128)(2,1)S(1)}, u32[]{:S(2)}, u32[]{:S(2)}) %collective-permute-start.81) | collective-permute-done | bytes 589856 | tf_op jit(solution)/shard_map/ppermute | solution.py:48
  (809 shorter events, 315.8 us)
Async XLA Ops:
  7.2 170.3 %all-gather.3.cloned.1.call-start = ((), (), s32[]{:S(2)}) async-start(), calls=%async_computation.4 | async-start | bytes 5308416 | tf_op jit(solution)/shard_map/all_gather | solution.py:698
  44.4 158.5 %all-gather.5.cloned.1.call-start = ((), (), s32[]{:S(2)}) async-start(), calls=%async_computation.5 | async-start | bytes 5308416 | tf_op jit(solution)/shard_map/all_gather | solution.py:728
  48.7 39.2 %collective-permute-start.10 = (bf16[256,1536]{1,0:T(8,128)(2,1)S(1)}, bf16[256,1536]{1,0:T(8,128)(2,1)S(1)}, u32[]{:S(2)}, u32[]{:S(2)}) collective-permute-start(bf16[256,1536]{1,0:T(8,128)(2,1)S(1)} %fusion.19.refs_0_), channel_id=1, source_target_pairs={{0,1},{1,0},{2,3},{3,2},{4,5},{5,4},{6,7},{7,6},{8,9},{9,8},{10,11... | collective-permute-start | bytes 2359304 | tf_op jit(solution)/shard_map/ppermute | solution.py:48
  49.9 39.6 %collective-permute-start.11 = (bf16[256,1536]{1,0:T(8,128)(2,1)S(1)}, bf16[256,1536]{1,0:T(8,128)(2,1)}, u32[]{:S(2)}, u32[]{:S(2)}) collective-permute-start(bf16[256,1536]{1,0:T(8,128)(2,1)S(1)} %fusion.19.refs_0_), channel_id=1, source_target_pairs={{0,2},{1,3},{2,0},{3,1},{4,6},{5,7},{6,4},{7,5},{8,10},{9,11},{10,... | collective-permute-start | bytes 2359304 | tf_op jit(solution)/shard_map/ppermute | solution.py:48
  50.7 25.8 %collective-permute-start.2 = (bf16[128,1536]{1,0:T(8,128)(2,1)}, bf16[128,1536]{1,0:T(8,128)(2,1)}, u32[]{:S(2)}, u32[]{:S(2)}) collective-permute-start(bf16[128,1536]{1,0:T(8,128)(2,1)} %slice.266), channel_id=1, source_target_pairs={{0,2},{1,3},{2,0},{3,1},{4,6},{5,7},{6,4},{7,5},{8,10},{9,11},{10,... | collective-permute-start | bytes 1179656 | tf_op jit(solution)/shard_map/ppermute | solution.py:48
  56.9 35.6 %collective-permute-start.7 = (bf16[192,384]{1,0:T(8,128)(2,1)}, bf16[192,384]{1,0:T(8,128)(2,1)}, u32[]{:S(2)}, u32[]{:S(2)}) collective-permute-start(bf16[192,384]{1,0:T(8,128)(2,1)} %dynamic-slice_bitcast_fusion.7), channel_id=1, source_target_pairs={{0,1},{1,0},{2,3},{3,2},{4,5},{5,4},{6,7},{7,6},{8,9},{9,8},{10,11... | collective-permute-start | bytes 442376 | tf_op jit(solution)/shard_map/ppermute | solution.py:48
  108.9 28.2 %collective-permute-start.15 = (bf16[2,768,128]{2,1,0:T(8,128)(2,1)}, bf16[2,768,128]{2,1,0:T(8,128)(2,1)}, u32[]{:S(2)}, u32[]{:S(2)}) collective-permute-start(bf16[2,768,128]{2,1,0:T(8,128)(2,1)} %pad_maximum_fusion.29), channel_id=1, source_target_pairs={{0,1},{1,0},{2,3},{3,2},{4,5},{5,4},{6,7},{7,6},{8,9},{9,8},{10,11... | collective-permute-start | bytes 1179656 | tf_op jit(solution)/shard_map/ppermute | solution.py:48
  110.5 387.6 %reduce-scatter.5.cloned.1.call-start = ((), (), s32[]{:S(2)}) async-start(), calls=%async_computation.6 | async-start | bytes 5308416 | tf_op jit(solution)/shard_map/reduce_scatter | solution.py:632
  111.4 28.8 %collective-permute-start.16 = (bf16[2,768,128]{2,1,0:T(8,128)(2,1)}, bf16[2,768,128]{2,1,0:T(8,128)(2,1)S(1)}, u32[]{:S(2)}, u32[]{:S(2)}) collective-permute-start(bf16[2,768,128]{2,1,0:T(8,128)(2,1)} %pad_maximum_fusion.29), channel_id=1, source_target_pairs={{0,2},{1,3},{2,0},{3,1},{4,6},{5,7},{6,4},{7,5},{8,10},{9,11},{10,... | collective-permute-start | bytes 1179656 | tf_op jit(solution)/shard_map/ppermute | solution.py:48
  111.9 29.2 %collective-permute-start.17 = (bf16[2,768,128]{2,1,0:T(8,128)(2,1)}, bf16[2,768,128]{2,1,0:T(8,128)(2,1)}, u32[]{:S(2)}, u32[]{:S(2)}) collective-permute-start(bf16[2,768,128]{2,1,0:T(8,128)(2,1)} %pad_maximum_fusion.29), channel_id=1, source_target_pairs={{0,3},{1,2},{2,1},{3,0},{4,7},{5,6},{6,5},{7,4},{8,11},{9,10},{10,... | collective-permute-start | bytes 1179656 | tf_op jit(solution)/shard_map/ppermute | solution.py:48
  145.1 43.5 %collective-permute-start.28 = (bf16[256,1536]{1,0:T(8,128)(2,1)S(1)}, bf16[256,1536]{1,0:T(8,128)(2,1)}, u32[]{:S(2)}, u32[]{:S(2)}) collective-permute-start(bf16[256,1536]{1,0:T(8,128)(2,1)S(1)} %get-tuple-element.271.refs_5_), channel_id=1, source_target_pairs={{0,1},{1,0},{2,3},{3,2},{4,5},{5,4},{6,7},{7,6},{8,9},{9,8},{10,11... | collective-permute-start | bytes 2359304 | tf_op jit(solution)/shard_map/ppermute | solution.py:48
  146.9 41.7 %collective-permute-start.29 = (bf16[256,1536]{1,0:T(8,128)(2,1)S(1)}, bf16[256,1536]{1,0:T(8,128)(2,1)}, u32[]{:S(2)}, u32[]{:S(2)}) collective-permute-start(bf16[256,1536]{1,0:T(8,128)(2,1)S(1)} %get-tuple-element.271.refs_5_), channel_id=1, source_target_pairs={{0,2},{1,3},{2,0},{3,1},{4,6},{5,7},{6,4},{7,5},{8,10},{9,11},{10,... | collective-permute-start | bytes 2359304 | tf_op jit(solution)/shard_map/ppermute | solution.py:48
  234.0 38.9 %collective-permute-start.40 = (bf16[256,1536]{1,0:T(8,128)(2,1)S(1)}, bf16[256,1536]{1,0:T(8,128)(2,1)S(1)}, u32[]{:S(2)}, u32[]{:S(2)}) collective-permute-start(bf16[256,1536]{1,0:T(8,128)(2,1)S(1)} %get-tuple-element.294.refs_5_), channel_id=1, source_target_pairs={{0,1},{1,0},{2,3},{3,2},{4,5},{5,4},{6,7},{7,6},{8,9},{9,8},{10,11... | collective-permute-start | bytes 2359304 | tf_op jit(solution)/shard_map/ppermute | solution.py:48
  234.3 38.6 %collective-permute-start.41 = (bf16[256,1536]{1,0:T(8,128)(2,1)S(1)}, bf16[256,1536]{1,0:T(8,128)(2,1)S(1)}, u32[]{:S(2)}, u32[]{:S(2)}) collective-permute-start(bf16[256,1536]{1,0:T(8,128)(2,1)S(1)} %get-tuple-element.294.refs_5_), channel_id=1, source_target_pairs={{0,2},{1,3},{2,0},{3,1},{4,6},{5,7},{6,4},{7,5},{8,10},{9,11},{10,... | collective-permute-start | bytes 2359304 | tf_op jit(solution)/shard_map/ppermute | solution.py:48
  236.1 36.8 %collective-permute-start.34 = (bf16[256,1536]{1,0:T(8,128)(2,1)S(1)}, bf16[256,1536]{1,0:T(8,128)(2,1)S(1)}, u32[]{:S(2)}, u32[]{:S(2)}) collective-permute-start(bf16[256,1536]{1,0:T(8,128)(2,1)S(1)} %add_convert_fusion.1.refs_0_), channel_id=1, source_target_pairs={{0,1},{1,0},{2,3},{3,2},{4,5},{5,4},{6,7},{7,6},{8,9},{9,8},{10,11... | collective-permute-start | bytes 2359304 | tf_op jit(solution)/shard_map/ppermute | solution.py:48
  241.4 31.5 %collective-permute-start.35 = (bf16[256,1536]{1,0:T(8,128)(2,1)S(1)}, bf16[256,1536]{1,0:T(8,128)(2,1)S(1)}, u32[]{:S(2)}, u32[]{:S(2)}) collective-permute-start(bf16[256,1536]{1,0:T(8,128)(2,1)S(1)} %add_convert_fusion.1.refs_0_), channel_id=1, source_target_pairs={{0,2},{1,3},{2,0},{3,1},{4,6},{5,7},{6,4},{7,5},{8,10},{9,11},{10,... | collective-permute-start | bytes 2359304 | tf_op jit(solution)/shard_map/ppermute | solution.py:48
  291.8 26.0 %collective-permute-start.44 = (bf16[128,1536]{1,0:T(8,128)(2,1)S(1)}, bf16[128,1536]{1,0:T(8,128)(2,1)S(1)}, u32[]{:S(2)}, u32[]{:S(2)}) collective-permute-start(bf16[128,1536]{1,0:T(8,128)(2,1)S(1)} %get-tuple-element.316), channel_id=1, source_target_pairs={{0,2},{1,3},{2,0},{3,1},{4,6},{5,7},{6,4},{7,5},{8,10},{9,11},{10,... | collective-permute-start | bytes 1179656 | tf_op jit(solution)/shard_map/ppermute | solution.py:48
  352.6 323.8 %reduce-scatter.11.cloned.1.call-start = ((), (), s32[]{:S(2)}) async-start(), calls=%async_computation.9 | async-start | bytes 5308416 | tf_op jit(solution)/shard_map/reduce_scatter | solution.py:632
  359.8 60.0 %collective-permute-start.51 = (bf16[256,1536]{1,0:T(8,128)(2,1)}, bf16[256,1536]{1,0:T(8,128)(2,1)}, u32[]{:S(2)}, u32[]{:S(2)}) collective-permute-start(bf16[256,1536]{1,0:T(8,128)(2,1)} %pad_maximum_fusion.21), channel_id=1, source_target_pairs={{0,2},{1,3},{2,0},{3,1},{4,6},{5,7},{6,4},{7,5},{8,10},{9,11},{10,... | collective-permute-start | bytes 2359304 | tf_op jit(solution)/shard_map/ppermute | solution.py:48
  362.4 57.5 %collective-permute-start.50 = (bf16[256,1536]{1,0:T(8,128)(2,1)}, bf16[256,1536]{1,0:T(8,128)(2,1)}, u32[]{:S(2)}, u32[]{:S(2)}) collective-permute-start(bf16[256,1536]{1,0:T(8,128)(2,1)} %pad_maximum_fusion.20), channel_id=1, source_target_pairs={{0,1},{1,0},{2,3},{3,2},{4,5},{5,4},{6,7},{7,6},{8,9},{9,8},{10,11... | collective-permute-start | bytes 2359304 | tf_op jit(solution)/shard_map/ppermute | solution.py:48
  415.1 55.9 %collective-permute-start.53 = (bf16[384,256]{1,0:T(8,128)(2,1)}, bf16[384,256]{1,0:T(8,128)(2,1)}, u32[]{:S(2)}, u32[]{:S(2)}) collective-permute-start(bf16[384,256]{1,0:T(8,128)(2,1)} %get-tuple-element.499), channel_id=1, source_target_pairs={{0,1},{1,0},{2,3},{3,2},{4,5},{5,4},{6,7},{7,6},{8,9},{9,8},{10,11... | collective-permute-start | bytes 589832 | tf_op jit(solution)/shard_map/ppermute | solution.py:48
  416.3 54.8 %collective-permute-start.54 = (bf16[384,256]{1,0:T(8,128)(2,1)}, bf16[384,256]{1,0:T(8,128)(2,1)}, u32[]{:S(2)}, u32[]{:S(2)}) collective-permute-start(bf16[384,256]{1,0:T(8,128)(2,1)} %get-tuple-element.498), channel_id=1, source_target_pairs={{0,2},{1,3},{2,0},{3,1},{4,6},{5,7},{6,4},{7,5},{8,10},{9,11},{10,... | collective-permute-start | bytes 589832 | tf_op jit(solution)/shard_map/ppermute | solution.py:48
  416.8 54.2 %collective-permute-start.55 = (bf16[384,256]{1,0:T(8,128)(2,1)}, bf16[384,256]{1,0:T(8,128)(2,1)}, u32[]{:S(2)}, u32[]{:S(2)}) collective-permute-start(bf16[384,256]{1,0:T(8,128)(2,1)} %get-tuple-element.497), channel_id=1, source_target_pairs={{0,3},{1,2},{2,1},{3,0},{4,7},{5,6},{6,5},{7,4},{8,11},{9,10},{10,... | collective-permute-start | bytes 589832 | tf_op jit(solution)/shard_map/ppermute | solution.py:48
  418.6 408.3 %reduce-scatter.9.cloned.1.call-start = ((), (), s32[]{:S(2)}) async-start(), calls=%async_computation.8 | async-start | bytes 5308416 | tf_op jit(solution)/shard_map/reduce_scatter | solution.py:632
  470.9 59.2 %collective-permute-start.52 = (bf16[4,4,3,192,384]{4,3,2,1,0:T(8,128)(2,1)}, bf16[4,4,3,192,384]{4,3,2,1,0:T(8,128)(2,1)}, u32[]{:S(2)}, u32[]{:S(2)}) collective-permute-start(bf16[4,4,3,192,384]{4,3,2,1,0:T(8,128)(2,1)} %whole_grad.2), channel_id=1, source_target_pairs={{0,4},{4,0},{8,12},{12,8},{16,20},{20,16},{24,28},{28,24},{1,5},{5... | collective-permute-start | bytes 21233672 | tf_op jit(solution)/shard_map/ppermute | solution.py:48
  514.1 315.4 %reduce-scatter.7.cloned.1.call-start = ((), (), s32[]{:S(2)}) async-start(), calls=%async_computation.7 | async-start | bytes 7864320 | tf_op jit(solution)/shard_map/reduce_scatter | solution.py:902
  519.3 44.7 %collective-permute-start.58 = (bf16[384,256]{1,0:T(8,128)(2,1)}, bf16[384,256]{1,0:T(8,128)(2,1)}, u32[]{:S(2)}, u32[]{:S(2)}) collective-permute-start(bf16[384,256]{1,0:T(8,128)(2,1)} %get-tuple-element.495), channel_id=1, source_target_pairs={{0,1},{1,0},{2,3},{3,2},{4,5},{5,4},{6,7},{7,6},{8,9},{9,8},{10,11... | collective-permute-start | bytes 589832 | tf_op jit(solution)/shard_map/ppermute | solution.py:48
  520.5 44.9 %collective-permute-start.59 = (bf16[384,256]{1,0:T(8,128)(2,1)}, bf16[384,256]{1,0:T(8,128)(2,1)}, u32[]{:S(2)}, u32[]{:S(2)}) collective-permute-start(bf16[384,256]{1,0:T(8,128)(2,1)} %get-tuple-element.494), channel_id=1, source_target_pairs={{0,2},{1,3},{2,0},{3,1},{4,6},{5,7},{6,4},{7,5},{8,10},{9,11},{10,... | collective-permute-start | bytes 589832 | tf_op jit(solution)/shard_map/ppermute | solution.py:48
  527.6 37.8 %collective-permute-start.60 = (bf16[384,256]{1,0:T(8,128)(2,1)S(1)}, bf16[384,256]{1,0:T(8,128)(2,1)S(1)}, u32[]{:S(2)}, u32[]{:S(2)}) collective-permute-start(bf16[384,256]{1,0:T(8,128)(2,1)S(1)} %copy-done.140), channel_id=1, source_target_pairs={{0,3},{1,2},{2,1},{3,0},{4,7},{5,6},{6,5},{7,4},{8,11},{9,10},{10,... | collective-permute-start | bytes 589832 | tf_op jit(solution)/shard_map/ppermute | solution.py:48
  528.9 96.1 %collective-permute-start.74 = (bf16[2,768,128]{2,1,0:T(8,128)(2,1)}, bf16[2,768,128]{2,1,0:T(8,128)(2,1)}, u32[]{:S(2)}, u32[]{:S(2)}) collective-permute-start(bf16[2,768,128]{2,1,0:T(8,128)(2,1)} %get-tuple-element.475), channel_id=1, source_target_pairs={{0,1},{1,0},{2,3},{3,2},{4,5},{5,4},{6,7},{7,6},{8,9},{9,8},{10,11... | collective-permute-start | bytes 1179656 | tf_op jit(solution)/shard_map/ppermute | solution.py:48
  530.1 96.0 %collective-permute-start.75 = (bf16[2,768,128]{2,1,0:T(8,128)(2,1)}, bf16[2,768,128]{2,1,0:T(8,128)(2,1)}, u32[]{:S(2)}, u32[]{:S(2)}) collective-permute-start(bf16[2,768,128]{2,1,0:T(8,128)(2,1)} %get-tuple-element.476), channel_id=1, source_target_pairs={{0,2},{1,3},{2,0},{3,1},{4,6},{5,7},{6,4},{7,5},{8,10},{9,11},{10,... | collective-permute-start | bytes 1179656 | tf_op jit(solution)/shard_map/ppermute | solution.py:48
  564.0 63.0 %collective-permute-start.76 = (bf16[2,768,128]{2,1,0:T(8,128)(2,1)}, bf16[2,768,128]{2,1,0:T(8,128)(2,1)}, u32[]{:S(2)}, u32[]{:S(2)}) collective-permute-start(bf16[2,768,128]{2,1,0:T(8,128)(2,1)} %get-tuple-element.473), channel_id=1, source_target_pairs={{0,3},{1,2},{2,1},{3,0},{4,7},{5,6},{6,5},{7,4},{8,11},{9,10},{10,... | collective-permute-start | bytes 1179656 | tf_op jit(solution)/shard_map/ppermute | solution.py:48
  567.9 31.5 %collective-permute-start.61 = (bf16[1152,384]{1,0:T(8,128)(2,1)}, bf16[1152,384]{1,0:T(8,128)(2,1)}, u32[]{:S(2)}, u32[]{:S(2)}) collective-permute-start(bf16[1152,384]{1,0:T(8,128)(2,1)} %bitcast.53), channel_id=1, source_target_pairs={{0,2},{1,3},{2,0},{3,1},{4,6},{5,7},{6,4},{7,5},{8,10},{9,11},{10,... | collective-permute-start | bytes 2654216 | tf_op jit(solution)/shard_map/ppermute | solution.py:48
  569.1 31.4 %collective-permute-start.62 = (bf16[1152,384]{1,0:T(8,128)(2,1)}, bf16[1152,384]{1,0:T(8,128)(2,1)}, u32[]{:S(2)}, u32[]{:S(2)}) collective-permute-start(bf16[1152,384]{1,0:T(8,128)(2,1)} %bitcast.54), channel_id=1, source_target_pairs={{0,1},{1,0},{2,3},{3,2},{4,5},{5,4},{6,7},{7,6},{8,9},{9,8},{10,11... | collective-permute-start | bytes 2654216 | tf_op jit(solution)/shard_map/ppermute | solution.py:48
  599.4 88.6 %collective-permute-start.68 = (bf16[256,1536]{1,0:T(8,128)(2,1)}, bf16[256,1536]{1,0:T(8,128)(2,1)}, u32[]{:S(2)}, u32[]{:S(2)}) collective-permute-start(bf16[256,1536]{1,0:T(8,128)(2,1)} %pad_maximum_fusion.25), channel_id=1, source_target_pairs={{0,1},{1,0},{2,3},{3,2},{4,5},{5,4},{6,7},{7,6},{8,9},{9,8},{10,11... | collective-permute-start | bytes 2359304 | tf_op jit(solution)/shard_map/ppermute | solution.py:48
  600.6 88.5 %collective-permute-start.69 = (bf16[256,1536]{1,0:T(8,128)(2,1)}, bf16[256,1536]{1,0:T(8,128)(2,1)}, u32[]{:S(2)}, u32[]{:S(2)}) collective-permute-start(bf16[256,1536]{1,0:T(8,128)(2,1)} %pad_maximum_fusion.26), channel_id=1, source_target_pairs={{0,2},{1,3},{2,0},{3,1},{4,6},{5,7},{6,4},{7,5},{8,10},{9,11},{10,... | collective-permute-start | bytes 2359304 | tf_op jit(solution)/shard_map/ppermute | solution.py:48
  625.0 37.3 %collective-permute-start.70 = (bf16[128,1536]{1,0:T(8,128)(2,1)}, bf16[128,1536]{1,0:T(8,128)(2,1)}, u32[]{:S(2)}, u32[]{:S(2)}) collective-permute-start(bf16[128,1536]{1,0:T(8,128)(2,1)} %get-tuple-element.466), channel_id=1, source_target_pairs={{0,2},{1,3},{2,0},{3,1},{4,6},{5,7},{6,4},{7,5},{8,10},{9,11},{10,... | collective-permute-start | bytes 1179656 | tf_op jit(solution)/shard_map/ppermute | solution.py:48
  626.1 36.2 %collective-permute-start.71 = (bf16[128,1536]{1,0:T(8,128)(2,1)}, bf16[128,1536]{1,0:T(8,128)(2,1)}, u32[]{:S(2)}, u32[]{:S(2)}) collective-permute-start(bf16[128,1536]{1,0:T(8,128)(2,1)} %get-tuple-element.465), channel_id=1, source_target_pairs={{0,1},{1,0},{2,3},{3,2},{4,5},{5,4},{6,7},{7,6},{8,9},{9,8},{10,11... | collective-permute-start | bytes 1179656 | tf_op jit(solution)/shard_map/ppermute | solution.py:48
  664.6 34.1 %collective-permute-start.72 = (bf16[256,1536]{1,0:T(8,128)(2,1)}, bf16[256,1536]{1,0:T(8,128)(2,1)}, u32[]{:S(2)}, u32[]{:S(2)}) collective-permute-start(bf16[256,1536]{1,0:T(8,128)(2,1)} %pad_maximum_fusion.27), channel_id=1, source_target_pairs={{0,1},{1,0},{2,3},{3,2},{4,5},{5,4},{6,7},{7,6},{8,9},{9,8},{10,11... | collective-permute-start | bytes 2359304 | tf_op jit(solution)/shard_map/ppermute | solution.py:48
  668.5 37.2 %collective-permute-start.73 = (bf16[256,1536]{1,0:T(8,128)(2,1)}, bf16[256,1536]{1,0:T(8,128)(2,1)}, u32[]{:S(2)}, u32[]{:S(2)}) collective-permute-start(bf16[256,1536]{1,0:T(8,128)(2,1)} %pad_maximum_fusion.28), channel_id=1, source_target_pairs={{0,2},{1,3},{2,0},{3,1},{4,6},{5,7},{6,4},{7,5},{8,10},{9,11},{10,... | collective-permute-start | bytes 2359304 | tf_op jit(solution)/shard_map/ppermute | solution.py:48
  681.7 61.2 %collective-permute-start.79 = (bf16[2304,384]{1,0:T(8,128)(2,1)S(1)}, bf16[2304,384]{1,0:T(8,128)(2,1)S(1)}, u32[]{:S(2)}, u32[]{:S(2)}) collective-permute-start(bf16[2304,384]{1,0:T(8,128)(2,1)S(1)} %copy-done.107), channel_id=1, source_target_pairs={{0,2},{1,3},{2,0},{3,1},{4,6},{5,7},{6,4},{7,5},{8,10},{9,11},{10,... | collective-permute-start | bytes 5308424 | tf_op jit(solution)/shard_map/ppermute | solution.py:48
  688.0 54.9 %collective-permute-start.78 = (bf16[2304,384]{1,0:T(8,128)(2,1)S(1)}, bf16[2304,384]{1,0:T(8,128)(2,1)S(1)}, u32[]{:S(2)}, u32[]{:S(2)}) collective-permute-start(bf16[2304,384]{1,0:T(8,128)(2,1)S(1)} %copy-done.108), channel_id=1, source_target_pairs={{0,1},{1,0},{2,3},{3,2},{4,5},{5,4},{6,7},{7,6},{8,9},{9,8},{10,11... | collective-permute-start | bytes 5308424 | tf_op jit(solution)/shard_map/ppermute | solution.py:48
  689.1 59.1 %collective-permute-start.77 = (bf16[4,192,1536]{2,1,0:T(8,128)(2,1)S(1)}, bf16[4,192,1536]{2,1,0:T(8,128)(2,1)S(1)}, u32[]{:S(2)}, u32[]{:S(2)}) collective-permute-start(bf16[4,192,1536]{2,1,0:T(8,128)(2,1)S(1)} %copy-done.106), channel_id=1, source_target_pairs={{0,4},{4,0},{8,12},{12,8},{16,20},{20,16},{24,28},{28,24},{1,5},{5... | collective-permute-start | bytes 7077896 | tf_op jit(solution)/shard_map/ppermute | solution.py:48
  744.5 32.3 %collective-permute-start.84 = (bf16[576,384]{1,0:T(8,128)(2,1)S(1)}, bf16[576,384]{1,0:T(8,128)(2,1)S(1)}, u32[]{:S(2)}, u32[]{:S(2)}) collective-permute-start(bf16[576,384]{1,0:T(8,128)(2,1)S(1)} %get-tuple-element.472), channel_id=1, source_target_pairs={{0,16},{4,20},{8,24},{12,28},{16,0},{20,4},{24,8},{28,12},{1,17},{... | collective-permute-start | bytes 1327112 | tf_op jit(solution)/shard_map/ppermute | solution.py:48
  747.0 31.2 %collective-permute-start.85 = (bf16[576,384]{1,0:T(8,128)(2,1)S(1)}, bf16[576,384]{1,0:T(8,128)(2,1)S(1)}, u32[]{:S(2)}, u32[]{:S(2)}) collective-permute-start(bf16[576,384]{1,0:T(8,128)(2,1)S(1)} %get-tuple-element.471), channel_id=1, source_target_pairs={{0,24},{4,28},{8,16},{12,20},{16,8},{20,12},{24,0},{28,4},{1,25},{... | collective-permute-start | bytes 1327112 | tf_op jit(solution)/shard_map/ppermute | solution.py:48
  749.0 42.3 %collective-permute-start.80 = (bf16[192,1536]{1,0:T(8,128)(2,1)S(1)}, bf16[192,1536]{1,0:T(8,128)(2,1)S(1)}, u32[]{:S(2)}, u32[]{:S(2)}) collective-permute-start(bf16[192,1536]{1,0:T(8,128)(2,1)S(1)} %get-tuple-element.467), channel_id=1, source_target_pairs={{0,8},{4,12},{8,0},{12,4},{16,24},{20,28},{24,16},{28,20},{1,9},{5... | collective-permute-start | bytes 1769480 | tf_op jit(solution)/shard_map/ppermute | solution.py:48
  749.5 75.4 %collective-permute-start.81 = (bf16[192,1536]{1,0:T(8,128)(2,1)S(1)}, bf16[192,1536]{1,0:T(8,128)(2,1)S(1)}, u32[]{:S(2)}, u32[]{:S(2)}) collective-permute-start(bf16[192,1536]{1,0:T(8,128)(2,1)S(1)} %get-tuple-element.469), channel_id=1, source_target_pairs={{0,16},{4,20},{8,24},{12,28},{16,0},{20,4},{24,8},{28,12},{1,17},{... | collective-permute-start | bytes 1769480 | tf_op jit(solution)/shard_map/ppermute | solution.py:48
  766.1 58.9 %collective-permute-start.82 = (bf16[192,1536]{1,0:T(8,128)(2,1)S(1)}, bf16[192,1536]{1,0:T(8,128)(2,1)S(1)}, u32[]{:S(2)}, u32[]{:S(2)}) collective-permute-start(bf16[192,1536]{1,0:T(8,128)(2,1)S(1)} %get-tuple-element.468), channel_id=1, source_target_pairs={{0,24},{4,28},{8,16},{12,20},{16,8},{20,12},{24,0},{28,4},{1,25},{... | collective-permute-start | bytes 1769480 | tf_op jit(solution)/shard_map/ppermute | solution.py:48
  (246 other events, 2438.4 us)
Sparse Core Ops, SparseCore 0:
  44.5 52.0 all-gather.2
  110.6 51.8 all-gather.4
  352.7 55.2 reduce-scatter.4
  418.7 54.9 reduce-scatter.10
  514.2 55.0 reduce-scatter.8
  597.3 110.1 reduce-scatter.6

commit v5 on v4

v5 whole, which is shorter than its diff:
```python
import functools
import math

import jax
import jax.numpy as jnp
from jax import lax
from jax.experimental import pallas as pl
from jax.experimental.pallas import tpu as pltpu
from jax.sharding import PartitionSpec as P

HEAD_DIM = 64
HALF = HEAD_DIM // 2
FACTOR = 1.0 / math.sqrt(HEAD_DIM)

norm_eps = 1e-05

f32 = jnp.float32
bf16 = jnp.bfloat16


def dot(left, right, left_axis, right_axis):
    return lax.dot_general(
        left, right, (((left_axis,), (right_axis,)), ((), ())), preferred_element_type=f32
    )


def norm_forward(values, gain, shift):
    center = values - jnp.mean(values, axis=-1, keepdims=True)
    scale = lax.rsqrt(jnp.mean(center * center, axis=-1, keepdims=True) + norm_eps)
    normal = center * scale
    return (normal * gain + shift, normal, scale)


def norm_backward(grad, normal, scale, gain):
    inner = grad * gain
    return scale * (
        inner
        - jnp.mean(inner, axis=-1, keepdims=True)
        - normal * jnp.mean(inner * normal, axis=-1, keepdims=True)
    )


def bits_of(size):
    return [1 << place for place in range(size.bit_length() - 1)]


def swap(values, axis, k):
    return lax.ppermute(values, axis, [(i, i ^ k) for i in range(lax.axis_size(axis))])


def after(values, *others):
    return lax.optimization_barrier((values,) + others)[0]


class Spread:
    def __init__(self, values):
        self.values = values
        self.last = ()
        size = lax.axis_size("mp")
        partners = (1, 2) if size == 4 else range(1, size)
        self.first = tuple(swap(values, "mp", k) for k in partners)

    def second_step(self):
        if lax.axis_size("mp") == 4:
            one, two = self.first
            half = one.shape[0] // 2
            self.last = (swap(one[:half], "mp", 2), swap(two[half:], "mp", 1))

    def pieces(self):
        return [self.values, *self.first, *self.last]


def place(blocks, axis):
    here = lax.axis_index("mp")
    step = blocks[0].shape[axis]
    shape = list(blocks[0].shape)
    shape[axis] = step * len(blocks)
    result = jnp.zeros(shape, blocks[0].dtype)
    for k, block in enumerate(blocks):
        result = lax.dynamic_update_slice_in_dim(result, block, (here ^ k) * step, axis)
    return result


def gathered(values):
    return exchange(jnp.broadcast_to(values[None], (lax.axis_size("mp"),) + values.shape))


def exchange(blocks):
    return lax.all_to_all(blocks, "mp", 0, 0)


class Settle:
    def __init__(self, blocks):
        here = lax.axis_index("mp")
        size = blocks.shape[0]
        self.mine = [lax.dynamic_index_in_dim(blocks, here ^ k, 0, False) for k in range(size)]
        self.came = ()

    def first_step(self):
        if len(self.mine) == 4:
            half = self.mine[3].shape[0] // 2
            self.came = (swap(self.mine[3][:half], "mp", 2), swap(self.mine[3][half:], "mp", 1))

    def add(self):
        if len(self.mine) == 4:
            _, one, two, _ = self.mine
            high, low = self.came
            half = high.shape[0]
            one = jnp.concatenate([plus(one[:half], high), one[half:]], axis=0)
            two = jnp.concatenate([two[:half], plus(two[half:], low)], axis=0)
            self.mine = [self.mine[0], one, two]

    def second_step(self):
        return [self.mine[0]] + [swap(self.mine[k], "mp", k) for k in range(1, len(self.mine))]


def plus(left, right):
    return (left.astype(f32) + right.astype(f32)).astype(bf16)


def total(terms):
    result = terms[0].astype(f32)
    for k in range(1, len(terms)):
        result = result + terms[k].astype(f32)
    return result


def all_sum(values):
    for axis in ("dp", "mp"):
        for bit in bits_of(lax.axis_size(axis)):
            values = values + swap(values, axis, bit)
    return values


def core_half(blocks):
    core = lax.axis_index("dp") & 1
    pairs = blocks.reshape((blocks.shape[0] // 2, 2) + blocks.shape[1:])
    mine = lax.dynamic_index_in_dim(pairs, core, 1, False)
    other = lax.dynamic_index_in_dim(pairs, 1 - core, 1, False)
    return (mine, swap(other, "dp", 1))


class Chain:
    def __init__(self):
        self.last = ()

    def hold(self, values):
        return after(values, *self.last) if self.last else values

    def mark(self, *values):
        self.last = values

    def arrive(self, values):
        values = self.hold(values)
        self.mark(values)
        return values


def plus(left, right):
    return (left.astype(f32) + right.astype(f32)).astype(bf16)


def total(terms):
    result = terms[0].astype(f32)
    for term in terms[1:]:
        result = result + term.astype(f32)
    return result


def all_sum(values):
    for axis in ("dp", "mp"):
        for bit in bits_of(lax.axis_size(axis)):
            values = values + swap(values, axis, bit)
    return values


def core_half(blocks):
    core = lax.axis_index("dp") & 1
    pairs = blocks.reshape((blocks.shape[0] // 2, 2) + blocks.shape[1:])
    mine = lax.dynamic_index_in_dim(pairs, core, 1, False)
    other = lax.dynamic_index_in_dim(pairs, 1 - core, 1, False)
    return (mine, swap(other, "dp", 1))


def chips_sum(blocks):
    here = lax.axis_index("dp") >> 1
    mine = [
        lax.dynamic_index_in_dim(blocks, here ^ k, 0, False) for k in range(blocks.shape[0])
    ]
    return total([mine[0]] + [swap(mine[k], "dp", 2 * k) for k in range(1, len(mine))])


def self_forward_kernel(q_ref, k_ref, v_ref, pk_ref, pv_ref, o_ref, l_ref):
    parts = head_parts(q_ref.shape[0])
    scores = [dot(k_ref[part], q_ref[part], 0, 0) for part in parts]
    for head, part in enumerate(parts):
        front = q_ref[part].astype(f32) * pk_ref[part].astype(f32)
        front = jnp.sum(front, axis=0, keepdims=True)
        top = jnp.maximum(jnp.max(scores[head], axis=0, keepdims=True), front)
        weights = jnp.exp(scores[head] - top)
        front_weight = jnp.exp(front - top)
        total = jnp.sum(weights, axis=0, keepdims=True) + front_weight
        mixed = dot(v_ref[part], weights.astype(bf16), 1, 0)
        mixed = mixed + pv_ref[part].astype(f32) * front_weight.astype(bf16).astype(f32)
        mixed = (mixed * (1.0 / total)).astype(bf16)
        frames = o_ref.shape[2]
        for k in range(o_ref.shape[0]):
            o_ref[k, part] = mixed[:, k * frames : (k + 1) * frames]
        l_ref[head] = top + jnp.log(total)


def self_backward_kernel(
    block,
    q_ref,
    k_ref,
    v_ref,
    g_ref,
    o_ref,
    l_ref,
    pk_ref,
    pv_ref,
    cos_ref,
    sin_ref,
    d_ref,
    dpk_ref,
    dpv_ref,
):
    frames = q_ref.shape[1]
    keys = k_ref[...]
    values = v_ref[...]
    front_key = pk_ref[...].astype(f32)
    front_value = pv_ref[...].astype(f32)
    grad_keys = jnp.zeros((HEAD_DIM, frames), f32)
    grad_values = jnp.zeros((HEAD_DIM, frames), f32)
    grad_front_key = jnp.zeros((HEAD_DIM, 1), f32)
    grad_front_value = jnp.zeros((HEAD_DIM, 1), f32)
    whole_grads = jnp.concatenate([g_ref[k] for k in range(g_ref.shape[0])], axis=1)
    whole_mixed = jnp.concatenate([o_ref[k] for k in range(o_ref.shape[0])], axis=1)
    for start in range(0, frames, block):
        part = slice(start, start + block)
        queries = q_ref[:, part]
        grads = whole_grads[:, part]
        wide_queries = queries.astype(f32)
        wide_grads = grads.astype(f32)
        logsum = l_ref[0, :, part]
        mixsum = jnp.sum(whole_mixed[:, part].astype(f32) * wide_grads, axis=0, keepdims=True)
        probs = jnp.exp(dot(keys, queries, 0, 0) - logsum)
        grad_probs = dot(values, grads, 0, 0)
        grad_scores = (probs * (grad_probs - mixsum)).astype(bf16)
        grad_values = grad_values + dot(grads, probs.astype(bf16), 1, 1)
        grad_keys = grad_keys + dot(queries, grad_scores, 1, 1)
        grad_queries = dot(keys, grad_scores, 1, 0)
        front = jnp.exp(jnp.sum(wide_queries * front_key, axis=0, keepdims=True) - logsum)
        grad_front = jnp.sum(wide_grads * front_value, axis=0, keepdims=True)
        grad_front = (front * (grad_front - mixsum)).astype(bf16).astype(f32)
        front = front.astype(bf16).astype(f32)
        grad_front_key += jnp.sum(wide_queries * grad_front, axis=1, keepdims=True)
        grad_front_value += jnp.sum(wide_grads * front, axis=1, keepdims=True)
        grad_queries = (grad_queries + front_key * grad_front) * FACTOR
        cosine = cos_ref[:, part]
        sine = sin_ref[:, part]
        upper, lower = grad_queries[:HALF], grad_queries[HALF:]
        d_ref[0, :HALF, part] = (upper * cosine + lower * sine).astype(bf16)
        d_ref[0, HALF:, part] = (lower * cosine - upper * sine).astype(bf16)
    cosine = cos_ref[...]
    sine = sin_ref[...]
    upper, lower = grad_keys[:HALF], grad_keys[HALF:]
    d_ref[1, :HALF, :] = (upper * cosine + lower * sine).astype(bf16)
    d_ref[1, HALF:, :] = (lower * cosine - upper * sine).astype(bf16)
    d_ref[2] = grad_values.astype(bf16)
    dpk_ref[...] = grad_front_key.astype(bf16)
    dpv_ref[...] = grad_front_value.astype(bf16)


def head_parts(rows):
    return [slice(at, at + HEAD_DIM) for at in range(0, rows, HEAD_DIM)]


def fetch(core, out_halves, out, wholes, targets, sems):
    mine, other = out_halves
    size, half, _ = mine.shape
    copies = []
    for k in range(size):
        for source, part in ((mine, core), (other, 1 - core)):
            at = pl.multiple_of((2 * k + part) * half, 16)
            target = out.at[pl.ds(at, half)]
            copies.append(pltpu.make_async_copy(source.at[k], target, sems.at[len(copies)]))
    first = len(copies)
    for source, target in zip(wholes, targets):
        copies.append(pltpu.make_async_copy(source, target, sems.at[len(copies)]))

    def start_out():
        for copy in copies[:first]:
            copy.start()

    def start_whole(k):
        copies[first + k].start()

    def get_out():
        for copy in copies[:first]:
            copy.wait()
        return out[...]

    def get_whole(k):
        copies[first + k].wait()
        return targets[k]

    return start_out, start_whole, get_out, get_whole


def local_forward_kernel(
    clip, n_ref, core_ref, order_ref, mixed_ref, x_ref, norm_ref, mem_ref, wo_mine, wo_other, cq_hbm, co_hbm, *refs
):
    first_ref, second_ref, two_ref, q_ref, o_ref, l_ref, three_ref, wo, cq, co, sems = refs
    start_out, start_whole, get_out, get_whole = fetch(
        core_ref[0], (wo_mine, wo_other), wo, (cq_hbm, co_hbm), (cq, co), sems
    )
    start_out()
    start_whole(0)
    start_whole(1)
    groups, depth, slots = mem_ref.shape
    local = depth // 2
    live = lax.broadcasted_iota(jnp.int32, (slots, 1), 0) < n_ref[clip]
    first = x_ref[...].astype(f32) + dot(mixed_ref[...], get_out(), 0, 0)
    first_ref[...] = first
    two = norm_forward(first, norm_ref[0:1], norm_ref[1:2])[0].astype(bf16)
    two_ref[...] = two
    weight = get_whole(0)
    for k in range(groups):
        q_ref[k * local : (k + 1) * local] = (dot(two, weight[k], 1, 0) * FACTOR).astype(bf16).T
    for group in range(groups):
        parts = head_parts(local)
        there = order_ref[group]
        at = group * local
        queries = [q_ref[at + p.start : at + p.stop] for p in parts]
        scores = [dot(mem_ref[there, p], q, 0, 0) for p, q in zip(parts, queries)]
        scores = [jnp.where(live, s, -1e30) for s in scores]
        tops = [jnp.max(s, axis=0, keepdims=True) for s in scores]
        weights = [jnp.exp(s - top) for s, top in zip(scores, tops)]
        totals = [jnp.sum(w, axis=0, keepdims=True) for w in weights]
        for head, p in enumerate(parts):
            values = mem_ref[there, local + p.start : local + p.stop]
            mixed = dot(values, weights[head].astype(bf16), 1, 0)
            o_ref[at + p.start : at + p.stop] = (mixed * (1.0 / totals[head])).astype(bf16)
            l_ref[group * len(parts) + head] = tops[head] + jnp.log(totals[head])
    weight = get_whole(1)
    second = first
    for k in range(groups):
        second = second + dot(o_ref[k * local : (k + 1) * local], weight[k], 0, 1)
    second_ref[...] = second
    three_ref[...] = norm_forward(second, norm_ref[2:3], norm_ref[3:4])[0].astype(bf16)


def local_specs(clip, count, rows, width, memory):
    groups, depth, slots = memory.shape
    heads = groups * depth // 2 // HEAD_DIM
    wide = pl.BlockSpec((rows, width), lambda i: (0, 0))
    turned = pl.BlockSpec((width, rows), lambda i: (0, 0))
    sums = pl.BlockSpec((heads, 1, rows), lambda i: (0, 0, 0))
    norms = pl.BlockSpec((4, width), lambda i: (0, 0))
    mem = pl.BlockSpec((groups, depth, slots // count), lambda i: (0, 0, clip))
    return (wide, turned, sums, norms, mem, heads)


def local_forward(clip, count, lengths, core, order, mixed, frames, norms, memory, weights):
    rows, width = frames.shape
    wide, turned, sums, norm_spec, mem, heads = local_specs(clip, count, rows, width, memory)
    return pl.pallas_call(
        functools.partial(local_forward_kernel, clip),
        grid=(1,),
        in_specs=[pl.BlockSpec(memory_space=pltpu.SMEM)] * 3
        + [turned, wide, norm_spec, mem]
        + [pl.BlockSpec(memory_space=pl.ANY)] * 4,
        out_specs=[wide, wide, wide, turned, turned, sums, wide],
        out_shape=[
            shape_of((rows, width), f32),
            shape_of((rows, width), f32),
            shape_of((rows, width), bf16),
            shape_of((width, rows), bf16),
            shape_of((width, rows), bf16),
            shape_of((heads, 1, rows), f32),
            shape_of((rows, width), bf16),
        ],
        scratch_shapes=[pltpu.VMEM((width, width), bf16)]
        + [pltpu.VMEM(weights[2].shape, bf16)] * 2
        + [pltpu.SemaphoreType.DMA((2 * memory.shape[0] + 2,))],
        compiler_params=params(),
        cost_estimate=cost(11.3),
        name="local_forward",
    )(lengths, core, order, mixed, frames, norms, memory, *weights)


def local_backward_kernel(
    clip,
    n_ref,
    core_ref,
    order_ref,
    b_ref,
    cot_ref,
    first_ref,
    second_ref,
    q_ref,
    o_ref,
    l_ref,
    norm_ref,
    mem_ref,
    wo_mine,
    wo_other,
    cq_hbm,
    co_hbm,
    *refs,
):
    cross_ref, self_ref, one_ref, dq_ref, d_ref, g_ref, term_ref, grads_ref, wo, cq, co, sems = refs
    start_out, start_whole, get_out, get_whole = fetch(
        core_ref[0], (wo_mine, wo_other), wo, (cq_hbm, co_hbm), (cq, co), sems
    )
    start_whole(1)
    start_whole(0)
    start_out()
    groups, depth, slots = mem_ref.shape
    local = depth // 2
    heads = local // HEAD_DIM
    live = lax.broadcasted_iota(jnp.int32, (slots, 1), 0) < n_ref[clip]

    back = total([b_ref[k] for k in range(b_ref.shape[0])])
    _, normal, scale = norm_forward(second_ref[...], norm_ref[2:3], norm_ref[3:4])
    term_ref[2:3] = jnp.sum(back * normal, axis=0, keepdims=True)
    term_ref[3:4] = jnp.sum(back, axis=0, keepdims=True)
    grad_two = cot_ref[...].astype(f32) + norm_backward(back, normal, scale, norm_ref[2:3])
    cross_in = grad_two.astype(bf16)
    cross_ref[...] = cross_in
    weight = get_whole(1)
    for k in range(groups):
        grads_ref[k * local : (k + 1) * local] = dot(cross_in, weight[k], 1, 0).astype(bf16).T
    for group in range(groups):
        for head, part in enumerate(head_parts(local)):
            there = slice(group * local + part.start, group * local + part.stop)
            queries = q_ref[there]
            keys = mem_ref[order_ref[group], part]
            grads = grads_ref[there]
            mixsum = jnp.sum(o_ref[there].astype(f32) * grads.astype(f32), axis=0, keepdims=True)
            scores = jnp.where(live, dot(keys, queries, 0, 0), -1e30)
            probs = jnp.exp(scores - l_ref[group * heads + head])
            values = slice(local + part.start, local + part.stop)
            grad_probs = dot(mem_ref[order_ref[group], values], grads, 0, 0)
            grad_scores = (probs * (grad_probs - mixsum)).astype(bf16)
            dq_ref[there] = (dot(keys, grad_scores, 1, 0) * FACTOR).astype(bf16)
            d_ref[group, part] = dot(queries, grad_scores, 1, 1).astype(bf16)
            d_ref[group, values] = dot(grads, probs.astype(bf16), 1, 1).astype(bf16)
    weight = get_whole(0)
    back = jnp.zeros(grad_two.shape, f32)
    for k in range(groups):
        back = back + dot(dq_ref[k * local : (k + 1) * local], weight[k], 0, 1)
    _, normal, scale = norm_forward(first_ref[...], norm_ref[0:1], norm_ref[1:2])
    term_ref[0:1] = jnp.sum(back * normal, axis=0, keepdims=True)
    term_ref[1:2] = jnp.sum(back, axis=0, keepdims=True)
    grad_one = grad_two + norm_backward(back, normal, scale, norm_ref[0:1])
    one_ref[...] = grad_one
    self_in = grad_one.astype(bf16)
    self_ref[...] = self_in
    g_ref[...] = dot(get_out(), self_in, 1, 1).astype(bf16)


def local_backward(
    clip, count, lengths, core, order, back, cotangent, first, second, cross, norms, memory, weights
):
    rows, width = cotangent.shape
    wide, turned, sums, norm_spec, mem, heads = local_specs(clip, count, rows, width, memory)
    groups, depth, slots = memory.shape
    slots = slots // count
    return pl.pallas_call(
        functools.partial(local_backward_kernel, clip),
        grid=(1,),
        in_specs=[
            pl.BlockSpec(memory_space=pltpu.SMEM),
            pl.BlockSpec(memory_space=pltpu.SMEM),
            pl.BlockSpec(memory_space=pltpu.SMEM),
            pl.BlockSpec(back.shape, lambda i: (0, 0, 0)),
            wide,
            wide,
            wide,
            turned,
            turned,
            sums,
            norm_spec,
            mem,
        ]
        + [pl.BlockSpec(memory_space=pl.ANY)] * 4,
        out_specs=[
            wide,
            wide,
            wide,
            turned,
            pl.BlockSpec((groups, depth, slots), lambda i: (0, 0, 0)),
            turned,
            norm_spec,
        ],
        out_shape=[
            shape_of((rows, width), bf16),
            shape_of((rows, width), bf16),
            shape_of((rows, width), f32),
            shape_of((width, rows), bf16),
            shape_of((groups, depth, slots), bf16),
            shape_of((width, rows), bf16),
            shape_of((4, width), f32),
        ],
        scratch_shapes=[pltpu.VMEM((width, rows), bf16)]
        + [pltpu.VMEM((width, width), bf16)]
        + [pltpu.VMEM(weights[2].shape, bf16)] * 2
        + [pltpu.SemaphoreType.DMA((2 * groups + 2,))],
        compiler_params=params(),
        cost_estimate=cost(5),
        name="local_backward",
    )(lengths, core, order, back, cotangent, first, second, *cross, norms, memory, *weights)


def cost(micros):
    micros = 0.4 * micros
    return pl.CostEstimate(
        flops=int(micros * 1.15e9), bytes_accessed=int(micros * 3.6e6), transcendentals=0
    )


def shape_of(shape, kind):
    return jax.ShapeDtypeStruct(shape, kind)


def params():
    return pltpu.CompilerParams(vmem_limit_bytes=48 * 2**20)


def self_forward(turned, front_keys, front_values):
    size = lax.axis_size("mp")
    heads = front_keys.shape[0] // HEAD_DIM
    frames = turned.shape[1]
    step = 3 if heads % 3 == 0 else 1
    rows = step * HEAD_DIM
    steps = heads // step

    def at(third):
        return pl.BlockSpec((rows, frames), lambda h: (third * steps + h, 0))

    column = pl.BlockSpec((rows, 1), lambda h: (h, 0))
    return pl.pallas_call(
        self_forward_kernel,
        grid=(steps,),
        in_specs=[at(0), at(1), at(2), column, column],
        out_specs=[
            pl.BlockSpec((size, rows, frames // size), lambda h: (0, h, 0)),
            pl.BlockSpec((step, 1, frames), lambda h: (h, 0, 0)),
        ],
        out_shape=[
            shape_of((size, heads * HEAD_DIM, frames // size), bf16),
            shape_of((heads, 1, frames), f32),
        ],
        compiler_params=params(),
        cost_estimate=cost(8.7),
        name="self_forward",
    )(turned, turned, turned, front_keys, front_values)


def self_backward(turned, grads, mixed, logsum, front_keys, front_values, cosine, sine):
    heads = front_keys.shape[0] // HEAD_DIM
    frames = turned.shape[1]

    def at(third):
        return pl.BlockSpec((HEAD_DIM, frames), lambda h: (third * heads + h, 0))

    column = pl.BlockSpec((HEAD_DIM, 1), lambda h: (h, 0))
    size = lax.axis_size("mp")
    blocks = pl.BlockSpec((size, HEAD_DIM, frames // size), lambda h: (0, h, 0))
    angles = pl.BlockSpec((HALF, frames), lambda h: (0, 0))
    return pl.pallas_call(
        functools.partial(self_backward_kernel, min(256, frames)),
        grid=(heads,),
        in_specs=[
            at(0),
            at(1),
            at(2),
            blocks,
            blocks,
            pl.BlockSpec((1, 1, frames), lambda h: (h, 0, 0)),
            column,
            column,
            angles,
            angles,
        ],
        out_specs=[
            pl.BlockSpec((3, HEAD_DIM, frames), lambda h: (0, h, 0)),
            column,
            column,
        ],
        out_shape=[
            shape_of((3, heads * HEAD_DIM, frames), bf16),
            shape_of((heads * HEAD_DIM, 1), bf16),
            shape_of((heads * HEAD_DIM, 1), bf16),
        ],
        compiler_params=params(),
        cost_estimate=cost(18),
        name="self_backward",
    )(turned, turned, turned, grads, mixed, logsum, front_keys, front_values, cosine, sine)


def block_refs(refs, size):
    if len(refs) == size:
        return [[ref] for ref in refs]
    return [refs[0:1], refs[1:2], refs[2:3], refs[3:5]]


def block_value(refs):
    parts = [ref[...] for ref in refs]
    return parts[0] if len(parts) == 1 else jnp.concatenate(parts, axis=0)


def whole_specs(arrays):
    return [pl.BlockSpec(array.shape, lambda j, *_: (0, 0)) for array in arrays]


def project_kernel(
    size, given, heads, n_ref, p_ref, norm_ref, wq_ref, wk_ref, wv_ref, cos_ref, sin_ref, *refs
):
    d_ref, x_ref, front_ref, w_ref = refs[-4:]
    blocks = block_refs(refs[:given], size)
    local = heads * HEAD_DIM

    @pl.when(pl.program_id(0) == 0)
    def _():
        for third, ref in enumerate((wq_ref, wk_ref, wv_ref)):
            w_ref[third * local : (third + 1) * local] = ref[...].T
        prefix = norm_forward(p_ref[...], norm_ref[0:1], norm_ref[1:2])[0].astype(bf16)
        front_ref[...] = dot(w_ref[local:], prefix, 1, 1).astype(bf16)

    for k in range(size):

        @pl.when(pl.program_id(0) == k)
        def _(k=k):
            frames = block_value(blocks[k])
            x_ref[0] = frames
            raw = dot(w_ref[...], frames, 1, 1)
            cosine = cos_ref[...]
            sine = sin_ref[...]
            for head in range(2 * heads):
                at = head * HEAD_DIM
                upper = raw[at : at + HALF]
                lower = raw[at + HALF : at + HEAD_DIM]
                first = upper * cosine - lower * sine
                second = lower * cosine + upper * sine
                if head < heads:
                    first, second = first * FACTOR, second * FACTOR
                d_ref[at : at + HALF] = first.astype(bf16)
                d_ref[at + HALF : at + HEAD_DIM] = second.astype(bf16)
            d_ref[2 * local :] = raw[2 * local :].astype(bf16)


def project(clip, count, order, picked, norms, pieces, weights, cosine, sine, earlier):
    size = lax.axis_size("mp")
    width, local = weights[0].shape
    depth = 3 * local
    rows = pieces[0].shape[0]
    angles = pl.BlockSpec((HALF, rows), lambda k, n: (0, n[k]))
    return pl.pallas_call(
        functools.partial(project_kernel, size, len(pieces), local // HEAD_DIM),
        grid_spec=pltpu.PrefetchScalarGridSpec(
            num_scalar_prefetch=1,
            grid=(size,),
            in_specs=whole_specs([picked, norms] + weights)
            + [angles, angles]
            + whole_specs(pieces)
            + [pl.BlockSpec(memory_space=pl.ANY)] * len(earlier),
            out_specs=[
                pl.BlockSpec((depth, rows), lambda k, n: (0, n[k])),
                pl.BlockSpec((1, rows, width), lambda k, n: (clip, n[k], 0)),
                pl.BlockSpec((2 * local, picked.shape[0]), lambda k, n: (0, 0)),
            ],
            scratch_shapes=[pltpu.VMEM((depth, width), bf16)],
        ),
        out_shape=[
            shape_of((depth, size * rows), bf16),
            shape_of((count, size * rows, width), bf16),
            shape_of((2 * local, picked.shape[0]), bf16),
        ],
        input_output_aliases={8 + len(pieces): 1} if earlier else {},
        compiler_params=params(),
        cost_estimate=cost(8),
        name="project",
    )(order, picked, norms, *weights, cosine, sine, *pieces, *earlier)


def glu_kernel(size, given, n_ref, gate_ref, up_ref, down_ref, *refs):
    h_ref, dg_ref, du_ref, x_ref, c_ref = refs[-5:]
    blocks = block_refs(refs[:given], size)
    grads = block_refs(refs[given : 2 * given], size)
    rows = h_ref.shape[1] // size

    @pl.when(pl.program_id(0) == 0)
    def _():
        for k in range(size):
            there = pl.ds(pl.multiple_of(n_ref[k] * rows, rows), rows)
            x_ref[0, there] = block_value(blocks[k])
            c_ref[0, there] = block_value(grads[k])

    for k in range(size):
        frames = block_value(blocks[k])
        there = pl.ds(pl.multiple_of(n_ref[k] * rows, rows), rows)
        gate = dot(frames, gate_ref[...], 1, 0)
        upper = dot(frames, up_ref[...], 1, 0)
        grad_hidden = dot(block_value(grads[k]), down_ref[...], 1, 1)
        sigma = 1.0 / (1.0 + jnp.exp(-gate))
        silu = gate * sigma
        h_ref[0, there] = (silu * upper).astype(bf16)
        dg_ref[0, there] = (grad_hidden * upper * (sigma + silu * (1.0 - sigma))).astype(bf16)
        du_ref[0, there] = (grad_hidden * silu).astype(bf16)


def glu(clip, count, order, pieces, grads, w_gate, w_up, w_down, earlier):
    size = lax.axis_size("mp")
    width, hidden = w_gate.shape
    rows = size * pieces[0].shape[0]
    block = 256
    columns = pl.BlockSpec((width, block), lambda j: (0, j))
    out = pl.BlockSpec((1, rows, block), lambda j: (clip, 0, j))
    whole = pl.BlockSpec((1, rows, width), lambda j: (clip, 0, 0))
    return pl.pallas_call(
        functools.partial(glu_kernel, size, len(pieces)),
        grid=(hidden // block,),
        in_specs=[
            pl.BlockSpec(memory_space=pltpu.SMEM),
            columns,
            columns,
            pl.BlockSpec((block, width), lambda j: (j, 0)),
        ]
        + whole_specs(pieces)
        + whole_specs(grads)
        + [pl.BlockSpec(memory_space=pl.ANY)] * len(earlier),
        out_specs=[out, out, out, whole, whole],
        out_shape=[shape_of((count, rows, hidden), bf16)] * 3
        + [shape_of((count, rows, width), bf16)] * 2,
        input_output_aliases={4 + 2 * len(pieces) + i: i for i in range(len(earlier))},
        compiler_params=params(),
        cost_estimate=cost(22),
        name="glu",
    )(order, w_gate, w_up, w_down, *pieces, *grads, *earlier)


def glu_back_kernel(dg_ref, du_ref, gate_ref, up_ref, o_ref):
    size, rows, _ = o_ref.shape
    for k in range(size):
        part = slice(k * rows, (k + 1) * rows)
        back = dot(dg_ref[0, part], gate_ref[...], 1, 1) + dot(du_ref[0, part], up_ref[...], 1, 1)
        o_ref[k] = back.astype(bf16)


def glu_back(clip, grad_gate, grad_upper, w_gate, w_up):
    size = lax.axis_size("mp")
    _, frames, hidden = grad_gate.shape
    rows = frames // size
    width = w_gate.shape[0]
    block = 256
    whole = pl.BlockSpec((1, frames, hidden), lambda j: (clip, 0, 0))
    part = pl.BlockSpec((block, hidden), lambda j: (j, 0))
    return pl.pallas_call(
        glu_back_kernel,
        grid=(width // block,),
        in_specs=[whole, whole, part, part],
        out_specs=pl.BlockSpec((size, rows, block), lambda j: (0, 0, j)),
        out_shape=shape_of((size, rows, width), bf16),
        compiler_params=params(),
        cost_estimate=cost(14.5),
        name="glu_back",
    )(grad_gate, grad_upper, w_gate, w_up)


def whole_grad_kernel(chips, n, count, given, core_ref, *refs):
    o_ref = refs[-2] if not given else refs[-1]
    turned_ref = refs[-1] if not given else refs[0]
    y_refs = refs[1:] if given else refs[n * count :]
    depth = o_ref.shape[3]

    if not given:

        @pl.when(pl.program_id(0) == 0)
        def _():
            for w in range(n):
                parts = [ref[...] for ref in refs[w * count : (w + 1) * count]]
                turned_ref[w] = jnp.concatenate(parts, axis=0).T

    for w in range(n):
        right = jnp.concatenate([ref[...] for ref in y_refs[w * count : (w + 1) * count]], axis=1)
        for z in range(chips):
            at = pl.multiple_of((2 * z + core_ref[0]) * depth, depth)
            result = dot(turned_ref[w, pl.ds(at, depth)], right, 1, 1)
            if given:
                result = result + refs[1 + n * count][0, z, w].astype(f32)
            o_ref[0, z, w] = result.astype(bf16)


def whole_grad(core, groups, lefts, rights, earlier):
    size = lax.axis_size("mp")
    n = len(rights)
    count = len(rights[0])
    rows = rights[0][0].shape[1]
    local = rights[0][0].shape[0] // size
    width = lefts.shape[1] if earlier else lefts[0][0].shape[1]
    chips = groups // 2
    depth = width // groups
    out = pl.BlockSpec((1, chips, n, depth, local), lambda m: (m, 0, 0, 0, 0))
    turned = pl.BlockSpec((n, width, count * rows), lambda m: (0, 0, 0))
    right = pl.BlockSpec((local, rows), lambda m: (m, 0))
    left = pl.BlockSpec((rows, width), lambda m: (0, 0))
    out_shape = shape_of((size, chips, n, depth, local), bf16)
    turned_shape = shape_of((n, width, count * rows), bf16)
    rights = [array for pair in rights for array in pair]
    lefts = [lefts] if earlier else [array for pair in lefts for array in pair]
    return pl.pallas_call(
        functools.partial(whole_grad_kernel, chips, n, count, len(earlier)),
        grid=(size,),
        in_specs=[pl.BlockSpec(memory_space=pltpu.SMEM)]
        + [turned if earlier else left] * len(lefts)
        + [right] * len(rights)
        + [out] * len(earlier),
        out_specs=out if earlier else [out, turned],
        out_shape=out_shape if earlier else [out_shape, turned_shape],
        compiler_params=params(),
        cost_estimate=cost(12),
        name="whole_grad",
    )(core, *lefts, *rights, *earlier)


def branch_kernel(x_ref, w_ref, o_ref):
    o_ref[0, 0] = dot(x_ref[0], w_ref[...], 1, 0).astype(bf16)


def branch_blocks(hidden, w_down):
    size = lax.axis_size("mp")
    count, frames, depth = hidden.shape
    width = w_down.shape[1]
    rows = frames // size
    return pl.pallas_call(
        branch_kernel,
        grid=(count, size),
        in_specs=[
            pl.BlockSpec((1, rows, depth), lambda b, k: (b, k, 0)),
            pl.BlockSpec((depth, width), lambda b, k: (0, 0)),
        ],
        out_specs=pl.BlockSpec((1, 1, rows, width), lambda b, k: (k, b, 0, 0)),
        out_shape=shape_of((size, count, rows, width), bf16),
        compiler_params=params(),
        cost_estimate=cost(13.2),
        name="branch",
    )(hidden, w_down)


def weight_grad_kernel(x_ref, g_ref, o_ref):
    o_ref[...] = dot(x_ref[...], g_ref[...], 0, 0).astype(bf16)


def weight_grad(frames, grads):
    frames = frames.reshape(-1, frames.shape[-1])
    grads = grads.reshape(-1, grads.shape[-1])
    rows, width = frames.shape
    hidden = grads.shape[1]
    block = 256
    return pl.pallas_call(
        weight_grad_kernel,
        grid=(width // block,),
        in_specs=[
            pl.BlockSpec((rows, block), lambda i: (0, i)),
            pl.BlockSpec((rows, hidden), lambda i: (0, 0)),
        ],
        out_specs=pl.BlockSpec((block, hidden), lambda i: (i, 0)),
        out_shape=shape_of((width, hidden), bf16),
        compiler_params=params(),
        cost_estimate=cost(10),
        name="weight_grad",
    )(frames, grads)


def self_weight_grad_kernel(count, x_ref, p_ref, f_ref, *refs):
    d_refs = refs[:count]
    w_refs = refs[count : count + 3]
    o_ref, gain_ref, shift_ref, sum_ref = refs[count + 3 :]
    local = w_refs[0].shape[1]

    @pl.when(pl.program_id(0) == 0)
    def _():
        ones = jnp.ones((8, x_ref.shape[1]), bf16)
        for third in range(3):
            part = slice(third * local, (third + 1) * local)
            sums = jnp.zeros((8, local), f32)
            for b in range(count):
                sums = sums + dot(ones, d_refs[b][third], 1, 1) + f_ref[b : b + 1, part]
            sum_ref[:, part] = sums

    gain = jnp.zeros(gain_ref.shape, f32)
    shift = jnp.zeros(shift_ref.shape, f32)
    result = jnp.zeros((x_ref.shape[2], 3 * local), f32)
    for b in range(count):
        grads = d_refs[b][...].reshape(3 * local, -1)
        result = result + dot(x_ref[b], grads, 0, 1) + p_ref[:, b : b + 1] * f_ref[b : b + 1]
    o_ref[...] = result.astype(bf16)
    for third in range(3):
        part = slice(third * local, (third + 1) * local)
        weight = w_refs[third][...].astype(f32)
        gain = gain + jnp.sum(weight * result[:, part], axis=1, keepdims=True)
        shift = shift + jnp.sum(weight * sum_ref[0:1, part], axis=1, keepdims=True)
    gain_ref[...] = gain
    shift_ref[...] = shift


def self_weight_grad(frames, prefix, grads, front, weights):
    count, rows, width = frames.shape
    local = grads[0].shape[1]
    depth = 3 * local
    block = 256
    weight = pl.BlockSpec((block, local), lambda i: (i, 0))
    column = pl.BlockSpec((block, 1), lambda i: (i, 0))
    return pl.pallas_call(
        functools.partial(self_weight_grad_kernel, count),
        grid=(width // block,),
        in_specs=[
            pl.BlockSpec((count, rows, block), lambda i: (0, 0, i)),
            pl.BlockSpec((block, count), lambda i: (i, 0)),
            pl.BlockSpec((count, depth), lambda i: (0, 0)),
        ]
        + [pl.BlockSpec((3, local, rows), lambda i: (0, 0, 0))] * count
        + [weight] * 3,
        out_specs=[pl.BlockSpec((block, depth), lambda i: (i, 0)), column, column],
        out_shape=[shape_of((width, depth), bf16)] + [shape_of((width, 1), f32)] * 2,
        scratch_shapes=[pltpu.VMEM((8, depth), f32)],
        compiler_params=params(),
        cost_estimate=cost(12),
        name="self_weight_grad",
    )(frames, prefix.T.astype(f32), front.astype(f32), *grads, *weights)


def self_back_kernel(d_ref, wq_ref, wk_ref, wv_ref, o_ref):
    local = wq_ref.shape[1]
    back = jnp.zeros(o_ref.shape[1:], f32)
    for third, ref in enumerate((wq_ref, wk_ref, wv_ref)):
        back = back + dot(d_ref[third], ref[...], 0, 1)
    o_ref[0] = back.astype(bf16)


def self_back(grads, weights):
    size = lax.axis_size("mp")
    _, local, frames = grads.shape
    width = weights[0].shape[0]
    rows = frames // size
    return pl.pallas_call(
        self_back_kernel,
        grid=(size,),
        in_specs=[pl.BlockSpec((3, local, rows), lambda k: (0, 0, k))] + whole_specs(weights),
        out_specs=pl.BlockSpec((1, rows, width), lambda k: (k, 0, 0)),
        out_shape=shape_of((size, rows, width), bf16),
        compiler_params=params(),
        cost_estimate=cost(7),
        name="self_back",
    )(grads, *weights)


def turning(frames):
    places = (jnp.arange(frames) + 1).astype(f32)
    rates = jnp.exp(jnp.arange(HALF).astype(f32) * (-2.0 * math.log(10000.0) / HEAD_DIM))
    angles = rates[:, None] * places[None, :]
    return (jnp.cos(angles), jnp.sin(angles))


def sum_over_clips(values, axis):
    return lax.psum_scatter(values.astype(bf16), "dp", scatter_dimension=axis, tiled=True)


def shards(
    frames_in,
    prompt,
    lengths,
    tsteps,
    table,
    gain_one,
    shift_one,
    gain_two,
    shift_two,
    gain_three,
    shift_three,
    w_query,
    w_key,
    w_value,
    w_out,
    c_query,
    c_key,
    c_value,
    c_out,
    w_gate,
    w_up,
    w_down,
    cotangent,
):
    size = lax.axis_size("mp")
    groups = lax.axis_size("dp")
    count, rows, width = frames_in.shape
    clips = range(count)
    local = w_query.shape[1]
    here = lax.axis_index("mp")
    there = lax.axis_index("dp")
    core = there & 1
    chain = Chain()
    hold, mark, arrive = chain.hold, chain.mark, chain.arrive

    def joined(parts, axis):
        return jnp.concatenate(parts, axis=axis)

    order = jnp.stack([here ^ k for k in range(size)]).astype(jnp.int32)
    this_core = jnp.stack([core]).astype(jnp.int32)
    depth = width // groups
    side = jnp.stack(
        [
            lax.dynamic_slice_in_dim(c_query, there * depth, depth, 0),
            lax.dynamic_slice_in_dim(c_out, there * depth, depth, 1).T,
        ]
    )
    side = lax.all_gather(side, "mp", axis=0)
    ones, low = [], []
    for b in clips:
        ones.append(norm_forward(hold(frames_in[b]).astype(f32), gain_one, shift_one))
        low.append(ones[b][0].astype(bf16))
        mark(low[b])
        if b == 0:
            spread_one = [Spread(low[0])]
            spread_one[0].first = arrive(spread_one[0].first)
            spread_one[0].second_step()
        else:
            spread_one.append(Spread(low[b]))
    tokens = prompt.reshape(-1, prompt.shape[-1])
    memory = [dot(hold(part), tokens, 0, 1).astype(bf16) for part in (c_key, c_value)]
    mark(*memory)
    memory = joined(memory, 0)
    side = arrive(side)
    c_query_all = lax.all_gather(side[:, 0], "dp", axis=1, tiled=True)
    c_out_all = lax.all_gather(side[:, 1], "dp", axis=1, tiled=True)
    cosine, sine = turning(size * rows)
    picked = [lax.dynamic_slice_in_dim(hold(table), tsteps[b], 1, 0) for b in clips]
    mark(*picked)
    picked = joined(picked + [jnp.ones((8 - count, width), f32)], 0)
    norm_one = jnp.stack([gain_one, shift_one])
    half = lax.dynamic_slice_in_dim(hold(w_out), core * (local // 2), local // 2, 0)
    mark(half)
    spread_one[0].last = arrive(spread_one[0].last)

    turned, mixed_part, logsum, mixed = [], [], [], []
    frames_one = ()
    weights = [w_query, w_key, w_value]
    for b in clips:
        if b:
            spread_one[b].last = arrive(spread_one[b].last)
        pieces = hold(spread_one[b].pieces())
        out, frames_one, front = project(
            b, count, order, picked, norm_one, pieces, weights, cosine, sine, list(frames_one)
        )
        frames_one = (frames_one,)
        turned.append(out)
        mark(out)
        if b == 0:
            front_keys = [front[:local, c : c + 1] for c in clips]
            front_values = [front[local:, c : c + 1] for c in clips]
            for later in spread_one[1:]:
                later.first = arrive(later.first)
                later.second_step()
            halves = gathered(hold(half))
        else:
            memory = hold(memory)
            memory = [memory] + [swap(memory, "mp", k) for k in range(1, size)]
            halves = arrive(halves)
            other = swap(halves, "dp", 1)
            mixed[0] = exchange(hold(mixed[0]))
        out, sums = self_forward(hold(turned[b]), front_keys[b], front_values[b])
        mixed_part.append(out)
        logsum.append(sums)
        mixed.append(out)
        mark(out)
    frames_one = frames_one[0]
    mixed[0] = arrive(mixed[0])
    for b in clips[1:]:
        mixed[b] = exchange(hold(mixed[b]))
    memory = jnp.stack(arrive(memory))
    mark(memory)
    spread_down = [Spread(hold(cotangent[0]))]
    other = arrive(other)
    local_weights = (halves, other, c_query_all, c_out_all)

    norms = jnp.stack([gain_two, shift_two, gain_three, shift_three])
    first, normed_two, cross, second, low, spread_three = [], [], [], [], [], []
    for b in clips:
        mixed[b] = hold(mixed[b]).reshape(size * local, rows)
        parts = local_forward(
            b, count, lengths, this_core, order, mixed[b], frames_in[b], norms, memory, local_weights
        )
        first.append(parts[0])
        second.append(parts[1])
        normed_two.append(parts[2])
        cross.append(parts[3:6])
        low.append(parts[6])
        mark(low[b])
        if b == 0:
            spread_three.append(Spread(low[b]))
            spread_down[0].first = arrive(spread_down[0].first)
            spread_down[0].second_step()

    back_three = []
    parts = ()
    spread_down[0].last = arrive(spread_down[0].last)
    spread_three[0].first = arrive(spread_three[0].first)
    spread_three[0].second_step()
    spread_three.extend(Spread(hold(later)) for later in low[1:])
    spread_three[0].last = arrive(spread_three[0].last)
    spread_down.extend(Spread(hold(later)) for later in cotangent[1:])
    for b in clips:
        pieces = hold(spread_three[b].pieces())
        parts = glu(
            b, count, order, pieces, spread_down[b].pieces(), w_gate, w_up, w_down, list(parts)
        )
        mark(parts[1])
        if b == 0:
            for later in spread_three[1:] + spread_down[1:]:
                later.first = arrive(later.first)
                later.second_step()
        grad_gate, grad_upper = hold((parts[1], parts[2]))
        back = glu_back(b, grad_gate, grad_upper, w_gate, w_up)
        mark(back)
        if b == 0:
            for later in spread_three[1:] + spread_down[1:]:
                later.last = arrive(later.last)
        else:
            back_three[b - 1] = arrive(back_three[b - 1])
        back_three.append(exchange(hold(back)))

    hidden, grad_gate, grad_upper, frames_three, down_in = parts
    raw_w_down = weight_grad(hold(down_in), hidden)
    grad_w_down = sum_over_clips(raw_w_down, 0)
    mark(raw_w_down)
    branch = branch_blocks(hold(hidden), w_down)
    mark(branch)
    branch = lax.psum_scatter(branch, "mp", scatter_dimension=0, tiled=True)[0]
    raw_w_gate = weight_grad(hold(frames_three), grad_gate)
    grad_w_gate = sum_over_clips(raw_w_gate, 0)
    mark(raw_w_gate)

    grad_one, cross_in, self_in = [], [], []
    grad_cross_query, grad_memory, grad_mixed, norm_terms = [], [], [], []
    for b in clips:
        if b:
            back_three[b] = arrive(back_three[b])
            grad_mixed[b - 1] = exchange(hold(grad_mixed[b - 1]))
        parts = local_backward(
            b,
            count,
            lengths,
            this_core,
            order,
            hold(back_three[b]),
            cotangent[b],
            first[b],
            second[b],
            cross[b],
            norms,
            memory,
            local_weights,
        )
        cross_in.append(parts[0])
        self_in.append(parts[1])
        grad_one.append(parts[2])
        grad_cross_query.append(parts[3])
        grad_memory.append(parts[4])
        norm_terms.append(parts[6])
        mark(parts[5])
        grad_mixed.append(parts[5].reshape(size, local, rows))
    for b in clips[:-1]:
        grad_mixed[b] = arrive(grad_mixed[b])
    grad_mixed[-1] = exchange(hold(grad_mixed[-1]))

    grad_memory = Settle(joined(hold(grad_memory), 2))
    mark(*grad_memory.mine)
    grad_memory = grad_memory.second_step()
    rights = (grad_cross_query, [part[1] for part in cross], mixed)
    other_raws, lefts = whole_grad(
        1 - this_core, groups, (normed_two, hold(cross_in), self_in), rights, []
    )
    mark(other_raws)
    other_raws = swap(other_raws, "dp", 1)
    raw_w_up = weight_grad(hold(frames_three), grad_upper)
    grad_w_up = sum_over_clips(raw_w_up, 0)
    mark(raw_w_up)
    raws = whole_grad(this_core, groups, lefts, rights, [arrive(other_raws)])
    mark(raws)
    raws = Settle(hold(raws).reshape(size, -1, local))
    mark(*raws.mine)
    raws.first_step()

    grad_self, grad_front, back_one = [], [], []
    for b in clips:
        grads, grad_front_key, grad_front_value = self_backward(
            turned[b],
            hold(grad_mixed[b]),
            mixed_part[b],
            logsum[b],
            front_keys[b],
            front_values[b],
            cosine,
            sine,
        )
        grad_self.append(grads)
        grad_front.append(joined([grad_front_key, grad_front_value], 0))
        mark(grads)
        if b + 1 < count:
            grad_mixed[b + 1] = arrive(grad_mixed[b + 1])
            raws.came = arrive(raws.came)
            raws.add()
            mark(*raws.mine)
            raws = raws.second_step()
            back = self_back(hold(grad_self[b]), weights)
            mark(back)
            back_one.append(exchange(hold(back)))
            grad_memory = total(arrive(grad_memory)).astype(bf16)
            low_memory = [
                dot(tokens, part, 0, 1).astype(bf16) for part in jnp.split(grad_memory, 2, axis=0)
            ]
            mark(*low_memory)
            low_memory = [part.reshape(groups, -1, local) for part in low_memory]
            mine, other = core_half(joined(low_memory, 1))

    raws = total(arrive(raws)).astype(bf16).reshape(groups // 2, 3, -1, local)
    memory_half = plus(mine, arrive(other))
    mark(raws, memory_half)
    raws = joined([raws, memory_half[:, None]], 1)
    cores = [list(range(c, groups, 2)) for c in range(2)]
    raws = lax.psum_scatter(raws, "dp", scatter_dimension=0, axis_index_groups=cores, tiled=True)[0]
    prefix_normed, prefix_normal, prefix_scale = norm_forward(
        picked[:count], gain_one, shift_one
    )
    prefix_low = prefix_normed.astype(bf16)
    grad_front = joined(grad_front, 1)
    wide_front = joined([jnp.zeros((count, local), bf16), grad_front.T], 1)
    low_w_self, gain_term, shift_term = self_weight_grad(
        frames_one, prefix_low, hold(grad_self), wide_front, weights
    )
    grad_w_self = sum_over_clips(low_w_self, 0)
    mark(low_w_self)
    back = self_back(hold(grad_self[-1]), weights)
    mark(back)
    back_one = arrive(back_one)
    back_one.append(exchange(hold(back)))

    def wide(value):
        return value.astype(f32)

    small = []
    gain_term, shift_term = gain_term[:, 0], shift_term[:, 0]
    small.append((gain_term - shift_one * shift_term) / gain_one)
    small.append(shift_term)
    norm_terms = sum(norm_terms[1:], norm_terms[0])
    steps = jnp.where(here == 0, tsteps, 0).astype(f32)
    steps = lax.dynamic_update_slice(jnp.zeros((width,), f32), steps, (there * count,))

    back_prefix = dot(grad_front[:local], w_key, 0, 1) + dot(grad_front[local:], w_value, 0, 1)
    grad_picked = norm_backward(back_prefix, prefix_normal, prefix_scale, gain_one)
    spots = jnp.arange(groups)[:, None, None] == there
    spots = jnp.where(spots, grad_picked[None], 0.0).reshape(groups * count, width)
    small = hold(joined([jnp.stack(small), norm_terms, steps[None], spots], 0))
    small = all_sum(small)
    all_steps = small[6, : groups * count]
    matches = jnp.arange(table.shape[0])[:, None].astype(f32) == all_steps[None, :]
    grad_table = jnp.dot(matches.astype(f32), small[7:], precision=lax.Precision.HIGHEST)

    mark(small)
    back_one[-1] = arrive(back_one[-1])
    back_one = [total(terms) for terms in back_one]
    grad_frames = [
        grad_one[b] + norm_backward(back_one[b], ones[b][1], ones[b][2], gain_one) for b in clips
    ]
    mark(grad_table, *grad_frames)
    grad_w_down = wide(arrive(grad_w_down).T)
    branch = arrive(branch)
    output = [second[b] + branch[b].astype(f32) for b in clips]
    grad_w_gate = wide(arrive(grad_w_gate))
    grad_w_up = arrive(grad_w_up)
    raws = arrive(raws).astype(f32)
    grad_w_self = arrive(grad_w_self)

    depth_c = prompt.shape[-1] // groups

    return (
        jnp.stack(output),
        jnp.stack(grad_frames),
        grad_table,
        small[0],
        small[1],
        small[2],
        small[3],
        small[4],
        small[5],
        wide(grad_w_self[:, :local]),
        wide(grad_w_self[:, local : 2 * local]),
        wide(grad_w_self[:, 2 * local :]),
        raws[2].T,
        raws[0],
        raws[3, :depth_c],
        raws[3, depth_c:],
        raws[1].T,
        grad_w_gate,
        wide(grad_w_up),
        grad_w_down,
    )


def solution(mesh):
    placed = (
        P("dp", "mp", None),
        P("dp", None, None),
        P("dp"),
        P("dp"),
        P(),
        P(),
        P(),
        P(),
        P(),
        P(),
        P(),
        P(None, "mp"),
        P(None, "mp"),
        P(None, "mp"),
        P("mp", None),
        P(None, "mp"),
        P(None, "mp"),
        P(None, "mp"),
        P("mp", None),
        P(None, "mp"),
        P(None, "mp"),
        P("mp", None),
        P("dp", "mp", None),
    )
    return jax.shard_map(
        shards,
        mesh=mesh,
        in_specs=placed,
        out_specs=(
            P("dp", "mp", None),
            P("dp", "mp", None),
            P(),
            P(),
            P(),
            P(),
            P(),
            P(),
            P(),
            P("dp", "mp"),
            P("dp", "mp"),
            P("dp", "mp"),
            P("mp", "dp"),
            P("dp", "mp"),
            P("dp", "mp"),
            P("dp", "mp"),
            P("mp", "dp"),
            P("dp", "mp"),
            P("dp", "mp"),
            P("mp", "dp"),
        ),
        check_vma=False,
    )
```

time: 857 us -> 781 us (0.911)
  matrix products: 131 us -> 10.7 us
  Pallas kernels: 205 us -> 313 us
  other arithmetic: 93.3 us -> 48 us
    dot_general x26 -> x6, matrix products: 126 us -> 5.43 us  [dot(): lax.dot_general(left, right, (((left_axis,), (right_axis,)), ((), ())), p...]
    pallas_call x12 -> x19, Pallas kernels: 124 us -> 232 us  [the longest x3 42.9 us: weight_grad(): pl.pallas_call(weight_grad_kernel, grid=(width // block,), in_specs=[pl.B...]
    ppermute x86 -> x42, waiting for transfers between devices: 198 us -> 118 us  [swap(): lax.ppermute(values, axis, [(i, i ^ k) for i in range(lax.axis_size(axis))])]
    all_to_all x0 -> x9, waiting for transfers between devices: none -> 68.5 us  [exchange(): return lax.all_to_all(blocks, 'mp', 0, 0)]
    ppermute x86 -> x42, starting transfers between devices: 92.8 us -> 48.1 us  [swap(): lax.ppermute(values, axis, [(i, i ^ k) for i in range(lax.axis_size(axis))])]
    all_to_all x0 -> x9, starting transfers between devices: none -> 39.5 us  [exchange(): return lax.all_to_all(blocks, 'mp', 0, 0)]
    concatenate x9 -> x4, other arithmetic: 13.2 us -> 2.63 us  [joined(): return jnp.concatenate(parts, axis=axis)]
    convert_element_type x9 -> x2, other arithmetic: 11.5 us -> 2.58 us  [plus(): return (left.astype(f32) + right.astype(f32)).astype(bf16)]
  transfers between devices with their start and end apart: 92 -> 60, of which waited for: 26 -> 22; matrix products, arithmetic and copies ran while one was open for 33% -> 12% of each run, Pallas kernels for 23% -> 39%
where the time goes in v5:
time: 781 us; the launch traced here: 771 us
  Pallas kernels  313 us (40%)
  waiting for transfers between devices  196 us (25%)
  local copies, waits for them, and re-layouts  94.7 us (12%)
  starting transfers between devices  88.4 us (11%)
  other arithmetic  48 us (6%)
  between operations  20.2 us (3%)
  matrix products  10.7 us (1%)
    ppermute x42, waiting for transfers between devices, swap(): lax.ppermute(values, axis, [(i, i ^ k) for i in range(lax.axis_size(axis))])  118 us
    all_to_all x9, waiting for transfers between devices, exchange(): return lax.all_to_all(blocks, 'mp', 0, 0)  68.5 us
    unnamed x322, local copies, waits for them, and re-layouts  55.9 us
    ppermute x42, starting transfers between devices, swap(): lax.ppermute(values, axis, [(i, i ^ k) for i in range(lax.axis_size(axis))])  48.1 us
    pallas_call x2, Pallas kernels, glu(): pl.pallas_call(functools.partial(glu_kernel, size, len(pieces)), grid=(hi...  44.2 us
    pallas_call x3, Pallas kernels, weight_grad(): pl.pallas_call(weight_grad_kernel, grid=(width // block,), in_specs=[pl.B...  42.9 us
    all_to_all x9, starting transfers between devices, exchange(): return lax.all_to_all(blocks, 'mp', 0, 0)  39.5 us
    pallas_call x2, Pallas kernels, self_backward(): pl.pallas_call(functools.partial(self_backward_kernel, min(256, frames)),...  36.8 us
  transfers between devices with their start and end apart: 60, of which 22 were waited for; matrix products, arithmetic and copies ran while one was open for 12% of the time, Pallas kernels for 39%

profile of v5, /device:TPU:0, one launch (start us, length us, event | category | flops | bytes accessed | tf_op | source)
XLA Modules:
  0.0 771.1 jit_solution(14565912072956338146)
XLA Ops:
  21.2 13.8 %collective-permute-done.refs_1_ = bf16[256,1536]{1,0:T(8,128)(2,1)S(1)} collective-permute-done((bf16[256,1536]{1,0:T(8,128)(2,1)S(1)}, bf16[256,1536]{1,0:T(8,128)(2,1)S(1)}, u32[]{:S(2)}, u32[]{:S(2)}) %collective-permute-start) | collective-permute-done | bytes 786464 | tf_op jit(solution)/shard_map/ppermute | solution.py:48
  40.6 8.8 %all-gather.7.cloned.1.call-done = bf16[8,192,384]{2,1,0:T(8,128)(2,1)} async-done(((bf16[2,192,384]{2,1,0:T(8,128)(2,1)}), bf16[8,192,384]{2,1,0:T(8,128)(2,1)}) %all-gather.7.cloned.1.call-update) | async-done | bytes 1179664 | tf_op jit(solution)/shard_map/all_gather | solution.py:1020
  65.3 24.0 %collective-permute-done.2.refs_3_ = bf16[128,1536]{1,0:T(8,128)(2,1)S(1)} collective-permute-done((bf16[128,1536]{1,0:T(8,128)(2,1)S(1)}, bf16[128,1536]{1,0:T(8,128)(2,1)S(1)}, u32[]{:S(2)}, u32[]{:S(2)}) %collective-permute-start.2) | collective-permute-done | bytes 393248 | tf_op jit(solution)/shard_map/ppermute | solution.py:48
  90.7 8.8 %project.2 = (bf16[1152,1024]{1,0:T(8,128)(2,1)}, bf16[2,1024,1536]{2,1,0:T(8,128)(2,1)}, bf16[768,8]{1,0:T(8,128)(2,1)S(1)}) custom-call(s32[4]{0:T(128)S(1)} %pad_add_fusion.n_ref.order_ref, f32[8,1536]{1,0:T(8,128)S(1)} %maximum_maximum_fusion.p_ref, f32[2,1536]{1,0:T(2,128)S(1)} %pad_maximum_fusion.9.norm_ref, bf16[1536,384]{1,0:T(8,128)(2,1)S(1)} %copy-done.89, ...), custom_call_target="tpu_custom_call" | custom-call | flops 3680000000 | bytes 11520000 | tf_op jit(solution)/shard_map/project/pallas_call | solution.py:661
  101.1 4.7 all-to-all-start
  112.4 9.3 %self_forward.2 = (bf16[4,384,256]{2,1,0:T(8,128)(2,1)}, f32[6,1,1024]{2,1,0:T(1,128)S(1)}) custom-call(bf16[1152,1024]{1,0:T(8,128)(2,1)S(1)} %copy-done.110, bf16[1152,1024]{1,0:T(8,128)(2,1)S(1)} %copy-done.110, bf16[1152,1024]{1,0:T(8,128)(2,1)S(1)} %copy-done.110, bf16[384,1]{1,0:T(8,128)(2,1)S(1)} %get-tuple-element.421.pk_ref, ...), custom_call_target="tpu_custom_call" | custom-call | flops 4001999872 | bytes 12528000 | tf_op jit(solution)/shard_map/self_forward/pallas_call | solution.py:544
  121.7 19.2 %collective-permute-done.6.refs_3_ = bf16[128,1536]{1,0:T(8,128)(2,1)S(1)} collective-permute-done((bf16[128,1536]{1,0:T(8,128)(2,1)S(1)}, bf16[128,1536]{1,0:T(8,128)(2,1)S(1)}, u32[]{:S(2)}, u32[]{:S(2)}) %collective-permute-start.6) | collective-permute-done | bytes 393248 | tf_op jit(solution)/shard_map/ppermute | solution.py:48
  141.1 9.1 %project.3 = (bf16[1152,1024]{1,0:T(8,128)(2,1)}, bf16[2,1024,1536]{2,1,0:T(8,128)(2,1)}, bf16[768,8]{1,0:T(8,128)(2,1)}) custom-call(s32[4]{0:T(128)S(1)} %pad_add_fusion.n_ref.order_ref, f32[8,1536]{1,0:T(8,128)S(1)} %maximum_maximum_fusion.p_ref, f32[2,1536]{1,0:T(2,128)S(1)} %pad_maximum_fusion.9.norm_ref, ...), custom_call_target="tpu_custom_call", output_to_operand_aliasing={{1}: (13, {})} | custom-call | flops 3680000000 | bytes 11520000 | tf_op jit(solution)/shard_map/project/pallas_call | solution.py:661
  162.4 8.6 %self_forward.3 = (bf16[4,384,256]{2,1,0:T(8,128)(2,1)S(1)}, f32[6,1,1024]{2,1,0:T(1,128)S(1)}) custom-call(bf16[1152,1024]{1,0:T(8,128)(2,1)S(1)} %copy-done.101, bf16[1152,1024]{1,0:T(8,128)(2,1)S(1)} %copy-done.101, bf16[1152,1024]{1,0:T(8,128)(2,1)S(1)} %copy-done.101, bf16[384,1]{1,0:T(8,128)(2,1)S(1)} %copy-done.70, bf16[384,1]{1,0:T(8,128)(2,1)S(1)} %copy-done.68), custom_call_target="tpu_custom_call" | custom-call | flops 4001999872 | bytes 12528000 | tf_op jit(solution)/shard_map/self_forward/pallas_call | solution.py:544
  171.0 12.5 %all-to-all-done.1 = bf16[4,384,256]{2,1,0:T(8,128)(2,1)S(1)} async-done(((bf16[4,384,256]{2,1,0:T(8,128)(2,1)}), bf16[4,384,256]{2,1,0:T(8,128)(2,1)S(1)}, u32[]{:S(2)}, u32[]{:S(2)}) %all-to-all-start.1) | async-done | bytes 786464 | tf_op jit(solution)/shard_map/all_to_all | solution.py:89
  189.5 4.0 all-to-all-start.2
  194.7 12.0 %local_forward.2 = (f32[256,1536]{1,0:T(8,128)}, f32[256,1536]{1,0:T(8,128)}, bf16[256,1536]{1,0:T(8,128)(2,1)S(1)}, bf16[1536,256]{1,0:T(8,128)(2,1)S(1)}, bf16...) custom-call(s32[2]{0:T(128)S(1)} %copy-done.88, s32[1]{0:T(128)} %bitcast.core_ref, ...), custom_call_target="tpu_custom_call" | custom-call | flops 5198000128 | bytes 16272000 | tf_op jit(solution)/shard_map/local_forward/pallas_call | solution.py:368
  218.6 11.9 %local_forward.3 = (f32[256,1536]{1,0:T(8,128)}, f32[256,1536]{1,0:T(8,128)}, bf16[256,1536]{1,0:T(8,128)(2,1)S(1)}, bf16[1536,256]{1,0:T(8,128)(2,1)S(1)}, bf16...) custom-call(s32[2]{0:T(128)S(1)} %copy-done.88, s32[1]{0:T(128)} %bitcast.core_ref, ...), custom_call_target="tpu_custom_call" | custom-call | flops 5198000128 | bytes 16272000 | tf_op jit(solution)/shard_map/local_forward/pallas_call | solution.py:368
  232.1 8.3 %collective-permute-done.16.refs_8_ = bf16[128,1536]{1,0:T(8,128)(2,1)S(1)} collective-permute-done((bf16[128,1536]{1,0:T(8,128)(2,1)}, bf16[128,1536]{1,0:T(8,128)(2,1)S(1)}, u32[]{:S(2)}, u32[]{:S(2)}) %collective-permute-start.16) | collective-permute-done | bytes 393248 | tf_op jit(solution)/shard_map/ppermute | solution.py:48
  246.4 6.9 collective-permute-done.20.refs_3_
  258.4 22.6 %glu.2 = (bf16[2,1024,1536]{2,1,0:T(8,128)(2,1)}, bf16[2,1024,1536]{2,1,0:T(8,128)(2,1)}, bf16[2,1024,1536]{2,1,0:T(8,128)(2,1)}, bf16[2,1024,1536]{2,1,0:T(8,128)(2,1)}, bf16[2,1024,1536]{2,1,0:T(8,128)(2,1)}) custom-call(s32[4]{0:T(128)S(1)} %pad_add_fusion.n_ref.order_ref, bf16[1536,1536]{1,0:T(8,128)(2,1)} %gate_ref.7, bf16[1536,1536]{1,0:T(8,128)(2,1)} %up_ref.7, ...), custom_call_target="tpu_custom_call" | custom-call | flops 10119999488 | bytes 31680000 | tf_op jit(solution)/shard_map/glu/pallas_call | solution.py:723
  284.1 5.7 collective-permute-done.24.refs_6_
  291.1 14.5 %glu_back.2 = bf16[4,256,1536]{2,1,0:T(8,128)(2,1)S(1)} custom-call(bf16[2,1024,1536]{2,1,0:T(8,128)(2,1)} %get-tuple-element.266.dg_ref.refs_11_, bf16[2,1024,1536]{2,1,0:T(8,128)(2,1)} %get-tuple-element.267.du_ref.refs_12_, bf16[1536,1536]{1,0:T(8,128)(2,1)} %gate_ref.7, bf16[1536,1536]{1,0:T(8,128)(2,1)} %up_ref.7), custom_call_target="tpu_custom_call" | custom-call | flops 6670000128 | bytes 20880000 | tf_op jit(solution)/shard_map/glu_back/pallas_call | solution.py:761
  309.6 4.6 all-to-all-start.3
  319.6 21.6 %glu.3 = (bf16[2,1024,1536]{2,1,0:T(8,128)(2,1)}, bf16[2,1024,1536]{2,1,0:T(8,128)(2,1)}, bf16[2,1024,1536]{2,1,0:T(8,128)(2,1)}, bf16[2,1024,1536]{2,1,0:T(8,128)(2,1)}, bf16[2,1024,1536]{2,1,0:T(8,128)(2,1)}) custom-call(s32[4]{0:T(128)S(1)} %pad_add_fusion.n_ref.order_ref, ...), custom_call_target="tpu_custom_call", output_to_operand_aliasing={{0}: (14, {}), {1}: (15, {}), {2}: (16, {}), {3}: (17, {}),... | custom-call | flops 10119999488 | bytes 31680000 | tf_op jit(solution)/shard_map/glu/pallas_call | solution.py:723
  341.2 14.5 %glu_back.3 = bf16[4,256,1536]{2,1,0:T(8,128)(2,1)S(1)} custom-call(bf16[2,1024,1536]{2,1,0:T(8,128)(2,1)} %get-tuple-element.285.dg_ref, bf16[2,1024,1536]{2,1,0:T(8,128)(2,1)} %get-tuple-element.286.du_ref, bf16[1536,1536]{1,0:T(8,128)(2,1)} %gate_ref.7, bf16[1536,1536]{1,0:T(8,128)(2,1)} %up_ref.7), custom_call_target="tpu_custom_call" | custom-call | flops 6670000128 | bytes 20880000 | tf_op jit(solution)/shard_map/glu_back/pallas_call | solution.py:761
  357.4 14.1 %weight_grad.3 = bf16[1536,1536]{1,0:T(8,128)(2,1)S(1)} custom-call(bf16[2048,1536]{1,0:T(8,128)(2,1)} %bitcast.163, bf16[2048,1536]{1,0:T(8,128)(2,1)} %bitcast.162), custom_call_target="tpu_custom_call" | custom-call | flops 4600000000 | bytes 14400000 | tf_op jit(solution)/shard_map/weight_grad/pallas_call | solution.py:863
  376.0 13.4 %branch.1 = bf16[4,2,256,1536]{3,2,1,0:T(8,128)(2,1)} custom-call(bf16[2,1024,1536]{2,1,0:T(8,128)(2,1)} %get-tuple-element.289.x_ref, bf16[1536,1536]{1,0:T(8,128)(2,1)S(1)} %copy-done.7), custom_call_target="tpu_custom_call" | custom-call | flops 6072000000 | bytes 19008000 | tf_op jit(solution)/shard_map/branch/pallas_call | solution.py:838
  389.5 14.4 %weight_grad.4 = bf16[1536,1536]{1,0:T(8,128)(2,1)S(1)} custom-call(bf16[2048,1536]{1,0:T(8,128)(2,1)} %bitcast.157, bf16[2048,1536]{1,0:T(8,128)(2,1)} %bitcast.155), custom_call_target="tpu_custom_call" | custom-call | flops 4600000000 | bytes 14400000 | tf_op jit(solution)/shard_map/weight_grad/pallas_call | solution.py:863
  406.1 4.8 all-to-all-start.4
  411.0 16.9 %local_backward.2 = (bf16[256,1536]{1,0:T(8,128)(2,1)S(1)}, bf16[256,1536]{1,0:T(8,128)(2,1)S(1)}, f32[256,1536]{1,0:T(8,128)}, bf16[1536,256]{1,0:T(8,128)(2,1)...) custom-call(s32[2]{0:T(128)S(1)} %copy-done.88, s32[1]{0:T(128)} %bitcast.core_ref, ...), custom_call_target="tpu_custom_call" | custom-call | flops 2300000000 | bytes 7200000 | tf_op jit(solution)/shard_map/local_backward/pallas_call | solution.py:471
  431.5 18.1 %all-to-all-done.4.b_ref = bf16[4,256,1536]{2,1,0:T(8,128)(2,1)} async-done(((bf16[4,256,1536]{2,1,0:T(8,128)(2,1)}), bf16[4,256,1536]{2,1,0:T(8,128)(2,1)}, u32[]{:S(2)}, u32[]{:S(2)}) %all-to-all-start.4) | async-done | bytes 3145760 | tf_op jit(solution)/shard_map/all_to_all | solution.py:89
  449.6 4.2 all-to-all-start.5
  454.4 16.6 %local_backward.3 = (bf16[256,1536]{1,0:T(8,128)(2,1)S(1)}, bf16[256,1536]{1,0:T(8,128)(2,1)S(1)}, f32[256,1536]{1,0:T(8,128)}, bf16[1536,256]{1,0:T(8,128)(2,1)...) custom-call(s32[2]{0:T(128)S(1)} %copy-done.88, s32[1]{0:T(128)} %bitcast.core_ref, ...), custom_call_target="tpu_custom_call" | custom-call | flops 2300000000 | bytes 7200000 | tf_op jit(solution)/shard_map/local_backward/pallas_call | solution.py:471
  479.9 12.3 %whole_grad.2 = (bf16[4,4,3,192,384]{4,3,2,1,0:T(8,128)(2,1)}, bf16[3,1536,512]{2,1,0:T(8,128)(2,1)}) custom-call(s32[1]{0:T(128)S(6)} %sub.72.core_ref, bf16[256,1536]{1,0:T(8,128)(2,1)S(1)} %copy-done.107, bf16[256,1536]{1,0:T(8,128)(2,1)S(1)} %copy-done.109, bf16[256,1536]{1,0:T(8,128)(2,1)S(1)} %copy-done.94, bf16[256,1536]{1,0:T(8,128)(2,1)S(1)} %copy-done.98, ...), custom_call_target="tpu_custom_call" | custom-call | flops 5520000000 | bytes 17280000 | tf_op jit(solution)/shard_map/whole_grad/pallas_call | solution.py:814
  492.1 14.4 %weight_grad.5 = bf16[1536,1536]{1,0:T(8,128)(2,1)S(1)} custom-call(bf16[2048,1536]{1,0:T(8,128)(2,1)} %bitcast.158, bf16[2048,1536]{1,0:T(8,128)(2,1)} %bitcast.156), custom_call_target="tpu_custom_call" | custom-call | flops 4600000000 | bytes 14400000 | tf_op jit(solution)/shard_map/weight_grad/pallas_call | solution.py:863
  513.9 4.2 all-to-all-start.6
  521.7 11.4 %whole_grad.3 = bf16[4,4,3,192,384]{4,3,2,1,0:T(8,128)(2,1)} custom-call(s32[1]{0:T(128)} %bitcast.core_ref, bf16[3,1536,512]{2,1,0:T(8,128)(2,1)} %get-tuple-element.324.refs_0_, bf16[1536,256]{1,0:T(8,128)(2,1)S(1)} %copy-done.31, bf16[1536,256]{1,0:T(8,128)(2,1)S(1)} %copy-done.33, bf16[1536,256]{1,0:T(8,128)(2,1)S(1)} %copy-done.9, ...), custom_call_target="tpu_custom_call" | custom-call | flops 5520000000 | bytes 17280000 | tf_op jit(solution)/shard_map/whole_grad/pallas_call | solution.py:814
  533.1 3.6 dynamic-slice_bitcast_fusion.2
  543.2 18.3 %self_backward.2 = (bf16[3,384,1024]{2,1,0:T(8,128)(2,1)S(1)}, bf16[384,1]{1,0:T(8,128)(2,1)S(1)}, bf16[384,1]{1,0:T(8,128)(2,1)S(1)}) custom-call(bf16[1152,1024]{1,0:T(8,128)(2,1)} %get-tuple-element.214.q_ref.k_ref.v_ref, bf16[1152,1024]{1,0:T(8,128)(2,1)} %get-tuple-element.214.q_ref.k_ref.v_ref, ...), custom_call_target="tpu_custom_call" | custom-call | flops 8280000000 | bytes 25920000 | tf_op jit(solution)/shard_map/self_backward/pallas_call | solution.py:573
  570.1 6.9 self_back.2
  586.2 18.5 %self_backward.3 = (bf16[3,384,1024]{2,1,0:T(8,128)(2,1)S(1)}, bf16[384,1]{1,0:T(8,128)(2,1)S(1)}, bf16[384,1]{1,0:T(8,128)(2,1)S(1)}) custom-call(bf16[1152,1024]{1,0:T(8,128)(2,1)} %get-tuple-element.229.q_ref.k_ref.v_ref, bf16[1152,1024]{1,0:T(8,128)(2,1)} %get-tuple-element.229.q_ref.k_ref.v_ref, ...), custom_call_target="tpu_custom_call" | custom-call | flops 8280000000 | bytes 25920000 | tf_op jit(solution)/shard_map/self_backward/pallas_call | solution.py:573
  615.2 4.8 all-to-all-start.7
  623.8 15.8 %self_weight_grad.1 = (bf16[1536,1152]{1,0:T(8,128)(2,1)}, f32[1536,1]{1,0:T(8,128)S(1)}, f32[1536,1]{1,0:T(8,128)S(1)}) custom-call(bf16[2,1024,1536]{2,1,0:T(8,128)(2,1)} %get-tuple-element.290.x_ref, f32[1536,2]{1,0:T(8,128)S(1)} %get-tuple-element.414.p_ref, f32[2,1152]{1,0:T(2,128)S(1)} %pad_convert_fusion.f_ref, bf16[3,384,1024]{2,1,0:T(8,128)(2,1)} %copy-done.102, ...), custom_call_target="tpu_custom_call" | custom-call | flops 5520000000 | bytes 17280000 | tf_op jit(solution)/shard_map/self_weight_grad/pallas_call | solution.py:917
  644.2 6.9 self_back.3
  651.2 4.8 all-to-all-done.7
  656.0 4.7 all-to-all-start.8
  663.8 32.5 %all-to-all-done.8 = bf16[4,256,1536]{2,1,0:T(8,128)(2,1)} async-done(((bf16[4,256,1536]{2,1,0:T(8,128)(2,1)}), bf16[4,256,1536]{2,1,0:T(8,128)(2,1)}, u32[]{:S(2)}, u32[]{:S(2)}) %all-to-all-start.8) | async-done | bytes 3145760 | tf_op jit(solution)/shard_map/all_to_all | solution.py:89
  699.1 8.7 %collective-permute-done.38 = f32[23,1536]{1,0:T(8,128)S(1)} collective-permute-done((f32[23,1536]{1,0:T(8,128)S(1)}, f32[23,1536]{1,0:T(8,128)S(1)}, u32[]{:S(2)}, u32[]{:S(2)}) %collective-permute-start.38) | collective-permute-done | bytes 141344 | tf_op jit(solution)/shard_map/ppermute | solution.py:48
  709.9 14.2 %collective-permute-done.39 = f32[23,1536]{1,0:T(8,128)S(1)} collective-permute-done((f32[23,1536]{1,0:T(8,128)S(1)}, f32[23,1536]{1,0:T(8,128)S(1)}, u32[]{:S(2)}, u32[]{:S(2)}) %collective-permute-start.39) | collective-permute-done | bytes 141344 | tf_op jit(solution)/shard_map/ppermute | solution.py:48
  725.7 3.7 collective-permute-done.40
  734.7 3.7 fusion.49
  738.5 5.3 fusion.36
  (553 shorter events, 208.3 us)
Async XLA Ops:
  7.2 42.1 %all-gather.7.cloned.1.call-start = ((), (), s32[]{:S(2)}) async-start(), calls=%async_computation.20 | async-start | bytes 1474560 | tf_op jit(solution)/shard_map/all_gather | solution.py:1020
  11.4 23.7 %collective-permute-start = (bf16[256,1536]{1,0:T(8,128)(2,1)S(1)}, bf16[256,1536]{1,0:T(8,128)(2,1)S(1)}, u32[]{:S(2)}, u32[]{:S(2)}) collective-permute-start(bf16[256,1536]{1,0:T(8,128)(2,1)S(1)} %fusion.21.refs_0_), channel_id=1, source_target_pairs={{0,1},{1,0},{2,3},{3,2},{4,5},{5,4},{6,7},{7,6},{8,9},{9,8},{10,11... | collective-permute-start | bytes 2359304 | tf_op jit(solution)/shard_map/ppermute | solution.py:48
  18.8 174.7 %all-gather.9.cloned.1.call-start = ((), (), s32[]{:S(2)}) async-start(), calls=%async_computation.21 | async-start | bytes 5308416 | tf_op jit(solution)/shard_map/all_gather | solution.py:1037
  51.8 141.7 %all-gather.11.cloned.1.call-start = ((), (), s32[]{:S(2)}) async-start(), calls=%async_computation.22 | async-start | bytes 5308416 | tf_op jit(solution)/shard_map/all_gather | solution.py:1038
  60.3 39.2 %collective-permute-start.4 = (bf16[256,1536]{1,0:T(8,128)(2,1)}, bf16[256,1536]{1,0:T(8,128)(2,1)}, u32[]{:S(2)}, u32[]{:S(2)}) collective-permute-start(bf16[256,1536]{1,0:T(8,128)(2,1)} %fusion.14.refs_0_), channel_id=1, source_target_pairs={{0,1},{1,0},{2,3},{3,2},{4,5},{5,4},{6,7},{7,6},{8,9},{9,8},{10,11... | collective-permute-start | bytes 2359304 | tf_op jit(solution)/shard_map/ppermute | solution.py:48
  61.7 37.7 %collective-permute-start.5 = (bf16[256,1536]{1,0:T(8,128)(2,1)}, bf16[256,1536]{1,0:T(8,128)(2,1)}, u32[]{:S(2)}, u32[]{:S(2)}) collective-permute-start(bf16[256,1536]{1,0:T(8,128)(2,1)} %fusion.14.refs_0_), channel_id=1, source_target_pairs={{0,2},{1,3},{2,0},{3,1},{4,6},{5,7},{6,4},{7,5},{8,10},{9,11},{10,... | collective-permute-start | bytes 2359304 | tf_op jit(solution)/shard_map/ppermute | solution.py:48
  62.2 27.1 %collective-permute-start.2 = (bf16[128,1536]{1,0:T(8,128)(2,1)S(1)}, bf16[128,1536]{1,0:T(8,128)(2,1)S(1)}, u32[]{:S(2)}, u32[]{:S(2)}) collective-permute-start(bf16[128,1536]{1,0:T(8,128)(2,1)S(1)} %slice.188), channel_id=1, source_target_pairs={{0,2},{1,3},{2,0},{3,1},{4,6},{5,7},{6,4},{7,5},{8,10},{9,11},{10,... | collective-permute-start | bytes 1179656 | tf_op jit(solution)/shard_map/ppermute | solution.py:48
  63.8 25.6 %collective-permute-start.3 = (bf16[128,1536]{1,0:T(8,128)(2,1)S(1)}, bf16[128,1536]{1,0:T(8,128)(2,1)S(1)}, u32[]{:S(2)}, u32[]{:S(2)}) collective-permute-start(bf16[128,1536]{1,0:T(8,128)(2,1)S(1)} %slice.189), channel_id=1, source_target_pairs={{0,1},{1,0},{2,3},{3,2},{4,5},{5,4},{6,7},{7,6},{8,9},{9,8},{10,11... | collective-permute-start | bytes 1179656 | tf_op jit(solution)/shard_map/ppermute | solution.py:48
  101.1 49.1 %all-to-all-start = ((bf16[4,192,1536]{2,1,0:T(8,128)(2,1)}), bf16[4,192,1536]{2,1,0:T(8,128)(2,1)}, u32[]{:S(2)}, u32[]{:S(2)}) async-start(bf16[4,192,1536]{2,1,0:T(8,128)(2,1)} %broadcast_in_dim.47), calls=%async_computation | async-start | bytes 4718592 | tf_op jit(solution)/shard_map/all_to_all | solution.py:89
  108.0 32.9 %collective-permute-start.6 = (bf16[128,1536]{1,0:T(8,128)(2,1)S(1)}, bf16[128,1536]{1,0:T(8,128)(2,1)S(1)}, u32[]{:S(2)}, u32[]{:S(2)}) collective-permute-start(bf16[128,1536]{1,0:T(8,128)(2,1)S(1)} %slice.192), channel_id=1, source_target_pairs={{0,2},{1,3},{2,0},{3,1},{4,6},{5,7},{6,4},{7,5},{8,10},{9,11},{10,... | collective-permute-start | bytes 1179656 | tf_op jit(solution)/shard_map/ppermute | solution.py:48
  110.1 30.9 %collective-permute-start.7 = (bf16[128,1536]{1,0:T(8,128)(2,1)S(1)}, bf16[128,1536]{1,0:T(8,128)(2,1)S(1)}, u32[]{:S(2)}, u32[]{:S(2)}) collective-permute-start(bf16[128,1536]{1,0:T(8,128)(2,1)S(1)} %slice.193), channel_id=1, source_target_pairs={{0,1},{1,0},{2,3},{3,2},{4,5},{5,4},{6,7},{7,6},{8,9},{9,8},{10,11... | collective-permute-start | bytes 1179656 | tf_op jit(solution)/shard_map/ppermute | solution.py:48
  150.2 43.3 %collective-permute-start.8 = (bf16[4,192,1536]{2,1,0:T(8,128)(2,1)}, bf16[4,192,1536]{2,1,0:T(8,128)(2,1)}, u32[]{:S(2)}, u32[]{:S(2)}) collective-permute-start(bf16[4,192,1536]{2,1,0:T(8,128)(2,1)} %all-to-all-done.wo_mine), channel_id=1, source_target_pairs={{0,4},{4,0},{8,12},{12,8},{16,20},{20,16},{24,28},{28,24},{1,5},{5... | collective-permute-start | bytes 7077896 | tf_op jit(solution)/shard_map/ppermute | solution.py:48
  153.7 29.9 %collective-permute-start.10 = (bf16[768,256]{1,0:T(8,128)(2,1)}, bf16[768,256]{1,0:T(8,128)(2,1)}, u32[]{:S(2)}, u32[]{:S(2)}) collective-permute-start(bf16[768,256]{1,0:T(8,128)(2,1)} %pad_maximum_fusion.6), channel_id=1, source_target_pairs={{0,2},{1,3},{2,0},{3,1},{4,6},{5,7},{6,4},{7,5},{8,10},{9,11},{10,... | collective-permute-start | bytes 1179656 | tf_op jit(solution)/shard_map/ppermute | solution.py:48
  155.1 28.5 %collective-permute-start.11 = (bf16[768,256]{1,0:T(8,128)(2,1)}, bf16[768,256]{1,0:T(8,128)(2,1)}, u32[]{:S(2)}, u32[]{:S(2)}) collective-permute-start(bf16[768,256]{1,0:T(8,128)(2,1)} %pad_maximum_fusion.6), channel_id=1, source_target_pairs={{0,3},{1,2},{2,1},{3,0},{4,7},{5,6},{6,5},{7,4},{8,11},{9,10},{10,... | collective-permute-start | bytes 1179656 | tf_op jit(solution)/shard_map/ppermute | solution.py:48
  156.6 27.0 %collective-permute-start.9 = (bf16[768,256]{1,0:T(8,128)(2,1)}, bf16[768,256]{1,0:T(8,128)(2,1)}, u32[]{:S(2)}, u32[]{:S(2)}) collective-permute-start(bf16[768,256]{1,0:T(8,128)(2,1)} %pad_maximum_fusion.6), channel_id=1, source_target_pairs={{0,1},{1,0},{2,3},{3,2},{4,5},{5,4},{6,7},{7,6},{8,9},{9,8},{10,11... | collective-permute-start | bytes 1179656 | tf_op jit(solution)/shard_map/ppermute | solution.py:48
  157.1 26.4 %all-to-all-start.1 = ((bf16[4,384,256]{2,1,0:T(8,128)(2,1)}), bf16[4,384,256]{2,1,0:T(8,128)(2,1)S(1)}, u32[]{:S(2)}, u32[]{:S(2)}) async-start(bf16[4,384,256]{2,1,0:T(8,128)(2,1)} %get-tuple-element.228.o_ref), calls=%async_computation.1 | async-start | bytes 1572864 | tf_op jit(solution)/shard_map/all_to_all | solution.py:89
  186.5 25.4 %collective-permute-start.12 = (bf16[256,1536]{1,0:T(8,128)(2,1)}, bf16[256,1536]{1,0:T(8,128)(2,1)}, u32[]{:S(2)}, u32[]{:S(2)}) collective-permute-start(bf16[256,1536]{1,0:T(8,128)(2,1)} %get-tuple-element.241.refs_5_.cot_ref), channel_id=1, source_target_pairs={{0,1},{1,0},{2,3},{3,2},{4,5},{5,4},{6,7},{7,6},{8,9},{9,8},{10,11... | collective-permute-start | bytes 2359304 | tf_op jit(solution)/shard_map/ppermute | solution.py:48
  187.9 25.0 %collective-permute-start.13 = (bf16[256,1536]{1,0:T(8,128)(2,1)}, bf16[256,1536]{1,0:T(8,128)(2,1)}, u32[]{:S(2)}, u32[]{:S(2)}) collective-permute-start(bf16[256,1536]{1,0:T(8,128)(2,1)} %get-tuple-element.241.refs_5_.cot_ref), channel_id=1, source_target_pairs={{0,2},{1,3},{2,0},{3,1},{4,6},{5,7},{6,4},{7,5},{8,10},{9,11},{10,... | collective-permute-start | bytes 2359304 | tf_op jit(solution)/shard_map/ppermute | solution.py:48
  189.5 27.5 %all-to-all-start.2 = ((bf16[4,384,256]{2,1,0:T(8,128)(2,1)}), bf16[4,384,256]{2,1,0:T(8,128)(2,1)S(1)}, u32[]{:S(2)}, u32[]{:S(2)}) async-start(bf16[4,384,256]{2,1,0:T(8,128)(2,1)} %copy-done.34), calls=%async_computation.2 | async-start | bytes 1572864 | tf_op jit(solution)/shard_map/all_to_all | solution.py:89
  208.5 31.8 %collective-permute-start.14 = (bf16[256,1536]{1,0:T(8,128)(2,1)}, bf16[256,1536]{1,0:T(8,128)(2,1)S(1)}, u32[]{:S(2)}, u32[]{:S(2)}) collective-permute-start(bf16[256,1536]{1,0:T(8,128)(2,1)} %get-tuple-element.254.refs_0_), channel_id=1, source_target_pairs={{0,1},{1,0},{2,3},{3,2},{4,5},{5,4},{6,7},{7,6},{8,9},{9,8},{10,11... | collective-permute-start | bytes 2359304 | tf_op jit(solution)/shard_map/ppermute | solution.py:48
  210.5 29.9 %collective-permute-start.15 = (bf16[256,1536]{1,0:T(8,128)(2,1)}, bf16[256,1536]{1,0:T(8,128)(2,1)}, u32[]{:S(2)}, u32[]{:S(2)}) collective-permute-start(bf16[256,1536]{1,0:T(8,128)(2,1)} %get-tuple-element.254.refs_0_), channel_id=1, source_target_pairs={{0,2},{1,3},{2,0},{3,1},{4,6},{5,7},{6,4},{7,5},{8,10},{9,11},{10,... | collective-permute-start | bytes 2359304 | tf_op jit(solution)/shard_map/ppermute | solution.py:48
  217.0 23.3 %collective-permute-start.16 = (bf16[128,1536]{1,0:T(8,128)(2,1)}, bf16[128,1536]{1,0:T(8,128)(2,1)S(1)}, u32[]{:S(2)}, u32[]{:S(2)}) collective-permute-start(bf16[128,1536]{1,0:T(8,128)(2,1)} %slice.199), channel_id=1, source_target_pairs={{0,2},{1,3},{2,0},{3,1},{4,6},{5,7},{6,4},{7,5},{8,10},{9,11},{10,... | collective-permute-start | bytes 1179656 | tf_op jit(solution)/shard_map/ppermute | solution.py:48
  244.5 36.5 %collective-permute-start.18 = (bf16[256,1536]{1,0:T(8,128)(2,1)S(1)}, bf16[256,1536]{1,0:T(8,128)(2,1)S(1)}, u32[]{:S(2)}, u32[]{:S(2)}) collective-permute-start(bf16[256,1536]{1,0:T(8,128)(2,1)S(1)} %get-tuple-element.272.refs_0_), channel_id=1, source_target_pairs={{0,1},{1,0},{2,3},{3,2},{4,5},{5,4},{6,7},{7,6},{8,9},{9,8},{10,11... | collective-permute-start | bytes 2359304 | tf_op jit(solution)/shard_map/ppermute | solution.py:48
  246.1 35.0 %collective-permute-start.19 = (bf16[256,1536]{1,0:T(8,128)(2,1)S(1)}, bf16[256,1536]{1,0:T(8,128)(2,1)S(1)}, u32[]{:S(2)}, u32[]{:S(2)}) collective-permute-start(bf16[256,1536]{1,0:T(8,128)(2,1)S(1)} %get-tuple-element.272.refs_0_), channel_id=1, source_target_pairs={{0,2},{1,3},{2,0},{3,1},{4,6},{5,7},{6,4},{7,5},{8,10},{9,11},{10,... | collective-permute-start | bytes 2359304 | tf_op jit(solution)/shard_map/ppermute | solution.py:48
  256.1 33.7 %collective-permute-start.24 = (bf16[256,1536]{1,0:T(8,128)(2,1)S(1)}, bf16[256,1536]{1,0:T(8,128)(2,1)S(1)}, u32[]{:S(2)}, u32[]{:S(2)}) collective-permute-start(bf16[256,1536]{1,0:T(8,128)(2,1)S(1)} %get-tuple-element.263.refs_5_.cot_ref), channel_id=1, source_target_pairs={{0,1},{1,0},{2,3},{3,2},{4,5},{5,4},{6,7},{7,6},{8,9},{9,8},{10,11... | collective-permute-start | bytes 2359304 | tf_op jit(solution)/shard_map/ppermute | solution.py:48
  256.5 33.3 %collective-permute-start.25 = (bf16[256,1536]{1,0:T(8,128)(2,1)S(1)}, bf16[256,1536]{1,0:T(8,128)(2,1)S(1)}, u32[]{:S(2)}, u32[]{:S(2)}) collective-permute-start(bf16[256,1536]{1,0:T(8,128)(2,1)S(1)} %get-tuple-element.263.refs_5_.cot_ref), channel_id=1, source_target_pairs={{0,2},{1,3},{2,0},{3,1},{4,6},{5,7},{6,4},{7,5},{8,10},{9,11},{10,... | collective-permute-start | bytes 2359304 | tf_op jit(solution)/shard_map/ppermute | solution.py:48
  281.1 26.2 %collective-permute-start.22 = (bf16[128,1536]{1,0:T(8,128)(2,1)S(1)}, bf16[128,1536]{1,0:T(8,128)(2,1)S(1)}, u32[]{:S(2)}, u32[]{:S(2)}) collective-permute-start(bf16[128,1536]{1,0:T(8,128)(2,1)S(1)} %slice.203), channel_id=1, source_target_pairs={{0,2},{1,3},{2,0},{3,1},{4,6},{5,7},{6,4},{7,5},{8,10},{9,11},{10,... | collective-permute-start | bytes 1179656 | tf_op jit(solution)/shard_map/ppermute | solution.py:48
  282.5 24.8 %collective-permute-start.23 = (bf16[128,1536]{1,0:T(8,128)(2,1)S(1)}, bf16[128,1536]{1,0:T(8,128)(2,1)S(1)}, u32[]{:S(2)}, u32[]{:S(2)}) collective-permute-start(bf16[128,1536]{1,0:T(8,128)(2,1)S(1)} %slice.204), channel_id=1, source_target_pairs={{0,1},{1,0},{2,3},{3,2},{4,5},{5,4},{6,7},{7,6},{8,9},{9,8},{10,11... | collective-permute-start | bytes 1179656 | tf_op jit(solution)/shard_map/ppermute | solution.py:48
  309.6 47.8 %all-to-all-start.3 = ((bf16[4,256,1536]{2,1,0:T(8,128)(2,1)}), bf16[4,256,1536]{2,1,0:T(8,128)(2,1)}, u32[]{:S(2)}, u32[]{:S(2)}) async-start(bf16[4,256,1536]{2,1,0:T(8,128)(2,1)} %copy-done.6), calls=%async_computation.3 | async-start | bytes 6291456 | tf_op jit(solution)/shard_map/all_to_all | solution.py:89
  314.2 432.8 %reduce-scatter.9.cloned.1.call-start = ((), (), s32[]{:S(2)}) async-start(), calls=%async_computation.15 | async-start | bytes 5308416 | tf_op jit(solution)/shard_map/reduce_scatter | solution.py:969
  373.7 373.4 %reduce-scatter.19.cloned.1.call-start = ((), (), s32[]{:S(2)}) async-start(), calls=%async_computation.23 | async-start | bytes 7864320
  389.4 357.6 %reduce-scatter.17.cloned.1.call-start = ((), (), s32[]{:S(2)}) async-start(), calls=%async_computation.19 | async-start | bytes 5308416 | tf_op jit(solution)/shard_map/reduce_scatter | solution.py:969
  406.1 43.5 %all-to-all-start.4 = ((bf16[4,256,1536]{2,1,0:T(8,128)(2,1)}), bf16[4,256,1536]{2,1,0:T(8,128)(2,1)}, u32[]{:S(2)}, u32[]{:S(2)}) async-start(bf16[4,256,1536]{2,1,0:T(8,128)(2,1)} %copy-done.5), calls=%async_computation.5 | async-start | bytes 6291456 | tf_op jit(solution)/shard_map/all_to_all | solution.py:89
  449.6 25.8 %all-to-all-start.5 = ((bf16[4,384,256]{2,1,0:T(8,128)(2,1)}), bf16[4,384,256]{2,1,0:T(8,128)(2,1)}, u32[]{:S(2)}, u32[]{:S(2)}) async-start(bf16[4,384,256]{2,1,0:T(8,128)(2,1)} %bitcast.154), calls=%async_computation.6 | async-start | bytes 1572864 | tf_op jit(solution)/shard_map/all_to_all | solution.py:89
  453.8 295.6 %reduce-scatter.15.cloned.1.call-start = ((), (), s32[]{:S(2)}) async-start(), calls=%async_computation.18 | async-start | bytes 5308416 | tf_op jit(solution)/shard_map/reduce_scatter | solution.py:969
  492.1 26.0 %collective-permute-start.28 = (bf16[4,4,3,192,384]{4,3,2,1,0:T(8,128)(2,1)}, bf16[4,4,3,192,384]{4,3,2,1,0:T(8,128)(2,1)}, u32[]{:S(2)}, u32[]{:S(2)}) collective-permute-start(bf16[4,4,3,192,384]{4,3,2,1,0:T(8,128)(2,1)} %get-tuple-element.325), channel_id=1, source_target_pairs={{0,4},{4,0},{8,12},{12,8},{16,20},{20,16},{24,28},{28,24},{1,5},{5... | collective-permute-start | bytes 21233672 | tf_op jit(solution)/shard_map/ppermute | solution.py:48
  510.1 66.9 %collective-permute-start.29 = (bf16[768,256]{1,0:T(8,128)(2,1)}, bf16[768,256]{1,0:T(8,128)(2,1)}, u32[]{:S(2)}, u32[]{:S(2)}) collective-permute-start(bf16[768,256]{1,0:T(8,128)(2,1)} %get-tuple-element.400), channel_id=1, source_target_pairs={{0,1},{1,0},{2,3},{3,2},{4,5},{5,4},{6,7},{7,6},{8,9},{9,8},{10,11... | collective-permute-start | bytes 1179656 | tf_op jit(solution)/shard_map/ppermute | solution.py:48
  512.5 64.6 %collective-permute-start.30 = (bf16[768,256]{1,0:T(8,128)(2,1)}, bf16[768,256]{1,0:T(8,128)(2,1)}, u32[]{:S(2)}, u32[]{:S(2)}) collective-permute-start(bf16[768,256]{1,0:T(8,128)(2,1)} %get-tuple-element.399), channel_id=1, source_target_pairs={{0,2},{1,3},{2,0},{3,1},{4,6},{5,7},{6,4},{7,5},{8,10},{9,11},{10,... | collective-permute-start | bytes 1179656 | tf_op jit(solution)/shard_map/ppermute | solution.py:48
  513.9 63.1 %collective-permute-start.31 = (bf16[768,256]{1,0:T(8,128)(2,1)}, bf16[768,256]{1,0:T(8,128)(2,1)}, u32[]{:S(2)}, u32[]{:S(2)}) collective-permute-start(bf16[768,256]{1,0:T(8,128)(2,1)} %get-tuple-element.398), channel_id=1, source_target_pairs={{0,3},{1,2},{2,1},{3,0},{4,7},{5,6},{6,5},{7,4},{8,11},{9,10},{10,... | collective-permute-start | bytes 1179656 | tf_op jit(solution)/shard_map/ppermute | solution.py:48
  513.9 48.9 %all-to-all-start.6 = ((bf16[4,384,256]{2,1,0:T(8,128)(2,1)}), bf16[4,384,256]{2,1,0:T(8,128)(2,1)}, u32[]{:S(2)}, u32[]{:S(2)}) async-start(bf16[4,384,256]{2,1,0:T(8,128)(2,1)} %bitcast.153), calls=%async_computation.7 | async-start | bytes 1572864 | tf_op jit(solution)/shard_map/all_to_all | solution.py:89
  518.1 241.2 %reduce-scatter.13.cloned.1.call-start = ((), (), s32[]{:S(2)}) async-start(), calls=%async_computation.17 | async-start | bytes 2949120 | tf_op jit(solution)/shard_map/reduce_scatter | solution.py:1234
  536.7 26.1 %collective-permute-start.32 = (bf16[1152,384]{1,0:T(8,128)(2,1)}, bf16[1152,384]{1,0:T(8,128)(2,1)}, u32[]{:S(2)}, u32[]{:S(2)}) collective-permute-start(bf16[1152,384]{1,0:T(8,128)(2,1)} %get-tuple-element.389), channel_id=1, source_target_pairs={{0,2},{1,3},{2,0},{3,1},{4,6},{5,7},{6,4},{7,5},{8,10},{9,11},{10,... | collective-permute-start | bytes 2654216 | tf_op jit(solution)/shard_map/ppermute | solution.py:48
  538.7 24.2 %collective-permute-start.33 = (bf16[1152,384]{1,0:T(8,128)(2,1)}, bf16[1152,384]{1,0:T(8,128)(2,1)}, u32[]{:S(2)}, u32[]{:S(2)}) collective-permute-start(bf16[1152,384]{1,0:T(8,128)(2,1)} %get-tuple-element.390), channel_id=1, source_target_pairs={{0,1},{1,0},{2,3},{3,2},{4,5},{5,4},{6,7},{7,6},{8,9},{9,8},{10,11... | collective-permute-start | bytes 2654216 | tf_op jit(solution)/shard_map/ppermute | solution.py:48
  566.7 39.8 %collective-permute-start.35 = (bf16[2304,384]{1,0:T(8,128)(2,1)}, bf16[2304,384]{1,0:T(8,128)(2,1)}, u32[]{:S(2)}, u32[]{:S(2)}) collective-permute-start(bf16[2304,384]{1,0:T(8,128)(2,1)} %pad_maximum_fusion.4), channel_id=1, source_target_pairs={{0,2},{1,3},{2,0},{3,1},{4,6},{5,7},{6,4},{7,5},{8,10},{9,11},{10,... | collective-permute-start | bytes 5308424 | tf_op jit(solution)/shard_map/ppermute | solution.py:48
  568.7 39.4 %collective-permute-start.34 = (bf16[2304,384]{1,0:T(8,128)(2,1)}, bf16[2304,384]{1,0:T(8,128)(2,1)}, u32[]{:S(2)}, u32[]{:S(2)}) collective-permute-start(bf16[2304,384]{1,0:T(8,128)(2,1)} %pad_maximum_fusion.3), channel_id=1, source_target_pairs={{0,1},{1,0},{2,3},{3,2},{4,5},{5,4},{6,7},{7,6},{8,9},{9,8},{10,11... | collective-permute-start | bytes 5308424 | tf_op jit(solution)/shard_map/ppermute | solution.py:48
  615.2 40.8 %all-to-all-start.7 = ((bf16[4,256,1536]{2,1,0:T(8,128)(2,1)}), bf16[4,256,1536]{2,1,0:T(8,128)(2,1)}, u32[]{:S(2)}, u32[]{:S(2)}) async-start(bf16[4,256,1536]{2,1,0:T(8,128)(2,1)} %self_back.2), calls=%async_computation.8 | async-start | bytes 6291456 | tf_op jit(solution)/shard_map/all_to_all | solution.py:89
  656.0 40.3 %all-to-all-start.8 = ((bf16[4,256,1536]{2,1,0:T(8,128)(2,1)}), bf16[4,256,1536]{2,1,0:T(8,128)(2,1)}, u32[]{:S(2)}, u32[]{:S(2)}) async-start(bf16[4,256,1536]{2,1,0:T(8,128)(2,1)} %self_back.3), calls=%async_computation.9 | async-start | bytes 6291456 | tf_op jit(solution)/shard_map/all_to_all | solution.py:89
  660.7 101.5 %reduce-scatter.11.cloned.1.call-start = ((), (), s32[]{:S(2)}) async-start(), calls=%async_computation.16 | async-start | bytes 3981312 | tf_op jit(solution)/shard_map/reduce_scatter | solution.py:969
  (172 other events, 1827.2 us)
Sparse Core Ops, SparseCore 0:
  19.0 30.3 all-gather.6
  51.9 51.6 all-gather.8
  105.3 50.5 all-gather.10
  373.8 56.1 reduce-scatter.8
  432.8 80.0 reduce-scatter.18
  515.1 54.9 reduce-scatter.16
  572.4 53.3 reduce-scatter.14
  628.0 46.3 reduce-scatter.12
  676.8 49.6 reduce-scatter.10

commit v6 on v5

--- a/solution.py
+++ b/solution.py
@@ -509,7 +509,7 @@
         + [pltpu.VMEM(weights[2].shape, bf16)] * 2
         + [pltpu.SemaphoreType.DMA((2 * groups + 2,))],
         compiler_params=params(),
-        cost_estimate=cost(5),
+        cost_estimate=cost(40),
         name="local_backward",
     )(lengths, core, order, back, cotangent, first, second, *cross, norms, memory, *weights)
 
@@ -596,7 +596,7 @@
             shape_of((heads * HEAD_DIM, 1), bf16),
         ],
         compiler_params=params(),
-        cost_estimate=cost(18),
+        cost_estimate=cost(45),
         name="self_backward",
     )(turned, turned, turned, grads, mixed, logsum, front_keys, front_values, cosine, sine)
 
@@ -821,7 +821,7 @@
         out_specs=out if earlier else [out, turned],
         out_shape=out_shape if earlier else [out_shape, turned_shape],
         compiler_params=params(),
-        cost_estimate=cost(12),
+        cost_estimate=cost(30),
         name="whole_grad",
     )(core, *lefts, *rights, *earlier)
 
@@ -1044,13 +1044,16 @@
     half = lax.dynamic_slice_in_dim(hold(w_out), core * (local // 2), local // 2, 0)
     mark(half)
     spread_one[0].last = arrive(spread_one[0].last)
+    for later in spread_one[1:]:
+        later.first = arrive(later.first)
+        later.second_step()
+        later.last = arrive(later.last)
+    halves = gathered(hold(half))
 
     turned, mixed_part, logsum, mixed = [], [], [], []
     frames_one = ()
     weights = [w_query, w_key, w_value]
     for b in clips:
-        if b:
-            spread_one[b].last = arrive(spread_one[b].last)
         pieces = hold(spread_one[b].pieces())
         out, frames_one, front = project(
             b, count, order, picked, norm_one, pieces, weights, cosine, sine, list(frames_one)
@@ -1061,10 +1064,6 @@
         if b == 0:
             front_keys = [front[:local, c : c + 1] for c in clips]
             front_values = [front[local:, c : c + 1] for c in clips]
-            for later in spread_one[1:]:
-                later.first = arrive(later.first)
-                later.second_step()
-            halves = gathered(hold(half))
         else:
             memory = hold(memory)
             memory = [memory] + [swap(memory, "mp", k) for k in range(1, size)]

time: 781 us -> 766 us (0.981)
  waiting for transfers between devices: 196 us -> 170 us
  local copies, waits for them, and re-layouts: 94.7 us -> 112 us
    all_to_all x9, waiting for transfers between devices: 68.5 us -> 48.4 us  [exchange(): return lax.all_to_all(blocks, 'mp', 0, 0)]
    unnamed x322 -> x348, local copies, waits for them, and re-layouts: 55.9 us -> 68.7 us
  transfers between devices with their start and end apart: 60 -> 60, of which waited for: 22 -> 22; matrix products, arithmetic and copies ran while one was open for 12% -> 12% of each run, Pallas kernels for 39% -> 40%
where the time goes in v6:
time: 766 us; the launch traced here: 758 us
  Pallas kernels  314 us (41%)
  waiting for transfers between devices  170 us (22%)
  local copies, waits for them, and re-layouts  112 us (15%)
  starting transfers between devices  88.2 us (12%)
  other arithmetic  44.4 us (6%)
  between operations  19.9 us (3%)
  matrix products  9.75 us (1%)
    ppermute x42, waiting for transfers between devices, swap(): lax.ppermute(values, axis, [(i, i ^ k) for i in range(lax.axis_size(axis))])  111 us
    unnamed x348, local copies, waits for them, and re-layouts  68.7 us
    all_to_all x9, waiting for transfers between devices, exchange(): return lax.all_to_all(blocks, 'mp', 0, 0)  48.4 us
    ppermute x42, starting transfers between devices, swap(): lax.ppermute(values, axis, [(i, i ^ k) for i in range(lax.axis_size(axis))])  47 us
    pallas_call x2, Pallas kernels, glu(): pl.pallas_call(functools.partial(glu_kernel, size, len(pieces)), grid=(hi...  44 us
    pallas_call x3, Pallas kernels, weight_grad(): pl.pallas_call(weight_grad_kernel, grid=(width // block,), in_specs=[pl.B...  42.9 us
    all_to_all x9, starting transfers between devices, exchange(): return lax.all_to_all(blocks, 'mp', 0, 0)  40.7 us
    pallas_call x2, Pallas kernels, self_backward(): pl.pallas_call(functools.partial(self_backward_kernel, min(256, frames)),...  36.7 us
  transfers between devices with their start and end apart: 60, of which 22 were waited for; matrix products, arithmetic and copies ran while one was open for 12% of the time, Pallas kernels for 40%

profile of v6, /device:TPU:0, one launch (start us, length us, event | category | flops | bytes accessed | tf_op | source)
XLA Modules:
  0.0 758.1 jit_solution(17395707547817140223)
XLA Ops:
  21.2 13.8 %collective-permute-done.refs_1_ = bf16[256,1536]{1,0:T(8,128)(2,1)S(1)} collective-permute-done((bf16[256,1536]{1,0:T(8,128)(2,1)S(1)}, bf16[256,1536]{1,0:T(8,128)(2,1)S(1)}, u32[]{:S(2)}, u32[]{:S(2)}) %collective-permute-start) | collective-permute-done | bytes 786464 | tf_op jit(solution)/shard_map/ppermute | solution.py:48
  39.9 9.4 %all-gather.7.cloned.1.call-done = bf16[8,192,384]{2,1,0:T(8,128)(2,1)} async-done(((bf16[2,192,384]{2,1,0:T(8,128)(2,1)}), bf16[8,192,384]{2,1,0:T(8,128)(2,1)}) %all-gather.7.cloned.1.call-update) | async-done | bytes 1179664 | tf_op jit(solution)/shard_map/all_gather | solution.py:1020
  67.2 14.2 %collective-permute-done.2.refs_3_ = bf16[128,1536]{1,0:T(8,128)(2,1)S(1)} collective-permute-done((bf16[128,1536]{1,0:T(8,128)(2,1)S(1)}, bf16[128,1536]{1,0:T(8,128)(2,1)S(1)}, u32[]{:S(2)}, u32[]{:S(2)}) %collective-permute-start.2) | collective-permute-done | bytes 393248 | tf_op jit(solution)/shard_map/ppermute | solution.py:48
  87.2 5.4 collective-permute-done.6.refs_3_
  97.3 4.8 all-to-all-start
  106.6 8.7 %project.2 = (bf16[1152,1024]{1,0:T(8,128)(2,1)}, bf16[2,1024,1536]{2,1,0:T(8,128)(2,1)}, bf16[768,8]{1,0:T(8,128)(2,1)S(1)}) custom-call(s32[4]{0:T(128)S(1)} %pad_add_fusion.n_ref.order_ref, f32[8,1536]{1,0:T(8,128)S(1)} %maximum_maximum_fusion.p_ref, f32[2,1536]{1,0:T(2,128)S(1)} %pad_maximum_fusion.9.norm_ref, bf16[1536,384]{1,0:T(8,128)(2,1)S(1)} %copy-done.71, ...), custom_call_target="tpu_custom_call" | custom-call | flops 3680000000 | bytes 11520000 | tf_op jit(solution)/shard_map/project/pallas_call | solution.py:661
  117.9 9.3 %self_forward.2 = (bf16[4,384,256]{2,1,0:T(8,128)(2,1)}, f32[6,1,1024]{2,1,0:T(1,128)S(1)}) custom-call(bf16[1152,1024]{1,0:T(8,128)(2,1)S(1)} %copy-done.101, bf16[1152,1024]{1,0:T(8,128)(2,1)S(1)} %copy-done.101, bf16[1152,1024]{1,0:T(8,128)(2,1)S(1)} %copy-done.101, bf16[384,1]{1,0:T(8,128)(2,1)S(1)} %get-tuple-element.421.pk_ref, ...), custom_call_target="tpu_custom_call" | custom-call | flops 4001999872 | bytes 12528000 | tf_op jit(solution)/shard_map/self_forward/pallas_call | solution.py:544
  127.3 9.3 %project.3 = (bf16[1152,1024]{1,0:T(8,128)(2,1)}, bf16[2,1024,1536]{2,1,0:T(8,128)(2,1)}, bf16[768,8]{1,0:T(8,128)(2,1)}) custom-call(s32[4]{0:T(128)S(1)} %pad_add_fusion.n_ref.order_ref, f32[8,1536]{1,0:T(8,128)S(1)} %maximum_maximum_fusion.p_ref, f32[2,1536]{1,0:T(2,128)S(1)} %pad_maximum_fusion.9.norm_ref, ...), custom_call_target="tpu_custom_call", output_to_operand_aliasing={{1}: (13, {})} | custom-call | flops 3680000000 | bytes 11520000 | tf_op jit(solution)/shard_map/project/pallas_call | solution.py:661
  143.6 4.1 all-to-all-start.1
  149.5 9.3 %self_forward.3 = (bf16[4,384,256]{2,1,0:T(8,128)(2,1)}, f32[6,1,1024]{2,1,0:T(1,128)S(1)}) custom-call(bf16[1152,1024]{1,0:T(8,128)(2,1)S(1)} %copy-done.84, bf16[1152,1024]{1,0:T(8,128)(2,1)S(1)} %copy-done.84, bf16[1152,1024]{1,0:T(8,128)(2,1)S(1)} %copy-done.84, bf16[384,1]{1,0:T(8,128)(2,1)S(1)} %copy-done.55, bf16[384,1]{1,0:T(8,128)(2,1)S(1)} %copy-done.53), custom_call_target="tpu_custom_call" | custom-call | flops 4001999872 | bytes 12528000 | tf_op jit(solution)/shard_map/self_forward/pallas_call | solution.py:544
  158.8 11.4 %all-to-all-done.1 = bf16[4,384,256]{2,1,0:T(8,128)(2,1)S(1)} async-done(((bf16[4,384,256]{2,1,0:T(8,128)(2,1)}), bf16[4,384,256]{2,1,0:T(8,128)(2,1)S(1)}, u32[]{:S(2)}, u32[]{:S(2)}) %all-to-all-start.1) | async-done | bytes 786464 | tf_op jit(solution)/shard_map/all_to_all | solution.py:89
  176.4 3.9 all-to-all-start.2
  181.5 12.0 %local_forward.2 = (f32[256,1536]{1,0:T(8,128)}, f32[256,1536]{1,0:T(8,128)}, bf16[256,1536]{1,0:T(8,128)(2,1)S(1)}, bf16[1536,256]{1,0:T(8,128)(2,1)S(1)}, bf16...) custom-call(s32[2]{0:T(128)S(1)} %copy-done.83, s32[1]{0:T(128)} %bitcast.core_ref, ...), custom_call_target="tpu_custom_call" | custom-call | flops 5198000128 | bytes 16272000 | tf_op jit(solution)/shard_map/local_forward/pallas_call | solution.py:368
  206.4 11.9 %local_forward.3 = (f32[256,1536]{1,0:T(8,128)}, f32[256,1536]{1,0:T(8,128)}, bf16[256,1536]{1,0:T(8,128)(2,1)S(1)}, bf16[1536,256]{1,0:T(8,128)(2,1)S(1)}, bf16...) custom-call(s32[2]{0:T(128)S(1)} %copy-done.83, s32[1]{0:T(128)} %bitcast.core_ref, ...), custom_call_target="tpu_custom_call" | custom-call | flops 5198000128 | bytes 16272000 | tf_op jit(solution)/shard_map/local_forward/pallas_call | solution.py:368
  221.6 6.6 collective-permute-done.16.refs_8_
  233.5 6.9 collective-permute-done.20.refs_3_
  245.0 22.5 %glu.2 = (bf16[2,1024,1536]{2,1,0:T(8,128)(2,1)}, bf16[2,1024,1536]{2,1,0:T(8,128)(2,1)}, bf16[2,1024,1536]{2,1,0:T(8,128)(2,1)}, bf16[2,1024,1536]{2,1,0:T(8,128)(2,1)}, bf16[2,1024,1536]{2,1,0:T(8,128)(2,1)}) custom-call(s32[4]{0:T(128)S(1)} %pad_add_fusion.n_ref.order_ref, bf16[1536,1536]{1,0:T(8,128)(2,1)} %gate_ref.7, bf16[1536,1536]{1,0:T(8,128)(2,1)} %up_ref.7, ...), custom_call_target="tpu_custom_call" | custom-call | flops 10119999488 | bytes 31680000 | tf_op jit(solution)/shard_map/glu/pallas_call | solution.py:723
  270.0 5.8 collective-permute-done.24.refs_6_
  277.8 14.5 %glu_back.2 = bf16[4,256,1536]{2,1,0:T(8,128)(2,1)S(1)} custom-call(bf16[2,1024,1536]{2,1,0:T(8,128)(2,1)} %get-tuple-element.266.dg_ref.refs_11_, bf16[2,1024,1536]{2,1,0:T(8,128)(2,1)} %get-tuple-element.267.du_ref.refs_12_, bf16[1536,1536]{1,0:T(8,128)(2,1)} %gate_ref.7, bf16[1536,1536]{1,0:T(8,128)(2,1)} %up_ref.7), custom_call_target="tpu_custom_call" | custom-call | flops 6670000128 | bytes 20880000 | tf_op jit(solution)/shard_map/glu_back/pallas_call | solution.py:761
  296.2 4.7 all-to-all-start.3
  306.2 21.5 %glu.3 = (bf16[2,1024,1536]{2,1,0:T(8,128)(2,1)}, bf16[2,1024,1536]{2,1,0:T(8,128)(2,1)}, bf16[2,1024,1536]{2,1,0:T(8,128)(2,1)}, bf16[2,1024,1536]{2,1,0:T(8,128)(2,1)}, bf16[2,1024,1536]{2,1,0:T(8,128)(2,1)}) custom-call(s32[4]{0:T(128)S(1)} %pad_add_fusion.n_ref.order_ref, ...), custom_call_target="tpu_custom_call", output_to_operand_aliasing={{0}: (14, {}), {1}: (15, {}), {2}: (16, {}), {3}: (17, {}),... | custom-call | flops 10119999488 | bytes 31680000 | tf_op jit(solution)/shard_map/glu/pallas_call | solution.py:723
  327.7 14.5 %glu_back.3 = bf16[4,256,1536]{2,1,0:T(8,128)(2,1)S(1)} custom-call(bf16[2,1024,1536]{2,1,0:T(8,128)(2,1)} %get-tuple-element.285.dg_ref, bf16[2,1024,1536]{2,1,0:T(8,128)(2,1)} %get-tuple-element.286.du_ref, bf16[1536,1536]{1,0:T(8,128)(2,1)} %gate_ref.7, bf16[1536,1536]{1,0:T(8,128)(2,1)} %up_ref.7), custom_call_target="tpu_custom_call" | custom-call | flops 6670000128 | bytes 20880000 | tf_op jit(solution)/shard_map/glu_back/pallas_call | solution.py:761
  343.9 14.1 %weight_grad.3 = bf16[1536,1536]{1,0:T(8,128)(2,1)S(1)} custom-call(bf16[2048,1536]{1,0:T(8,128)(2,1)} %bitcast.159, bf16[2048,1536]{1,0:T(8,128)(2,1)} %bitcast.158), custom_call_target="tpu_custom_call" | custom-call | flops 4600000000 | bytes 14400000 | tf_op jit(solution)/shard_map/weight_grad/pallas_call | solution.py:863
  362.6 13.4 %branch.1 = bf16[4,2,256,1536]{3,2,1,0:T(8,128)(2,1)} custom-call(bf16[2,1024,1536]{2,1,0:T(8,128)(2,1)} %get-tuple-element.289.x_ref, bf16[1536,1536]{1,0:T(8,128)(2,1)S(1)} %copy-done.7), custom_call_target="tpu_custom_call" | custom-call | flops 6072000000 | bytes 19008000 | tf_op jit(solution)/shard_map/branch/pallas_call | solution.py:838
  376.0 4.7 all-to-all-start.4
  381.0 14.2 %weight_grad.4 = bf16[1536,1536]{1,0:T(8,128)(2,1)S(1)} custom-call(bf16[2048,1536]{1,0:T(8,128)(2,1)} %bitcast.156, bf16[2048,1536]{1,0:T(8,128)(2,1)} %bitcast.154), custom_call_target="tpu_custom_call" | custom-call | flops 4600000000 | bytes 14400000 | tf_op jit(solution)/shard_map/weight_grad/pallas_call | solution.py:863
  398.5 16.9 %local_backward.2 = (bf16[256,1536]{1,0:T(8,128)(2,1)S(1)}, bf16[256,1536]{1,0:T(8,128)(2,1)S(1)}, f32[256,1536]{1,0:T(8,128)}, bf16[1536,256]{1,0:T(8,128)(2,1)...) custom-call(s32[2]{0:T(128)S(1)} %copy-done.83, s32[1]{0:T(128)} %bitcast.core_ref, ...), custom_call_target="tpu_custom_call" | custom-call | flops 18400000000 | bytes 57600000 | tf_op jit(solution)/shard_map/local_backward/pallas_call | solution.py:471
  420.0 4.7 all-to-all-start.5
  424.7 17.6 %local_backward.3 = (bf16[256,1536]{1,0:T(8,128)(2,1)S(1)}, bf16[256,1536]{1,0:T(8,128)(2,1)S(1)}, f32[256,1536]{1,0:T(8,128)}, bf16[1536,256]{1,0:T(8,128)(2,1)...) custom-call(s32[2]{0:T(128)S(1)} %copy-done.83, s32[1]{0:T(128)} %bitcast.core_ref, ...), custom_call_target="tpu_custom_call" | custom-call | flops 18400000000 | bytes 57600000 | tf_op jit(solution)/shard_map/local_backward/pallas_call | solution.py:471
  450.6 12.3 %whole_grad.2 = (bf16[4,4,3,192,384]{4,3,2,1,0:T(8,128)(2,1)}, bf16[3,1536,512]{2,1,0:T(8,128)(2,1)}) custom-call(s32[1]{0:T(128)S(6)} %sub.72.core_ref, bf16[256,1536]{1,0:T(8,128)(2,1)S(1)} %copy-done.94, bf16[256,1536]{1,0:T(8,128)(2,1)S(1)} %copy-done.96, bf16[256,1536]{1,0:T(8,128)(2,1)S(1)} %copy-done.112, bf16[256,1536]{1,0:T(8,128)(2,1)S(1)} %copy-done.116, ...), custom_call_target="tpu_custom_call" | custom-call | flops 13799999488 | bytes 43200000 | tf_op jit(solution)/shard_map/whole_grad/pallas_call | solution.py:814
  467.1 4.2 all-to-all-start.6
  471.3 14.6 %weight_grad.5 = bf16[1536,1536]{1,0:T(8,128)(2,1)S(1)} custom-call(bf16[2048,1536]{1,0:T(8,128)(2,1)} %bitcast.157, bf16[2048,1536]{1,0:T(8,128)(2,1)} %bitcast.155), custom_call_target="tpu_custom_call" | custom-call | flops 4600000000 | bytes 14400000 | tf_op jit(solution)/shard_map/weight_grad/pallas_call | solution.py:863
  494.0 11.4 %whole_grad.3 = bf16[4,4,3,192,384]{4,3,2,1,0:T(8,128)(2,1)} custom-call(s32[1]{0:T(128)} %bitcast.core_ref, bf16[3,1536,512]{2,1,0:T(8,128)(2,1)} %get-tuple-element.324.refs_0_, bf16[1536,256]{1,0:T(8,128)(2,1)S(1)} %copy-done.108, bf16[1536,256]{1,0:T(8,128)(2,1)S(1)} %copy-done.110, bf16[1536,256]{1,0:T(8,128)(2,1)S(1)} %copy-done.90, ...), custom_call_target="tpu_custom_call" | custom-call | flops 13799999488 | bytes 43200000 | tf_op jit(solution)/shard_map/whole_grad/pallas_call | solution.py:814
  505.4 3.8 dynamic-slice_bitcast_fusion.2
  515.5 18.2 %self_backward.2 = (bf16[3,384,1024]{2,1,0:T(8,128)(2,1)S(1)}, bf16[384,1]{1,0:T(8,128)(2,1)S(1)}, bf16[384,1]{1,0:T(8,128)(2,1)S(1)}) custom-call(bf16[1152,1024]{1,0:T(8,128)(2,1)} %get-tuple-element.216.q_ref.k_ref.v_ref, bf16[1152,1024]{1,0:T(8,128)(2,1)} %get-tuple-element.216.q_ref.k_ref.v_ref, ...), custom_call_target="tpu_custom_call" | custom-call | flops 20700000256 | bytes 64800000 | tf_op jit(solution)/shard_map/self_backward/pallas_call | solution.py:573
  543.4 6.9 self_back.2
  558.6 18.5 %self_backward.3 = (bf16[3,384,1024]{2,1,0:T(8,128)(2,1)S(1)}, bf16[384,1]{1,0:T(8,128)(2,1)S(1)}, bf16[384,1]{1,0:T(8,128)(2,1)S(1)}) custom-call(bf16[1152,1024]{1,0:T(8,128)(2,1)} %get-tuple-element.229.q_ref.k_ref.v_ref, bf16[1152,1024]{1,0:T(8,128)(2,1)} %get-tuple-element.229.q_ref.k_ref.v_ref, ...), custom_call_target="tpu_custom_call" | custom-call | flops 20700000256 | bytes 64800000 | tf_op jit(solution)/shard_map/self_backward/pallas_call | solution.py:573
  577.2 19.7 %collective-permute-done.35 = bf16[2304,384]{1,0:T(8,128)(2,1)S(1)} collective-permute-done((bf16[2304,384]{1,0:T(8,128)(2,1)}, bf16[2304,384]{1,0:T(8,128)(2,1)S(1)}, u32[]{:S(2)}, u32[]{:S(2)}) %collective-permute-start.35) | collective-permute-done | bytes 1769504 | tf_op jit(solution)/shard_map/ppermute | solution.py:48
  602.3 4.8 all-to-all-start.7
  611.0 15.7 %self_weight_grad.1 = (bf16[1536,1152]{1,0:T(8,128)(2,1)}, f32[1536,1]{1,0:T(8,128)S(1)}, f32[1536,1]{1,0:T(8,128)S(1)}) custom-call(bf16[2,1024,1536]{2,1,0:T(8,128)(2,1)} %get-tuple-element.290.x_ref, f32[1536,2]{1,0:T(8,128)S(1)} %get-tuple-element.414.p_ref, f32[2,1152]{1,0:T(2,128)S(1)} %pad_convert_fusion.f_ref, bf16[3,384,1024]{2,1,0:T(8,128)(2,1)} %copy-done.85, ...), custom_call_target="tpu_custom_call" | custom-call | flops 5520000000 | bytes 17280000 | tf_op jit(solution)/shard_map/self_weight_grad/pallas_call | solution.py:917
  631.4 6.9 self_back.3
  638.3 3.9 all-to-all-done.7
  642.2 4.7 all-to-all-start.8
  650.1 32.5 %all-to-all-done.8 = bf16[4,256,1536]{2,1,0:T(8,128)(2,1)} async-done(((bf16[4,256,1536]{2,1,0:T(8,128)(2,1)}), bf16[4,256,1536]{2,1,0:T(8,128)(2,1)}, u32[]{:S(2)}, u32[]{:S(2)}) %all-to-all-start.8) | async-done | bytes 3145760 | tf_op jit(solution)/shard_map/all_to_all | solution.py:89
  685.5 8.5 %collective-permute-done.38 = f32[23,1536]{1,0:T(8,128)S(1)} collective-permute-done((f32[23,1536]{1,0:T(8,128)S(1)}, f32[23,1536]{1,0:T(8,128)S(1)}, u32[]{:S(2)}, u32[]{:S(2)}) %collective-permute-start.38) | collective-permute-done | bytes 141344 | tf_op jit(solution)/shard_map/ppermute | solution.py:48
  696.1 13.9 %collective-permute-done.39 = f32[23,1536]{1,0:T(8,128)S(1)} collective-permute-done((f32[23,1536]{1,0:T(8,128)S(1)}, f32[23,1536]{1,0:T(8,128)S(1)}, u32[]{:S(2)}, u32[]{:S(2)}) %collective-permute-start.39) | collective-permute-done | bytes 141344 | tf_op jit(solution)/shard_map/ppermute | solution.py:48
  720.5 3.8 fusion.49
  724.4 5.3 fusion.36
  (579 shorter events, 218.0 us)
Async XLA Ops:
  7.2 42.1 %all-gather.7.cloned.1.call-start = ((), (), s32[]{:S(2)}) async-start(), calls=%async_computation.20 | async-start | bytes 1474560 | tf_op jit(solution)/shard_map/all_gather | solution.py:1020
  11.4 23.7 %collective-permute-start = (bf16[256,1536]{1,0:T(8,128)(2,1)S(1)}, bf16[256,1536]{1,0:T(8,128)(2,1)S(1)}, u32[]{:S(2)}, u32[]{:S(2)}) collective-permute-start(bf16[256,1536]{1,0:T(8,128)(2,1)S(1)} %fusion.21.refs_0_), channel_id=1, source_target_pairs={{0,1},{1,0},{2,3},{3,2},{4,5},{5,4},{6,7},{7,6},{8,9},{9,8},{10,11... | collective-permute-start | bytes 2359304 | tf_op jit(solution)/shard_map/ppermute | solution.py:48
  14.4 22.3 %collective-permute-start.1 = (bf16[256,1536]{1,0:T(8,128)(2,1)S(1)}, bf16[256,1536]{1,0:T(8,128)(2,1)}, u32[]{:S(2)}, u32[]{:S(2)}) collective-permute-start(bf16[256,1536]{1,0:T(8,128)(2,1)S(1)} %fusion.21.refs_0_), channel_id=1, source_target_pairs={{0,2},{1,3},{2,0},{3,1},{4,6},{5,7},{6,4},{7,5},{8,10},{9,11},{10,... | collective-permute-start | bytes 2359304 | tf_op jit(solution)/shard_map/ppermute | solution.py:48
  18.8 161.5 %all-gather.9.cloned.1.call-start = ((), (), s32[]{:S(2)}) async-start(), calls=%async_computation.21 | async-start | bytes 5308416 | tf_op jit(solution)/shard_map/all_gather | solution.py:1037
  51.8 128.6 %all-gather.11.cloned.1.call-start = ((), (), s32[]{:S(2)}) async-start(), calls=%async_computation.22 | async-start | bytes 5308416 | tf_op jit(solution)/shard_map/all_gather | solution.py:1038
  52.5 29.0 %collective-permute-start.4 = (bf16[256,1536]{1,0:T(8,128)(2,1)S(1)}, bf16[256,1536]{1,0:T(8,128)(2,1)}, u32[]{:S(2)}, u32[]{:S(2)}) collective-permute-start(bf16[256,1536]{1,0:T(8,128)(2,1)S(1)} %fusion.14.refs_0_), channel_id=1, source_target_pairs={{0,1},{1,0},{2,3},{3,2},{4,5},{5,4},{6,7},{7,6},{8,9},{9,8},{10,11... | collective-permute-start | bytes 2359304 | tf_op jit(solution)/shard_map/ppermute | solution.py:48
  54.0 27.4 %collective-permute-start.5 = (bf16[256,1536]{1,0:T(8,128)(2,1)S(1)}, bf16[256,1536]{1,0:T(8,128)(2,1)}, u32[]{:S(2)}, u32[]{:S(2)}) collective-permute-start(bf16[256,1536]{1,0:T(8,128)(2,1)S(1)} %fusion.14.refs_0_), channel_id=1, source_target_pairs={{0,2},{1,3},{2,0},{3,1},{4,6},{5,7},{6,4},{7,5},{8,10},{9,11},{10,... | collective-permute-start | bytes 2359304 | tf_op jit(solution)/shard_map/ppermute | solution.py:48
  97.3 39.4 %all-to-all-start = ((bf16[4,192,1536]{2,1,0:T(8,128)(2,1)}), bf16[4,192,1536]{2,1,0:T(8,128)(2,1)}, u32[]{:S(2)}, u32[]{:S(2)}) async-start(bf16[4,192,1536]{2,1,0:T(8,128)(2,1)} %broadcast_in_dim.47), calls=%async_computation | async-start | bytes 4718592 | tf_op jit(solution)/shard_map/all_to_all | solution.py:89
  136.6 43.7 %collective-permute-start.8 = (bf16[4,192,1536]{2,1,0:T(8,128)(2,1)}, bf16[4,192,1536]{2,1,0:T(8,128)(2,1)}, u32[]{:S(2)}, u32[]{:S(2)}) collective-permute-start(bf16[4,192,1536]{2,1,0:T(8,128)(2,1)} %all-to-all-done.wo_mine), channel_id=1, source_target_pairs={{0,4},{4,0},{8,12},{12,8},{16,20},{20,16},{24,28},{28,24},{1,5},{5... | collective-permute-start | bytes 7077896 | tf_op jit(solution)/shard_map/ppermute | solution.py:48
  140.1 30.1 %collective-permute-start.10 = (bf16[768,256]{1,0:T(8,128)(2,1)}, bf16[768,256]{1,0:T(8,128)(2,1)}, u32[]{:S(2)}, u32[]{:S(2)}) collective-permute-start(bf16[768,256]{1,0:T(8,128)(2,1)} %pad_maximum_fusion.6), channel_id=1, source_target_pairs={{0,2},{1,3},{2,0},{3,1},{4,6},{5,7},{6,4},{7,5},{8,10},{9,11},{10,... | collective-permute-start | bytes 1179656 | tf_op jit(solution)/shard_map/ppermute | solution.py:48
  142.0 28.2 %collective-permute-start.11 = (bf16[768,256]{1,0:T(8,128)(2,1)}, bf16[768,256]{1,0:T(8,128)(2,1)}, u32[]{:S(2)}, u32[]{:S(2)}) collective-permute-start(bf16[768,256]{1,0:T(8,128)(2,1)} %pad_maximum_fusion.6), channel_id=1, source_target_pairs={{0,3},{1,2},{2,1},{3,0},{4,7},{5,6},{6,5},{7,4},{8,11},{9,10},{10,... | collective-permute-start | bytes 1179656 | tf_op jit(solution)/shard_map/ppermute | solution.py:48
  143.6 26.6 %collective-permute-start.9 = (bf16[768,256]{1,0:T(8,128)(2,1)}, bf16[768,256]{1,0:T(8,128)(2,1)}, u32[]{:S(2)}, u32[]{:S(2)}) collective-permute-start(bf16[768,256]{1,0:T(8,128)(2,1)} %pad_maximum_fusion.6), channel_id=1, source_target_pairs={{0,1},{1,0},{2,3},{3,2},{4,5},{5,4},{6,7},{7,6},{8,9},{9,8},{10,11... | collective-permute-start | bytes 1179656 | tf_op jit(solution)/shard_map/ppermute | solution.py:48
  143.6 26.6 %all-to-all-start.1 = ((bf16[4,384,256]{2,1,0:T(8,128)(2,1)}), bf16[4,384,256]{2,1,0:T(8,128)(2,1)S(1)}, u32[]{:S(2)}, u32[]{:S(2)}) async-start(bf16[4,384,256]{2,1,0:T(8,128)(2,1)} %get-tuple-element.228.o_ref), calls=%async_computation.1 | async-start | bytes 1572864 | tf_op jit(solution)/shard_map/all_to_all | solution.py:89
  173.2 25.6 %collective-permute-start.12 = (bf16[256,1536]{1,0:T(8,128)(2,1)}, bf16[256,1536]{1,0:T(8,128)(2,1)}, u32[]{:S(2)}, u32[]{:S(2)}) collective-permute-start(bf16[256,1536]{1,0:T(8,128)(2,1)} %get-tuple-element.241.refs_5_.cot_ref), channel_id=1, source_target_pairs={{0,1},{1,0},{2,3},{3,2},{4,5},{5,4},{6,7},{7,6},{8,9},{9,8},{10,11... | collective-permute-start | bytes 2359304 | tf_op jit(solution)/shard_map/ppermute | solution.py:48
  175.8 25.0 %collective-permute-start.13 = (bf16[256,1536]{1,0:T(8,128)(2,1)}, bf16[256,1536]{1,0:T(8,128)(2,1)}, u32[]{:S(2)}, u32[]{:S(2)}) collective-permute-start(bf16[256,1536]{1,0:T(8,128)(2,1)} %get-tuple-element.241.refs_5_.cot_ref), channel_id=1, source_target_pairs={{0,2},{1,3},{2,0},{3,1},{4,6},{5,7},{6,4},{7,5},{8,10},{9,11},{10,... | collective-permute-start | bytes 2359304 | tf_op jit(solution)/shard_map/ppermute | solution.py:48
  176.4 28.5 %all-to-all-start.2 = ((bf16[4,384,256]{2,1,0:T(8,128)(2,1)}), bf16[4,384,256]{2,1,0:T(8,128)(2,1)S(1)}, u32[]{:S(2)}, u32[]{:S(2)}) async-start(bf16[4,384,256]{2,1,0:T(8,128)(2,1)} %get-tuple-element.240.o_ref), calls=%async_computation.2 | async-start | bytes 1572864 | tf_op jit(solution)/shard_map/all_to_all | solution.py:89
  195.3 32.9 %collective-permute-start.14 = (bf16[256,1536]{1,0:T(8,128)(2,1)}, bf16[256,1536]{1,0:T(8,128)(2,1)S(1)}, u32[]{:S(2)}, u32[]{:S(2)}) collective-permute-start(bf16[256,1536]{1,0:T(8,128)(2,1)} %get-tuple-element.254.refs_0_), channel_id=1, source_target_pairs={{0,1},{1,0},{2,3},{3,2},{4,5},{5,4},{6,7},{7,6},{8,9},{9,8},{10,11... | collective-permute-start | bytes 2359304 | tf_op jit(solution)/shard_map/ppermute | solution.py:48
  197.3 30.9 %collective-permute-start.15 = (bf16[256,1536]{1,0:T(8,128)(2,1)}, bf16[256,1536]{1,0:T(8,128)(2,1)}, u32[]{:S(2)}, u32[]{:S(2)}) collective-permute-start(bf16[256,1536]{1,0:T(8,128)(2,1)} %get-tuple-element.254.refs_0_), channel_id=1, source_target_pairs={{0,2},{1,3},{2,0},{3,1},{4,6},{5,7},{6,4},{7,5},{8,10},{9,11},{10,... | collective-permute-start | bytes 2359304 | tf_op jit(solution)/shard_map/ppermute | solution.py:48
  204.9 23.3 %collective-permute-start.16 = (bf16[128,1536]{1,0:T(8,128)(2,1)}, bf16[128,1536]{1,0:T(8,128)(2,1)S(1)}, u32[]{:S(2)}, u32[]{:S(2)}) collective-permute-start(bf16[128,1536]{1,0:T(8,128)(2,1)} %slice.199), channel_id=1, source_target_pairs={{0,2},{1,3},{2,0},{3,1},{4,6},{5,7},{6,4},{7,5},{8,10},{9,11},{10,... | collective-permute-start | bytes 1179656 | tf_op jit(solution)/shard_map/ppermute | solution.py:48
  205.5 22.7 %collective-permute-start.17 = (bf16[128,1536]{1,0:T(8,128)(2,1)}, bf16[128,1536]{1,0:T(8,128)(2,1)S(1)}, u32[]{:S(2)}, u32[]{:S(2)}) collective-permute-start(bf16[128,1536]{1,0:T(8,128)(2,1)} %slice.200), channel_id=1, source_target_pairs={{0,1},{1,0},{2,3},{3,2},{4,5},{5,4},{6,7},{7,6},{8,9},{9,8},{10,11... | collective-permute-start | bytes 1179656 | tf_op jit(solution)/shard_map/ppermute | solution.py:48
  230.6 37.0 %collective-permute-start.18 = (bf16[256,1536]{1,0:T(8,128)(2,1)S(1)}, bf16[256,1536]{1,0:T(8,128)(2,1)S(1)}, u32[]{:S(2)}, u32[]{:S(2)}) collective-permute-start(bf16[256,1536]{1,0:T(8,128)(2,1)S(1)} %get-tuple-element.272.refs_0_), channel_id=1, source_target_pairs={{0,1},{1,0},{2,3},{3,2},{4,5},{5,4},{6,7},{7,6},{8,9},{9,8},{10,11... | collective-permute-start | bytes 2359304 | tf_op jit(solution)/shard_map/ppermute | solution.py:48
  232.1 35.4 %collective-permute-start.19 = (bf16[256,1536]{1,0:T(8,128)(2,1)S(1)}, bf16[256,1536]{1,0:T(8,128)(2,1)S(1)}, u32[]{:S(2)}, u32[]{:S(2)}) collective-permute-start(bf16[256,1536]{1,0:T(8,128)(2,1)S(1)} %get-tuple-element.272.refs_0_), channel_id=1, source_target_pairs={{0,2},{1,3},{2,0},{3,1},{4,6},{5,7},{6,4},{7,5},{8,10},{9,11},{10,... | collective-permute-start | bytes 2359304 | tf_op jit(solution)/shard_map/ppermute | solution.py:48
  242.1 33.7 %collective-permute-start.24 = (bf16[256,1536]{1,0:T(8,128)(2,1)S(1)}, bf16[256,1536]{1,0:T(8,128)(2,1)S(1)}, u32[]{:S(2)}, u32[]{:S(2)}) collective-permute-start(bf16[256,1536]{1,0:T(8,128)(2,1)S(1)} %get-tuple-element.263.refs_5_.cot_ref), channel_id=1, source_target_pairs={{0,1},{1,0},{2,3},{3,2},{4,5},{5,4},{6,7},{7,6},{8,9},{9,8},{10,11... | collective-permute-start | bytes 2359304 | tf_op jit(solution)/shard_map/ppermute | solution.py:48
  242.6 33.2 %collective-permute-start.25 = (bf16[256,1536]{1,0:T(8,128)(2,1)S(1)}, bf16[256,1536]{1,0:T(8,128)(2,1)S(1)}, u32[]{:S(2)}, u32[]{:S(2)}) collective-permute-start(bf16[256,1536]{1,0:T(8,128)(2,1)S(1)} %get-tuple-element.263.refs_5_.cot_ref), channel_id=1, source_target_pairs={{0,2},{1,3},{2,0},{3,1},{4,6},{5,7},{6,4},{7,5},{8,10},{9,11},{10,... | collective-permute-start | bytes 2359304 | tf_op jit(solution)/shard_map/ppermute | solution.py:48
  267.6 26.4 %collective-permute-start.22 = (bf16[128,1536]{1,0:T(8,128)(2,1)S(1)}, bf16[128,1536]{1,0:T(8,128)(2,1)S(1)}, u32[]{:S(2)}, u32[]{:S(2)}) collective-permute-start(bf16[128,1536]{1,0:T(8,128)(2,1)S(1)} %slice.203), channel_id=1, source_target_pairs={{0,2},{1,3},{2,0},{3,1},{4,6},{5,7},{6,4},{7,5},{8,10},{9,11},{10,... | collective-permute-start | bytes 1179656 | tf_op jit(solution)/shard_map/ppermute | solution.py:48
  268.4 25.5 %collective-permute-start.23 = (bf16[128,1536]{1,0:T(8,128)(2,1)S(1)}, bf16[128,1536]{1,0:T(8,128)(2,1)S(1)}, u32[]{:S(2)}, u32[]{:S(2)}) collective-permute-start(bf16[128,1536]{1,0:T(8,128)(2,1)S(1)} %slice.204), channel_id=1, source_target_pairs={{0,1},{1,0},{2,3},{3,2},{4,5},{5,4},{6,7},{7,6},{8,9},{9,8},{10,11... | collective-permute-start | bytes 1179656 | tf_op jit(solution)/shard_map/ppermute | solution.py:48
  275.9 18.8 %collective-permute-start.26 = (bf16[128,1536]{1,0:T(8,128)(2,1)S(1)}, bf16[128,1536]{1,0:T(8,128)(2,1)S(1)}, u32[]{:S(2)}, u32[]{:S(2)}) collective-permute-start(bf16[128,1536]{1,0:T(8,128)(2,1)S(1)} %slice.206), channel_id=1, source_target_pairs={{0,2},{1,3},{2,0},{3,1},{4,6},{5,7},{6,4},{7,5},{8,10},{9,11},{10,... | collective-permute-start | bytes 1179656 | tf_op jit(solution)/shard_map/ppermute | solution.py:48
  296.2 47.7 %all-to-all-start.3 = ((bf16[4,256,1536]{2,1,0:T(8,128)(2,1)}), bf16[4,256,1536]{2,1,0:T(8,128)(2,1)}, u32[]{:S(2)}, u32[]{:S(2)}) async-start(bf16[4,256,1536]{2,1,0:T(8,128)(2,1)} %copy-done.6), calls=%async_computation.3 | async-start | bytes 6291456 | tf_op jit(solution)/shard_map/all_to_all | solution.py:89
  300.9 432.1 %reduce-scatter.9.cloned.1.call-start = ((), (), s32[]{:S(2)}) async-start(), calls=%async_computation.15 | async-start | bytes 5308416 | tf_op jit(solution)/shard_map/reduce_scatter | solution.py:969
  360.2 372.8 %reduce-scatter.19.cloned.1.call-start = ((), (), s32[]{:S(2)}) async-start(), calls=%async_computation.23 | async-start | bytes 7864320
  376.0 44.0 %all-to-all-start.4 = ((bf16[4,256,1536]{2,1,0:T(8,128)(2,1)}), bf16[4,256,1536]{2,1,0:T(8,128)(2,1)}, u32[]{:S(2)}, u32[]{:S(2)}) async-start(bf16[4,256,1536]{2,1,0:T(8,128)(2,1)} %copy-done.5), calls=%async_computation.5 | async-start | bytes 6291456 | tf_op jit(solution)/shard_map/all_to_all | solution.py:89
  380.7 352.3 %reduce-scatter.17.cloned.1.call-start = ((), (), s32[]{:S(2)}) async-start(), calls=%async_computation.19 | async-start | bytes 5308416 | tf_op jit(solution)/shard_map/reduce_scatter | solution.py:969
  420.0 25.9 %all-to-all-start.5 = ((bf16[4,384,256]{2,1,0:T(8,128)(2,1)}), bf16[4,384,256]{2,1,0:T(8,128)(2,1)S(1)}, u32[]{:S(2)}, u32[]{:S(2)}) async-start(bf16[4,384,256]{2,1,0:T(8,128)(2,1)} %bitcast.153), calls=%async_computation.6 | async-start | bytes 1572864 | tf_op jit(solution)/shard_map/all_to_all | solution.py:89
  462.9 25.2 %collective-permute-start.28 = (bf16[4,4,3,192,384]{4,3,2,1,0:T(8,128)(2,1)}, bf16[4,4,3,192,384]{4,3,2,1,0:T(8,128)(2,1)}, u32[]{:S(2)}, u32[]{:S(2)}) collective-permute-start(bf16[4,4,3,192,384]{4,3,2,1,0:T(8,128)(2,1)} %get-tuple-element.325), channel_id=1, source_target_pairs={{0,4},{4,0},{8,12},{12,8},{16,20},{20,16},{24,28},{28,24},{1,5},{5... | collective-permute-start | bytes 21233672 | tf_op jit(solution)/shard_map/ppermute | solution.py:48
  463.6 86.8 %collective-permute-start.29 = (bf16[768,256]{1,0:T(8,128)(2,1)}, bf16[768,256]{1,0:T(8,128)(2,1)}, u32[]{:S(2)}, u32[]{:S(2)}) collective-permute-start(bf16[768,256]{1,0:T(8,128)(2,1)} %get-tuple-element.400), channel_id=1, source_target_pairs={{0,1},{1,0},{2,3},{3,2},{4,5},{5,4},{6,7},{7,6},{8,9},{9,8},{10,11... | collective-permute-start | bytes 1179656 | tf_op jit(solution)/shard_map/ppermute | solution.py:48
  465.5 84.9 %collective-permute-start.30 = (bf16[768,256]{1,0:T(8,128)(2,1)}, bf16[768,256]{1,0:T(8,128)(2,1)}, u32[]{:S(2)}, u32[]{:S(2)}) collective-permute-start(bf16[768,256]{1,0:T(8,128)(2,1)} %get-tuple-element.399), channel_id=1, source_target_pairs={{0,2},{1,3},{2,0},{3,1},{4,6},{5,7},{6,4},{7,5},{8,10},{9,11},{10,... | collective-permute-start | bytes 1179656 | tf_op jit(solution)/shard_map/ppermute | solution.py:48
  466.9 83.5 %collective-permute-start.31 = (bf16[768,256]{1,0:T(8,128)(2,1)}, bf16[768,256]{1,0:T(8,128)(2,1)}, u32[]{:S(2)}, u32[]{:S(2)}) collective-permute-start(bf16[768,256]{1,0:T(8,128)(2,1)} %get-tuple-element.398), channel_id=1, source_target_pairs={{0,3},{1,2},{2,1},{3,0},{4,7},{5,6},{6,5},{7,4},{8,11},{9,10},{10,... | collective-permute-start | bytes 1179656 | tf_op jit(solution)/shard_map/ppermute | solution.py:48
  467.1 69.4 %all-to-all-start.6 = ((bf16[4,384,256]{2,1,0:T(8,128)(2,1)}), bf16[4,384,256]{2,1,0:T(8,128)(2,1)}, u32[]{:S(2)}, u32[]{:S(2)}) async-start(bf16[4,384,256]{2,1,0:T(8,128)(2,1)} %bitcast.39), calls=%async_computation.7 | async-start | bytes 1572864 | tf_op jit(solution)/shard_map/all_to_all | solution.py:89
  471.3 264.1 %reduce-scatter.15.cloned.1.call-start = ((), (), s32[]{:S(2)}) async-start(), calls=%async_computation.18 | async-start | bytes 5308416 | tf_op jit(solution)/shard_map/reduce_scatter | solution.py:969
  488.1 258.4 %reduce-scatter.13.cloned.1.call-start = ((), (), s32[]{:S(2)}) async-start(), calls=%async_computation.17 | async-start | bytes 2949120 | tf_op jit(solution)/shard_map/reduce_scatter | solution.py:1233
  509.2 27.2 %collective-permute-start.32 = (bf16[1152,384]{1,0:T(8,128)(2,1)}, bf16[1152,384]{1,0:T(8,128)(2,1)}, u32[]{:S(2)}, u32[]{:S(2)}) collective-permute-start(bf16[1152,384]{1,0:T(8,128)(2,1)} %get-tuple-element.389), channel_id=1, source_target_pairs={{0,2},{1,3},{2,0},{3,1},{4,6},{5,7},{6,4},{7,5},{8,10},{9,11},{10,... | collective-permute-start | bytes 2654216 | tf_op jit(solution)/shard_map/ppermute | solution.py:48
  511.0 25.4 %collective-permute-start.33 = (bf16[1152,384]{1,0:T(8,128)(2,1)}, bf16[1152,384]{1,0:T(8,128)(2,1)}, u32[]{:S(2)}, u32[]{:S(2)}) collective-permute-start(bf16[1152,384]{1,0:T(8,128)(2,1)} %get-tuple-element.390), channel_id=1, source_target_pairs={{0,1},{1,0},{2,3},{3,2},{4,5},{5,4},{6,7},{7,6},{8,9},{9,8},{10,11... | collective-permute-start | bytes 2654216 | tf_op jit(solution)/shard_map/ppermute | solution.py:48
  556.6 40.3 %collective-permute-start.35 = (bf16[2304,384]{1,0:T(8,128)(2,1)}, bf16[2304,384]{1,0:T(8,128)(2,1)S(1)}, u32[]{:S(2)}, u32[]{:S(2)}) collective-permute-start(bf16[2304,384]{1,0:T(8,128)(2,1)} %pad_maximum_fusion.4), channel_id=1, source_target_pairs={{0,2},{1,3},{2,0},{3,1},{4,6},{5,7},{6,4},{7,5},{8,10},{9,11},{10,... | collective-permute-start | bytes 5308424 | tf_op jit(solution)/shard_map/ppermute | solution.py:48
  557.2 40.0 %collective-permute-start.34 = (bf16[2304,384]{1,0:T(8,128)(2,1)}, bf16[2304,384]{1,0:T(8,128)(2,1)S(1)}, u32[]{:S(2)}, u32[]{:S(2)}) collective-permute-start(bf16[2304,384]{1,0:T(8,128)(2,1)} %pad_maximum_fusion.3), channel_id=1, source_target_pairs={{0,1},{1,0},{2,3},{3,2},{4,5},{5,4},{6,7},{7,6},{8,9},{9,8},{10,11... | collective-permute-start | bytes 5308424 | tf_op jit(solution)/shard_map/ppermute | solution.py:48
  558.5 38.7 %collective-permute-start.36 = (bf16[4,192,384]{2,1,0:T(8,128)(2,1)S(1)}, bf16[4,192,384]{2,1,0:T(8,128)(2,1)S(1)}, u32[]{:S(2)}, u32[]{:S(2)}) collective-permute-start(bf16[4,192,384]{2,1,0:T(8,128)(2,1)S(1)} %fusion.33), channel_id=1, source_target_pairs={{0,4},{4,0},{8,12},{12,8},{16,20},{20,16},{24,28},{28,24},{1,5},{5... | collective-permute-start | bytes 1769480 | tf_op jit(solution)/shard_map/ppermute | solution.py:48
  602.3 39.9 %all-to-all-start.7 = ((bf16[4,256,1536]{2,1,0:T(8,128)(2,1)}), bf16[4,256,1536]{2,1,0:T(8,128)(2,1)}, u32[]{:S(2)}, u32[]{:S(2)}) async-start(bf16[4,256,1536]{2,1,0:T(8,128)(2,1)} %self_back.2), calls=%async_computation.8 | async-start | bytes 6291456 | tf_op jit(solution)/shard_map/all_to_all | solution.py:89
  642.2 40.3 %all-to-all-start.8 = ((bf16[4,256,1536]{2,1,0:T(8,128)(2,1)}), bf16[4,256,1536]{2,1,0:T(8,128)(2,1)}, u32[]{:S(2)}, u32[]{:S(2)}) async-start(bf16[4,256,1536]{2,1,0:T(8,128)(2,1)} %self_back.3), calls=%async_computation.9 | async-start | bytes 6291456 | tf_op jit(solution)/shard_map/all_to_all | solution.py:89
  647.0 102.3 %reduce-scatter.11.cloned.1.call-start = ((), (), s32[]{:S(2)}) async-start(), calls=%async_computation.16 | async-start | bytes 3981312 | tf_op jit(solution)/shard_map/reduce_scatter | solution.py:969
  (185 other events, 1582.1 us)
Sparse Core Ops, SparseCore 0:
  19.0 30.3 all-gather.6
  51.9 51.6 all-gather.8
  105.2 50.4 all-gather.10
  360.3 56.3 reduce-scatter.8
  419.5 92.7 reduce-scatter.18
  514.5 54.9 reduce-scatter.16
  571.8 53.3 reduce-scatter.14
  627.5 46.3 reduce-scatter.12
  676.2 48.4 reduce-scatter.10

commit v7 on v6

--- a/solution.py
+++ b/solution.py
@@ -526,7 +526,7 @@
 
 
 def params():
-    return pltpu.CompilerParams(vmem_limit_bytes=48 * 2**20)
+    return pltpu.CompilerParams(vmem_limit_bytes=58 * 2**20)
 
 
 def self_forward(turned, front_keys, front_values):

time: 766 us -> 734 us (0.958)
  local copies, waits for them, and re-layouts: 112 us -> 40.5 us
  Pallas kernels: 314 us -> 340 us
    unnamed x348 -> x154, local copies, waits for them, and re-layouts: 68.7 us -> 8.02 us
  transfers between devices with their start and end apart: 60 -> 60, of which waited for: 22 -> 23; matrix products, arithmetic and copies ran while one was open for 12% -> 12% of each run, Pallas kernels for 40% -> 45%
where the time goes in v7:
time: 734 us; the launch traced here: 727 us
  Pallas kernels  340 us (46%)
  waiting for transfers between devices  177 us (24%)
  starting transfers between devices  89.1 us (12%)
  other arithmetic  50.5 us (7%)
  local copies, waits for them, and re-layouts  40.5 us (6%)
  between operations  19.4 us (3%)
  matrix products  11.3 us (2%)
    ppermute x42, waiting for transfers between devices, swap(): lax.ppermute(values, axis, [(i, i ^ k) for i in range(lax.axis_size(axis))])  114 us
    all_to_all x9, waiting for transfers between devices, exchange(): return lax.all_to_all(blocks, 'mp', 0, 0)  50.5 us
    ppermute x42, starting transfers between devices, swap(): lax.ppermute(values, axis, [(i, i ^ k) for i in range(lax.axis_size(axis))])  48.9 us
    pallas_call x3, Pallas kernels, weight_grad(): pl.pallas_call(weight_grad_kernel, grid=(width // block,), in_specs=[pl.B...  45.6 us
    pallas_call x2, Pallas kernels, glu(): pl.pallas_call(functools.partial(glu_kernel, size, len(pieces)), grid=(hi...  44.2 us
    all_to_all x9, starting transfers between devices, exchange(): return lax.all_to_all(blocks, 'mp', 0, 0)  39.8 us
    pallas_call x2, Pallas kernels, self_backward(): pl.pallas_call(functools.partial(self_backward_kernel, min(256, frames)),...  38.4 us
    pallas_call x2, Pallas kernels, local_backward(): pl.pallas_call(functools.partial(local_backward_kernel, clip), grid=(1,),...  36.3 us
  transfers between devices with their start and end apart: 60, of which 23 were waited for; matrix products, arithmetic and copies ran while one was open for 12% of the time, Pallas kernels for 45%

profile of v7, /device:TPU:0, one launch (start us, length us, event | category | flops | bytes accessed | tf_op | source)
XLA Modules:
  0.0 727.4 jit_solution(2277299470780146395)
XLA Ops:
  23.0 10.9 %collective-permute-done.refs_1_ = bf16[256,1536]{1,0:T(8,128)(2,1)} collective-permute-done((bf16[256,1536]{1,0:T(8,128)(2,1)S(1)}, bf16[256,1536]{1,0:T(8,128)(2,1)}, u32[]{:S(2)}, u32[]{:S(2)}) %collective-permute-start) | collective-permute-done | bytes 786464 | tf_op jit(solution)/shard_map/ppermute | solution.py:48
  39.7 11.4 %all-gather.7.cloned.1.call-done = bf16[8,192,384]{2,1,0:T(8,128)(2,1)} async-done(((bf16[2,192,384]{2,1,0:T(8,128)(2,1)}), bf16[8,192,384]{2,1,0:T(8,128)(2,1)}) %all-gather.7.cloned.1.call-update) | async-done | bytes 1179664 | tf_op jit(solution)/shard_map/all_gather | solution.py:1020
  66.6 16.7 %collective-permute-done.2.refs_3_ = bf16[128,1536]{1,0:T(8,128)(2,1)S(1)} collective-permute-done((bf16[128,1536]{1,0:T(8,128)(2,1)S(1)}, bf16[128,1536]{1,0:T(8,128)(2,1)S(1)}, u32[]{:S(2)}, u32[]{:S(2)}) %collective-permute-start.2) | collective-permute-done | bytes 393248 | tf_op jit(solution)/shard_map/ppermute | solution.py:48
  87.7 5.4 collective-permute-done.6.refs_3_
  96.3 3.9 all-to-all-start
  101.5 10.4 %project.2 = (bf16[1152,1024]{1,0:T(8,128)(2,1)}, bf16[2,1024,1536]{2,1,0:T(8,128)(2,1)}, bf16[768,8]{1,0:T(8,128)(2,1)}) custom-call(s32[4]{0:T(128)} %pad_add_fusion.n_ref.order_ref, f32[8,1536]{1,0:T(8,128)} %maximum_maximum_fusion.p_ref, f32[2,1536]{1,0:T(2,128)} %pad_maximum_fusion.9.norm_ref, bf16[1536,384]{1,0:T(8,128)(2,1)} %wq_ref.7, ...), custom_call_target="tpu_custom_call" | custom-call | flops 3680000000 | bytes 11520000 | tf_op jit(solution)/shard_map/project/pallas_call | solution.py:661
  113.9 10.9 %self_forward.2 = (bf16[4,384,256]{2,1,0:T(8,128)(2,1)}, f32[6,1,1024]{2,1,0:T(1,128)}) custom-call(bf16[1152,1024]{1,0:T(8,128)(2,1)} %get-tuple-element.216.q_ref.k_ref.v_ref, bf16[1152,1024]{1,0:T(8,128)(2,1)} %get-tuple-element.216.q_ref.k_ref.v_ref, bf16[1152,1024]{1,0:T(8,128)(2,1)} %get-tuple-element.216.q_ref.k_ref.v_ref, ...), custom_call_target="tpu_custom_call" | custom-call | flops 4001999872 | bytes 12528000 | tf_op jit(solution)/shard_map/self_forward/pallas_call | solution.py:544
  124.8 11.2 %project.3 = (bf16[1152,1024]{1,0:T(8,128)(2,1)}, bf16[2,1024,1536]{2,1,0:T(8,128)(2,1)}, bf16[768,8]{1,0:T(8,128)(2,1)}) custom-call(s32[4]{0:T(128)} %pad_add_fusion.n_ref.order_ref, f32[8,1536]{1,0:T(8,128)} %maximum_maximum_fusion.p_ref, f32[2,1536]{1,0:T(2,128)} %pad_maximum_fusion.9.norm_ref, ...), custom_call_target="tpu_custom_call", output_to_operand_aliasing={{1}: (13, {})} | custom-call | flops 3680000000 | bytes 11520000 | tf_op jit(solution)/shard_map/project/pallas_call | solution.py:661
  144.7 4.2 all-to-all-start.1
  150.2 10.7 %self_forward.3 = (bf16[4,384,256]{2,1,0:T(8,128)(2,1)}, f32[6,1,1024]{2,1,0:T(1,128)}) custom-call(bf16[1152,1024]{1,0:T(8,128)(2,1)} %get-tuple-element.229.q_ref.k_ref.v_ref, bf16[1152,1024]{1,0:T(8,128)(2,1)} %get-tuple-element.229.q_ref.k_ref.v_ref, bf16[1152,1024]{1,0:T(8,128)(2,1)} %get-tuple-element.229.q_ref.k_ref.v_ref, ...), custom_call_target="tpu_custom_call" | custom-call | flops 4001999872 | bytes 12528000 | tf_op jit(solution)/shard_map/self_forward/pallas_call | solution.py:544
  161.0 9.9 %all-to-all-done.1 = bf16[4,384,256]{2,1,0:T(8,128)(2,1)} async-done(((bf16[4,384,256]{2,1,0:T(8,128)(2,1)}), bf16[4,384,256]{2,1,0:T(8,128)(2,1)}, u32[]{:S(2)}, u32[]{:S(2)}) %all-to-all-start.1) | async-done | bytes 786464 | tf_op jit(solution)/shard_map/all_to_all | solution.py:89
  176.6 4.4 all-to-all-start.2
  181.1 12.7 %local_forward.2 = (f32[256,1536]{1,0:T(8,128)}, f32[256,1536]{1,0:T(8,128)}, bf16[256,1536]{1,0:T(8,128)(2,1)}, bf16[1536,256]{1,0:T(8,128)(2,1)}, bf16[1536,25...) custom-call(s32[2]{0:T(128)} %n_ref.7, s32[1]{0:T(128)} %bitcast.core_ref, ...), custom_call_target="tpu_custom_call" | custom-call | flops 5198000128 | bytes 16272000 | tf_op jit(solution)/shard_map/local_forward/pallas_call | solution.py:368
  197.3 3.8 collective-permute-done.13.refs_7_
  206.8 13.0 %local_forward.3 = (f32[256,1536]{1,0:T(8,128)}, f32[256,1536]{1,0:T(8,128)}, bf16[256,1536]{1,0:T(8,128)(2,1)}, bf16[1536,256]{1,0:T(8,128)(2,1)}, bf16[1536,25...) custom-call(s32[2]{0:T(128)} %n_ref.7, s32[1]{0:T(128)} %bitcast.core_ref, ...), custom_call_target="tpu_custom_call" | custom-call | flops 5198000128 | bytes 16272000 | tf_op jit(solution)/shard_map/local_forward/pallas_call | solution.py:368
  219.8 8.6 %collective-permute-done.16.refs_8_ = bf16[128,1536]{1,0:T(8,128)(2,1)S(1)} collective-permute-done((bf16[128,1536]{1,0:T(8,128)(2,1)S(1)}, bf16[128,1536]{1,0:T(8,128)(2,1)S(1)}, u32[]{:S(2)}, u32[]{:S(2)}) %collective-permute-start.16) | collective-permute-done | bytes 393248 | tf_op jit(solution)/shard_map/ppermute | solution.py:48
  233.3 7.9 %collective-permute-done.20.refs_3_ = bf16[128,1536]{1,0:T(8,128)(2,1)S(1)} collective-permute-done((bf16[128,1536]{1,0:T(8,128)(2,1)S(1)}, bf16[128,1536]{1,0:T(8,128)(2,1)S(1)}, u32[]{:S(2)}, u32[]{:S(2)}) %collective-permute-start.20) | collective-permute-done | bytes 393248 | tf_op jit(solution)/shard_map/ppermute | solution.py:48
  244.4 22.1 %glu.2 = (bf16[2,1024,1536]{2,1,0:T(8,128)(2,1)}, bf16[2,1024,1536]{2,1,0:T(8,128)(2,1)}, bf16[2,1024,1536]{2,1,0:T(8,128)(2,1)}, bf16[2,1024,1536]{2,1,0:T(8,128)(2,1)}, bf16[2,1024,1536]{2,1,0:T(8,128)(2,1)}) custom-call(s32[4]{0:T(128)} %pad_add_fusion.n_ref.order_ref, bf16[1536,1536]{1,0:T(8,128)(2,1)} %gate_ref.7, bf16[1536,1536]{1,0:T(8,128)(2,1)} %up_ref.7, ...), custom_call_target="tpu_custom_call" | custom-call | flops 10119999488 | bytes 31680000 | tf_op jit(solution)/shard_map/glu/pallas_call | solution.py:723
  269.2 6.4 collective-permute-done.24.refs_6_
  277.5 15.2 %glu_back.2 = bf16[4,256,1536]{2,1,0:T(8,128)(2,1)} custom-call(bf16[2,1024,1536]{2,1,0:T(8,128)(2,1)} %get-tuple-element.266.dg_ref.refs_11_, bf16[2,1024,1536]{2,1,0:T(8,128)(2,1)} %get-tuple-element.267.du_ref.refs_12_, bf16[1536,1536]{1,0:T(8,128)(2,1)} %gate_ref.7, bf16[1536,1536]{1,0:T(8,128)(2,1)} %up_ref.7), custom_call_target="tpu_custom_call" | custom-call | flops 6670000128 | bytes 20880000 | tf_op jit(solution)/shard_map/glu_back/pallas_call | solution.py:761
  293.7 4.6 all-to-all-start.3
  298.4 22.0 %glu.3 = (bf16[2,1024,1536]{2,1,0:T(8,128)(2,1)}, bf16[2,1024,1536]{2,1,0:T(8,128)(2,1)}, bf16[2,1024,1536]{2,1,0:T(8,128)(2,1)}, bf16[2,1024,1536]{2,1,0:T(8,128)(2,1)}, bf16[2,1024,1536]{2,1,0:T(8,128)(2,1)}) custom-call(s32[4]{0:T(128)} %pad_add_fusion.n_ref.order_ref, ...), custom_call_target="tpu_custom_call", output_to_operand_aliasing={{0}: (14, {}), {1}: (15, {}), {2}: (16, {}), {3}: (17, {}),... | custom-call | flops 10119999488 | bytes 31680000 | tf_op jit(solution)/shard_map/glu/pallas_call | solution.py:723
  320.5 15.2 %glu_back.3 = bf16[4,256,1536]{2,1,0:T(8,128)(2,1)} custom-call(bf16[2,1024,1536]{2,1,0:T(8,128)(2,1)} %get-tuple-element.285.dg_ref, bf16[2,1024,1536]{2,1,0:T(8,128)(2,1)} %get-tuple-element.286.du_ref, bf16[1536,1536]{1,0:T(8,128)(2,1)} %gate_ref.7, bf16[1536,1536]{1,0:T(8,128)(2,1)} %up_ref.7), custom_call_target="tpu_custom_call" | custom-call | flops 6670000128 | bytes 20880000 | tf_op jit(solution)/shard_map/glu_back/pallas_call | solution.py:761
  335.7 15.0 %weight_grad.3 = bf16[1536,1536]{1,0:T(8,128)(2,1)} custom-call(bf16[2048,1536]{1,0:T(8,128)(2,1)} %bitcast.152, bf16[2048,1536]{1,0:T(8,128)(2,1)} %bitcast.151), custom_call_target="tpu_custom_call" | custom-call | flops 4600000000 | bytes 14400000 | tf_op jit(solution)/shard_map/weight_grad/pallas_call | solution.py:863
  350.7 14.8 %branch.1 = bf16[4,2,256,1536]{3,2,1,0:T(8,128)(2,1)} custom-call(bf16[2,1024,1536]{2,1,0:T(8,128)(2,1)} %get-tuple-element.289.x_ref, bf16[1536,1536]{1,0:T(8,128)(2,1)} %w_ref.1), custom_call_target="tpu_custom_call" | custom-call | flops 6072000000 | bytes 19008000 | tf_op jit(solution)/shard_map/branch/pallas_call | solution.py:838
  365.6 4.7 all-to-all-start.4
  370.4 15.6 %weight_grad.4 = bf16[1536,1536]{1,0:T(8,128)(2,1)} custom-call(bf16[2048,1536]{1,0:T(8,128)(2,1)} %bitcast.149, bf16[2048,1536]{1,0:T(8,128)(2,1)} %bitcast.147), custom_call_target="tpu_custom_call" | custom-call | flops 4600000000 | bytes 14400000 | tf_op jit(solution)/shard_map/weight_grad/pallas_call | solution.py:863
  386.0 18.2 %local_backward.2 = (bf16[256,1536]{1,0:T(8,128)(2,1)}, bf16[256,1536]{1,0:T(8,128)(2,1)}, f32[256,1536]{1,0:T(8,128)}, bf16[1536,256]{1,0:T(8,128)(2,1)}, bf16[...) custom-call(s32[2]{0:T(128)} %n_ref.7, s32[1]{0:T(128)} %bitcast.core_ref, ...), custom_call_target="tpu_custom_call" | custom-call | flops 18400000000 | bytes 57600000 | tf_op jit(solution)/shard_map/local_backward/pallas_call | solution.py:471
  404.2 4.2 all-to-all-start.5
  408.4 18.1 %local_backward.3 = (bf16[256,1536]{1,0:T(8,128)(2,1)}, bf16[256,1536]{1,0:T(8,128)(2,1)}, f32[256,1536]{1,0:T(8,128)}, bf16[1536,256]{1,0:T(8,128)(2,1)}, bf16[...) custom-call(s32[2]{0:T(128)} %n_ref.7, s32[1]{0:T(128)} %bitcast.core_ref, ...), custom_call_target="tpu_custom_call" | custom-call | flops 18400000000 | bytes 57600000 | tf_op jit(solution)/shard_map/local_backward/pallas_call | solution.py:471
  429.4 14.2 %whole_grad.2 = (bf16[4,4,3,192,384]{4,3,2,1,0:T(8,128)(2,1)}, bf16[3,1536,512]{2,1,0:T(8,128)(2,1)}) custom-call(s32[1]{0:T(128)S(6)} %sub.72.core_ref, bf16[256,1536]{1,0:T(8,128)(2,1)} %get-tuple-element.310.refs_0_, bf16[256,1536]{1,0:T(8,128)(2,1)} %get-tuple-element.311.refs_1_, bf16[256,1536]{1,0:T(8,128)(2,1)} %get-tuple-element.318.refs_2_, ...), custom_call_target="tpu_custom_call" | custom-call | flops 13799999488 | bytes 43200000 | tf_op jit(solution)/shard_map/whole_grad/pallas_call | solution.py:814
  447.8 4.2 all-to-all-start.6
  452.0 15.0 %weight_grad.5 = bf16[1536,1536]{1,0:T(8,128)(2,1)} custom-call(bf16[2048,1536]{1,0:T(8,128)(2,1)} %bitcast.150, bf16[2048,1536]{1,0:T(8,128)(2,1)} %bitcast.148), custom_call_target="tpu_custom_call" | custom-call | flops 4600000000 | bytes 14400000 | tf_op jit(solution)/shard_map/weight_grad/pallas_call | solution.py:863
  467.2 13.0 %whole_grad.3 = bf16[4,4,3,192,384]{4,3,2,1,0:T(8,128)(2,1)} custom-call(s32[1]{0:T(128)} %bitcast.core_ref, bf16[3,1536,512]{2,1,0:T(8,128)(2,1)} %get-tuple-element.324.refs_0_, bf16[1536,256]{1,0:T(8,128)(2,1)} %get-tuple-element.322.refs_6_.refs_1_, bf16[1536,256]{1,0:T(8,128)(2,1)} %get-tuple-element.323.refs_7_.refs_2_, ...), custom_call_target="tpu_custom_call" | custom-call | flops 13799999488 | bytes 43200000 | tf_op jit(solution)/shard_map/whole_grad/pallas_call | solution.py:814
  488.9 19.2 %self_backward.2 = (bf16[3,384,1024]{2,1,0:T(8,128)(2,1)}, bf16[384,1]{1,0:T(8,128)(2,1)}, bf16[384,1]{1,0:T(8,128)(2,1)}) custom-call(bf16[1152,1024]{1,0:T(8,128)(2,1)} %get-tuple-element.216.q_ref.k_ref.v_ref, bf16[1152,1024]{1,0:T(8,128)(2,1)} %get-tuple-element.216.q_ref.k_ref.v_ref, bf16[1152,1024]{1,0:T(8,128)(2,1)} %get-tuple-element.216.q_ref.k_ref.v_ref, ...), custom_call_target="tpu_custom_call" | custom-call | flops 20700000256 | bytes 64800000 | tf_op jit(solution)/shard_map/self_backward/pallas_call | solution.py:573
  508.1 3.8 collective-permute-done.32
  517.1 8.9 %self_back.2 = bf16[4,256,1536]{2,1,0:T(8,128)(2,1)} custom-call(bf16[3,384,1024]{2,1,0:T(8,128)(2,1)} %get-tuple-element.351.d_ref.refs_0_, bf16[1536,384]{1,0:T(8,128)(2,1)} %wq_ref.7, bf16[1536,384]{1,0:T(8,128)(2,1)} %wk_ref.7, bf16[1536,384]{1,0:T(8,128)(2,1)} %wv_ref.7), custom_call_target="tpu_custom_call" | custom-call | flops 3220000000 | bytes 10080000 | tf_op jit(solution)/shard_map/self_back/pallas_call | solution.py:949
  532.7 19.2 %self_backward.3 = (bf16[3,384,1024]{2,1,0:T(8,128)(2,1)}, bf16[384,1]{1,0:T(8,128)(2,1)}, bf16[384,1]{1,0:T(8,128)(2,1)}) custom-call(bf16[1152,1024]{1,0:T(8,128)(2,1)} %get-tuple-element.229.q_ref.k_ref.v_ref, bf16[1152,1024]{1,0:T(8,128)(2,1)} %get-tuple-element.229.q_ref.k_ref.v_ref, bf16[1152,1024]{1,0:T(8,128)(2,1)} %get-tuple-element.229.q_ref.k_ref.v_ref, ...), custom_call_target="tpu_custom_call" | custom-call | flops 20700000256 | bytes 64800000 | tf_op jit(solution)/shard_map/self_backward/pallas_call | solution.py:573
  551.9 19.4 %collective-permute-done.35 = bf16[2304,384]{1,0:T(8,128)(2,1)S(1)} collective-permute-done((bf16[2304,384]{1,0:T(8,128)(2,1)}, bf16[2304,384]{1,0:T(8,128)(2,1)S(1)}, u32[]{:S(2)}, u32[]{:S(2)}) %collective-permute-start.35) | collective-permute-done | bytes 1769504 | tf_op jit(solution)/shard_map/ppermute | solution.py:48
  578.1 4.9 all-to-all-start.7
  587.5 16.3 %self_weight_grad.1 = (bf16[1536,1152]{1,0:T(8,128)(2,1)}, f32[1536,1]{1,0:T(8,128)}, f32[1536,1]{1,0:T(8,128)}) custom-call(bf16[2,1024,1536]{2,1,0:T(8,128)(2,1)} %get-tuple-element.290.x_ref, f32[1536,2]{1,0:T(8,128)} %get-tuple-element.414.p_ref, f32[2,1152]{1,0:T(2,128)} %pad_convert_fusion.f_ref, ...), custom_call_target="tpu_custom_call" | custom-call | flops 5520000000 | bytes 17280000 | tf_op jit(solution)/shard_map/self_weight_grad/pallas_call | solution.py:917
  603.9 8.9 %self_back.3 = bf16[4,256,1536]{2,1,0:T(8,128)(2,1)} custom-call(bf16[3,384,1024]{2,1,0:T(8,128)(2,1)} %get-tuple-element.359.refs_1_.d_ref, bf16[1536,384]{1,0:T(8,128)(2,1)} %wq_ref.7, bf16[1536,384]{1,0:T(8,128)(2,1)} %wk_ref.7, bf16[1536,384]{1,0:T(8,128)(2,1)} %wv_ref.7), custom_call_target="tpu_custom_call" | custom-call | flops 3220000000 | bytes 10080000 | tf_op jit(solution)/shard_map/self_back/pallas_call | solution.py:949
  612.8 5.7 all-to-all-done.7
  618.5 4.7 all-to-all-start.8
  626.1 32.7 %all-to-all-done.8 = bf16[4,256,1536]{2,1,0:T(8,128)(2,1)} async-done(((bf16[4,256,1536]{2,1,0:T(8,128)(2,1)}), bf16[4,256,1536]{2,1,0:T(8,128)(2,1)}, u32[]{:S(2)}, u32[]{:S(2)}) %all-to-all-start.8) | async-done | bytes 3145760 | tf_op jit(solution)/shard_map/all_to_all | solution.py:89
  661.8 4.4 collective-permute-done.38
  668.7 12.0 %collective-permute-done.39 = f32[23,1536]{1,0:T(8,128)S(1)} collective-permute-done((f32[23,1536]{1,0:T(8,128)S(1)}, f32[23,1536]{1,0:T(8,128)S(1)}, u32[]{:S(2)}, u32[]{:S(2)}) %collective-permute-start.39) | collective-permute-done | bytes 141344 | tf_op jit(solution)/shard_map/ppermute | solution.py:48
  695.1 5.2 fusion.36
  (385 shorter events, 164.1 us)
Async XLA Ops:
  7.2 43.9 %all-gather.7.cloned.1.call-start = ((), (), s32[]{:S(2)}) async-start(), calls=%async_computation.20 | async-start | bytes 1474560 | tf_op jit(solution)/shard_map/all_gather | solution.py:1020
  11.4 22.6 %collective-permute-start = (bf16[256,1536]{1,0:T(8,128)(2,1)S(1)}, bf16[256,1536]{1,0:T(8,128)(2,1)}, u32[]{:S(2)}, u32[]{:S(2)}) collective-permute-start(bf16[256,1536]{1,0:T(8,128)(2,1)S(1)} %fusion.21.refs_0_), channel_id=1, source_target_pairs={{0,1},{1,0},{2,3},{3,2},{4,5},{5,4},{6,7},{7,6},{8,9},{9,8},{10,11... | collective-permute-start | bytes 2359304 | tf_op jit(solution)/shard_map/ppermute | solution.py:48
  14.4 22.1 %collective-permute-start.1 = (bf16[256,1536]{1,0:T(8,128)(2,1)S(1)}, bf16[256,1536]{1,0:T(8,128)(2,1)}, u32[]{:S(2)}, u32[]{:S(2)}) collective-permute-start(bf16[256,1536]{1,0:T(8,128)(2,1)S(1)} %fusion.21.refs_0_), channel_id=1, source_target_pairs={{0,2},{1,3},{2,0},{3,1},{4,6},{5,7},{6,4},{7,5},{8,10},{9,11},{10,... | collective-permute-start | bytes 2359304 | tf_op jit(solution)/shard_map/ppermute | solution.py:48
  22.0 159.0 %all-gather.9.cloned.1.call-start = ((), (), s32[]{:S(2)}) async-start(), calls=%async_computation.21 | async-start | bytes 5308416 | tf_op jit(solution)/shard_map/all_gather | solution.py:1037
  53.5 127.5 %all-gather.11.cloned.1.call-start = ((), (), s32[]{:S(2)}) async-start(), calls=%async_computation.22 | async-start | bytes 5308416 | tf_op jit(solution)/shard_map/all_gather | solution.py:1038
  54.3 29.0 %collective-permute-start.4 = (bf16[256,1536]{1,0:T(8,128)(2,1)S(1)}, bf16[256,1536]{1,0:T(8,128)(2,1)S(1)}, u32[]{:S(2)}, u32[]{:S(2)}) collective-permute-start(bf16[256,1536]{1,0:T(8,128)(2,1)S(1)} %fusion.14.refs_0_), channel_id=1, source_target_pairs={{0,1},{1,0},{2,3},{3,2},{4,5},{5,4},{6,7},{7,6},{8,9},{9,8},{10,11... | collective-permute-start | bytes 2359304 | tf_op jit(solution)/shard_map/ppermute | solution.py:48
  55.8 27.5 %collective-permute-start.5 = (bf16[256,1536]{1,0:T(8,128)(2,1)S(1)}, bf16[256,1536]{1,0:T(8,128)(2,1)}, u32[]{:S(2)}, u32[]{:S(2)}) collective-permute-start(bf16[256,1536]{1,0:T(8,128)(2,1)S(1)} %fusion.14.refs_0_), channel_id=1, source_target_pairs={{0,2},{1,3},{2,0},{3,1},{4,6},{5,7},{6,4},{7,5},{8,10},{9,11},{10,... | collective-permute-start | bytes 2359304 | tf_op jit(solution)/shard_map/ppermute | solution.py:48
  63.6 19.7 %collective-permute-start.2 = (bf16[128,1536]{1,0:T(8,128)(2,1)S(1)}, bf16[128,1536]{1,0:T(8,128)(2,1)S(1)}, u32[]{:S(2)}, u32[]{:S(2)}) collective-permute-start(bf16[128,1536]{1,0:T(8,128)(2,1)S(1)} %slice.188), channel_id=1, source_target_pairs={{0,2},{1,3},{2,0},{3,1},{4,6},{5,7},{6,4},{7,5},{8,10},{9,11},{10,... | collective-permute-start | bytes 1179656 | tf_op jit(solution)/shard_map/ppermute | solution.py:48
  96.3 39.7 %all-to-all-start = ((bf16[4,192,1536]{2,1,0:T(8,128)(2,1)}), bf16[4,192,1536]{2,1,0:T(8,128)(2,1)S(1)}, u32[]{:S(2)}, u32[]{:S(2)}) async-start(bf16[4,192,1536]{2,1,0:T(8,128)(2,1)} %broadcast_in_dim.47), calls=%async_computation | async-start | bytes 4718592 | tf_op jit(solution)/shard_map/all_to_all | solution.py:89
  136.0 45.0 %collective-permute-start.8 = (bf16[4,192,1536]{2,1,0:T(8,128)(2,1)S(1)}, bf16[4,192,1536]{2,1,0:T(8,128)(2,1)}, u32[]{:S(2)}, u32[]{:S(2)}) collective-permute-start(bf16[4,192,1536]{2,1,0:T(8,128)(2,1)S(1)} %all-to-all-done.wo_mine), channel_id=1, source_target_pairs={{0,4},{4,0},{8,12},{12,8},{16,20},{20,16},{24,28},{28,24},{1,5},{5... | collective-permute-start | bytes 7077896 | tf_op jit(solution)/shard_map/ppermute | solution.py:48
  141.1 29.8 %collective-permute-start.10 = (bf16[768,256]{1,0:T(8,128)(2,1)S(1)}, bf16[768,256]{1,0:T(8,128)(2,1)}, u32[]{:S(2)}, u32[]{:S(2)}) collective-permute-start(bf16[768,256]{1,0:T(8,128)(2,1)S(1)} %pad_maximum_fusion.6), channel_id=1, source_target_pairs={{0,2},{1,3},{2,0},{3,1},{4,6},{5,7},{6,4},{7,5},{8,10},{9,11},{10,... | collective-permute-start | bytes 1179656 | tf_op jit(solution)/shard_map/ppermute | solution.py:48
  143.0 27.9 %collective-permute-start.11 = (bf16[768,256]{1,0:T(8,128)(2,1)S(1)}, bf16[768,256]{1,0:T(8,128)(2,1)}, u32[]{:S(2)}, u32[]{:S(2)}) collective-permute-start(bf16[768,256]{1,0:T(8,128)(2,1)S(1)} %pad_maximum_fusion.6), channel_id=1, source_target_pairs={{0,3},{1,2},{2,1},{3,0},{4,7},{5,6},{6,5},{7,4},{8,11},{9,10},{10,... | collective-permute-start | bytes 1179656 | tf_op jit(solution)/shard_map/ppermute | solution.py:48
  144.4 26.5 %collective-permute-start.9 = (bf16[768,256]{1,0:T(8,128)(2,1)S(1)}, bf16[768,256]{1,0:T(8,128)(2,1)}, u32[]{:S(2)}, u32[]{:S(2)}) collective-permute-start(bf16[768,256]{1,0:T(8,128)(2,1)S(1)} %pad_maximum_fusion.6), channel_id=1, source_target_pairs={{0,1},{1,0},{2,3},{3,2},{4,5},{5,4},{6,7},{7,6},{8,9},{9,8},{10,11... | collective-permute-start | bytes 1179656 | tf_op jit(solution)/shard_map/ppermute | solution.py:48
  144.7 26.2 %all-to-all-start.1 = ((bf16[4,384,256]{2,1,0:T(8,128)(2,1)}), bf16[4,384,256]{2,1,0:T(8,128)(2,1)}, u32[]{:S(2)}, u32[]{:S(2)}) async-start(bf16[4,384,256]{2,1,0:T(8,128)(2,1)} %get-tuple-element.228.o_ref), calls=%async_computation.1 | async-start | bytes 1572864 | tf_op jit(solution)/shard_map/all_to_all | solution.py:89
  173.5 23.8 %collective-permute-start.12 = (bf16[256,1536]{1,0:T(8,128)(2,1)}, bf16[256,1536]{1,0:T(8,128)(2,1)}, u32[]{:S(2)}, u32[]{:S(2)}) collective-permute-start(bf16[256,1536]{1,0:T(8,128)(2,1)} %get-tuple-element.241.refs_5_.cot_ref), channel_id=1, source_target_pairs={{0,1},{1,0},{2,3},{3,2},{4,5},{5,4},{6,7},{7,6},{8,9},{9,8},{10,11... | collective-permute-start | bytes 2359304 | tf_op jit(solution)/shard_map/ppermute | solution.py:48
  176.1 25.0 %collective-permute-start.13 = (bf16[256,1536]{1,0:T(8,128)(2,1)}, bf16[256,1536]{1,0:T(8,128)(2,1)}, u32[]{:S(2)}, u32[]{:S(2)}) collective-permute-start(bf16[256,1536]{1,0:T(8,128)(2,1)} %get-tuple-element.241.refs_5_.cot_ref), channel_id=1, source_target_pairs={{0,2},{1,3},{2,0},{3,1},{4,6},{5,7},{6,4},{7,5},{8,10},{9,11},{10,... | collective-permute-start | bytes 2359304 | tf_op jit(solution)/shard_map/ppermute | solution.py:48
  176.6 28.7 %all-to-all-start.2 = ((bf16[4,384,256]{2,1,0:T(8,128)(2,1)}), bf16[4,384,256]{2,1,0:T(8,128)(2,1)}, u32[]{:S(2)}, u32[]{:S(2)}) async-start(bf16[4,384,256]{2,1,0:T(8,128)(2,1)} %get-tuple-element.240.o_ref), calls=%async_computation.2 | async-start | bytes 1572864 | tf_op jit(solution)/shard_map/all_to_all | solution.py:89
  193.8 34.6 %collective-permute-start.14 = (bf16[256,1536]{1,0:T(8,128)(2,1)}, bf16[256,1536]{1,0:T(8,128)(2,1)S(1)}, u32[]{:S(2)}, u32[]{:S(2)}) collective-permute-start(bf16[256,1536]{1,0:T(8,128)(2,1)} %get-tuple-element.254.refs_0_), channel_id=1, source_target_pairs={{0,1},{1,0},{2,3},{3,2},{4,5},{5,4},{6,7},{7,6},{8,9},{9,8},{10,11... | collective-permute-start | bytes 2359304 | tf_op jit(solution)/shard_map/ppermute | solution.py:48
  195.8 32.6 %collective-permute-start.15 = (bf16[256,1536]{1,0:T(8,128)(2,1)}, bf16[256,1536]{1,0:T(8,128)(2,1)S(1)}, u32[]{:S(2)}, u32[]{:S(2)}) collective-permute-start(bf16[256,1536]{1,0:T(8,128)(2,1)} %get-tuple-element.254.refs_0_), channel_id=1, source_target_pairs={{0,2},{1,3},{2,0},{3,1},{4,6},{5,7},{6,4},{7,5},{8,10},{9,11},{10,... | collective-permute-start | bytes 2359304 | tf_op jit(solution)/shard_map/ppermute | solution.py:48
  205.3 23.1 %collective-permute-start.16 = (bf16[128,1536]{1,0:T(8,128)(2,1)S(1)}, bf16[128,1536]{1,0:T(8,128)(2,1)S(1)}, u32[]{:S(2)}, u32[]{:S(2)}) collective-permute-start(bf16[128,1536]{1,0:T(8,128)(2,1)S(1)} %slice.199), channel_id=1, source_target_pairs={{0,2},{1,3},{2,0},{3,1},{4,6},{5,7},{6,4},{7,5},{8,10},{9,11},{10,... | collective-permute-start | bytes 1179656 | tf_op jit(solution)/shard_map/ppermute | solution.py:48
  205.8 22.5 %collective-permute-start.17 = (bf16[128,1536]{1,0:T(8,128)(2,1)S(1)}, bf16[128,1536]{1,0:T(8,128)(2,1)S(1)}, u32[]{:S(2)}, u32[]{:S(2)}) collective-permute-start(bf16[128,1536]{1,0:T(8,128)(2,1)S(1)} %slice.200), channel_id=1, source_target_pairs={{0,1},{1,0},{2,3},{3,2},{4,5},{5,4},{6,7},{7,6},{8,9},{9,8},{10,11... | collective-permute-start | bytes 1179656 | tf_op jit(solution)/shard_map/ppermute | solution.py:48
  230.4 36.1 %collective-permute-start.18 = (bf16[256,1536]{1,0:T(8,128)(2,1)S(1)}, bf16[256,1536]{1,0:T(8,128)(2,1)S(1)}, u32[]{:S(2)}, u32[]{:S(2)}) collective-permute-start(bf16[256,1536]{1,0:T(8,128)(2,1)S(1)} %copy-done.32), channel_id=1, source_target_pairs={{0,1},{1,0},{2,3},{3,2},{4,5},{5,4},{6,7},{7,6},{8,9},{9,8},{10,11... | collective-permute-start | bytes 2359304 | tf_op jit(solution)/shard_map/ppermute | solution.py:48
  231.9 34.7 %collective-permute-start.19 = (bf16[256,1536]{1,0:T(8,128)(2,1)S(1)}, bf16[256,1536]{1,0:T(8,128)(2,1)S(1)}, u32[]{:S(2)}, u32[]{:S(2)}) collective-permute-start(bf16[256,1536]{1,0:T(8,128)(2,1)S(1)} %copy-done.32), channel_id=1, source_target_pairs={{0,2},{1,3},{2,0},{3,1},{4,6},{5,7},{6,4},{7,5},{8,10},{9,11},{10,... | collective-permute-start | bytes 2359304 | tf_op jit(solution)/shard_map/ppermute | solution.py:48
  242.8 32.8 %collective-permute-start.24 = (bf16[256,1536]{1,0:T(8,128)(2,1)S(1)}, bf16[256,1536]{1,0:T(8,128)(2,1)S(1)}, u32[]{:S(2)}, u32[]{:S(2)}) collective-permute-start(bf16[256,1536]{1,0:T(8,128)(2,1)S(1)} %get-tuple-element.263.refs_5_.cot_ref), channel_id=1, source_target_pairs={{0,1},{1,0},{2,3},{3,2},{4,5},{5,4},{6,7},{7,6},{8,9},{9,8},{10,11... | collective-permute-start | bytes 2359304 | tf_op jit(solution)/shard_map/ppermute | solution.py:48
  243.3 32.3 %collective-permute-start.25 = (bf16[256,1536]{1,0:T(8,128)(2,1)S(1)}, bf16[256,1536]{1,0:T(8,128)(2,1)S(1)}, u32[]{:S(2)}, u32[]{:S(2)}) collective-permute-start(bf16[256,1536]{1,0:T(8,128)(2,1)S(1)} %get-tuple-element.263.refs_5_.cot_ref), channel_id=1, source_target_pairs={{0,2},{1,3},{2,0},{3,1},{4,6},{5,7},{6,4},{7,5},{8,10},{9,11},{10,... | collective-permute-start | bytes 2359304 | tf_op jit(solution)/shard_map/ppermute | solution.py:48
  266.6 26.1 %collective-permute-start.22 = (bf16[128,1536]{1,0:T(8,128)(2,1)S(1)}, bf16[128,1536]{1,0:T(8,128)(2,1)S(1)}, u32[]{:S(2)}, u32[]{:S(2)}) collective-permute-start(bf16[128,1536]{1,0:T(8,128)(2,1)S(1)} %slice.203), channel_id=1, source_target_pairs={{0,2},{1,3},{2,0},{3,1},{4,6},{5,7},{6,4},{7,5},{8,10},{9,11},{10,... | collective-permute-start | bytes 1179656 | tf_op jit(solution)/shard_map/ppermute | solution.py:48
  267.6 25.1 %collective-permute-start.23 = (bf16[128,1536]{1,0:T(8,128)(2,1)S(1)}, bf16[128,1536]{1,0:T(8,128)(2,1)}, u32[]{:S(2)}, u32[]{:S(2)}) collective-permute-start(bf16[128,1536]{1,0:T(8,128)(2,1)S(1)} %slice.204), channel_id=1, source_target_pairs={{0,1},{1,0},{2,3},{3,2},{4,5},{5,4},{6,7},{7,6},{8,9},{9,8},{10,11... | collective-permute-start | bytes 1179656 | tf_op jit(solution)/shard_map/ppermute | solution.py:48
  293.7 41.9 %all-to-all-start.3 = ((bf16[4,256,1536]{2,1,0:T(8,128)(2,1)}), bf16[4,256,1536]{2,1,0:T(8,128)(2,1)}, u32[]{:S(2)}, u32[]{:S(2)}) async-start(bf16[4,256,1536]{2,1,0:T(8,128)(2,1)} %glu_back.2), calls=%async_computation.3 | async-start | bytes 6291456 | tf_op jit(solution)/shard_map/all_to_all | solution.py:89
  298.4 405.3 %reduce-scatter.9.cloned.1.call-start = ((), (), s32[]{:S(2)}) async-start(), calls=%async_computation.15 | async-start | bytes 5308416 | tf_op jit(solution)/shard_map/reduce_scatter | solution.py:969
  350.7 352.9 %reduce-scatter.19.cloned.1.call-start = ((), (), s32[]{:S(2)}) async-start(), calls=%async_computation.23 | async-start | bytes 7864320
  365.6 38.6 %all-to-all-start.4 = ((bf16[4,256,1536]{2,1,0:T(8,128)(2,1)}), bf16[4,256,1536]{2,1,0:T(8,128)(2,1)}, u32[]{:S(2)}, u32[]{:S(2)}) async-start(bf16[4,256,1536]{2,1,0:T(8,128)(2,1)} %glu_back.3), calls=%async_computation.5 | async-start | bytes 6291456 | tf_op jit(solution)/shard_map/all_to_all | solution.py:89
  370.3 333.4 %reduce-scatter.17.cloned.1.call-start = ((), (), s32[]{:S(2)}) async-start(), calls=%async_computation.19 | async-start | bytes 5308416 | tf_op jit(solution)/shard_map/reduce_scatter | solution.py:969
  404.2 22.4 %all-to-all-start.5 = ((bf16[4,384,256]{2,1,0:T(8,128)(2,1)}), bf16[4,384,256]{2,1,0:T(8,128)(2,1)S(1)}, u32[]{:S(2)}, u32[]{:S(2)}) async-start(bf16[4,384,256]{2,1,0:T(8,128)(2,1)} %bitcast.171), calls=%async_computation.6 | async-start | bytes 1572864 | tf_op jit(solution)/shard_map/all_to_all | solution.py:89
  443.6 23.5 %collective-permute-start.28 = (bf16[4,4,3,192,384]{4,3,2,1,0:T(8,128)(2,1)}, bf16[4,4,3,192,384]{4,3,2,1,0:T(8,128)(2,1)}, u32[]{:S(2)}, u32[]{:S(2)}) collective-permute-start(bf16[4,4,3,192,384]{4,3,2,1,0:T(8,128)(2,1)} %get-tuple-element.325), channel_id=1, source_target_pairs={{0,4},{4,0},{8,12},{12,8},{16,20},{20,16},{24,28},{28,24},{1,5},{5... | collective-permute-start | bytes 21233672 | tf_op jit(solution)/shard_map/ppermute | solution.py:48
  444.3 81.7 %collective-permute-start.29 = (bf16[768,256]{1,0:T(8,128)(2,1)}, bf16[768,256]{1,0:T(8,128)(2,1)}, u32[]{:S(2)}, u32[]{:S(2)}) collective-permute-start(bf16[768,256]{1,0:T(8,128)(2,1)} %get-tuple-element.400), channel_id=1, source_target_pairs={{0,1},{1,0},{2,3},{3,2},{4,5},{5,4},{6,7},{7,6},{8,9},{9,8},{10,11... | collective-permute-start | bytes 1179656 | tf_op jit(solution)/shard_map/ppermute | solution.py:48
  446.2 79.8 %collective-permute-start.30 = (bf16[768,256]{1,0:T(8,128)(2,1)}, bf16[768,256]{1,0:T(8,128)(2,1)}, u32[]{:S(2)}, u32[]{:S(2)}) collective-permute-start(bf16[768,256]{1,0:T(8,128)(2,1)} %get-tuple-element.399), channel_id=1, source_target_pairs={{0,2},{1,3},{2,0},{3,1},{4,6},{5,7},{6,4},{7,5},{8,10},{9,11},{10,... | collective-permute-start | bytes 1179656 | tf_op jit(solution)/shard_map/ppermute | solution.py:48
  447.6 78.4 %collective-permute-start.31 = (bf16[768,256]{1,0:T(8,128)(2,1)}, bf16[768,256]{1,0:T(8,128)(2,1)}, u32[]{:S(2)}, u32[]{:S(2)}) collective-permute-start(bf16[768,256]{1,0:T(8,128)(2,1)} %get-tuple-element.398), channel_id=1, source_target_pairs={{0,3},{1,2},{2,1},{3,0},{4,7},{5,6},{6,5},{7,4},{8,11},{9,10},{10,... | collective-permute-start | bytes 1179656 | tf_op jit(solution)/shard_map/ppermute | solution.py:48
  447.8 60.3 %all-to-all-start.6 = ((bf16[4,384,256]{2,1,0:T(8,128)(2,1)}), bf16[4,384,256]{2,1,0:T(8,128)(2,1)}, u32[]{:S(2)}, u32[]{:S(2)}) async-start(bf16[4,384,256]{2,1,0:T(8,128)(2,1)} %bitcast.39), calls=%async_computation.7 | async-start | bytes 1572864 | tf_op jit(solution)/shard_map/all_to_all | solution.py:89
  452.0 254.0 %reduce-scatter.15.cloned.1.call-start = ((), (), s32[]{:S(2)}) async-start(), calls=%async_computation.18 | async-start | bytes 5308416 | tf_op jit(solution)/shard_map/reduce_scatter | solution.py:969
  467.1 248.8 %reduce-scatter.13.cloned.1.call-start = ((), (), s32[]{:S(2)}) async-start(), calls=%async_computation.17 | async-start | bytes 2949120 | tf_op jit(solution)/shard_map/reduce_scatter | solution.py:1233
  483.7 28.2 %collective-permute-start.32 = (bf16[1152,384]{1,0:T(8,128)(2,1)}, bf16[1152,384]{1,0:T(8,128)(2,1)}, u32[]{:S(2)}, u32[]{:S(2)}) collective-permute-start(bf16[1152,384]{1,0:T(8,128)(2,1)} %get-tuple-element.389), channel_id=1, source_target_pairs={{0,2},{1,3},{2,0},{3,1},{4,6},{5,7},{6,4},{7,5},{8,10},{9,11},{10,... | collective-permute-start | bytes 2654216 | tf_op jit(solution)/shard_map/ppermute | solution.py:48
  485.7 26.2 %collective-permute-start.33 = (bf16[1152,384]{1,0:T(8,128)(2,1)}, bf16[1152,384]{1,0:T(8,128)(2,1)}, u32[]{:S(2)}, u32[]{:S(2)}) collective-permute-start(bf16[1152,384]{1,0:T(8,128)(2,1)} %get-tuple-element.390), channel_id=1, source_target_pairs={{0,1},{1,0},{2,3},{3,2},{4,5},{5,4},{6,7},{7,6},{8,9},{9,8},{10,11... | collective-permute-start | bytes 2654216 | tf_op jit(solution)/shard_map/ppermute | solution.py:48
  530.5 40.9 %collective-permute-start.35 = (bf16[2304,384]{1,0:T(8,128)(2,1)}, bf16[2304,384]{1,0:T(8,128)(2,1)S(1)}, u32[]{:S(2)}, u32[]{:S(2)}) collective-permute-start(bf16[2304,384]{1,0:T(8,128)(2,1)} %pad_maximum_fusion.4), channel_id=1, source_target_pairs={{0,2},{1,3},{2,0},{3,1},{4,6},{5,7},{6,4},{7,5},{8,10},{9,11},{10,... | collective-permute-start | bytes 5308424 | tf_op jit(solution)/shard_map/ppermute | solution.py:48
  532.0 40.6 %collective-permute-start.34 = (bf16[2304,384]{1,0:T(8,128)(2,1)}, bf16[2304,384]{1,0:T(8,128)(2,1)}, u32[]{:S(2)}, u32[]{:S(2)}) collective-permute-start(bf16[2304,384]{1,0:T(8,128)(2,1)} %pad_maximum_fusion.3), channel_id=1, source_target_pairs={{0,1},{1,0},{2,3},{3,2},{4,5},{5,4},{6,7},{7,6},{8,9},{9,8},{10,11... | collective-permute-start | bytes 5308424 | tf_op jit(solution)/shard_map/ppermute | solution.py:48
  532.6 39.9 %collective-permute-start.36 = (bf16[4,192,384]{2,1,0:T(8,128)(2,1)S(1)}, bf16[4,192,384]{2,1,0:T(8,128)(2,1)S(1)}, u32[]{:S(2)}, u32[]{:S(2)}) collective-permute-start(bf16[4,192,384]{2,1,0:T(8,128)(2,1)S(1)} %fusion.33), channel_id=1, source_target_pairs={{0,4},{4,0},{8,12},{12,8},{16,20},{20,16},{24,28},{28,24},{1,5},{5... | collective-permute-start | bytes 1769480 | tf_op jit(solution)/shard_map/ppermute | solution.py:48
  578.1 40.4 %all-to-all-start.7 = ((bf16[4,256,1536]{2,1,0:T(8,128)(2,1)}), bf16[4,256,1536]{2,1,0:T(8,128)(2,1)}, u32[]{:S(2)}, u32[]{:S(2)}) async-start(bf16[4,256,1536]{2,1,0:T(8,128)(2,1)} %self_back.2), calls=%async_computation.8 | async-start | bytes 6291456 | tf_op jit(solution)/shard_map/all_to_all | solution.py:89
  618.5 40.3 %all-to-all-start.8 = ((bf16[4,256,1536]{2,1,0:T(8,128)(2,1)}), bf16[4,256,1536]{2,1,0:T(8,128)(2,1)}, u32[]{:S(2)}, u32[]{:S(2)}) async-start(bf16[4,256,1536]{2,1,0:T(8,128)(2,1)} %self_back.3), calls=%async_computation.9 | async-start | bytes 6291456 | tf_op jit(solution)/shard_map/all_to_all | solution.py:89
  623.2 95.5 %reduce-scatter.11.cloned.1.call-start = ((), (), s32[]{:S(2)}) async-start(), calls=%async_computation.16 | async-start | bytes 3981312 | tf_op jit(solution)/shard_map/reduce_scatter | solution.py:969
  (88 other events, 1053.9 us)
Sparse Core Ops, SparseCore 0:
  22.1 28.9 all-gather.6
  53.6 51.6 all-gather.8
  107.0 50.5 all-gather.10
  350.8 56.3 reduce-scatter.8
  410.0 90.5 reduce-scatter.18
  502.8 53.8 reduce-scatter.16
  559.0 53.2 reduce-scatter.14
  614.7 46.4 reduce-scatter.12
  663.4 43.0 reduce-scatter.10

commit v8 on v7

--- a/solution.py
+++ b/solution.py
@@ -526,7 +526,7 @@
 
 
 def params():
-    return pltpu.CompilerParams(vmem_limit_bytes=58 * 2**20)
+    return pltpu.CompilerParams(vmem_limit_bytes=60 * 2**20)
 
 
 def self_forward(turned, front_keys, front_values):

time: 734 us -> 736 us (level)
  transfers between devices with their start and end apart: 60 -> 60, of which waited for: 23 -> 23; matrix products, arithmetic and copies ran while one was open for 12% -> 13% of each run, Pallas kernels for 45% -> 45%
where the time goes in v8:
time: 736 us; the launch traced here: 730 us
  Pallas kernels  340 us (46%)
  waiting for transfers between devices  177 us (24%)
  starting transfers between devices  88.2 us (12%)
  other arithmetic  51.9 us (7%)
  local copies, waits for them, and re-layouts  42.7 us (6%)
  between operations  19.3 us (3%)
  matrix products  11.2 us (2%)
    ppermute x42, waiting for transfers between devices, swap(): lax.ppermute(values, axis, [(i, i ^ k) for i in range(lax.axis_size(axis))])  114 us
    all_to_all x9, waiting for transfers between devices, exchange(): return lax.all_to_all(blocks, 'mp', 0, 0)  50.6 us
    ppermute x42, starting transfers between devices, swap(): lax.ppermute(values, axis, [(i, i ^ k) for i in range(lax.axis_size(axis))])  48 us
    pallas_call x3, Pallas kernels, weight_grad(): pl.pallas_call(weight_grad_kernel, grid=(width // block,), in_specs=[pl.B...  45.6 us
    pallas_call x2, Pallas kernels, glu(): pl.pallas_call(functools.partial(glu_kernel, size, len(pieces)), grid=(hi...  44.3 us
    all_to_all x9, starting transfers between devices, exchange(): return lax.all_to_all(blocks, 'mp', 0, 0)  39.8 us
    pallas_call x2, Pallas kernels, self_backward(): pl.pallas_call(functools.partial(self_backward_kernel, min(256, frames)),...  38.4 us
    pallas_call x2, Pallas kernels, local_backward(): pl.pallas_call(functools.partial(local_backward_kernel, clip), grid=(1,),...  36.3 us
  transfers between devices with their start and end apart: 60, of which 23 were waited for; matrix products, arithmetic and copies ran while one was open for 13% of the time, Pallas kernels for 45%

profile of v8, /device:TPU:0, one launch (start us, length us, event | category | flops | bytes accessed | tf_op | source)
XLA Modules:
  0.0 730.0 jit_solution(4863970921733646044)
XLA Ops:
  23.0 10.9 %collective-permute-done.refs_1_ = bf16[256,1536]{1,0:T(8,128)(2,1)} collective-permute-done((bf16[256,1536]{1,0:T(8,128)(2,1)S(1)}, bf16[256,1536]{1,0:T(8,128)(2,1)}, u32[]{:S(2)}, u32[]{:S(2)}) %collective-permute-start) | collective-permute-done | bytes 786464 | tf_op jit(solution)/shard_map/ppermute | solution.py:48
  39.7 11.4 %all-gather.7.cloned.1.call-done = bf16[8,192,384]{2,1,0:T(8,128)(2,1)} async-done(((bf16[2,192,384]{2,1,0:T(8,128)(2,1)}), bf16[8,192,384]{2,1,0:T(8,128)(2,1)}) %all-gather.7.cloned.1.call-update) | async-done | bytes 1179664 | tf_op jit(solution)/shard_map/all_gather | solution.py:1020
  66.6 16.7 %collective-permute-done.2.refs_3_ = bf16[128,1536]{1,0:T(8,128)(2,1)S(1)} collective-permute-done((bf16[128,1536]{1,0:T(8,128)(2,1)S(1)}, bf16[128,1536]{1,0:T(8,128)(2,1)S(1)}, u32[]{:S(2)}, u32[]{:S(2)}) %collective-permute-start.2) | collective-permute-done | bytes 393248 | tf_op jit(solution)/shard_map/ppermute | solution.py:48
  87.8 5.4 collective-permute-done.6.refs_3_
  96.3 3.9 all-to-all-start
  101.6 10.4 %project.2 = (bf16[1152,1024]{1,0:T(8,128)(2,1)}, bf16[2,1024,1536]{2,1,0:T(8,128)(2,1)}, bf16[768,8]{1,0:T(8,128)(2,1)}) custom-call(s32[4]{0:T(128)} %pad_add_fusion.n_ref.order_ref, f32[8,1536]{1,0:T(8,128)} %maximum_maximum_fusion.p_ref, f32[2,1536]{1,0:T(2,128)} %pad_maximum_fusion.9.norm_ref, bf16[1536,384]{1,0:T(8,128)(2,1)} %wq_ref.7, ...), custom_call_target="tpu_custom_call" | custom-call | flops 3680000000 | bytes 11520000 | tf_op jit(solution)/shard_map/project/pallas_call | solution.py:661
  113.9 10.9 %self_forward.2 = (bf16[4,384,256]{2,1,0:T(8,128)(2,1)}, f32[6,1,1024]{2,1,0:T(1,128)}) custom-call(bf16[1152,1024]{1,0:T(8,128)(2,1)} %get-tuple-element.216.q_ref.k_ref.v_ref, bf16[1152,1024]{1,0:T(8,128)(2,1)} %get-tuple-element.216.q_ref.k_ref.v_ref, bf16[1152,1024]{1,0:T(8,128)(2,1)} %get-tuple-element.216.q_ref.k_ref.v_ref, ...), custom_call_target="tpu_custom_call" | custom-call | flops 4001999872 | bytes 12528000 | tf_op jit(solution)/shard_map/self_forward/pallas_call | solution.py:544
  124.9 11.1 %project.3 = (bf16[1152,1024]{1,0:T(8,128)(2,1)}, bf16[2,1024,1536]{2,1,0:T(8,128)(2,1)}, bf16[768,8]{1,0:T(8,128)(2,1)}) custom-call(s32[4]{0:T(128)} %pad_add_fusion.n_ref.order_ref, f32[8,1536]{1,0:T(8,128)} %maximum_maximum_fusion.p_ref, f32[2,1536]{1,0:T(2,128)} %pad_maximum_fusion.9.norm_ref, ...), custom_call_target="tpu_custom_call", output_to_operand_aliasing={{1}: (13, {})} | custom-call | flops 3680000000 | bytes 11520000 | tf_op jit(solution)/shard_map/project/pallas_call | solution.py:661
  144.7 4.2 all-to-all-start.1
  150.3 10.7 %self_forward.3 = (bf16[4,384,256]{2,1,0:T(8,128)(2,1)}, f32[6,1,1024]{2,1,0:T(1,128)}) custom-call(bf16[1152,1024]{1,0:T(8,128)(2,1)} %get-tuple-element.229.q_ref.k_ref.v_ref, bf16[1152,1024]{1,0:T(8,128)(2,1)} %get-tuple-element.229.q_ref.k_ref.v_ref, bf16[1152,1024]{1,0:T(8,128)(2,1)} %get-tuple-element.229.q_ref.k_ref.v_ref, ...), custom_call_target="tpu_custom_call" | custom-call | flops 4001999872 | bytes 12528000 | tf_op jit(solution)/shard_map/self_forward/pallas_call | solution.py:544
  161.0 10.0 %all-to-all-done.1 = bf16[4,384,256]{2,1,0:T(8,128)(2,1)} async-done(((bf16[4,384,256]{2,1,0:T(8,128)(2,1)}), bf16[4,384,256]{2,1,0:T(8,128)(2,1)}, u32[]{:S(2)}, u32[]{:S(2)}) %all-to-all-start.1) | async-done | bytes 786464 | tf_op jit(solution)/shard_map/all_to_all | solution.py:89
  176.7 4.4 all-to-all-start.2
  181.1 12.7 %local_forward.2 = (f32[256,1536]{1,0:T(8,128)}, f32[256,1536]{1,0:T(8,128)}, bf16[256,1536]{1,0:T(8,128)(2,1)}, bf16[1536,256]{1,0:T(8,128)(2,1)}, bf16[1536,25...) custom-call(s32[2]{0:T(128)} %n_ref.7, s32[1]{0:T(128)} %bitcast.core_ref, ...), custom_call_target="tpu_custom_call" | custom-call | flops 5198000128 | bytes 16272000 | tf_op jit(solution)/shard_map/local_forward/pallas_call | solution.py:368
  197.4 3.8 collective-permute-done.13.refs_7_
  206.8 13.0 %local_forward.3 = (f32[256,1536]{1,0:T(8,128)}, f32[256,1536]{1,0:T(8,128)}, bf16[256,1536]{1,0:T(8,128)(2,1)}, bf16[1536,256]{1,0:T(8,128)(2,1)}, bf16[1536,25...) custom-call(s32[2]{0:T(128)} %n_ref.7, s32[1]{0:T(128)} %bitcast.core_ref, ...), custom_call_target="tpu_custom_call" | custom-call | flops 5198000128 | bytes 16272000 | tf_op jit(solution)/shard_map/local_forward/pallas_call | solution.py:368
  219.8 8.6 %collective-permute-done.16.refs_8_ = bf16[128,1536]{1,0:T(8,128)(2,1)S(1)} collective-permute-done((bf16[128,1536]{1,0:T(8,128)(2,1)S(1)}, bf16[128,1536]{1,0:T(8,128)(2,1)S(1)}, u32[]{:S(2)}, u32[]{:S(2)}) %collective-permute-start.16) | collective-permute-done | bytes 393248 | tf_op jit(solution)/shard_map/ppermute | solution.py:48
  232.7 7.9 %collective-permute-done.20.refs_3_ = bf16[128,1536]{1,0:T(8,128)(2,1)S(1)} collective-permute-done((bf16[128,1536]{1,0:T(8,128)(2,1)S(1)}, bf16[128,1536]{1,0:T(8,128)(2,1)S(1)}, u32[]{:S(2)}, u32[]{:S(2)}) %collective-permute-start.20) | collective-permute-done | bytes 393248 | tf_op jit(solution)/shard_map/ppermute | solution.py:48
  243.5 22.1 %glu.2 = (bf16[2,1024,1536]{2,1,0:T(8,128)(2,1)}, bf16[2,1024,1536]{2,1,0:T(8,128)(2,1)}, bf16[2,1024,1536]{2,1,0:T(8,128)(2,1)}, bf16[2,1024,1536]{2,1,0:T(8,128)(2,1)}, bf16[2,1024,1536]{2,1,0:T(8,128)(2,1)}) custom-call(s32[4]{0:T(128)} %pad_add_fusion.n_ref.order_ref, bf16[1536,1536]{1,0:T(8,128)(2,1)} %gate_ref.7, bf16[1536,1536]{1,0:T(8,128)(2,1)} %up_ref.7, ...), custom_call_target="tpu_custom_call" | custom-call | flops 10119999488 | bytes 31680000 | tf_op jit(solution)/shard_map/glu/pallas_call | solution.py:723
  268.6 6.5 collective-permute-done.24.refs_6_
  279.4 15.2 %glu_back.2 = bf16[4,256,1536]{2,1,0:T(8,128)(2,1)} custom-call(bf16[2,1024,1536]{2,1,0:T(8,128)(2,1)} %get-tuple-element.266.dg_ref.refs_11_, bf16[2,1024,1536]{2,1,0:T(8,128)(2,1)} %get-tuple-element.267.du_ref.refs_12_, bf16[1536,1536]{1,0:T(8,128)(2,1)} %gate_ref.7, bf16[1536,1536]{1,0:T(8,128)(2,1)} %up_ref.7), custom_call_target="tpu_custom_call" | custom-call | flops 6670000128 | bytes 20880000 | tf_op jit(solution)/shard_map/glu_back/pallas_call | solution.py:761
  295.6 4.6 all-to-all-start.3
  300.3 22.1 %glu.3 = (bf16[2,1024,1536]{2,1,0:T(8,128)(2,1)}, bf16[2,1024,1536]{2,1,0:T(8,128)(2,1)}, bf16[2,1024,1536]{2,1,0:T(8,128)(2,1)}, bf16[2,1024,1536]{2,1,0:T(8,128)(2,1)}, bf16[2,1024,1536]{2,1,0:T(8,128)(2,1)}) custom-call(s32[4]{0:T(128)} %pad_add_fusion.n_ref.order_ref, ...), custom_call_target="tpu_custom_call", output_to_operand_aliasing={{0}: (14, {}), {1}: (15, {}), {2}: (16, {}), {3}: (17, {}),... | custom-call | flops 10119999488 | bytes 31680000 | tf_op jit(solution)/shard_map/glu/pallas_call | solution.py:723
  322.4 15.2 %glu_back.3 = bf16[4,256,1536]{2,1,0:T(8,128)(2,1)} custom-call(bf16[2,1024,1536]{2,1,0:T(8,128)(2,1)} %get-tuple-element.285.dg_ref, bf16[2,1024,1536]{2,1,0:T(8,128)(2,1)} %get-tuple-element.286.du_ref, bf16[1536,1536]{1,0:T(8,128)(2,1)} %gate_ref.7, bf16[1536,1536]{1,0:T(8,128)(2,1)} %up_ref.7), custom_call_target="tpu_custom_call" | custom-call | flops 6670000128 | bytes 20880000 | tf_op jit(solution)/shard_map/glu_back/pallas_call | solution.py:761
  337.6 15.0 %weight_grad.3 = bf16[1536,1536]{1,0:T(8,128)(2,1)} custom-call(bf16[2048,1536]{1,0:T(8,128)(2,1)} %bitcast.152, bf16[2048,1536]{1,0:T(8,128)(2,1)} %bitcast.151), custom_call_target="tpu_custom_call" | custom-call | flops 4600000000 | bytes 14400000 | tf_op jit(solution)/shard_map/weight_grad/pallas_call | solution.py:863
  352.7 14.8 %branch.1 = bf16[4,2,256,1536]{3,2,1,0:T(8,128)(2,1)} custom-call(bf16[2,1024,1536]{2,1,0:T(8,128)(2,1)} %get-tuple-element.289.x_ref, bf16[1536,1536]{1,0:T(8,128)(2,1)} %w_ref.1), custom_call_target="tpu_custom_call" | custom-call | flops 6072000000 | bytes 19008000 | tf_op jit(solution)/shard_map/branch/pallas_call | solution.py:838
  367.5 4.7 all-to-all-start.4
  372.3 15.6 %weight_grad.4 = bf16[1536,1536]{1,0:T(8,128)(2,1)} custom-call(bf16[2048,1536]{1,0:T(8,128)(2,1)} %bitcast.149, bf16[2048,1536]{1,0:T(8,128)(2,1)} %bitcast.147), custom_call_target="tpu_custom_call" | custom-call | flops 4600000000 | bytes 14400000 | tf_op jit(solution)/shard_map/weight_grad/pallas_call | solution.py:863
  387.9 18.2 %local_backward.2 = (bf16[256,1536]{1,0:T(8,128)(2,1)}, bf16[256,1536]{1,0:T(8,128)(2,1)}, f32[256,1536]{1,0:T(8,128)}, bf16[1536,256]{1,0:T(8,128)(2,1)}, bf16[...) custom-call(s32[2]{0:T(128)} %n_ref.7, s32[1]{0:T(128)} %bitcast.core_ref, ...), custom_call_target="tpu_custom_call" | custom-call | flops 18400000000 | bytes 57600000 | tf_op jit(solution)/shard_map/local_backward/pallas_call | solution.py:471
  406.1 4.2 all-to-all-start.5
  410.4 18.1 %local_backward.3 = (bf16[256,1536]{1,0:T(8,128)(2,1)}, bf16[256,1536]{1,0:T(8,128)(2,1)}, f32[256,1536]{1,0:T(8,128)}, bf16[1536,256]{1,0:T(8,128)(2,1)}, bf16[...) custom-call(s32[2]{0:T(128)} %n_ref.7, s32[1]{0:T(128)} %bitcast.core_ref, ...), custom_call_target="tpu_custom_call" | custom-call | flops 18400000000 | bytes 57600000 | tf_op jit(solution)/shard_map/local_backward/pallas_call | solution.py:471
  431.4 14.2 %whole_grad.2 = (bf16[4,4,3,192,384]{4,3,2,1,0:T(8,128)(2,1)}, bf16[3,1536,512]{2,1,0:T(8,128)(2,1)}) custom-call(s32[1]{0:T(128)S(6)} %sub.72.core_ref, bf16[256,1536]{1,0:T(8,128)(2,1)} %get-tuple-element.310.refs_0_, bf16[256,1536]{1,0:T(8,128)(2,1)} %get-tuple-element.311.refs_1_, bf16[256,1536]{1,0:T(8,128)(2,1)} %get-tuple-element.318.refs_2_, ...), custom_call_target="tpu_custom_call" | custom-call | flops 13799999488 | bytes 43200000 | tf_op jit(solution)/shard_map/whole_grad/pallas_call | solution.py:814
  449.8 4.2 all-to-all-start.6
  454.1 15.0 %weight_grad.5 = bf16[1536,1536]{1,0:T(8,128)(2,1)} custom-call(bf16[2048,1536]{1,0:T(8,128)(2,1)} %bitcast.150, bf16[2048,1536]{1,0:T(8,128)(2,1)} %bitcast.148), custom_call_target="tpu_custom_call" | custom-call | flops 4600000000 | bytes 14400000 | tf_op jit(solution)/shard_map/weight_grad/pallas_call | solution.py:863
  469.2 12.9 %whole_grad.3 = bf16[4,4,3,192,384]{4,3,2,1,0:T(8,128)(2,1)} custom-call(s32[1]{0:T(128)} %bitcast.core_ref, bf16[3,1536,512]{2,1,0:T(8,128)(2,1)} %get-tuple-element.324.refs_0_, bf16[1536,256]{1,0:T(8,128)(2,1)} %get-tuple-element.322.refs_6_.refs_1_, bf16[1536,256]{1,0:T(8,128)(2,1)} %get-tuple-element.323.refs_7_.refs_2_, ...), custom_call_target="tpu_custom_call" | custom-call | flops 13799999488 | bytes 43200000 | tf_op jit(solution)/shard_map/whole_grad/pallas_call | solution.py:814
  490.8 19.2 %self_backward.2 = (bf16[3,384,1024]{2,1,0:T(8,128)(2,1)}, bf16[384,1]{1,0:T(8,128)(2,1)}, bf16[384,1]{1,0:T(8,128)(2,1)}) custom-call(bf16[1152,1024]{1,0:T(8,128)(2,1)} %get-tuple-element.216.q_ref.k_ref.v_ref, bf16[1152,1024]{1,0:T(8,128)(2,1)} %get-tuple-element.216.q_ref.k_ref.v_ref, bf16[1152,1024]{1,0:T(8,128)(2,1)} %get-tuple-element.216.q_ref.k_ref.v_ref, ...), custom_call_target="tpu_custom_call" | custom-call | flops 20700000256 | bytes 64800000 | tf_op jit(solution)/shard_map/self_backward/pallas_call | solution.py:573
  519.0 8.9 %self_back.2 = bf16[4,256,1536]{2,1,0:T(8,128)(2,1)} custom-call(bf16[3,384,1024]{2,1,0:T(8,128)(2,1)} %get-tuple-element.351.d_ref.refs_0_, bf16[1536,384]{1,0:T(8,128)(2,1)} %wq_ref.7, bf16[1536,384]{1,0:T(8,128)(2,1)} %wk_ref.7, bf16[1536,384]{1,0:T(8,128)(2,1)} %wv_ref.7), custom_call_target="tpu_custom_call" | custom-call | flops 3220000000 | bytes 10080000 | tf_op jit(solution)/shard_map/self_back/pallas_call | solution.py:949
  535.3 19.2 %self_backward.3 = (bf16[3,384,1024]{2,1,0:T(8,128)(2,1)}, bf16[384,1]{1,0:T(8,128)(2,1)}, bf16[384,1]{1,0:T(8,128)(2,1)}) custom-call(bf16[1152,1024]{1,0:T(8,128)(2,1)} %get-tuple-element.229.q_ref.k_ref.v_ref, bf16[1152,1024]{1,0:T(8,128)(2,1)} %get-tuple-element.229.q_ref.k_ref.v_ref, bf16[1152,1024]{1,0:T(8,128)(2,1)} %get-tuple-element.229.q_ref.k_ref.v_ref, ...), custom_call_target="tpu_custom_call" | custom-call | flops 20700000256 | bytes 64800000 | tf_op jit(solution)/shard_map/self_backward/pallas_call | solution.py:573
  554.5 18.8 %collective-permute-done.35 = bf16[2304,384]{1,0:T(8,128)(2,1)} collective-permute-done((bf16[2304,384]{1,0:T(8,128)(2,1)}, bf16[2304,384]{1,0:T(8,128)(2,1)}, u32[]{:S(2)}, u32[]{:S(2)}) %collective-permute-start.35) | collective-permute-done | bytes 1769504 | tf_op jit(solution)/shard_map/ppermute | solution.py:48
  580.6 4.9 all-to-all-start.7
  590.0 16.4 %self_weight_grad.1 = (bf16[1536,1152]{1,0:T(8,128)(2,1)}, f32[1536,1]{1,0:T(8,128)}, f32[1536,1]{1,0:T(8,128)}) custom-call(bf16[2,1024,1536]{2,1,0:T(8,128)(2,1)} %get-tuple-element.290.x_ref, f32[1536,2]{1,0:T(8,128)} %get-tuple-element.414.p_ref, f32[2,1152]{1,0:T(2,128)} %pad_convert_fusion.f_ref, ...), custom_call_target="tpu_custom_call" | custom-call | flops 5520000000 | bytes 17280000 | tf_op jit(solution)/shard_map/self_weight_grad/pallas_call | solution.py:917
  606.4 8.8 %self_back.3 = bf16[4,256,1536]{2,1,0:T(8,128)(2,1)} custom-call(bf16[3,384,1024]{2,1,0:T(8,128)(2,1)} %get-tuple-element.359.refs_1_.d_ref, bf16[1536,384]{1,0:T(8,128)(2,1)} %wq_ref.7, bf16[1536,384]{1,0:T(8,128)(2,1)} %wk_ref.7, bf16[1536,384]{1,0:T(8,128)(2,1)} %wv_ref.7), custom_call_target="tpu_custom_call" | custom-call | flops 3220000000 | bytes 10080000 | tf_op jit(solution)/shard_map/self_back/pallas_call | solution.py:949
  615.2 5.7 all-to-all-done.7
  621.0 4.6 all-to-all-start.8
  628.5 32.7 %all-to-all-done.8 = bf16[4,256,1536]{2,1,0:T(8,128)(2,1)} async-done(((bf16[4,256,1536]{2,1,0:T(8,128)(2,1)}), bf16[4,256,1536]{2,1,0:T(8,128)(2,1)}, u32[]{:S(2)}, u32[]{:S(2)}) %all-to-all-start.8) | async-done | bytes 3145760 | tf_op jit(solution)/shard_map/all_to_all | solution.py:89
  664.1 4.5 collective-permute-done.38
  671.0 12.3 %collective-permute-done.39 = f32[23,1536]{1,0:T(8,128)S(1)} collective-permute-done((f32[23,1536]{1,0:T(8,128)S(1)}, f32[23,1536]{1,0:T(8,128)S(1)}, u32[]{:S(2)}, u32[]{:S(2)}) %collective-permute-start.39) | collective-permute-done | bytes 141344 | tf_op jit(solution)/shard_map/ppermute | solution.py:48
  693.8 3.7 fusion.49
  697.6 5.2 fusion.36
  (381 shorter events, 166.9 us)
Async XLA Ops:
  7.2 43.9 %all-gather.7.cloned.1.call-start = ((), (), s32[]{:S(2)}) async-start(), calls=%async_computation.20 | async-start | bytes 1474560 | tf_op jit(solution)/shard_map/all_gather | solution.py:1020
  11.4 22.6 %collective-permute-start = (bf16[256,1536]{1,0:T(8,128)(2,1)S(1)}, bf16[256,1536]{1,0:T(8,128)(2,1)}, u32[]{:S(2)}, u32[]{:S(2)}) collective-permute-start(bf16[256,1536]{1,0:T(8,128)(2,1)S(1)} %fusion.21.refs_0_), channel_id=1, source_target_pairs={{0,1},{1,0},{2,3},{3,2},{4,5},{5,4},{6,7},{7,6},{8,9},{9,8},{10,11... | collective-permute-start | bytes 2359304 | tf_op jit(solution)/shard_map/ppermute | solution.py:48
  14.4 22.1 %collective-permute-start.1 = (bf16[256,1536]{1,0:T(8,128)(2,1)S(1)}, bf16[256,1536]{1,0:T(8,128)(2,1)}, u32[]{:S(2)}, u32[]{:S(2)}) collective-permute-start(bf16[256,1536]{1,0:T(8,128)(2,1)S(1)} %fusion.21.refs_0_), channel_id=1, source_target_pairs={{0,2},{1,3},{2,0},{3,1},{4,6},{5,7},{6,4},{7,5},{8,10},{9,11},{10,... | collective-permute-start | bytes 2359304 | tf_op jit(solution)/shard_map/ppermute | solution.py:48
  22.0 159.1 %all-gather.9.cloned.1.call-start = ((), (), s32[]{:S(2)}) async-start(), calls=%async_computation.21 | async-start | bytes 5308416 | tf_op jit(solution)/shard_map/all_gather | solution.py:1037
  53.6 127.6 %all-gather.11.cloned.1.call-start = ((), (), s32[]{:S(2)}) async-start(), calls=%async_computation.22 | async-start | bytes 5308416 | tf_op jit(solution)/shard_map/all_gather | solution.py:1038
  54.3 29.0 %collective-permute-start.4 = (bf16[256,1536]{1,0:T(8,128)(2,1)S(1)}, bf16[256,1536]{1,0:T(8,128)(2,1)S(1)}, u32[]{:S(2)}, u32[]{:S(2)}) collective-permute-start(bf16[256,1536]{1,0:T(8,128)(2,1)S(1)} %fusion.14.refs_0_), channel_id=1, source_target_pairs={{0,1},{1,0},{2,3},{3,2},{4,5},{5,4},{6,7},{7,6},{8,9},{9,8},{10,11... | collective-permute-start | bytes 2359304 | tf_op jit(solution)/shard_map/ppermute | solution.py:48
  55.8 27.5 %collective-permute-start.5 = (bf16[256,1536]{1,0:T(8,128)(2,1)S(1)}, bf16[256,1536]{1,0:T(8,128)(2,1)}, u32[]{:S(2)}, u32[]{:S(2)}) collective-permute-start(bf16[256,1536]{1,0:T(8,128)(2,1)S(1)} %fusion.14.refs_0_), channel_id=1, source_target_pairs={{0,2},{1,3},{2,0},{3,1},{4,6},{5,7},{6,4},{7,5},{8,10},{9,11},{10,... | collective-permute-start | bytes 2359304 | tf_op jit(solution)/shard_map/ppermute | solution.py:48
  63.6 19.6 %collective-permute-start.2 = (bf16[128,1536]{1,0:T(8,128)(2,1)S(1)}, bf16[128,1536]{1,0:T(8,128)(2,1)S(1)}, u32[]{:S(2)}, u32[]{:S(2)}) collective-permute-start(bf16[128,1536]{1,0:T(8,128)(2,1)S(1)} %slice.188), channel_id=1, source_target_pairs={{0,2},{1,3},{2,0},{3,1},{4,6},{5,7},{6,4},{7,5},{8,10},{9,11},{10,... | collective-permute-start | bytes 1179656 | tf_op jit(solution)/shard_map/ppermute | solution.py:48
  96.3 39.7 %all-to-all-start = ((bf16[4,192,1536]{2,1,0:T(8,128)(2,1)}), bf16[4,192,1536]{2,1,0:T(8,128)(2,1)S(1)}, u32[]{:S(2)}, u32[]{:S(2)}) async-start(bf16[4,192,1536]{2,1,0:T(8,128)(2,1)} %broadcast_in_dim.47), calls=%async_computation | async-start | bytes 4718592 | tf_op jit(solution)/shard_map/all_to_all | solution.py:89
  136.0 45.0 %collective-permute-start.8 = (bf16[4,192,1536]{2,1,0:T(8,128)(2,1)S(1)}, bf16[4,192,1536]{2,1,0:T(8,128)(2,1)}, u32[]{:S(2)}, u32[]{:S(2)}) collective-permute-start(bf16[4,192,1536]{2,1,0:T(8,128)(2,1)S(1)} %all-to-all-done.wo_mine), channel_id=1, source_target_pairs={{0,4},{4,0},{8,12},{12,8},{16,20},{20,16},{24,28},{28,24},{1,5},{5... | collective-permute-start | bytes 7077896 | tf_op jit(solution)/shard_map/ppermute | solution.py:48
  141.1 29.8 %collective-permute-start.10 = (bf16[768,256]{1,0:T(8,128)(2,1)S(1)}, bf16[768,256]{1,0:T(8,128)(2,1)}, u32[]{:S(2)}, u32[]{:S(2)}) collective-permute-start(bf16[768,256]{1,0:T(8,128)(2,1)S(1)} %pad_maximum_fusion.6), channel_id=1, source_target_pairs={{0,2},{1,3},{2,0},{3,1},{4,6},{5,7},{6,4},{7,5},{8,10},{9,11},{10,... | collective-permute-start | bytes 1179656 | tf_op jit(solution)/shard_map/ppermute | solution.py:48
  143.0 27.9 %collective-permute-start.11 = (bf16[768,256]{1,0:T(8,128)(2,1)S(1)}, bf16[768,256]{1,0:T(8,128)(2,1)}, u32[]{:S(2)}, u32[]{:S(2)}) collective-permute-start(bf16[768,256]{1,0:T(8,128)(2,1)S(1)} %pad_maximum_fusion.6), channel_id=1, source_target_pairs={{0,3},{1,2},{2,1},{3,0},{4,7},{5,6},{6,5},{7,4},{8,11},{9,10},{10,... | collective-permute-start | bytes 1179656 | tf_op jit(solution)/shard_map/ppermute | solution.py:48
  144.5 26.5 %collective-permute-start.9 = (bf16[768,256]{1,0:T(8,128)(2,1)S(1)}, bf16[768,256]{1,0:T(8,128)(2,1)}, u32[]{:S(2)}, u32[]{:S(2)}) collective-permute-start(bf16[768,256]{1,0:T(8,128)(2,1)S(1)} %pad_maximum_fusion.6), channel_id=1, source_target_pairs={{0,1},{1,0},{2,3},{3,2},{4,5},{5,4},{6,7},{7,6},{8,9},{9,8},{10,11... | collective-permute-start | bytes 1179656 | tf_op jit(solution)/shard_map/ppermute | solution.py:48
  144.7 26.3 %all-to-all-start.1 = ((bf16[4,384,256]{2,1,0:T(8,128)(2,1)}), bf16[4,384,256]{2,1,0:T(8,128)(2,1)}, u32[]{:S(2)}, u32[]{:S(2)}) async-start(bf16[4,384,256]{2,1,0:T(8,128)(2,1)} %get-tuple-element.228.o_ref), calls=%async_computation.1 | async-start | bytes 1572864 | tf_op jit(solution)/shard_map/all_to_all | solution.py:89
  173.6 23.8 %collective-permute-start.12 = (bf16[256,1536]{1,0:T(8,128)(2,1)}, bf16[256,1536]{1,0:T(8,128)(2,1)}, u32[]{:S(2)}, u32[]{:S(2)}) collective-permute-start(bf16[256,1536]{1,0:T(8,128)(2,1)} %get-tuple-element.241.refs_5_.cot_ref), channel_id=1, source_target_pairs={{0,1},{1,0},{2,3},{3,2},{4,5},{5,4},{6,7},{7,6},{8,9},{9,8},{10,11... | collective-permute-start | bytes 2359304 | tf_op jit(solution)/shard_map/ppermute | solution.py:48
  176.1 25.0 %collective-permute-start.13 = (bf16[256,1536]{1,0:T(8,128)(2,1)}, bf16[256,1536]{1,0:T(8,128)(2,1)}, u32[]{:S(2)}, u32[]{:S(2)}) collective-permute-start(bf16[256,1536]{1,0:T(8,128)(2,1)} %get-tuple-element.241.refs_5_.cot_ref), channel_id=1, source_target_pairs={{0,2},{1,3},{2,0},{3,1},{4,6},{5,7},{6,4},{7,5},{8,10},{9,11},{10,... | collective-permute-start | bytes 2359304 | tf_op jit(solution)/shard_map/ppermute | solution.py:48
  176.7 28.7 %all-to-all-start.2 = ((bf16[4,384,256]{2,1,0:T(8,128)(2,1)}), bf16[4,384,256]{2,1,0:T(8,128)(2,1)}, u32[]{:S(2)}, u32[]{:S(2)}) async-start(bf16[4,384,256]{2,1,0:T(8,128)(2,1)} %get-tuple-element.240.o_ref), calls=%async_computation.2 | async-start | bytes 1572864 | tf_op jit(solution)/shard_map/all_to_all | solution.py:89
  193.9 34.6 %collective-permute-start.14 = (bf16[256,1536]{1,0:T(8,128)(2,1)}, bf16[256,1536]{1,0:T(8,128)(2,1)S(1)}, u32[]{:S(2)}, u32[]{:S(2)}) collective-permute-start(bf16[256,1536]{1,0:T(8,128)(2,1)} %get-tuple-element.254.refs_0_), channel_id=1, source_target_pairs={{0,1},{1,0},{2,3},{3,2},{4,5},{5,4},{6,7},{7,6},{8,9},{9,8},{10,11... | collective-permute-start | bytes 2359304 | tf_op jit(solution)/shard_map/ppermute | solution.py:48
  195.9 32.6 %collective-permute-start.15 = (bf16[256,1536]{1,0:T(8,128)(2,1)}, bf16[256,1536]{1,0:T(8,128)(2,1)S(1)}, u32[]{:S(2)}, u32[]{:S(2)}) collective-permute-start(bf16[256,1536]{1,0:T(8,128)(2,1)} %get-tuple-element.254.refs_0_), channel_id=1, source_target_pairs={{0,2},{1,3},{2,0},{3,1},{4,6},{5,7},{6,4},{7,5},{8,10},{9,11},{10,... | collective-permute-start | bytes 2359304 | tf_op jit(solution)/shard_map/ppermute | solution.py:48
  205.4 23.1 %collective-permute-start.16 = (bf16[128,1536]{1,0:T(8,128)(2,1)S(1)}, bf16[128,1536]{1,0:T(8,128)(2,1)S(1)}, u32[]{:S(2)}, u32[]{:S(2)}) collective-permute-start(bf16[128,1536]{1,0:T(8,128)(2,1)S(1)} %slice.199), channel_id=1, source_target_pairs={{0,2},{1,3},{2,0},{3,1},{4,6},{5,7},{6,4},{7,5},{8,10},{9,11},{10,... | collective-permute-start | bytes 1179656 | tf_op jit(solution)/shard_map/ppermute | solution.py:48
  205.9 22.5 %collective-permute-start.17 = (bf16[128,1536]{1,0:T(8,128)(2,1)S(1)}, bf16[128,1536]{1,0:T(8,128)(2,1)S(1)}, u32[]{:S(2)}, u32[]{:S(2)}) collective-permute-start(bf16[128,1536]{1,0:T(8,128)(2,1)S(1)} %slice.200), channel_id=1, source_target_pairs={{0,1},{1,0},{2,3},{3,2},{4,5},{5,4},{6,7},{7,6},{8,9},{9,8},{10,11... | collective-permute-start | bytes 1179656 | tf_op jit(solution)/shard_map/ppermute | solution.py:48
  229.8 35.8 %collective-permute-start.18 = (bf16[256,1536]{1,0:T(8,128)(2,1)}, bf16[256,1536]{1,0:T(8,128)(2,1)S(1)}, u32[]{:S(2)}, u32[]{:S(2)}) collective-permute-start(bf16[256,1536]{1,0:T(8,128)(2,1)} %get-tuple-element.272.refs_0_), channel_id=1, source_target_pairs={{0,1},{1,0},{2,3},{3,2},{4,5},{5,4},{6,7},{7,6},{8,9},{9,8},{10,11... | collective-permute-start | bytes 2359304 | tf_op jit(solution)/shard_map/ppermute | solution.py:48
  231.4 34.3 %collective-permute-start.19 = (bf16[256,1536]{1,0:T(8,128)(2,1)}, bf16[256,1536]{1,0:T(8,128)(2,1)S(1)}, u32[]{:S(2)}, u32[]{:S(2)}) collective-permute-start(bf16[256,1536]{1,0:T(8,128)(2,1)} %get-tuple-element.272.refs_0_), channel_id=1, source_target_pairs={{0,2},{1,3},{2,0},{3,1},{4,6},{5,7},{6,4},{7,5},{8,10},{9,11},{10,... | collective-permute-start | bytes 2359304 | tf_op jit(solution)/shard_map/ppermute | solution.py:48
  241.4 33.7 %collective-permute-start.24 = (bf16[256,1536]{1,0:T(8,128)(2,1)S(1)}, bf16[256,1536]{1,0:T(8,128)(2,1)S(1)}, u32[]{:S(2)}, u32[]{:S(2)}) collective-permute-start(bf16[256,1536]{1,0:T(8,128)(2,1)S(1)} %get-tuple-element.263.refs_5_.cot_ref), channel_id=1, source_target_pairs={{0,1},{1,0},{2,3},{3,2},{4,5},{5,4},{6,7},{7,6},{8,9},{9,8},{10,11... | collective-permute-start | bytes 2359304 | tf_op jit(solution)/shard_map/ppermute | solution.py:48
  242.2 33.0 %collective-permute-start.25 = (bf16[256,1536]{1,0:T(8,128)(2,1)S(1)}, bf16[256,1536]{1,0:T(8,128)(2,1)}, u32[]{:S(2)}, u32[]{:S(2)}) collective-permute-start(bf16[256,1536]{1,0:T(8,128)(2,1)S(1)} %get-tuple-element.263.refs_5_.cot_ref), channel_id=1, source_target_pairs={{0,2},{1,3},{2,0},{3,1},{4,6},{5,7},{6,4},{7,5},{8,10},{9,11},{10,... | collective-permute-start | bytes 2359304 | tf_op jit(solution)/shard_map/ppermute | solution.py:48
  265.7 28.8 %collective-permute-start.22 = (bf16[128,1536]{1,0:T(8,128)(2,1)S(1)}, bf16[128,1536]{1,0:T(8,128)(2,1)S(1)}, u32[]{:S(2)}, u32[]{:S(2)}) collective-permute-start(bf16[128,1536]{1,0:T(8,128)(2,1)S(1)} %slice.203), channel_id=1, source_target_pairs={{0,2},{1,3},{2,0},{3,1},{4,6},{5,7},{6,4},{7,5},{8,10},{9,11},{10,... | collective-permute-start | bytes 1179656 | tf_op jit(solution)/shard_map/ppermute | solution.py:48
  267.3 27.3 %collective-permute-start.23 = (bf16[128,1536]{1,0:T(8,128)(2,1)}, bf16[128,1536]{1,0:T(8,128)(2,1)}, u32[]{:S(2)}, u32[]{:S(2)}) collective-permute-start(bf16[128,1536]{1,0:T(8,128)(2,1)} %slice.204), channel_id=1, source_target_pairs={{0,1},{1,0},{2,3},{3,2},{4,5},{5,4},{6,7},{7,6},{8,9},{9,8},{10,11... | collective-permute-start | bytes 1179656 | tf_op jit(solution)/shard_map/ppermute | solution.py:48
  295.6 42.0 %all-to-all-start.3 = ((bf16[4,256,1536]{2,1,0:T(8,128)(2,1)}), bf16[4,256,1536]{2,1,0:T(8,128)(2,1)}, u32[]{:S(2)}, u32[]{:S(2)}) async-start(bf16[4,256,1536]{2,1,0:T(8,128)(2,1)} %glu_back.2), calls=%async_computation.3 | async-start | bytes 6291456 | tf_op jit(solution)/shard_map/all_to_all | solution.py:89
  300.2 405.9 %reduce-scatter.9.cloned.1.call-start = ((), (), s32[]{:S(2)}) async-start(), calls=%async_computation.15 | async-start | bytes 5308416 | tf_op jit(solution)/shard_map/reduce_scatter | solution.py:969
  352.6 353.6 %reduce-scatter.19.cloned.1.call-start = ((), (), s32[]{:S(2)}) async-start(), calls=%async_computation.23 | async-start | bytes 7864320
  367.5 38.6 %all-to-all-start.4 = ((bf16[4,256,1536]{2,1,0:T(8,128)(2,1)}), bf16[4,256,1536]{2,1,0:T(8,128)(2,1)}, u32[]{:S(2)}, u32[]{:S(2)}) async-start(bf16[4,256,1536]{2,1,0:T(8,128)(2,1)} %glu_back.3), calls=%async_computation.5 | async-start | bytes 6291456 | tf_op jit(solution)/shard_map/all_to_all | solution.py:89
  372.3 333.9 %reduce-scatter.17.cloned.1.call-start = ((), (), s32[]{:S(2)}) async-start(), calls=%async_computation.19 | async-start | bytes 5308416 | tf_op jit(solution)/shard_map/reduce_scatter | solution.py:969
  406.1 22.4 %all-to-all-start.5 = ((bf16[4,384,256]{2,1,0:T(8,128)(2,1)}), bf16[4,384,256]{2,1,0:T(8,128)(2,1)S(1)}, u32[]{:S(2)}, u32[]{:S(2)}) async-start(bf16[4,384,256]{2,1,0:T(8,128)(2,1)} %bitcast.171), calls=%async_computation.6 | async-start | bytes 1572864 | tf_op jit(solution)/shard_map/all_to_all | solution.py:89
  445.6 23.6 %collective-permute-start.28 = (bf16[4,4,3,192,384]{4,3,2,1,0:T(8,128)(2,1)}, bf16[4,4,3,192,384]{4,3,2,1,0:T(8,128)(2,1)}, u32[]{:S(2)}, u32[]{:S(2)}) collective-permute-start(bf16[4,4,3,192,384]{4,3,2,1,0:T(8,128)(2,1)} %get-tuple-element.325), channel_id=1, source_target_pairs={{0,4},{4,0},{8,12},{12,8},{16,20},{20,16},{24,28},{28,24},{1,5},{5... | collective-permute-start | bytes 21233672 | tf_op jit(solution)/shard_map/ppermute | solution.py:48
  446.3 81.6 %collective-permute-start.29 = (bf16[768,256]{1,0:T(8,128)(2,1)}, bf16[768,256]{1,0:T(8,128)(2,1)}, u32[]{:S(2)}, u32[]{:S(2)}) collective-permute-start(bf16[768,256]{1,0:T(8,128)(2,1)} %get-tuple-element.400), channel_id=1, source_target_pairs={{0,1},{1,0},{2,3},{3,2},{4,5},{5,4},{6,7},{7,6},{8,9},{9,8},{10,11... | collective-permute-start | bytes 1179656 | tf_op jit(solution)/shard_map/ppermute | solution.py:48
  448.2 79.7 %collective-permute-start.30 = (bf16[768,256]{1,0:T(8,128)(2,1)}, bf16[768,256]{1,0:T(8,128)(2,1)}, u32[]{:S(2)}, u32[]{:S(2)}) collective-permute-start(bf16[768,256]{1,0:T(8,128)(2,1)} %get-tuple-element.399), channel_id=1, source_target_pairs={{0,2},{1,3},{2,0},{3,1},{4,6},{5,7},{6,4},{7,5},{8,10},{9,11},{10,... | collective-permute-start | bytes 1179656 | tf_op jit(solution)/shard_map/ppermute | solution.py:48
  449.6 78.3 %collective-permute-start.31 = (bf16[768,256]{1,0:T(8,128)(2,1)}, bf16[768,256]{1,0:T(8,128)(2,1)}, u32[]{:S(2)}, u32[]{:S(2)}) collective-permute-start(bf16[768,256]{1,0:T(8,128)(2,1)} %get-tuple-element.398), channel_id=1, source_target_pairs={{0,3},{1,2},{2,1},{3,0},{4,7},{5,6},{6,5},{7,4},{8,11},{9,10},{10,... | collective-permute-start | bytes 1179656 | tf_op jit(solution)/shard_map/ppermute | solution.py:48
  449.8 60.2 %all-to-all-start.6 = ((bf16[4,384,256]{2,1,0:T(8,128)(2,1)}), bf16[4,384,256]{2,1,0:T(8,128)(2,1)}, u32[]{:S(2)}, u32[]{:S(2)}) async-start(bf16[4,384,256]{2,1,0:T(8,128)(2,1)} %bitcast.39), calls=%async_computation.7 | async-start | bytes 1572864 | tf_op jit(solution)/shard_map/all_to_all | solution.py:89
  454.0 254.5 %reduce-scatter.15.cloned.1.call-start = ((), (), s32[]{:S(2)}) async-start(), calls=%async_computation.18 | async-start | bytes 5308416 | tf_op jit(solution)/shard_map/reduce_scatter | solution.py:969
  469.1 249.3 %reduce-scatter.13.cloned.1.call-start = ((), (), s32[]{:S(2)}) async-start(), calls=%async_computation.17 | async-start | bytes 2949120 | tf_op jit(solution)/shard_map/reduce_scatter | solution.py:1233
  485.7 28.1 %collective-permute-start.32 = (bf16[1152,384]{1,0:T(8,128)(2,1)}, bf16[1152,384]{1,0:T(8,128)(2,1)}, u32[]{:S(2)}, u32[]{:S(2)}) collective-permute-start(bf16[1152,384]{1,0:T(8,128)(2,1)} %get-tuple-element.389), channel_id=1, source_target_pairs={{0,2},{1,3},{2,0},{3,1},{4,6},{5,7},{6,4},{7,5},{8,10},{9,11},{10,... | collective-permute-start | bytes 2654216 | tf_op jit(solution)/shard_map/ppermute | solution.py:48
  487.7 26.1 %collective-permute-start.33 = (bf16[1152,384]{1,0:T(8,128)(2,1)}, bf16[1152,384]{1,0:T(8,128)(2,1)}, u32[]{:S(2)}, u32[]{:S(2)}) collective-permute-start(bf16[1152,384]{1,0:T(8,128)(2,1)} %get-tuple-element.390), channel_id=1, source_target_pairs={{0,1},{1,0},{2,3},{3,2},{4,5},{5,4},{6,7},{7,6},{8,9},{9,8},{10,11... | collective-permute-start | bytes 2654216 | tf_op jit(solution)/shard_map/ppermute | solution.py:48
  532.3 41.0 %collective-permute-start.35 = (bf16[2304,384]{1,0:T(8,128)(2,1)}, bf16[2304,384]{1,0:T(8,128)(2,1)}, u32[]{:S(2)}, u32[]{:S(2)}) collective-permute-start(bf16[2304,384]{1,0:T(8,128)(2,1)} %pad_maximum_fusion.4), channel_id=1, source_target_pairs={{0,2},{1,3},{2,0},{3,1},{4,6},{5,7},{6,4},{7,5},{8,10},{9,11},{10,... | collective-permute-start | bytes 5308424 | tf_op jit(solution)/shard_map/ppermute | solution.py:48
  533.9 40.6 %collective-permute-start.34 = (bf16[2304,384]{1,0:T(8,128)(2,1)}, bf16[2304,384]{1,0:T(8,128)(2,1)}, u32[]{:S(2)}, u32[]{:S(2)}) collective-permute-start(bf16[2304,384]{1,0:T(8,128)(2,1)} %pad_maximum_fusion.3), channel_id=1, source_target_pairs={{0,1},{1,0},{2,3},{3,2},{4,5},{5,4},{6,7},{7,6},{8,9},{9,8},{10,11... | collective-permute-start | bytes 5308424 | tf_op jit(solution)/shard_map/ppermute | solution.py:48
  535.3 39.1 %collective-permute-start.36 = (bf16[4,192,384]{2,1,0:T(8,128)(2,1)}, bf16[4,192,384]{2,1,0:T(8,128)(2,1)S(1)}, u32[]{:S(2)}, u32[]{:S(2)}) collective-permute-start(bf16[4,192,384]{2,1,0:T(8,128)(2,1)} %fusion.33), channel_id=1, source_target_pairs={{0,4},{4,0},{8,12},{12,8},{16,20},{20,16},{24,28},{28,24},{1,5},{5... | collective-permute-start | bytes 1769480 | tf_op jit(solution)/shard_map/ppermute | solution.py:48
  580.6 40.4 %all-to-all-start.7 = ((bf16[4,256,1536]{2,1,0:T(8,128)(2,1)}), bf16[4,256,1536]{2,1,0:T(8,128)(2,1)}, u32[]{:S(2)}, u32[]{:S(2)}) async-start(bf16[4,256,1536]{2,1,0:T(8,128)(2,1)} %self_back.2), calls=%async_computation.8 | async-start | bytes 6291456 | tf_op jit(solution)/shard_map/all_to_all | solution.py:89
  621.0 40.3 %all-to-all-start.8 = ((bf16[4,256,1536]{2,1,0:T(8,128)(2,1)}), bf16[4,256,1536]{2,1,0:T(8,128)(2,1)}, u32[]{:S(2)}, u32[]{:S(2)}) async-start(bf16[4,256,1536]{2,1,0:T(8,128)(2,1)} %self_back.3), calls=%async_computation.9 | async-start | bytes 6291456 | tf_op jit(solution)/shard_map/all_to_all | solution.py:89
  625.6 95.6 %reduce-scatter.11.cloned.1.call-start = ((), (), s32[]{:S(2)}) async-start(), calls=%async_computation.16 | async-start | bytes 3981312 | tf_op jit(solution)/shard_map/reduce_scatter | solution.py:969
  (86 other events, 1043.7 us)
Sparse Core Ops, SparseCore 0:
  22.1 28.9 all-gather.6
  53.7 51.6 all-gather.8
  107.0 50.5 all-gather.10
  352.7 56.3 reduce-scatter.8
  411.9 90.4 reduce-scatter.18
  504.6 53.9 reduce-scatter.16
  560.9 53.3 reduce-scatter.14
  616.5 46.4 reduce-scatter.12
  665.3 43.4 reduce-scatter.10
